TPU v7x, 32 devices: a whole 2x2x4 slice. The times are simulated.
32 devices in a mesh: wide: 4 (over y, core), group: 8 (over z, x).
Axes of the slice: x: 2, y: 2, z: 4, core: 2. Of those that a mesh axis runs over, the one named last changes fastest.
Arguments:
- queries: bfloat16 [10240, 256], P(('wide', 'group')), may hold values from -32 to 32
- items: bfloat16 [10240, 256], P(('wide', 'group')), may hold values from -20 to 20
- item_owner: int32 [10240, 1], P(('wide', 'group')), may hold values from 0 to 7; in each aligned block of 320 rows (0 to 319, 320 to 639, ...) at most 80 rows name the same one
- item_offset: int32 [10240], P(('wide', 'group')), may hold values from 0 to 639
- sample_counts: int32 [10240], P(('wide', 'group')), may hold values from 1 to 4095
- table: float32 [20480, 256], P(('wide', 'group')), may hold values from -3 to 3
- accum: float32 [20480, 256], P(('wide', 'group')), may hold values from 0.001 to 0.1
Outputs:
- loss: float32 [10240], P(('wide', 'group'))
- query_grad: float32 [10240, 256], P(('wide', 'group'))
- table_new: float32 [20480, 256], P(('wide', 'group'))
- accum_new: float32 [20480, 256], P(('wide', 'group'))
Inputs may be any that keep to these rules, and one draw needn't show every extreme that they name: `item_owner`: among the items of one device, at most 80 have the same owner.
All inputs are finite; a program needn't handle non-finite values.
Results may differ from a plain program's by a relative error of at most 0.005.
Values may be sent and summed in bfloat16 or wider, within the bound.
No kernel may reach another device: no remote copies, remote signals or barrier semaphores. Data moves between devices by JAX's collectives and lax.ppermute only.
A program may use at most 64 MiB of HBM per device.

v0:
```python
import math

import jax
import jax.numpy as jnp
from jax import lax
from jax.sharding import PartitionSpec as P

D = 256


def shards(queries, items, item_owner, item_offset, sample_counts, table, accum):
    block = queries.shape[0]
    scale = 3.0 / math.sqrt(D)
    wide_pos = lax.axis_index("wide")
    contract_last = (((1,), (1,)), ((), ()))
    contract_first = (((0,), (0,)), ((), ()))
    all_items, all_counts, all_queries = (
        lax.all_gather(items, "wide", axis=0, tiled=True),
        lax.all_gather(sample_counts, "wide", axis=0, tiled=True),
        lax.all_gather(queries, "wide", axis=0, tiled=True),
    )
    logits = (
        lax.dot_general(queries, all_items, contract_last, preferred_element_type=jnp.float32)
        * scale
    )
    logits = logits - jnp.log(all_counts.astype(jnp.float32))[None, :]
    totals = jax.nn.logsumexp(logits, axis=1)
    columns = jnp.arange(all_items.shape[0], dtype=jnp.int32)
    targets = wide_pos * block + jnp.arange(block, dtype=jnp.int32)
    hits = (columns[None, :] == targets[:, None]).astype(jnp.float32)
    chosen = jnp.sum(logits * hits, axis=1)
    loss = totals - chosen
    weights = (jnp.exp(logits - totals[:, None]) - hits).astype(jnp.bfloat16)
    query_grad = jnp.dot(weights, all_items, preferred_element_type=jnp.float32) * scale
    all_totals = lax.all_gather(totals, "wide", axis=0, tiled=True)
    local_logits = (
        lax.dot_general(all_queries, items, contract_last, preferred_element_type=jnp.float32)
        * scale
    )
    local_logits = local_logits - jnp.log(sample_counts.astype(jnp.float32))[None, :]
    query_index = jnp.arange(all_queries.shape[0], dtype=jnp.int32)
    local_hits = (query_index[:, None] == targets[None, :]).astype(jnp.float32)
    local_weights = (jnp.exp(local_logits - all_totals[:, None]) - local_hits).astype(jnp.bfloat16)
    item_grad = (
        lax.dot_general(
            local_weights, all_queries, contract_first, preferred_element_type=jnp.float32
        )
        * scale
    )
    groups = lax.axis_size("group")
    capacity = 2 * block // groups
    owner = item_owner[:, 0]
    member = (owner[:, None] == jnp.arange(groups, dtype=jnp.int32)[None, :]).astype(jnp.int32)
    rank = jnp.sum((jnp.cumsum(member, axis=0) - 1) * member, axis=1)
    slot = owner * capacity + rank
    send_values = jnp.zeros((groups * capacity, D), jnp.float32).at[slot].set(item_grad)
    send_rows = jnp.full((groups * capacity,), table.shape[0], jnp.int32).at[slot].set(item_offset)
    got_values, got_rows = (
        lax.all_to_all(
            send_values.reshape(groups, capacity, D),
            "group",
            split_axis=0,
            concat_axis=0,
            tiled=True,
        ),
        lax.all_to_all(
            send_rows.reshape(groups, capacity), "group", split_axis=0, concat_axis=0, tiled=True
        ),
    )
    grad = (
        jnp.zeros(table.shape, jnp.float32)
        .at[got_rows.reshape(-1)]
        .add(got_values.reshape(-1, D), mode="drop")
    )
    accum_new = accum + grad * grad
    table_new = table - 0.1 * grad / (jnp.sqrt(accum_new) + 1e-08)
    return (loss, query_grad, table_new, accum_new)


def solution(mesh):
    placed = (
        P(("wide", "group"), None),
        P(("wide", "group"), None),
        P(("wide", "group"), None),
        P(("wide", "group")),
        P(("wide", "group")),
        P(("wide", "group"), None),
        P(("wide", "group"), None),
    )
    return jax.shard_map(
        shards,
        mesh=mesh,
        in_specs=placed,
        out_specs=(
            P(("wide", "group")),
            P(("wide", "group"), None),
            P(("wide", "group"), None),
            P(("wide", "group"), None),
        ),
        check_vma=False,
    )
```

profile of v0, /device:TPU:0, one launch (start us, length us, event | category | flops | bytes accessed | tf_op | source)
XLA Modules:
  0.0 82.2 jit_solution(13810421051104430959)
XLA Ops:
  0.6 0.0 copy-start
  0.6 0.7 reduce
  1.4 0.9 %reduce-window.6 = s32[8,3,128]{2,0,1:T(8,128)S(1)} reduce-window(s32[8,3,128]{2,0,1:T(8,128)S(1)} %convert_bitcast_fusion, s32[]{:T(128)} %constant.20.clone.1), window={size=1x1x128 pad=0_0x0_0x127_0}, to_apply=%region_3.0 | reduce-window | flops 390144 | bytes 24580 | tf_op jit(solution)/shard_map/reduce-window
  2.3 0.2 slice_reduce_fusion
  2.5 0.1 add_bitcast_fusion
  2.6 0.7 fusion.23
  3.3 3.1 %scatter_custom_fusion = s32[640]{0:T(1024)S(1)} fusion(s32[320]{0:T(512)S(1)} %fusion.23, s32[320]{0:T(512)} %param.10, s32[]{:T(128)} %constant.17.clone.1), kind=kCustom, calls=%fused_computation.45 | custom fusion | bytes 3072 | tf_op jit(solution)/shard_map/scatter | solution.py:57
  6.4 0.7 all_to_all.9
  7.1 7.3 %all-to-all-start = ((s32[8,1,80]{2,1,0:T(1,128)}), s32[8,1,80]{2,1,0:T(1,128)S(1)}, u32[]{:S(2)}, u32[]{:S(2)}) async-start(s32[8,1,80]{2,1,0:T(1,128)} %all_to_all.9), calls=%async_computation | async-start | bytes 8192 | tf_op jit(solution)/shard_map/all_to_all | solution.py:66
  14.4 0.7 convert_log_fusion.1
  15.0 1.2 %dynamic-slice = u32[1]{0:T(128)} dynamic-slice(u32[32]{0:T(128)} %constant.45, u32[]{:T(128)S(6)} %add.61), dynamic_slice_sizes={1} | dynamic-slice | bytes 12
  16.9 0.9 %dynamic-update-slice = s32[1280]{0:T(1024)S(1)} dynamic-update-slice(s32[1280]{0:T(1024)S(1)} %broadcast.79, s32[320]{0:T(512)} %param.11, u32[]{:T(128)} %bitcast) | dynamic-update-slice | bytes 2564
  17.8 5.0 %all-reduce.1 = s32[1280]{0:T(1024)S(1)} all-reduce(s32[1280]{0:T(1024)S(1)} %dynamic-update-slice), channel_id=1, replica_groups=mesh['wide'=4,'group'=8] {'wide'}, use_global_device_ids=true, to_apply=%add.1 | all-reduce | flops 1280 | bytes 10240
  22.8 7.5 %all_gather.12 = bf16[1280,256]{1,0:T(8,128)(2,1)S(1)} all-gather(bf16[320,256]{1,0:T(8,128)(2,1)} %param.8), channel_id=1, replica_groups=mesh['wide'=4,'group'=8] {'wide'}, dimensions={0}, use_global_device_ids=true | all-gather | bytes 819200 | tf_op jit(solution)/shard_map/all_gather | solution.py:18
  30.3 8.2 %all_gather.14 = bf16[1280,256]{1,0:T(8,128)(2,1)S(1)} all-gather(bf16[320,256]{1,0:T(8,128)(2,1)} %param.7), channel_id=1, replica_groups=mesh['wide'=4,'group'=8] {'wide'}, dimensions={0}, use_global_device_ids=true | all-gather | bytes 819200 | tf_op jit(solution)/shard_map/all_gather | solution.py:20
  38.5 0.0 copy-done
  38.5 0.0 copy-start.1
  38.5 0.5 fusion.26
  39.1 0.7 select_reduce_fusion
  39.7 0.1 fusion.25
  39.8 6.9 %all-reduce.2 = f32[1280]{0:T(1024)S(1)} all-reduce(f32[1280]{0:T(1024)S(1)} %get-tuple-element.8), channel_id=1, replica_groups=mesh['wide'=4,'group'=8] {'wide'}, use_global_device_ids=true, to_apply=%add.2 | all-reduce | flops 1280 | bytes 10240
  46.7 0.0 copy-done.1
  46.7 2.0 %fusion.7 = f32[320,256]{1,0:T(8,128)} fusion(bf16[1280,256]{1,0:T(8,128)(2,1)S(1)} %all_gather.14, bf16[320,256]{1,0:T(8,128)(2,1)S(1)} %copy-done.1, s32[320]{0:T(512)S(1)} %iota_add_fusion, f32[1280]{0:T(1024)S(1)} %all-reduce.2, f32[320]{0:T(512)S(1)} %convert_log_fusion.1), kind=kOutput, calls=%fused_computation.17 | convolution fusion | flops 422379520 | bytes 1154560 | tf_op jit(solution)/shard_map/dot_general | solution.py:45
  48.7 2.9 %scatter_custom_fusion.1 = f32[640,256]{1,0:T(8,128)} fusion(s32[320]{0:T(512)S(1)} %fusion.23, f32[320,256]{1,0:T(8,128)} %fusion.7, f32[]{:T(128)} %constant.14.clone.1), kind=kCustom, calls=%fused_computation.29 | custom fusion | bytes 655872 | tf_op jit(solution)/shard_map/scatter | solution.py:56
  51.6 0.0 all-to-all-done
  51.6 6.0 %all-to-all-start.1 = ((f32[8,80,256]{2,1,0:T(8,128)}), f32[8,80,256]{2,1,0:T(8,128)S(1)}, u32[]{:S(2)}, u32[]{:S(2)}) async-start(f32[8,80,256]{2,1,0:T(8,128)} %bitcast.4), calls=%async_computation.1 | async-start | bytes 1310720 | tf_op jit(solution)/shard_map/all_to_all | solution.py:59
  57.6 0.6 sub.60
  58.2 1.3 %convolution_multiply_fusion.2 = f32[320,256]{1,0:T(8,128)} fusion(bf16[1280,256]{1,0:T(8,128)(2,1)S(1)} %all_gather.12, f32[320,1280]{1,0:T(8,128)S(1)} %get-tuple-element.11, f32[320]{0:T(512)S(1)} %get-tuple-element.9, s32[320]{0:T(512)S(1)} %iota_add_fusion), kind=kOutput, calls=%fused_computation.18 | convolution fusion | flops 211845120 | bytes 2624000 | tf_op jit(solution)/shard_map/dot_general | solution.py:34
  59.5 0.5 broadcast.103
  60.0 0.7 reduce.10
  60.7 0.1 reshape.86
  60.8 13.0 %all-to-all-done.1 = f32[8,80,256]{2,1,0:T(8,128)S(1)} async-done(((f32[8,80,256]{2,1,0:T(8,128)}), f32[8,80,256]{2,1,0:T(8,128)S(1)}, u32[]{:S(2)}, u32[]{:S(2)}) %all-to-all-start.1) | async-done | bytes 655392 | tf_op jit(solution)/shard_map/all_to_all | solution.py:59
  73.8 5.7 %scatter_custom_fusion.2 = f32[640,256]{1,0:T(8,128)S(1)} fusion(s32[640]{0:T(1024)S(1)} %fusion.20, f32[640,256]{1,0:T(8,128)S(1)} %bitcast.16, f32[]{:T(128)} %constant.14.clone.1), kind=kCustom, calls=%fused_computation.27 | custom fusion | flops 163840 | bytes 655364 | tf_op jit(solution)/shard_map/scatter-add | solution.py:73
  79.5 2.7 %divide_subtract_fusion = (f32[640,256]{1,0:T(8,128)}, f32[640,256]{1,0:T(8,128)}) fusion(f32[640,256]{1,0:T(8,128)} %param.12, f32[640,256]{1,0:T(8,128)S(1)} %scatter_custom_fusion.2, f32[640,256]{1,0:T(8,128)} %param.13), kind=kLoop, calls=%fused_computation.25 | loop fusion | flops 983040 | bytes 3276800 | tf_op jit(solution)/shard_map/sub | solution.py:76
  (10 shorter events, 0.1 us)
Async XLA Ops:
  0.6 37.9 %copy-start = (bf16[320,256]{1,0:T(8,128)(2,1)S(1)}, bf16[320,256]{1,0:T(8,128)(2,1)}, u32[]{:S(2)}) copy-start(bf16[320,256]{1,0:T(8,128)(2,1)} %param.7) | copy-start | bytes 491524
  7.1 44.5 %all-to-all-start = ((s32[8,1,80]{2,1,0:T(1,128)}), s32[8,1,80]{2,1,0:T(1,128)S(1)}, u32[]{:S(2)}, u32[]{:S(2)}) async-start(s32[8,1,80]{2,1,0:T(1,128)} %all_to_all.9), calls=%async_computation | async-start | bytes 8192 | tf_op jit(solution)/shard_map/all_to_all | solution.py:66
  38.5 8.2 %copy-start.1 = (bf16[320,256]{1,0:T(8,128)(2,1)S(1)}, bf16[320,256]{1,0:T(8,128)(2,1)}, u32[]{:S(2)}) copy-start(bf16[320,256]{1,0:T(8,128)(2,1)} %param.8) | copy-start | bytes 491524
  51.6 22.2 %all-to-all-start.1 = ((f32[8,80,256]{2,1,0:T(8,128)}), f32[8,80,256]{2,1,0:T(8,128)S(1)}, u32[]{:S(2)}, u32[]{:S(2)}) async-start(f32[8,80,256]{2,1,0:T(8,128)} %bitcast.4), calls=%async_computation.1 | async-start | bytes 1310720 | tf_op jit(solution)/shard_map/all_to_all | solution.py:59
where the time goes:
time: 82.7 us; the launch traced here: 82.2 us
  blocking collectives  27.5 us (33%)
  other arithmetic  13.5 us (16%)
  starting transfers between devices  13.3 us (16%)
  waiting for transfers between devices  13 us (16%)
  local copies, waits for them, and re-layouts  9.59 us (12%)
  matrix products  3.84 us (5%)
  between operations  1.39 us (2%)
    all_to_all x1, waiting for transfers between devices, shards(): lax.all_to_all(send_values.reshape(groups, capacity, D), 'group', split_a...  13 us
    unnamed x2, blocking collectives  11.9 us
    all_gather x1, blocking collectives, shards(): lax.all_gather(queries, 'wide', axis=0, tiled=True)  8.2 us
    all_gather x1, blocking collectives, shards(): lax.all_gather(items, 'wide', axis=0, tiled=True)  7.47 us
    all_to_all x1, starting transfers between devices, shards(): lax.all_to_all(send_rows.reshape(groups, capacity), 'group', split_axis=0...  7.25 us
    all_to_all x1, starting transfers between devices, shards(): lax.all_to_all(send_values.reshape(groups, capacity, D), 'group', split_a...  6 us
    scatter-add x1, other arithmetic, shards(): grad = jnp.zeros(table.shape, jnp.float32).at[got_rows.reshape(-1)].add(g...  5.69 us
    scatter x1, local copies, waits for them, and re-layouts, shards(): jnp.full((groups * capacity,), table.shape[0], jnp.int32).at[slot]  3.08 us
  transfers between devices with their start and end apart: 2, of which 1 were waited for; matrix products, arithmetic and copies ran while one was open for 15% of the time, Pallas kernels for 0%

commit v1 on v0

v1 whole, which is shorter than its diff:
```python
import functools
import math

import jax
import jax.numpy as jnp
from jax import lax
from jax.experimental import pallas as pl
from jax.experimental.pallas import tpu as pltpu
from jax.sharding import PartitionSpec as P

D = 256
SCALE = 3.0 / math.sqrt(D)
LANES = 128
TAIL = 8
MIB = 1 << 20
NT = (((1,), (1,)), ((), ()))
TN = (((0,), (0,)), ((), ()))
F32 = jnp.float32
BF16 = jnp.bfloat16


def dot(a, b, dims=(((1,), (0,)), ((), ()))):
    return lax.dot_general(a, b, dims, preferred_element_type=F32)


def spread(column, width):
    pieces = [column] * (width // LANES)
    if width % LANES:
        pieces.append(column[:, : width % LANES])
    return jnp.concatenate(pieces, axis=1)


def code(x):
    y = x * x
    return jnp.where(x < 0, -y, y) * y


def decode(u):
    root = lax.rsqrt(lax.rsqrt(jnp.abs(u)))
    return jnp.where(u < 0, -root, root)


def route_kernel(groups, capacity, owner_ref, offset_ref, pick_ref, tail_ref):
    block = owner_ref.shape[1]
    owner = owner_ref[...]
    member = lax.broadcasted_iota(jnp.int32, (groups, block), 0) == owner
    before = lax.broadcasted_iota(jnp.int32, (block, block), 0) < lax.broadcasted_iota(
        jnp.int32, (block, block), 1
    )
    ranks = dot(member.astype(BF16), before.astype(BF16))
    rank = jnp.sum(jnp.where(member, ranks, 0.0), axis=0, keepdims=True).astype(jnp.int32)
    offset = offset_ref[...]
    high = jnp.broadcast_to((offset // LANES).astype(F32), (TAIL, block)).astype(BF16)
    low = jnp.broadcast_to((offset % LANES).astype(F32), (TAIL, block)).astype(BF16)
    slots = lax.broadcasted_iota(jnp.int32, (LANES, block), 0)
    here = slots == rank
    for g in range(groups):
        pick = (here & (owner == g)).astype(F32).astype(BF16)
        pick_ref[g] = pick[:capacity]
        tail_ref[g] = jnp.concatenate([dot(high, pick, NT), dot(low, pick, NT)], axis=1).astype(BF16)


def own_kernel(n, q_ref, *refs):
    item_refs, count_refs = refs[:n], refs[n : 2 * n]
    loss_ref, query_grad_ref, mine_ref, mate_ref, bias_ref, logits_ref = refs[2 * n :]
    block = q_ref.shape[0]
    q = q_ref[...]
    top = None
    for b in range(n):
        row = jnp.log(count_refs[b][...])
        bias = jnp.transpose(jnp.broadcast_to(row, (LANES, block)))
        bias_ref[b] = bias
        logits = dot(item_refs[b][...], q, NT) * SCALE - spread(bias, block)
        logits_ref[b] = logits
        high = jnp.max(logits, axis=0, keepdims=True)
        top = high if top is None else jnp.maximum(top, high)
    hit = lax.broadcasted_iota(jnp.int32, (block, block), 0) == lax.broadcasted_iota(
        jnp.int32, (block, block), 1
    )
    chosen = jnp.sum(jnp.where(hit, logits_ref[0], 0.0), axis=0, keepdims=True)
    total = jnp.zeros((1, block), F32)
    for b in range(n):
        e = jnp.exp(logits_ref[b] - top)
        logits_ref[b] = e
        total += jnp.sum(e, axis=0, keepdims=True)
    loss_ref[...] = top + jnp.log(total) - chosen
    inverse = 1.0 / total
    query_grad = jnp.zeros((block, D), F32)
    for b in range(n):
        weights = logits_ref[b] * inverse
        if b == 0:
            weights = jnp.where(hit, weights - 1.0, weights)
        weights = weights.astype(BF16)
        if b < 2:
            (mine_ref, mate_ref)[b][...] = dot(weights, q)
        query_grad += dot(weights, item_refs[b][...], TN)
    query_grad_ref[...] = query_grad * SCALE


def far_kernel(n, q_ref, *refs):
    item_refs = refs[:n]
    bias_ref, mine_ref, mate_ref, mine_out, mate_out, logits_ref = refs[n:]
    block = q_ref.shape[0]
    q = q_ref[...]
    top = None
    for b in range(n):
        logits = dot(item_refs[b][...], q, NT) * SCALE - spread(bias_ref[b], block)
        logits_ref[b] = logits
        high = jnp.max(logits, axis=0, keepdims=True)
        top = high if top is None else jnp.maximum(top, high)
    total = jnp.zeros((1, block), F32)
    for b in range(n):
        e = jnp.exp(logits_ref[b] - top)
        if b < 2:
            logits_ref[b] = e
        total += jnp.sum(e, axis=0, keepdims=True)
    inverse = 1.0 / total
    mate_out[...] = mate_ref[...] + dot((logits_ref[1] * inverse).astype(BF16), q)
    mine_out[...] = mine_ref[...] + dot((logits_ref[0] * inverse).astype(BF16), q)


def pack_kernel(groups, capacity, pick_ref, tail_ref, mine_ref, other_ref, out_ref):
    grad = code((mine_ref[...] + other_ref[...]) * SCALE).astype(BF16)
    for g in range(groups):
        out_ref[g, :capacity] = dot(pick_ref[g], grad).astype(BF16)
        out_ref[g, capacity:] = tail_ref[g]


def update_kernel(groups, capacity, got_ref, table_ref, accum_ref, table_out, accum_out):
    rows = table_ref.shape[0]
    first = pl.program_id(0) * rows
    index = lax.broadcasted_iota(jnp.int32, (rows, LANES), 0) + first
    index = index.astype(F32)
    grad = jnp.zeros((rows, D), F32)
    for g in range(groups):
        tail = got_ref[g, capacity : capacity + TAIL].astype(F32)[:1]
        ids = tail[:, :LANES] * LANES + tail[:, LANES:]
        put = (index == ids).astype(F32).astype(BF16)
        values = decode(got_ref[g, :capacity].astype(F32))
        high = values.astype(BF16)
        low = (values - high.astype(F32)).astype(BF16)
        both = jnp.concatenate([high, low], axis=1)
        empty = jnp.zeros((LANES - capacity, 2 * D), BF16)
        sums = dot(put, jnp.concatenate([both, empty], axis=0))
        grad += sums[:, :D] + sums[:, D:]
    accum_new = accum_ref[...] + grad * grad
    accum_out[...] = accum_new
    table_out[...] = table_ref[...] - 0.1 * grad / (jnp.sqrt(accum_new) + 1e-08)


def call(kernel, outs, *args, scratch=(), limit=16, flops=0):
    return pl.pallas_call(
        kernel,
        out_shape=[jax.ShapeDtypeStruct(s, t) for s, t in outs],
        scratch_shapes=list(scratch),
        compiler_params=pltpu.CompilerParams(vmem_limit_bytes=limit * MIB),
        cost_estimate=pl.CostEstimate(flops=flops, bytes_accessed=1 << 20, transcendentals=0),
    )(*args)


def shards(queries, items, item_owner, item_offset, sample_counts, table, accum):
    block = queries.shape[0]
    n, groups = lax.axis_size("wide"), lax.axis_size("group")
    capacity = 2 * block // groups
    slots = -(-capacity // TAIL) * TAIL

    def swap(x, k):
        return lax.ppermute(x, "wide", [(i, i ^ k) for i in range(n)])

    counts = sample_counts.astype(F32).reshape(1, block)
    far_items = [swap(items, k) for k in range(2, n, 2)]
    far_queries = [swap(queries, k) for k in range(2, n, 2)]
    mate_items = swap(items, 1)
    far_counts = [swap(counts, k) for k in range(1, n)]
    mate_far_items = [swap(x, 1) for x in far_items]
    item_blocks = [items, mate_items]
    count_blocks = [counts, far_counts[0]]
    for k in range(len(far_items)):
        item_blocks += [far_items[k], mate_far_items[k]]
        count_blocks += [far_counts[2 * k + 1], far_counts[2 * k + 2]]

    pick, tail = call(
        functools.partial(route_kernel, groups, slots),
        [((groups, slots, block), BF16), ((groups, TAIL, D), BF16)],
        item_owner.reshape(1, block),
        item_offset.reshape(1, block),
        flops=2 * groups * block * block,
    )
    part = ((block, D), F32)
    logits = pltpu.VMEM((n, block, block), F32)
    limit = 8 + 4 * n
    loss, query_grad, mine, mate, bias = call(
        functools.partial(own_kernel, n),
        [((1, block), F32), part, part, part, ((n, block, LANES), F32)],
        queries,
        *item_blocks,
        *count_blocks,
        scratch=[logits],
        limit=limit,
        flops=6 * n * block * block * D,
    )
    for far in far_queries:
        mine, mate = call(
            functools.partial(far_kernel, n),
            [part, part],
            far,
            *item_blocks,
            bias,
            mine,
            mate,
            scratch=[logits],
            limit=limit,
            flops=4 * n * block * block * D,
        )
    other = swap(mate, 1)
    (packed,) = call(
        functools.partial(pack_kernel, groups, slots),
        [((groups, slots + TAIL, D), BF16)],
        pick,
        tail,
        mine,
        other,
        flops=2 * groups * slots * block * D,
    )
    got = lax.all_to_all(packed, "group", split_axis=0, concat_axis=0, tiled=True)

    rows = table.shape[0]
    step = rows // 5
    spec = pl.BlockSpec((step, D), lambda i: (i, 0))
    table_new, accum_new = pl.pallas_call(
        functools.partial(update_kernel, groups, slots),
        out_shape=[jax.ShapeDtypeStruct(table.shape, F32)] * 2,
        grid=(rows // step,),
        in_specs=[pl.BlockSpec(got.shape, lambda i: (0, 0, 0)), spec, spec],
        out_specs=[spec, spec],
        compiler_params=pltpu.CompilerParams(vmem_limit_bytes=16 * MIB),
    )(got, table, accum)
    return (loss.reshape(block), query_grad, table_new, accum_new)


def solution(mesh):
    placed = (
        P(("wide", "group"), None),
        P(("wide", "group"), None),
        P(("wide", "group"), None),
        P(("wide", "group")),
        P(("wide", "group")),
        P(("wide", "group"), None),
        P(("wide", "group"), None),
    )
    return jax.shard_map(
        shards,
        mesh=mesh,
        in_specs=placed,
        out_specs=(
            P(("wide", "group")),
            P(("wide", "group"), None),
            P(("wide", "group"), None),
            P(("wide", "group"), None),
        ),
        check_vma=False,
    )
```

time: 82.7 us -> 45.3 us (0.55)
  blocking collectives: 27.5 us -> 0 us
  other arithmetic: 13.5 us -> 1.28 us
  Pallas kernels: 0 us -> 9.56 us
  local copies, waits for them, and re-layouts: 9.59 us -> 2.53 us
  waiting for transfers between devices: 13 us -> 18.7 us
  matrix products: 3.84 us -> 0 us
  starting transfers between devices: 13.3 us -> 12.3 us
    all_gather x2 -> x0, blocking collectives: 15.7 us -> none  [the longest x1 8.2 us: shards(): lax.all_gather(queries, 'wide', axis=0, tiled=True)]
    unnamed x2 -> x0, blocking collectives: 11.9 us -> none
    pallas_call x0 -> x5, Pallas kernels: none -> 9.56 us  [the longest x4 5.87 us: call(): pl.pallas_call(kernel, out_shape=[jax.ShapeDtypeStruct(s, t) for s, t in...]
    ppermute x0 -> x8, waiting for transfers between devices: none -> 7.69 us  [swap(): return lax.ppermute(x, 'wide', [(i, i ^ k) for i in range(n)])]
    all_to_all x2 -> x1, starting transfers between devices: 13.3 us -> 6.15 us  [shards(): lax.all_to_all(packed, 'group', split_axis=0, concat_axis=0, tiled=True)]
    ppermute x0 -> x8, starting transfers between devices: none -> 6.15 us  [swap(): return lax.ppermute(x, 'wide', [(i, i ^ k) for i in range(n)])]
    scatter x2 -> x0, local copies, waits for them, and re-layouts: 5.96 us -> none  [the longest x1 3.08 us: shards(): jnp.full((groups * capacity,), table.shape[0], jnp.int32).at[slot]]
    scatter-add x1 -> x0, other arithmetic: 5.69 us -> none  [shards(): grad = jnp.zeros(table.shape, jnp.float32).at[got_rows.reshape(-1)].add(g...]
  transfers between devices with their start and end apart: 2 -> 9, of which waited for: 1 -> 4; matrix products, arithmetic and copies ran while one was open for 15% -> 3% of each run, Pallas kernels for 0% -> 8%
where the time goes in v1:
time: 45.3 us; the launch traced here: 45 us
  waiting for transfers between devices  18.7 us (41%)
  starting transfers between devices  12.3 us (27%)
  Pallas kernels  9.56 us (21%)
  local copies, waits for them, and re-layouts  2.53 us (6%)
  other arithmetic  1.28 us (3%)
  between operations  0.67 us (1%)
    all_to_all x1, waiting for transfers between devices, shards(): lax.all_to_all(packed, 'group', split_axis=0, concat_axis=0, tiled=True)  11 us
    ppermute x8, waiting for transfers between devices, swap(): return lax.ppermute(x, 'wide', [(i, i ^ k) for i in range(n)])  7.69 us
    ppermute x8, starting transfers between devices, swap(): return lax.ppermute(x, 'wide', [(i, i ^ k) for i in range(n)])  6.15 us
    all_to_all x1, starting transfers between devices, shards(): lax.all_to_all(packed, 'group', split_axis=0, concat_axis=0, tiled=True)  6.15 us
    pallas_call x4, Pallas kernels, call(): pl.pallas_call(kernel, out_shape=[jax.ShapeDtypeStruct(s, t) for s, t in...  5.87 us
    pallas_call x1, Pallas kernels, shards(): pl.pallas_call(functools.partial(update_kernel, groups, slots), out_shape...  3.69 us
    unnamed x14, local copies, waits for them, and re-layouts  2.52 us
  transfers between devices with their start and end apart: 9, of which 4 were waited for; matrix products, arithmetic and copies ran while one was open for 3% of the time, Pallas kernels for 8%

profile of v1, /device:TPU:0, one launch (start us, length us, event | category | flops | bytes accessed | tf_op | source)
XLA Modules:
  0.0 45.0 jit_solution(12099940039294359581)
XLA Ops:
  0.6 3.0 %collective-permute-start.1 = (bf16[320,256]{1,0:T(8,128)(2,1)}, bf16[320,256]{1,0:T(8,128)(2,1)S(1)}, u32[]{:S(2)}, u32[]{:S(2)}) collective-permute-start(bf16[320,256]{1,0:T(8,128)(2,1)} %refs_0_.3), channel_id=1, source_target_pairs={{0,16},{8,24},{16,0},{24,8},{1,17},{9,25},{17,1},{25,9},{2,18},{10... | collective-permute-start | bytes 491528 | tf_op jit(solution)/shard_map/ppermute | solution.py:168
  3.7 0.0 collective-permute-start
  3.7 4.4 %collective-permute-done.1.refs_2_ = bf16[320,256]{1,0:T(8,128)(2,1)S(1)} collective-permute-done((bf16[320,256]{1,0:T(8,128)(2,1)}, bf16[320,256]{1,0:T(8,128)(2,1)S(1)}, u32[]{:S(2)}, u32[]{:S(2)}) %collective-permute-start.1) | collective-permute-done | bytes 163872 | tf_op jit(solution)/shard_map/ppermute | solution.py:168
  8.1 0.0 collective-permute-start.2
  8.1 1.7 %collective-permute-start.6 = (bf16[320,256]{1,0:T(8,128)(2,1)}, bf16[320,256]{1,0:T(8,128)(2,1)S(1)}, u32[]{:S(2)}, u32[]{:S(2)}) collective-permute-start(bf16[320,256]{1,0:T(8,128)(2,1)} %q_ref.1), channel_id=1, source_target_pairs={{0,16},{8,24},{16,0},{24,8},{1,17},{9,25},{17,1},{25,9},{2,18},{10... | collective-permute-start | bytes 491528 | tf_op jit(solution)/shard_map/ppermute | solution.py:168
  9.8 0.7 %convert_element_type.3 = f32[320]{0:T(512)S(1)} convert(s32[320]{0:T(512)} %param.11) | non-fusion elementwise | flops 320 | bytes 2560 | tf_op jit(solution)/shard_map/convert_element_type | solution.py:170
  10.5 0.2 collective-permute-start.3
  10.7 0.3 collective-permute-start.4
  11.0 0.6 %collective-permute-done.3.refs_5_ = f32[1,320]{1,0:T(1,128)S(1)} collective-permute-done((f32[1,320]{1,0:T(1,128)S(1)}, f32[1,320]{1,0:T(1,128)S(1)}, u32[]{:S(2)}, u32[]{:S(2)}) %collective-permute-start.3) | collective-permute-done | bytes 1312 | tf_op jit(solution)/shard_map/ppermute | solution.py:168
  11.7 0.7 %collective-permute-start.5 = (f32[1,320]{1,0:T(1,128)S(1)}, f32[1,320]{1,0:T(1,128)S(1)}, u32[]{:S(2)}, u32[]{:S(2)}) collective-permute-start(f32[1,320]{1,0:T(1,128)S(1)} %reshape.20.refs_4_), channel_id=1, source_target_pairs={{0,24},{8,16},{16,8},{24,0},{1,25},{9,17},{17,9},{25,1},{2,26},{10... | collective-permute-start | bytes 3848 | tf_op jit(solution)/shard_map/ppermute | solution.py:168
  12.4 2.6 %collective-permute-done.4.refs_6_ = f32[1,320]{1,0:T(1,128)S(1)} collective-permute-done((f32[1,320]{1,0:T(1,128)S(1)}, f32[1,320]{1,0:T(1,128)S(1)}, u32[]{:S(2)}, u32[]{:S(2)}) %collective-permute-start.4) | collective-permute-done | bytes 1312 | tf_op jit(solution)/shard_map/ppermute | solution.py:168
  15.0 0.0 collective-permute-done.5.refs_7_
  15.0 0.0 collective-permute-done.refs_1_
  15.0 0.0 collective-permute-done.2.refs_3_
  15.0 0.0 copy-start.2
  15.0 0.9 %copy-done.2 = bf16[320,256]{1,0:T(8,128)(2,1)S(1)} copy-done((bf16[320,256]{1,0:T(8,128)(2,1)S(1)}, bf16[320,256]{1,0:T(8,128)(2,1)}, u32[]{:S(2)}) %copy-start.2) | copy-done | bytes 163864
  15.9 0.0 copy-start.4
  15.9 0.9 %copy-done.4 = bf16[320,256]{1,0:T(8,128)(2,1)S(1)} copy-done((bf16[320,256]{1,0:T(8,128)(2,1)S(1)}, bf16[320,256]{1,0:T(8,128)(2,1)}, u32[]{:S(2)}) %copy-start.4) | copy-done | bytes 163864
  16.8 0.0 copy-start.3
  16.8 2.8 %shard_map.102 = (f32[1,320]{1,0:T(1,128)S(1)}, f32[320,256]{1,0:T(8,128)}, f32[320,256]{1,0:T(8,128)S(1)}, f32[320,256]{1,0:T(8,128)S(1)}, f32[4,320,128]{2,1,0:T(8,128)S(1)}) custom-call(bf16[320,256]{1,0:T(8,128)(2,1)S(1)} %copy-done.4, bf16[320,256]{1,0:T(8,128)(2,1)S(1)} %copy-done.2, bf16[320,256]{1,0:T(8,128)(2,1)S(1)} %collective-permute-done.refs_1_, ...), custom_call_target="tpu_custom_call" | custom-call | flops 629145600 | bytes 1048576 | tf_op jit(solution)/shard_map/pallas_call | solution.py:152
  19.6 0.0 collective-permute-done.6.q_ref
  19.6 0.0 copy-done.3
  19.6 0.0 copy-start.6
  19.6 1.1 %shard_map.104 = (f32[320,256]{1,0:T(8,128)S(1)}, f32[320,256]{1,0:T(8,128)S(1)}) custom-call(bf16[320,256]{1,0:T(8,128)(2,1)S(1)} %collective-permute-done.6.q_ref, bf16[320,256]{1,0:T(8,128)(2,1)S(1)} %copy-done.3, bf16[320,256]{1,0:T(8,128)(2,1)S(1)} %collective-permute-done.refs_1_, bf16[320,256]{1,0:T(8,128)(2,1)S(1)} %collective-permute-done.1.refs_2_, ...), custom_call_target="tpu_custom_call" | custom-call | flops 419430400 | bytes 1048576 | tf_op jit(solution)/shard_map/pallas_call | solution.py:152
  20.7 0.1 collective-permute-start.7
  20.9 0.0 copy-done.6
  20.9 0.0 copy-start.5
  20.9 0.7 %copy-done.5 = s32[320,1]{0,1:T(1,128)S(1)} copy-done((s32[320,1]{0,1:T(1,128)S(1)}, s32[320,1]{0,1:T(1,128)}, u32[]{:S(2)}) %copy-start.5) | copy-done | bytes 1304
  21.5 0.8 %shard_map.103 = (bf16[8,80,320]{2,1,0:T(8,128)(2,1)S(1)}, bf16[8,8,256]{2,1,0:T(8,128)(2,1)S(1)}) custom-call(s32[1,320]{1,0:T(1,128)S(1)} %bitcast.1, s32[1,320]{1,0:T(1,128)S(1)} %reshape.23.offset_ref), custom_call_target="tpu_custom_call" | custom-call | flops 1638400 | bytes 1048576 | tf_op jit(solution)/shard_map/pallas_call | solution.py:152
  22.4 0.0 collective-permute-done.7.other_ref
  22.4 0.0 copy-start.1
  22.4 1.2 %shard_map.105 = bf16[8,88,256]{2,1,0:T(8,128)(2,1)} custom-call(bf16[8,80,320]{2,1,0:T(8,128)(2,1)S(1)} %get-tuple-element.17.pick_ref, bf16[8,8,256]{2,1,0:T(8,128)(2,1)S(1)} %get-tuple-element.18.tail_ref, f32[320,256]{1,0:T(8,128)S(1)} %get-tuple-element.22.mine_ref, f32[320,256]{1,0:T(8,128)S(1)} %collective-permute-done.7.other_ref), custom_call_target="tpu_custom_call" | custom-call | flops 104857600 | bytes 1048576 | tf_op jit(solution)/shard_map/pallas_call | solution.py:152
  23.6 0.0 copy-start
  23.6 6.1 %all-to-all-start = ((bf16[8,88,256]{2,1,0:T(8,128)(2,1)}), bf16[8,88,256]{2,1,0:T(8,128)(2,1)S(1)}, u32[]{:S(2)}, u32[]{:S(2)}) async-start(bf16[8,88,256]{2,1,0:T(8,128)(2,1)} %shard_map.105), calls=%async_computation | async-start | bytes 720896 | tf_op jit(solution)/shard_map/all_to_all | solution.py:225
  29.7 0.6 %reduce = f32[320]{0:T(512)} reduce(f32[1,320]{1,0:T(1,128)S(1)} %get-tuple-element.15, f32[]{:T(128)} %constant), dimensions={0}, to_apply=%get-tuple-element.15.reduce_sub_computation | reduce | bytes 2564 | tf_op jit(solution)/shard_map/pallas_call | solution.py:152
  30.3 11.0 %all-to-all-done.got_ref = bf16[8,88,256]{2,1,0:T(8,128)(2,1)S(1)} async-done(((bf16[8,88,256]{2,1,0:T(8,128)(2,1)}), bf16[8,88,256]{2,1,0:T(8,128)(2,1)S(1)}, u32[]{:S(2)}, u32[]{:S(2)}) %all-to-all-start) | async-done | bytes 360480 | tf_op jit(solution)/shard_map/all_to_all | solution.py:225
  41.3 0.0 copy-done.1
  41.3 0.0 copy-done
  41.3 3.7 %shard_map.106 = (f32[640,256]{1,0:T(8,128)}, f32[640,256]{1,0:T(8,128)}) custom-call(bf16[8,88,256]{2,1,0:T(8,128)(2,1)S(1)} %all-to-all-done.got_ref, f32[640,256]{1,0:T(8,128)S(1)} %copy-done, f32[640,256]{1,0:T(8,128)S(1)} %copy-done.1), custom_call_target="tpu_custom_call" | custom-call | tf_op jit(solution)/shard_map/pallas_call | solution.py:230
  (2 shorter events, 0.0 us)
Async XLA Ops:
  0.6 7.4 %collective-permute-start.1 = (bf16[320,256]{1,0:T(8,128)(2,1)}, bf16[320,256]{1,0:T(8,128)(2,1)S(1)}, u32[]{:S(2)}, u32[]{:S(2)}) collective-permute-start(bf16[320,256]{1,0:T(8,128)(2,1)} %refs_0_.3), channel_id=1, source_target_pairs={{0,16},{8,24},{16,0},{24,8},{1,17},{9,25},{17,1},{25,9},{2,18},{10... | collective-permute-start | bytes 491528 | tf_op jit(solution)/shard_map/ppermute | solution.py:168
  3.7 11.3 %collective-permute-start = (bf16[320,256]{1,0:T(8,128)(2,1)}, bf16[320,256]{1,0:T(8,128)(2,1)S(1)}, u32[]{:S(2)}, u32[]{:S(2)}) collective-permute-start(bf16[320,256]{1,0:T(8,128)(2,1)} %refs_0_.3), channel_id=1, source_target_pairs={{0,8},{8,0},{16,24},{24,16},{1,9},{9,1},{17,25},{25,17},{2,10},{10... | collective-permute-start | bytes 491528 | tf_op jit(solution)/shard_map/ppermute | solution.py:168
  8.1 6.9 %collective-permute-start.2 = (bf16[320,256]{1,0:T(8,128)(2,1)S(1)}, bf16[320,256]{1,0:T(8,128)(2,1)S(1)}, u32[]{:S(2)}, u32[]{:S(2)}) collective-permute-start(bf16[320,256]{1,0:T(8,128)(2,1)S(1)} %collective-permute-done.1.refs_2_), channel_id=1, source_target_pairs={{0,8},{8,0},{16,24},{24,16},{1,9},{9,1},{17,25},{25,17},{2,10},{10... | collective-permute-start | bytes 491528 | tf_op jit(solution)/shard_map/ppermute | solution.py:168
  8.1 11.5 %collective-permute-start.6 = (bf16[320,256]{1,0:T(8,128)(2,1)}, bf16[320,256]{1,0:T(8,128)(2,1)S(1)}, u32[]{:S(2)}, u32[]{:S(2)}) collective-permute-start(bf16[320,256]{1,0:T(8,128)(2,1)} %q_ref.1), channel_id=1, source_target_pairs={{0,16},{8,24},{16,0},{24,8},{1,17},{9,25},{17,1},{25,9},{2,18},{10... | collective-permute-start | bytes 491528 | tf_op jit(solution)/shard_map/ppermute | solution.py:168
  10.5 1.2 %collective-permute-start.3 = (f32[1,320]{1,0:T(1,128)S(1)}, f32[1,320]{1,0:T(1,128)S(1)}, u32[]{:S(2)}, u32[]{:S(2)}) collective-permute-start(f32[1,320]{1,0:T(1,128)S(1)} %reshape.20.refs_4_), channel_id=1, source_target_pairs={{0,8},{8,0},{16,24},{24,16},{1,9},{9,1},{17,25},{25,17},{2,10},{10... | collective-permute-start | bytes 3848 | tf_op jit(solution)/shard_map/ppermute | solution.py:168
  10.7 4.2 %collective-permute-start.4 = (f32[1,320]{1,0:T(1,128)S(1)}, f32[1,320]{1,0:T(1,128)S(1)}, u32[]{:S(2)}, u32[]{:S(2)}) collective-permute-start(f32[1,320]{1,0:T(1,128)S(1)} %reshape.20.refs_4_), channel_id=1, source_target_pairs={{0,16},{8,24},{16,0},{24,8},{1,17},{9,25},{17,1},{25,9},{2,18},{10... | collective-permute-start | bytes 3848 | tf_op jit(solution)/shard_map/ppermute | solution.py:168
  11.7 3.3 %collective-permute-start.5 = (f32[1,320]{1,0:T(1,128)S(1)}, f32[1,320]{1,0:T(1,128)S(1)}, u32[]{:S(2)}, u32[]{:S(2)}) collective-permute-start(f32[1,320]{1,0:T(1,128)S(1)} %reshape.20.refs_4_), channel_id=1, source_target_pairs={{0,24},{8,16},{16,8},{24,0},{1,25},{9,17},{17,9},{25,1},{2,26},{10... | collective-permute-start | bytes 3848 | tf_op jit(solution)/shard_map/ppermute | solution.py:168
  15.0 0.9 %copy-start.2 = (bf16[320,256]{1,0:T(8,128)(2,1)S(1)}, bf16[320,256]{1,0:T(8,128)(2,1)}, u32[]{:S(2)}) copy-start(bf16[320,256]{1,0:T(8,128)(2,1)} %refs_0_.3) | copy-start | bytes 491524
  15.9 0.9 %copy-start.4 = (bf16[320,256]{1,0:T(8,128)(2,1)S(1)}, bf16[320,256]{1,0:T(8,128)(2,1)}, u32[]{:S(2)}) copy-start(bf16[320,256]{1,0:T(8,128)(2,1)} %q_ref.1) | copy-start | bytes 491524
  16.8 2.8 %copy-start.3 = (bf16[320,256]{1,0:T(8,128)(2,1)S(1)}, bf16[320,256]{1,0:T(8,128)(2,1)}, u32[]{:S(2)}) copy-start(bf16[320,256]{1,0:T(8,128)(2,1)} %refs_0_.3) | copy-start | bytes 491524
  19.6 1.3 %copy-start.6 = (s32[320]{0:T(512)S(1)}, s32[320]{0:T(512)}, u32[]{:S(2)}) copy-start(s32[320]{0:T(512)} %param.10) | copy-start | bytes 3844
  20.7 1.7 %collective-permute-start.7 = (f32[320,256]{1,0:T(8,128)S(1)}, f32[320,256]{1,0:T(8,128)S(1)}, u32[]{:S(2)}, u32[]{:S(2)}) collective-permute-start(f32[320,256]{1,0:T(8,128)S(1)} %get-tuple-element.23), channel_id=1, source_target_pairs={{0,8},{8,0},{16,24},{24,16},{1,9},{9,1},{17,25},{25,17},{2,10},{10... | collective-permute-start | bytes 983048 | tf_op jit(solution)/shard_map/ppermute | solution.py:168
  20.9 0.7 %copy-start.5 = (s32[320,1]{0,1:T(1,128)S(1)}, s32[320,1]{0,1:T(1,128)}, u32[]{:S(2)}) copy-start(s32[320,1]{0,1:T(1,128)} %param.9) | copy-start | bytes 3844
  22.4 18.9 %copy-start.1 = (f32[640,256]{1,0:T(8,128)S(1)}, f32[640,256]{1,0:T(8,128)}, u32[]{:S(2)}) copy-start(f32[640,256]{1,0:T(8,128)} %accum_ref.1) | copy-start | bytes 1966084
  23.6 17.7 %copy-start = (f32[640,256]{1,0:T(8,128)S(1)}, f32[640,256]{1,0:T(8,128)}, u32[]{:S(2)}) copy-start(f32[640,256]{1,0:T(8,128)} %table_ref.1) | copy-start | bytes 1966084
  23.6 17.7 %all-to-all-start = ((bf16[8,88,256]{2,1,0:T(8,128)(2,1)}), bf16[8,88,256]{2,1,0:T(8,128)(2,1)S(1)}, u32[]{:S(2)}, u32[]{:S(2)}) async-start(bf16[8,88,256]{2,1,0:T(8,128)(2,1)} %shard_map.105), calls=%async_computation | async-start | bytes 720896 | tf_op jit(solution)/shard_map/all_to_all | solution.py:225

commit v2 on v1

v2 whole, which is shorter than its diff:
```python
import functools
import math

import jax
import jax.numpy as jnp
from jax import lax
from jax.experimental import pallas as pl
from jax.experimental.pallas import tpu as pltpu
from jax.sharding import PartitionSpec as P

D = 256
SCALE = 3.0 / math.sqrt(D)
LANES = 128
TAIL = 8
MIB = 1 << 20
NT = (((1,), (1,)), ((), ()))
TN = (((0,), (0,)), ((), ()))
F32 = jnp.float32
BF16 = jnp.bfloat16


def dot(a, b, dims=(((1,), (0,)), ((), ()))):
    return lax.dot_general(a, b, dims, preferred_element_type=F32)


def spread(column, width):
    pieces = [column] * (width // LANES)
    if width % LANES:
        pieces.append(column[:, : width % LANES])
    return jnp.concatenate(pieces, axis=1)


def code(x):
    y = x * x
    return jnp.where(x < 0, -y, y) * y


def decode(u):
    root = lax.rsqrt(lax.rsqrt(jnp.abs(u)))
    return jnp.where(u < 0, -root, root)


def diagonal(block):
    return lax.broadcasted_iota(jnp.int32, (block, block), 0) == lax.broadcasted_iota(
        jnp.int32, (block, block), 1
    )


def local_kernel(
    groups, slots, q_ref, item_ref, owner_ref, offset_ref, q_out, item_out, pick_ref, tail_ref
):
    q_out[...] = q_ref[...]
    item_out[...] = item_ref[...]
    block = owner_ref.shape[1]
    owner = owner_ref[...]
    member = lax.broadcasted_iota(jnp.int32, (groups, block), 0) == owner
    before = lax.broadcasted_iota(jnp.int32, (block, block), 0) < lax.broadcasted_iota(
        jnp.int32, (block, block), 1
    )
    ranks = dot(member.astype(BF16), before.astype(BF16))
    rank = jnp.sum(jnp.where(member, ranks, 0.0), axis=0, keepdims=True).astype(jnp.int32)
    offset = offset_ref[...]
    high = jnp.broadcast_to((offset // LANES).astype(F32), (TAIL, block)).astype(BF16)
    low = jnp.broadcast_to((offset % LANES).astype(F32), (TAIL, block)).astype(BF16)
    here = lax.broadcasted_iota(jnp.int32, (LANES, block), 0) == rank
    for g in range(groups):
        pick = (here & (owner == g)).astype(F32).astype(BF16)
        pick_ref[g * slots : (g + 1) * slots] = pick[:slots]
        tail_ref[g] = jnp.concatenate([dot(high, pick, NT), dot(low, pick, NT)], axis=1).astype(BF16)


def bias_kernel(n, *refs):
    for b in range(n):
        block = refs[b].shape[1]
        row = jnp.log(refs[b][...].astype(F32))
        refs[n][b] = jnp.transpose(jnp.broadcast_to(row, (LANES, block)))


def exponentials(n, q, item_refs, bias_ref, logits_ref):
    block = q.shape[0]
    top = None
    for b in range(n):
        logits = dot(item_refs[b][...], q, NT) * SCALE - spread(bias_ref[b], block)
        logits_ref[b] = logits
        high = jnp.max(logits, axis=0, keepdims=True)
        top = high if top is None else jnp.maximum(top, high)
    chosen = jnp.sum(jnp.where(diagonal(block), logits_ref[0], 0.0), axis=0, keepdims=True)
    total = jnp.zeros((1, block), F32)
    for b in range(n):
        e = jnp.exp(logits_ref[b] - top)
        logits_ref[b] = e
        total += jnp.sum(e, axis=0, keepdims=True)
    return top, total, chosen


def own_kernel(n, q_ref, *refs):
    item_refs = refs[:n]
    bias_ref, loss_ref, query_grad_ref, logits_ref = refs[n:]
    block = q_ref.shape[0]
    top, total, chosen = exponentials(n, q_ref[...], item_refs, bias_ref, logits_ref)
    loss_ref[...] = top + jnp.log(total) - chosen
    inverse = 1.0 / total
    query_grad = jnp.zeros((block, D), F32)
    for b in range(n):
        weights = logits_ref[b] * inverse
        if b == 0:
            weights = jnp.where(diagonal(block), weights - 1.0, weights)
        query_grad += dot(weights.astype(BF16), item_refs[b][...], TN)
    query_grad_ref[...] = query_grad * SCALE


def item_kernel(n, own, q_ref, *refs):
    item_refs = refs[:n]
    bias_ref, *before, mine_out, mate_out, logits_ref = refs[n:]
    block = q_ref.shape[0]
    q = q_ref[...]
    _, total, _ = exponentials(n, q, item_refs, bias_ref, logits_ref)
    inverse = 1.0 / total
    mate = dot((logits_ref[1] * inverse).astype(BF16), q)
    weights = logits_ref[0] * inverse
    if own:
        weights = jnp.where(diagonal(block), weights - 1.0, weights)
    mine = dot(weights.astype(BF16), q)
    if before:
        mine += before[0][...]
        mate += before[1][...]
    mine_out[...] = mine
    mate_out[...] = mate


def pack_kernel(groups, slots, pick_ref, tail_ref, mine_ref, other_ref, *out_refs):
    grad = code((mine_ref[...] + other_ref[...]) * SCALE).astype(BF16)
    picked = dot(pick_ref[...], grad).astype(BF16)
    for g in range(groups):
        out = out_refs[g] if len(out_refs) == groups else out_refs[0].at[g]
        out[:slots] = picked[g * slots : (g + 1) * slots]
        out[slots:] = tail_ref[g]


def update_kernel(groups, slots, *refs):
    got_refs = refs[:-6]
    table_ref, accum_ref, table_out, accum_out, values_ref, ids_ref = refs[-6:]
    rows = table_ref.shape[0]
    half = groups * LANES

    @pl.when(pl.program_id(0) == 0)
    def _():
        for g in range(groups):
            got = got_refs[g] if len(got_refs) == groups else got_refs[0].at[g]
            tail = got[slots : slots + TAIL].astype(F32)
            ids_ref[:, g * LANES : (g + 1) * LANES] = tail[:, :LANES] * LANES + tail[:, LANES:]
            values = decode(got[:slots].astype(F32))
            high = values.astype(BF16)
            low = (values - high.astype(F32)).astype(BF16)
            empty = jnp.zeros((LANES - slots, D), BF16)
            start = g * LANES
            values_ref[start : start + LANES] = jnp.concatenate([high, empty], axis=0)
            start += half
            values_ref[start : start + LANES] = jnp.concatenate([low, empty], axis=0)

    index = lax.broadcasted_iota(jnp.int32, (rows, half), 0) + pl.program_id(0) * rows
    put = (index.astype(F32) == ids_ref[:1]).astype(F32).astype(BF16)
    grad = dot(jnp.concatenate([put, put], axis=1), values_ref[...])
    accum_new = accum_ref[...] + grad * grad
    accum_out[...] = accum_new
    table_out[...] = table_ref[...] - 0.1 * grad / (jnp.sqrt(accum_new) + 1e-08)


def call(kernel, outs, *args, scratch=(), limit=16, flops=0):
    return pl.pallas_call(
        kernel,
        out_shape=[jax.ShapeDtypeStruct(s, t) for s, t in outs],
        scratch_shapes=list(scratch),
        compiler_params=pltpu.CompilerParams(vmem_limit_bytes=limit * MIB),
        cost_estimate=pl.CostEstimate(flops=flops, bytes_accessed=1024, transcendentals=0),
    )(*args)


def shards(queries, items, item_owner, item_offset, sample_counts, table, accum):
    block = queries.shape[0]
    n, groups = lax.axis_size("wide"), lax.axis_size("group")
    capacity = 2 * block // groups
    slots = -(-capacity // TAIL) * TAIL
    paired = groups <= 8

    def swap(x, k, axis="wide"):
        return lax.ppermute(x, axis, [(i, i ^ k) for i in range(lax.axis_size(axis))])

    far_counts = [swap(sample_counts, k) for k in range(2, n, 2)]
    far_items = [swap(items, k) for k in range(2, n, 2)]
    mate_counts = swap(sample_counts, 1)
    far_queries = [swap(queries, k) for k in range(2, n, 2)]
    mate_items = swap(items, 1)

    owner = item_owner.reshape(1, block)
    if paired:
        owner = owner ^ lax.axis_index("group")
    own_q, own_items, pick, tail = call(
        functools.partial(local_kernel, groups, slots),
        [
            ((block, D), BF16),
            ((block, D), BF16),
            ((groups * slots, block), BF16),
            ((groups, TAIL, D), BF16),
        ],
        queries,
        items,
        owner,
        item_offset.reshape(1, block),
        flops=1 << 30,
    )
    far_items, far_counts, own_items = lax.optimization_barrier((far_items, far_counts, own_items))
    item_blocks, count_blocks = [own_items, mate_items], [sample_counts, mate_counts]
    for far_item, far_count in zip(far_items, far_counts):
        item_blocks += [far_item, swap(far_item, 1)]
        count_blocks += [far_count, swap(far_count, 1)]
    (bias,) = call(
        functools.partial(bias_kernel, n),
        [((n, block, LANES), F32)],
        *[x.reshape(1, block) for x in count_blocks],
    )

    part = ((block, D), F32)
    logits = pltpu.VMEM((n, block, block), F32)
    limit = 8 + 4 * n
    mine, mate = call(
        functools.partial(item_kernel, n, True),
        [part, part],
        own_q,
        *item_blocks,
        bias,
        scratch=[logits],
        limit=limit,
    )
    for far in far_queries:
        mine, mate = call(
            functools.partial(item_kernel, n, False),
            [part, part],
            far,
            *item_blocks,
            bias,
            mine,
            mate,
            scratch=[logits],
            limit=limit,
        )
    other = swap(mate, 1)
    if paired:
        packets = [((slots + TAIL, D), BF16)] * groups
    else:
        packets = [((groups, slots + TAIL, D), BF16)]
    packed = call(
        functools.partial(pack_kernel, groups, slots), packets, pick, tail, mine, other
    )
    if paired:
        order = sorted(range(1, groups), key=lambda k: (k < groups // 2, k % 2, k))
        got = [packed[0]] + [swap(packed[k], k, "group") for k in order]
    else:
        got = [lax.all_to_all(packed[0], "group", split_axis=0, concat_axis=0, tiled=True)]
    loss, query_grad = call(
        functools.partial(own_kernel, n),
        [((1, block), F32), part],
        own_q,
        *item_blocks,
        bias,
        scratch=[logits],
        limit=limit,
        flops=6 * n * block * block * D,
    )

    rows = table.shape[0]
    step = rows // 5
    spec = pl.BlockSpec((step, D), lambda i: (i, 0))
    table_new, accum_new = pl.pallas_call(
        functools.partial(update_kernel, groups, slots),
        out_shape=[jax.ShapeDtypeStruct(table.shape, F32)] * 2,
        grid=(rows // step,),
        in_specs=[pl.BlockSpec(memory_space=pltpu.VMEM)] * len(got) + [spec, spec],
        out_specs=[spec, spec],
        scratch_shapes=[
            pltpu.VMEM((2 * groups * LANES, D), BF16),
            pltpu.VMEM((TAIL, groups * LANES), F32),
        ],
        compiler_params=pltpu.CompilerParams(vmem_limit_bytes=32 * MIB),
    )(*got, table, accum)
    return (loss.reshape(block), query_grad, table_new, accum_new)


def solution(mesh):
    placed = (
        P(("wide", "group"), None),
        P(("wide", "group"), None),
        P(("wide", "group"), None),
        P(("wide", "group")),
        P(("wide", "group")),
        P(("wide", "group"), None),
        P(("wide", "group"), None),
    )
    return jax.shard_map(
        shards,
        mesh=mesh,
        in_specs=placed,
        out_specs=(
            P(("wide", "group")),
            P(("wide", "group"), None),
            P(("wide", "group"), None),
            P(("wide", "group"), None),
        ),
        check_vma=False,
    )
```

time: 45.3 us -> 38.3 us (0.85)
  waiting for transfers between devices: 18.7 us -> 6.5 us
  starting transfers between devices: 12.3 us -> 17.3 us
  Pallas kernels: 9.56 us -> 10.7 us
  other arithmetic: 1.28 us -> 0.6 us
    ppermute x8 -> x15, starting transfers between devices: 6.15 us -> 17.3 us  [swap(): lax.ppermute(x, axis, [(i, i ^ k) for i in range(lax.axis_size(axis))])]
    all_to_all x1 -> x0, waiting for transfers between devices: 11 us -> none  [shards(): lax.all_to_all(packed, 'group', split_axis=0, concat_axis=0, tiled=True)]
    all_to_all x1 -> x0, starting transfers between devices: 6.15 us -> none  [shards(): lax.all_to_all(packed, 'group', split_axis=0, concat_axis=0, tiled=True)]
    pallas_call x4 -> x6, Pallas kernels: 5.87 us -> 7.32 us  [call(): pl.pallas_call(kernel, out_shape=[jax.ShapeDtypeStruct(s, t) for s, t in...]
    ppermute x8 -> x15, waiting for transfers between devices: 7.69 us -> 6.5 us  [swap(): lax.ppermute(x, axis, [(i, i ^ k) for i in range(lax.axis_size(axis))])]
    convert_element_type x1 -> x0, other arithmetic: 0.68 us -> none  [shards(): counts = sample_counts.astype(F32).reshape(1, block)]
    unnamed x14 -> x12, local copies, waits for them, and re-layouts: 2.52 us -> 2.28 us
  transfers between devices with their start and end apart: 9 -> 15, of which waited for: 4 -> 7; matrix products, arithmetic and copies ran while one was open for 3% -> 2% of each run, Pallas kernels for 8% -> 15%
where the time goes in v2:
time: 38.3 us; the launch traced here: 38.1 us
  starting transfers between devices  17.3 us (45%)
  Pallas kernels  10.7 us (28%)
  waiting for transfers between devices  6.5 us (17%)
  local copies, waits for them, and re-layouts  2.29 us (6%)
  between operations  0.72 us (2%)
  other arithmetic  0.6 us (2%)
    ppermute x15, starting transfers between devices, swap(): lax.ppermute(x, axis, [(i, i ^ k) for i in range(lax.axis_size(axis))])  17.3 us
    pallas_call x6, Pallas kernels, call(): pl.pallas_call(kernel, out_shape=[jax.ShapeDtypeStruct(s, t) for s, t in...  7.32 us
    ppermute x15, waiting for transfers between devices, swap(): lax.ppermute(x, axis, [(i, i ^ k) for i in range(lax.axis_size(axis))])  6.5 us
    pallas_call x1, Pallas kernels, shards(): pl.pallas_call(functools.partial(update_kernel, groups, slots), out_shape...  3.4 us
    unnamed x12, local copies, waits for them, and re-layouts  2.28 us
  transfers between devices with their start and end apart: 15, of which 7 were waited for; matrix products, arithmetic and copies ran while one was open for 2% of the time, Pallas kernels for 15%

profile of v2, /device:TPU:0, one launch (start us, length us, event | category | flops | bytes accessed | tf_op | source)
XLA Modules:
  0.0 38.1 jit_solution(13657596028548094787)
XLA Ops:
  0.6 3.0 %collective-permute-start = (bf16[320,256]{1,0:T(8,128)(2,1)}, bf16[320,256]{1,0:T(8,128)(2,1)S(1)}, u32[]{:S(2)}, u32[]{:S(2)}) collective-permute-start(bf16[320,256]{1,0:T(8,128)(2,1)} %item_ref.1), channel_id=1, source_target_pairs={{0,16},{8,24},{16,0},{24,8},{1,17},{9,25},{17,1},{25,9},{2,18},{10... | collective-permute-start | bytes 491528 | tf_op jit(solution)/shard_map/ppermute | solution.py:187
  3.7 0.0 collective-permute-start.2
  3.7 0.2 collective-permute-start.1
  3.8 0.0 copy-start.5
  3.8 0.7 %copy-done.5 = s32[320,1]{0,1:T(1,128)S(1)} copy-done((s32[320,1]{0,1:T(1,128)S(1)}, s32[320,1]{0,1:T(1,128)}, u32[]{:S(2)}) %copy-start.5) | copy-done | bytes 1304
  4.5 0.0 copy-start.3
  4.5 0.7 %copy-done.3 = s32[320]{0:T(512)S(1)} copy-done((s32[320]{0:T(512)S(1)}, s32[320]{0:T(512)}, u32[]{:S(2)}) %copy-start.3) | copy-done | bytes 1304
  5.2 0.0 copy-start.2
  5.2 0.9 %copy-done.2 = bf16[320,256]{1,0:T(8,128)(2,1)S(1)} copy-done((bf16[320,256]{1,0:T(8,128)(2,1)S(1)}, bf16[320,256]{1,0:T(8,128)(2,1)}, u32[]{:S(2)}) %copy-start.2) | copy-done | bytes 163864
  6.1 0.0 copy-start.4
  6.1 1.8 %shard_map.102 = (bf16[320,256]{1,0:T(8,128)(2,1)S(1)}, bf16[320,256]{1,0:T(8,128)(2,1)S(1)}, bf16[640,320]{1,0:T(8,128)(2,1)S(1)}, bf16[8,8,256]{2,1,0:T(8,128)(2,1)S(1)}) custom-call(bf16[320,256]{1,0:T(8,128)(2,1)} %q_ref.1, bf16[320,256]{1,0:T(8,128)(2,1)S(1)} %copy-done.2, s32[1,320]{1,0:T(1,128)S(1)} %xor_bitcast_fusion.owner_ref, ...), custom_call_target="tpu_custom_call" | custom-call | flops 1073741824 | bytes 1024 | tf_op jit(solution)/shard_map/pallas_call | solution.py:170
  7.9 0.3 collective-permute-done.1
  8.1 0.0 collective-permute-done.refs_2_
  8.1 0.2 collective-permute-start.3
  8.3 1.7 %collective-permute-start.6 = (bf16[320,256]{1,0:T(8,128)(2,1)}, bf16[320,256]{1,0:T(8,128)(2,1)S(1)}, u32[]{:S(2)}, u32[]{:S(2)}) collective-permute-start(bf16[320,256]{1,0:T(8,128)(2,1)} %q_ref.1), channel_id=1, source_target_pairs={{0,16},{8,24},{16,0},{24,8},{1,17},{9,25},{17,1},{25,9},{2,18},{10... | collective-permute-start | bytes 491528 | tf_op jit(solution)/shard_map/ppermute | solution.py:187
  10.1 0.0 copy-done.4
  10.1 0.0 collective-permute-start.4
  10.1 0.5 %collective-permute-start.5 = (s32[320]{0:T(512)S(1)}, s32[320]{0:T(512)S(1)}, u32[]{:S(2)}, u32[]{:S(2)}) collective-permute-start(s32[320]{0:T(512)S(1)} %collective-permute-done.1), channel_id=1, source_target_pairs={{0,8},{8,0},{16,24},{24,16},{1,9},{9,1},{17,25},{25,17},{2,10},{10... | collective-permute-start | bytes 3848 | tf_op jit(solution)/shard_map/ppermute | solution.py:187
  10.6 0.6 %collective-permute-done.4 = s32[320]{0:T(512)S(1)} collective-permute-done((s32[320]{0:T(512)S(1)}, s32[320]{0:T(512)S(1)}, u32[]{:S(2)}, u32[]{:S(2)}) %collective-permute-start.4) | collective-permute-done | bytes 1312 | tf_op jit(solution)/shard_map/ppermute | solution.py:187
  11.2 0.2 collective-permute-done.5
  11.4 0.3 shard_map.103.refs_4_
  11.7 0.0 collective-permute-done.2.refs_1_
  11.7 0.0 collective-permute-done.3.refs_3_
  11.7 1.2 %shard_map.105 = (f32[320,256]{1,0:T(8,128)S(1)}, f32[320,256]{1,0:T(8,128)S(1)}) custom-call(bf16[320,256]{1,0:T(8,128)(2,1)S(1)} %get-tuple-element.27.q_ref, bf16[320,256]{1,0:T(8,128)(2,1)S(1)} %get-tuple-element.29.refs_0_, bf16[320,256]{1,0:T(8,128)(2,1)S(1)} %collective-permute-done.2.refs_1_, bf16[320,256]{1,0:T(8,128)(2,1)S(1)} %collective-permute-done.refs_2_, ...), custom_call_target="tpu_custom_call" | custom-call | bytes 1024 | tf_op jit(solution)/shard_map/pallas_call | solution.py:170
  12.8 2.1 %collective-permute-done.6.q_ref = bf16[320,256]{1,0:T(8,128)(2,1)S(1)} collective-permute-done((bf16[320,256]{1,0:T(8,128)(2,1)}, bf16[320,256]{1,0:T(8,128)(2,1)S(1)}, u32[]{:S(2)}, u32[]{:S(2)}) %collective-permute-start.6) | collective-permute-done | bytes 163872 | tf_op jit(solution)/shard_map/ppermute | solution.py:187
  14.9 1.1 %shard_map.106 = (f32[320,256]{1,0:T(8,128)S(1)}, f32[320,256]{1,0:T(8,128)S(1)}) custom-call(bf16[320,256]{1,0:T(8,128)(2,1)S(1)} %collective-permute-done.6.q_ref, bf16[320,256]{1,0:T(8,128)(2,1)S(1)} %get-tuple-element.29.refs_0_, bf16[320,256]{1,0:T(8,128)(2,1)S(1)} %collective-permute-done.2.refs_1_, bf16[320,256]{1,0:T(8,128)(2,1)S(1)} %collective-permute-done.refs_2_, ...), custom_call_target="tpu_custom_call" | custom-call | bytes 1024 | tf_op jit(solution)/shard_map/pallas_call | solution.py:170
  16.1 0.1 collective-permute-start.7
  16.2 1.6 %collective-permute-done.7.other_ref = f32[320,256]{1,0:T(8,128)S(1)} collective-permute-done((f32[320,256]{1,0:T(8,128)S(1)}, f32[320,256]{1,0:T(8,128)S(1)}, u32[]{:S(2)}, u32[]{:S(2)}) %collective-permute-start.7) | collective-permute-done | bytes 327712 | tf_op jit(solution)/shard_map/ppermute | solution.py:187
  17.8 0.4 shard_map.107
  18.2 3.8 %collective-permute-start.10 = (bf16[88,256]{1,0:T(8,128)(2,1)S(1)}, bf16[88,256]{1,0:T(8,128)(2,1)S(1)}, u32[]{:S(2)}, u32[]{:S(2)}) collective-permute-start(bf16[88,256]{1,0:T(8,128)(2,1)S(1)} %get-tuple-element.43), channel_id=1, source_target_pairs={{0,5},{1,4},{2,7},{3,6},{4,1},{5,0},{6,3},{7,2},{8,13},{9,12},{10,... | collective-permute-start | bytes 135176 | tf_op jit(solution)/shard_map/ppermute | solution.py:187
  22.0 1.3 %collective-permute-start.11 = (bf16[88,256]{1,0:T(8,128)(2,1)S(1)}, bf16[88,256]{1,0:T(8,128)(2,1)S(1)}, u32[]{:S(2)}, u32[]{:S(2)}) collective-permute-start(bf16[88,256]{1,0:T(8,128)(2,1)S(1)} %get-tuple-element.44), channel_id=1, source_target_pairs={{0,7},{1,6},{2,5},{3,4},{4,3},{5,2},{6,1},{7,0},{8,15},{9,14},{10,... | collective-permute-start | bytes 135176 | tf_op jit(solution)/shard_map/ppermute | solution.py:187
  23.3 0.3 collective-permute-start.12
  23.6 1.2 %collective-permute-start.13 = (bf16[88,256]{1,0:T(8,128)(2,1)S(1)}, bf16[88,256]{1,0:T(8,128)(2,1)S(1)}, u32[]{:S(2)}, u32[]{:S(2)}) collective-permute-start(bf16[88,256]{1,0:T(8,128)(2,1)S(1)} %get-tuple-element.46), channel_id=1, source_target_pairs={{0,1},{1,0},{2,3},{3,2},{4,5},{5,4},{6,7},{7,6},{8,9},{9,8},{10,11... | collective-permute-start | bytes 135176 | tf_op jit(solution)/shard_map/ppermute | solution.py:187
  24.8 2.0 %collective-permute-start.14 = (bf16[88,256]{1,0:T(8,128)(2,1)S(1)}, bf16[88,256]{1,0:T(8,128)(2,1)S(1)}, u32[]{:S(2)}, u32[]{:S(2)}) collective-permute-start(bf16[88,256]{1,0:T(8,128)(2,1)S(1)} %get-tuple-element.47), channel_id=1, source_target_pairs={{0,3},{1,2},{2,1},{3,0},{4,7},{5,6},{6,5},{7,4},{8,11},{9,10},{10,... | collective-permute-start | bytes 135176 | tf_op jit(solution)/shard_map/ppermute | solution.py:187
  26.8 0.0 collective-permute-done.10.refs_3_
  26.8 1.7 %collective-permute-start.8 = (bf16[88,256]{1,0:T(8,128)(2,1)S(1)}, bf16[88,256]{1,0:T(8,128)(2,1)S(1)}, u32[]{:S(2)}, u32[]{:S(2)}) collective-permute-start(bf16[88,256]{1,0:T(8,128)(2,1)S(1)} %get-tuple-element.41), channel_id=1, source_target_pairs={{0,4},{1,5},{2,6},{3,7},{4,0},{5,1},{6,2},{7,3},{8,12},{9,13},{10,... | collective-permute-start | bytes 135176 | tf_op jit(solution)/shard_map/ppermute | solution.py:187
  28.5 0.4 %collective-permute-done.11.refs_4_ = bf16[88,256]{1,0:T(8,128)(2,1)S(1)} collective-permute-done((bf16[88,256]{1,0:T(8,128)(2,1)S(1)}, bf16[88,256]{1,0:T(8,128)(2,1)S(1)}, u32[]{:S(2)}, u32[]{:S(2)}) %collective-permute-start.11) | collective-permute-done | bytes 45088 | tf_op jit(solution)/shard_map/ppermute | solution.py:187
  28.9 1.3 %collective-permute-start.9 = (bf16[88,256]{1,0:T(8,128)(2,1)S(1)}, bf16[88,256]{1,0:T(8,128)(2,1)S(1)}, u32[]{:S(2)}, u32[]{:S(2)}) collective-permute-start(bf16[88,256]{1,0:T(8,128)(2,1)S(1)} %get-tuple-element.42), channel_id=1, source_target_pairs={{0,6},{1,7},{2,4},{3,5},{4,2},{5,3},{6,0},{7,1},{8,14},{9,15},{10,... | collective-permute-start | bytes 135176 | tf_op jit(solution)/shard_map/ppermute | solution.py:187
  30.2 2.6 %shard_map.104 = (f32[1,320]{1,0:T(1,128)S(1)}, f32[320,256]{1,0:T(8,128)}) custom-call(bf16[320,256]{1,0:T(8,128)(2,1)S(1)} %get-tuple-element.27.q_ref, bf16[320,256]{1,0:T(8,128)(2,1)S(1)} %get-tuple-element.29.refs_0_, bf16[320,256]{1,0:T(8,128)(2,1)S(1)} %collective-permute-done.2.refs_1_, bf16[320,256]{1,0:T(8,128)(2,1)S(1)} %collective-permute-done.refs_2_, ...), custom_call_target="tpu_custom_call" | custom-call | flops 629145600 | bytes 1024 | tf_op jit(solution)/shard_map/pallas_call | solution.py:170
  32.8 0.6 %reduce = f32[320]{0:T(512)} reduce(f32[1,320]{1,0:T(1,128)S(1)} %get-tuple-element.32, f32[]{:T(128)} %constant.4), dimensions={0}, to_apply=%get-tuple-element.32.reduce_sub_computation | reduce | bytes 2564 | tf_op jit(solution)/shard_map/pallas_call | solution.py:170
  33.4 0.0 collective-permute-done.12.refs_5_
  33.4 0.0 collective-permute-done.13.refs_6_
  33.4 0.0 collective-permute-done.14.refs_7_
  33.4 0.0 collective-permute-done.8.refs_1_
  33.4 1.3 %collective-permute-done.9.refs_2_ = bf16[88,256]{1,0:T(8,128)(2,1)S(1)} collective-permute-done((bf16[88,256]{1,0:T(8,128)(2,1)S(1)}, bf16[88,256]{1,0:T(8,128)(2,1)S(1)}, u32[]{:S(2)}, u32[]{:S(2)}) %collective-permute-start.9) | collective-permute-done | bytes 45088 | tf_op jit(solution)/shard_map/ppermute | solution.py:187
  34.7 0.0 copy-done
  34.7 0.0 copy-done.1
  34.7 3.4 %shard_map.108 = (f32[640,256]{1,0:T(8,128)}, f32[640,256]{1,0:T(8,128)}) custom-call(bf16[88,256]{1,0:T(8,128)(2,1)S(1)} %get-tuple-element.40.refs_0_, bf16[88,256]{1,0:T(8,128)(2,1)S(1)} %collective-permute-done.8.refs_1_, bf16[88,256]{1,0:T(8,128)(2,1)S(1)} %collective-permute-done.9.refs_2_, bf16[88,256]{1,0:T(8,128)(2,1)S(1)} %collective-permute-done.10.refs_3_, ...), custom_call_target="tpu_custom_call" | custom-call | tf_op jit(solution)/shard_map/pallas_call | solution.py:274
  (8 shorter events, 0.0 us)
Async XLA Ops:
  0.6 7.5 %collective-permute-start = (bf16[320,256]{1,0:T(8,128)(2,1)}, bf16[320,256]{1,0:T(8,128)(2,1)S(1)}, u32[]{:S(2)}, u32[]{:S(2)}) collective-permute-start(bf16[320,256]{1,0:T(8,128)(2,1)} %item_ref.1), channel_id=1, source_target_pairs={{0,16},{8,24},{16,0},{24,8},{1,17},{9,25},{17,1},{25,9},{2,18},{10... | collective-permute-start | bytes 491528 | tf_op jit(solution)/shard_map/ppermute | solution.py:187
  3.7 8.0 %collective-permute-start.2 = (bf16[320,256]{1,0:T(8,128)(2,1)}, bf16[320,256]{1,0:T(8,128)(2,1)S(1)}, u32[]{:S(2)}, u32[]{:S(2)}) collective-permute-start(bf16[320,256]{1,0:T(8,128)(2,1)} %item_ref.1), channel_id=1, source_target_pairs={{0,8},{8,0},{16,24},{24,16},{1,9},{9,1},{17,25},{25,17},{2,10},{10... | collective-permute-start | bytes 491528 | tf_op jit(solution)/shard_map/ppermute | solution.py:187
  3.7 4.5 %collective-permute-start.1 = (s32[320]{0:T(512)}, s32[320]{0:T(512)S(1)}, u32[]{:S(2)}, u32[]{:S(2)}) collective-permute-start(s32[320]{0:T(512)} %param.11), channel_id=1, source_target_pairs={{0,16},{8,24},{16,0},{24,8},{1,17},{9,25},{17,1},{25,9},{2,18},{10... | collective-permute-start | bytes 3848 | tf_op jit(solution)/shard_map/ppermute | solution.py:187
  3.8 0.7 %copy-start.5 = (s32[320,1]{0,1:T(1,128)S(1)}, s32[320,1]{0,1:T(1,128)}, u32[]{:S(2)}) copy-start(s32[320,1]{0,1:T(1,128)} %param.9) | copy-start | bytes 3844
  4.5 0.7 %copy-start.3 = (s32[320]{0:T(512)S(1)}, s32[320]{0:T(512)}, u32[]{:S(2)}) copy-start(s32[320]{0:T(512)} %param.10) | copy-start | bytes 3844
  5.2 0.9 %copy-start.2 = (bf16[320,256]{1,0:T(8,128)(2,1)S(1)}, bf16[320,256]{1,0:T(8,128)(2,1)}, u32[]{:S(2)}) copy-start(bf16[320,256]{1,0:T(8,128)(2,1)} %item_ref.1) | copy-start | bytes 491524
  6.1 3.9 %copy-start.4 = (s32[320]{0:T(512)S(1)}, s32[320]{0:T(512)}, u32[]{:S(2)}) copy-start(s32[320]{0:T(512)} %param.11) | copy-start | bytes 3844
  8.1 3.6 %collective-permute-start.3 = (bf16[320,256]{1,0:T(8,128)(2,1)S(1)}, bf16[320,256]{1,0:T(8,128)(2,1)S(1)}, u32[]{:S(2)}, u32[]{:S(2)}) collective-permute-start(bf16[320,256]{1,0:T(8,128)(2,1)S(1)} %collective-permute-done.refs_2_), channel_id=1, source_target_pairs={{0,8},{8,0},{16,24},{24,16},{1,9},{9,1},{17,25},{25,17},{2,10},{10... | collective-permute-start | bytes 491528 | tf_op jit(solution)/shard_map/ppermute | solution.py:187
  8.3 6.6 %collective-permute-start.6 = (bf16[320,256]{1,0:T(8,128)(2,1)}, bf16[320,256]{1,0:T(8,128)(2,1)S(1)}, u32[]{:S(2)}, u32[]{:S(2)}) collective-permute-start(bf16[320,256]{1,0:T(8,128)(2,1)} %q_ref.1), channel_id=1, source_target_pairs={{0,16},{8,24},{16,0},{24,8},{1,17},{9,25},{17,1},{25,9},{2,18},{10... | collective-permute-start | bytes 491528 | tf_op jit(solution)/shard_map/ppermute | solution.py:187
  10.1 1.2 %collective-permute-start.4 = (s32[320]{0:T(512)S(1)}, s32[320]{0:T(512)S(1)}, u32[]{:S(2)}, u32[]{:S(2)}) collective-permute-start(s32[320]{0:T(512)S(1)} %copy-done.4), channel_id=1, source_target_pairs={{0,8},{8,0},{16,24},{24,16},{1,9},{9,1},{17,25},{25,17},{2,10},{10... | collective-permute-start | bytes 3848 | tf_op jit(solution)/shard_map/ppermute | solution.py:187
  10.1 1.3 %collective-permute-start.5 = (s32[320]{0:T(512)S(1)}, s32[320]{0:T(512)S(1)}, u32[]{:S(2)}, u32[]{:S(2)}) collective-permute-start(s32[320]{0:T(512)S(1)} %collective-permute-done.1), channel_id=1, source_target_pairs={{0,8},{8,0},{16,24},{24,16},{1,9},{9,1},{17,25},{25,17},{2,10},{10... | collective-permute-start | bytes 3848 | tf_op jit(solution)/shard_map/ppermute | solution.py:187
  16.1 1.7 %collective-permute-start.7 = (f32[320,256]{1,0:T(8,128)S(1)}, f32[320,256]{1,0:T(8,128)S(1)}, u32[]{:S(2)}, u32[]{:S(2)}) collective-permute-start(f32[320,256]{1,0:T(8,128)S(1)} %get-tuple-element.39), channel_id=1, source_target_pairs={{0,8},{8,0},{16,24},{24,16},{1,9},{9,1},{17,25},{25,17},{2,10},{10... | collective-permute-start | bytes 983048 | tf_op jit(solution)/shard_map/ppermute | solution.py:187
  18.2 8.6 %collective-permute-start.10 = (bf16[88,256]{1,0:T(8,128)(2,1)S(1)}, bf16[88,256]{1,0:T(8,128)(2,1)S(1)}, u32[]{:S(2)}, u32[]{:S(2)}) collective-permute-start(bf16[88,256]{1,0:T(8,128)(2,1)S(1)} %get-tuple-element.43), channel_id=1, source_target_pairs={{0,5},{1,4},{2,7},{3,6},{4,1},{5,0},{6,3},{7,2},{8,13},{9,12},{10,... | collective-permute-start | bytes 135176 | tf_op jit(solution)/shard_map/ppermute | solution.py:187
  22.0 6.9 %collective-permute-start.11 = (bf16[88,256]{1,0:T(8,128)(2,1)S(1)}, bf16[88,256]{1,0:T(8,128)(2,1)S(1)}, u32[]{:S(2)}, u32[]{:S(2)}) collective-permute-start(bf16[88,256]{1,0:T(8,128)(2,1)S(1)} %get-tuple-element.44), channel_id=1, source_target_pairs={{0,7},{1,6},{2,5},{3,4},{4,3},{5,2},{6,1},{7,0},{8,15},{9,14},{10,... | collective-permute-start | bytes 135176 | tf_op jit(solution)/shard_map/ppermute | solution.py:187
  23.3 10.1 %collective-permute-start.12 = (bf16[88,256]{1,0:T(8,128)(2,1)S(1)}, bf16[88,256]{1,0:T(8,128)(2,1)S(1)}, u32[]{:S(2)}, u32[]{:S(2)}) collective-permute-start(bf16[88,256]{1,0:T(8,128)(2,1)S(1)} %get-tuple-element.45), channel_id=1, source_target_pairs={{0,2},{1,3},{2,0},{3,1},{4,6},{5,7},{6,4},{7,5},{8,10},{9,11},{10,... | collective-permute-start | bytes 135176 | tf_op jit(solution)/shard_map/ppermute | solution.py:187
  23.6 9.9 %collective-permute-start.13 = (bf16[88,256]{1,0:T(8,128)(2,1)S(1)}, bf16[88,256]{1,0:T(8,128)(2,1)S(1)}, u32[]{:S(2)}, u32[]{:S(2)}) collective-permute-start(bf16[88,256]{1,0:T(8,128)(2,1)S(1)} %get-tuple-element.46), channel_id=1, source_target_pairs={{0,1},{1,0},{2,3},{3,2},{4,5},{5,4},{6,7},{7,6},{8,9},{9,8},{10,11... | collective-permute-start | bytes 135176 | tf_op jit(solution)/shard_map/ppermute | solution.py:187
  24.8 8.6 %collective-permute-start.14 = (bf16[88,256]{1,0:T(8,128)(2,1)S(1)}, bf16[88,256]{1,0:T(8,128)(2,1)S(1)}, u32[]{:S(2)}, u32[]{:S(2)}) collective-permute-start(bf16[88,256]{1,0:T(8,128)(2,1)S(1)} %get-tuple-element.47), channel_id=1, source_target_pairs={{0,3},{1,2},{2,1},{3,0},{4,7},{5,6},{6,5},{7,4},{8,11},{9,10},{10,... | collective-permute-start | bytes 135176 | tf_op jit(solution)/shard_map/ppermute | solution.py:187
  26.8 6.6 %collective-permute-start.8 = (bf16[88,256]{1,0:T(8,128)(2,1)S(1)}, bf16[88,256]{1,0:T(8,128)(2,1)S(1)}, u32[]{:S(2)}, u32[]{:S(2)}) collective-permute-start(bf16[88,256]{1,0:T(8,128)(2,1)S(1)} %get-tuple-element.41), channel_id=1, source_target_pairs={{0,4},{1,5},{2,6},{3,7},{4,0},{5,1},{6,2},{7,3},{8,12},{9,13},{10,... | collective-permute-start | bytes 135176 | tf_op jit(solution)/shard_map/ppermute | solution.py:187
  28.9 5.9 %copy-start = (f32[640,256]{1,0:T(8,128)S(1)}, f32[640,256]{1,0:T(8,128)}, u32[]{:S(2)}) copy-start(f32[640,256]{1,0:T(8,128)} %refs_8_.1) | copy-start | bytes 1966084
  28.9 5.9 %copy-start.1 = (f32[640,256]{1,0:T(8,128)S(1)}, f32[640,256]{1,0:T(8,128)}, u32[]{:S(2)}) copy-start(f32[640,256]{1,0:T(8,128)} %refs_9_.1) | copy-start | bytes 1966084
  28.9 5.8 %collective-permute-start.9 = (bf16[88,256]{1,0:T(8,128)(2,1)S(1)}, bf16[88,256]{1,0:T(8,128)(2,1)S(1)}, u32[]{:S(2)}, u32[]{:S(2)}) collective-permute-start(bf16[88,256]{1,0:T(8,128)(2,1)S(1)} %get-tuple-element.42), channel_id=1, source_target_pairs={{0,6},{1,7},{2,4},{3,5},{4,2},{5,3},{6,0},{7,1},{8,14},{9,15},{10,... | collective-permute-start | bytes 135176 | tf_op jit(solution)/shard_map/ppermute | solution.py:187

commit v3 on v2

v3 whole, which is shorter than its diff:
```python
import functools
import math

import jax
import jax.numpy as jnp
from jax import lax
from jax.experimental import pallas as pl
from jax.experimental.pallas import tpu as pltpu
from jax.sharding import PartitionSpec as P

D = 256
SCALE = 3.0 / math.sqrt(D)
LANES = 128
TAIL = 8
ROW_CODES = 1 << 16
MIB = 1 << 20
NT = (((1,), (1,)), ((), ()))
TN = (((0,), (0,)), ((), ()))
F32 = jnp.float32
BF16 = jnp.bfloat16


def dot(a, b, dims=(((1,), (0,)), ((), ()))):
    return lax.dot_general(a, b, dims, preferred_element_type=F32)


def spread(column, width):
    pieces = [column] * (width // LANES)
    if width % LANES:
        pieces.append(column[:, : width % LANES])
    return jnp.concatenate(pieces, axis=1)


def code(x):
    y = x * x
    return jnp.where(x < 0, -y, y) * y


def decode(u):
    root = lax.rsqrt(lax.rsqrt(jnp.abs(u)))
    return jnp.where(u < 0, -root, root)


def diagonal(block):
    return lax.broadcasted_iota(jnp.int32, (block, block), 0) == lax.broadcasted_iota(
        jnp.int32, (block, block), 1
    )


def local_kernel(groups, slots, code_ref, pick_ref, tail_ref):
    block = code_ref.shape[1]
    owner = code_ref[...] // ROW_CODES
    offset = code_ref[...] % ROW_CODES
    member = lax.broadcasted_iota(jnp.int32, (groups, block), 0) == owner
    before = lax.broadcasted_iota(jnp.int32, (block, block), 0) < lax.broadcasted_iota(
        jnp.int32, (block, block), 1
    )
    ranks = dot(member.astype(BF16), before.astype(BF16))
    rank = jnp.sum(jnp.where(member, ranks, 0.0), axis=0, keepdims=True).astype(jnp.int32)
    high = jnp.broadcast_to((offset // LANES).astype(F32), (TAIL, block)).astype(BF16)
    low = jnp.broadcast_to((offset % LANES).astype(F32), (TAIL, block)).astype(BF16)
    here = lax.broadcasted_iota(jnp.int32, (LANES, block), 0) == rank
    for g in range(groups):
        pick = (here & (owner == g)).astype(F32).astype(BF16)
        pick_ref[g * slots : (g + 1) * slots] = pick[:slots]
        tail_ref[g] = jnp.concatenate([dot(high, pick, NT), dot(low, pick, NT)], axis=1).astype(BF16)


def bias_kernel(n, *refs):
    for b in range(n):
        block = refs[b].shape[1]
        row = jnp.log(refs[b][...].astype(F32))
        refs[n][b] = jnp.transpose(jnp.broadcast_to(row, (LANES, block)))


def item_kernel(n, m, own, *refs):
    q_refs, item_refs, bias_ref, refs = refs[:m], refs[m : m + n], refs[m + n], refs[m + n + 1 :]
    block = q_refs[0].shape[0]
    q = jnp.concatenate([ref[...] for ref in q_refs], axis=0)
    if own:
        mine_out, mate_out, loss_ref, weights_ref, logits_ref = refs
    else:
        mine_ref, mate_ref, mine_out, mate_out, logits_ref = refs
    top = None
    for b in range(n):
        logits = dot(item_refs[b][...], q, NT) * SCALE - spread(bias_ref[b], m * block)
        logits_ref[b] = logits
        high = jnp.max(logits, axis=0, keepdims=True)
        top = high if top is None else jnp.maximum(top, high)
    hit = lax.broadcasted_iota(jnp.int32, (block, m * block), 0) == lax.broadcasted_iota(
        jnp.int32, (block, m * block), 1
    )
    if own:
        chosen = jnp.sum(jnp.where(hit, logits_ref[0], 0.0), axis=0, keepdims=True)
    total = jnp.zeros((1, m * block), F32)
    for b in range(n):
        e = jnp.exp(logits_ref[b] - top)
        logits_ref[b] = e
        total += jnp.sum(e, axis=0, keepdims=True)
    inverse = 1.0 / total
    for b in range(n):
        if b > 1 and not own:
            continue
        weights = logits_ref[b] * inverse
        if b == 0 and own:
            weights = jnp.where(hit, weights - 1.0, weights)
        weights = weights.astype(BF16)
        if own:
            weights_ref[b] = weights[:, :block]
        if b < 2:
            part = dot(weights, q)
            if not own:
                part += (mine_ref, mate_ref)[b][...]
            (mine_out, mate_out)[b][...] = part
    if own:
        loss_ref[...] = (top + jnp.log(total) - chosen)[0, :block]


def query_kernel(n, weights_ref, *refs):
    item_refs, out_ref = refs[:n], refs[n]
    total = dot(weights_ref[0], item_refs[0][...], TN)
    for b in range(1, n):
        total += dot(weights_ref[b], item_refs[b][...], TN)
    out_ref[...] = total * SCALE


def pack_kernel(groups, slots, pick_ref, tail_ref, mine_ref, other_ref, *out_refs):
    grad = code((mine_ref[...] + other_ref[...]) * SCALE).astype(BF16)
    picked = dot(pick_ref[...], grad).astype(BF16)
    for g in range(groups):
        out = out_refs[g] if len(out_refs) == groups else out_refs[0].at[g]
        out[:slots] = picked[g * slots : (g + 1) * slots]
        out[slots:] = tail_ref[g]


def update_kernel(groups, slots, *refs):
    got_refs = refs[:-6]
    table_ref, accum_ref, table_out, accum_out, values_ref, ids_ref = refs[-6:]
    rows = table_ref.shape[0]
    half = groups * slots

    @pl.when(pl.program_id(0) == 0)
    def _():
        for g in range(groups):
            got = got_refs[g] if len(got_refs) == groups else got_refs[0].at[g]
            here = slice(g * slots, (g + 1) * slots)
            tail = got[slots : slots + TAIL].astype(F32)
            ids_ref[:, here] = tail[:, :slots] * LANES + tail[:, LANES : LANES + slots]
            values = decode(got[:slots].astype(F32))
            high = values.astype(BF16)
            values_ref[g * slots : (g + 1) * slots] = high
            low = (values - high.astype(F32)).astype(BF16)
            values_ref[half + g * slots : half + (g + 1) * slots] = low

    index = lax.broadcasted_iota(jnp.int32, (rows, half), 0) + pl.program_id(0) * rows
    put = (index.astype(F32) == ids_ref[:1]).astype(F32).astype(BF16)
    grad = dot(jnp.concatenate([put, put], axis=1), values_ref[...])
    accum_new = accum_ref[...] + grad * grad
    accum_out[...] = accum_new
    table_out[...] = table_ref[...] - 0.1 * grad / (jnp.sqrt(accum_new) + 1e-08)


def call(kernel, outs, *args, scratch=(), limit=16, flops=0):
    return pl.pallas_call(
        kernel,
        out_shape=[jax.ShapeDtypeStruct(s, t) for s, t in outs],
        scratch_shapes=list(scratch),
        compiler_params=pltpu.CompilerParams(vmem_limit_bytes=limit * MIB),
        cost_estimate=pl.CostEstimate(flops=flops, bytes_accessed=1024, transcendentals=0),
    )(*args)


def shards(queries, items, item_owner, item_offset, sample_counts, table, accum):
    block = queries.shape[0]
    n, groups = lax.axis_size("wide"), lax.axis_size("group")
    capacity = 2 * block // groups
    slots = -(-capacity // TAIL) * TAIL
    paired = groups <= 8

    def swap(x, k, axis="wide"):
        return lax.ppermute(x, axis, [(i, i ^ k) for i in range(lax.axis_size(axis))])

    far_counts = [swap(sample_counts, k) for k in range(2, n, 2)]
    far_items = [swap(items, k) for k in range(2, n, 2)]
    far_queries = [swap(queries, k) for k in range(2, n, 2)]

    owner = item_owner.reshape(1, block)
    if paired:
        owner = owner ^ lax.axis_index("group")
    pick, tail = call(
        functools.partial(local_kernel, groups, slots),
        [((groups * slots, block), BF16), ((groups, TAIL, D), BF16)],
        owner * ROW_CODES + item_offset.reshape(1, block),
        flops=1 << 30,
    )
    far_items, far_counts, tail = lax.optimization_barrier((far_items, far_counts, tail))
    item_blocks = [items, swap(items, 1)]
    count_blocks = [sample_counts, swap(sample_counts, 1)]
    for far_item, far_count in zip(far_items, far_counts):
        item_blocks += [far_item, swap(far_item, 1)]
        count_blocks += [far_count, swap(far_count, 1)]
    (bias,) = call(
        functools.partial(bias_kernel, n),
        [((n, block, LANES), F32)],
        *[x.reshape(1, block) for x in count_blocks],
    )

    part = ((block, D), F32)
    mine, mate, loss, weights = call(
        functools.partial(item_kernel, n, 2, True),
        [part, part, ((block,), F32), ((n, block, block), BF16)],
        queries,
        far_queries[0],
        *item_blocks,
        bias,
        scratch=[pltpu.VMEM((n, block, 2 * block), F32)],
        limit=8 + 4 * n,
    )
    for k in range(1, len(far_queries), 2):
        pair = far_queries[k : k + 2]
        mine, mate = call(
            functools.partial(item_kernel, n, len(pair), False),
            [part, part],
            *pair,
            *item_blocks,
            bias,
            mine,
            mate,
            scratch=[pltpu.VMEM((n, block, len(pair) * block), F32)],
            limit=8 + 4 * n,
        )
    other = swap(mate, 1)
    (query_grad,) = call(
        functools.partial(query_kernel, n), [part], weights, *item_blocks, flops=1 << 30
    )
    other, query_grad = lax.optimization_barrier((other, query_grad))
    if paired:
        packets = [((slots + TAIL, D), BF16)] * groups
    else:
        packets = [((groups, slots + TAIL, D), BF16)]
    packed = call(
        functools.partial(pack_kernel, groups, slots), packets, pick, tail, mine, other
    )
    if paired:
        order = sorted(range(1, groups), key=lambda k: (k < groups // 2, k % 2, k))
        got = [packed[0]] + [swap(packed[k], k, "group") for k in order]
    else:
        got = [lax.all_to_all(packed[0], "group", split_axis=0, concat_axis=0, tiled=True)]
    rows = table.shape[0]
    step = rows // 2
    spec = pl.BlockSpec((step, D), lambda i: (i, 0))
    table_new, accum_new = pl.pallas_call(
        functools.partial(update_kernel, groups, slots),
        out_shape=[jax.ShapeDtypeStruct(table.shape, F32)] * 2,
        grid=(rows // step,),
        in_specs=[pl.BlockSpec(memory_space=pltpu.VMEM)] * len(got) + [spec, spec],
        out_specs=[spec, spec],
        scratch_shapes=[
            pltpu.VMEM((2 * groups * slots, D), BF16),
            pltpu.VMEM((TAIL, groups * slots), F32),
        ],
        compiler_params=pltpu.CompilerParams(vmem_limit_bytes=32 * MIB),
    )(*got, table, accum)
    return (loss, query_grad, table_new, accum_new)


def solution(mesh):
    placed = (
        P(("wide", "group"), None),
        P(("wide", "group"), None),
        P(("wide", "group"), None),
        P(("wide", "group")),
        P(("wide", "group")),
        P(("wide", "group"), None),
        P(("wide", "group"), None),
    )
    return jax.shard_map(
        shards,
        mesh=mesh,
        in_specs=placed,
        out_specs=(
            P(("wide", "group")),
            P(("wide", "group"), None),
            P(("wide", "group"), None),
            P(("wide", "group"), None),
        ),
        check_vma=False,
    )
```

time: 38.3 us -> 33.5 us (0.87)
  Pallas kernels: 10.7 us -> 7.11 us
  local copies, waits for them, and re-layouts: 2.29 us -> 1.37 us
  other arithmetic: 0.6 us -> 0.02 us
    pallas_call x6 -> x5, Pallas kernels: 7.32 us -> 5.02 us  [call(): pl.pallas_call(kernel, out_shape=[jax.ShapeDtypeStruct(s, t) for s, t in...]
    pallas_call x1, Pallas kernels: 3.4 us -> 2.09 us  [shards(): pl.pallas_call(functools.partial(update_kernel, groups, slots), out_shape...]
    unnamed x12 -> x14, local copies, waits for them, and re-layouts: 2.28 us -> 1.36 us
    pallas_call x1 -> x0, other arithmetic: 0.6 us -> none  [call(): pl.pallas_call(kernel, out_shape=[jax.ShapeDtypeStruct(s, t) for s, t in...]
  transfers between devices with their start and end apart: 15 -> 15, of which waited for: 7 -> 8; matrix products, arithmetic and copies ran while one was open for 2% -> 0% of each run, Pallas kernels for 15% -> 7%
where the time goes in v3:
time: 33.5 us; the launch traced here: 33.3 us
  starting transfers between devices  17.5 us (52%)
  Pallas kernels  7.11 us (21%)
  waiting for transfers between devices  6.59 us (20%)
  local copies, waits for them, and re-layouts  1.37 us (4%)
  between operations  0.69 us (2%)
    ppermute x15, starting transfers between devices, swap(): lax.ppermute(x, axis, [(i, i ^ k) for i in range(lax.axis_size(axis))])  17.5 us
    ppermute x15, waiting for transfers between devices, swap(): lax.ppermute(x, axis, [(i, i ^ k) for i in range(lax.axis_size(axis))])  6.59 us
    pallas_call x5, Pallas kernels, call(): pl.pallas_call(kernel, out_shape=[jax.ShapeDtypeStruct(s, t) for s, t in...  5.02 us
    pallas_call x1, Pallas kernels, shards(): pl.pallas_call(functools.partial(update_kernel, groups, slots), out_shape...  2.09 us
    unnamed x14, local copies, waits for them, and re-layouts  1.36 us
  transfers between devices with their start and end apart: 15, of which 8 were waited for; matrix products, arithmetic and copies ran while one was open for 0% of the time, Pallas kernels for 7%

profile of v3, /device:TPU:0, one launch (start us, length us, event | category | flops | bytes accessed | tf_op | source)
XLA Modules:
  0.0 33.3 jit_solution(2944098121220515968)
XLA Ops:
  0.6 3.0 %collective-permute-start.2 = (bf16[320,256]{1,0:T(8,128)(2,1)}, bf16[320,256]{1,0:T(8,128)(2,1)S(1)}, u32[]{:S(2)}, u32[]{:S(2)}) collective-permute-start(bf16[320,256]{1,0:T(8,128)(2,1)} %refs_0_.3), channel_id=1, source_target_pairs={{0,16},{8,24},{16,0},{24,8},{1,17},{9,25},{17,1},{25,9},{2,18},{10... | collective-permute-start | bytes 491528 | tf_op jit(solution)/shard_map/ppermute | solution.py:181
  3.7 0.0 collective-permute-start.1
  3.7 0.2 collective-permute-start.3
  3.8 1.9 %collective-permute-start = (bf16[320,256]{1,0:T(8,128)(2,1)}, bf16[320,256]{1,0:T(8,128)(2,1)S(1)}, u32[]{:S(2)}, u32[]{:S(2)}) collective-permute-start(bf16[320,256]{1,0:T(8,128)(2,1)} %refs_0_.2), channel_id=1, source_target_pairs={{0,16},{8,24},{16,0},{24,8},{1,17},{9,25},{17,1},{25,9},{2,18},{10... | collective-permute-start | bytes 491528 | tf_op jit(solution)/shard_map/ppermute | solution.py:181
  5.7 0.0 copy-start.6
  5.7 0.7 %copy-done.6 = s32[320,1]{0,1:T(1,128)S(1)} copy-done((s32[320,1]{0,1:T(1,128)S(1)}, s32[320,1]{0,1:T(1,128)}, u32[]{:S(2)}) %copy-start.6) | copy-done | bytes 1304
  6.4 0.0 copy-start.4
  6.4 0.7 %copy-done.4 = s32[320]{0:T(512)S(1)} copy-done((s32[320]{0:T(512)S(1)}, s32[320]{0:T(512)}, u32[]{:S(2)}) %copy-start.4) | copy-done | bytes 1304
  7.1 0.8 %shard_map.102 = (bf16[640,320]{1,0:T(8,128)(2,1)S(1)}, bf16[8,8,256]{2,1,0:T(8,128)(2,1)S(1)}) custom-call(s32[1,320]{1,0:T(1,128)S(1)} %add.6.code_ref), custom_call_target="tpu_custom_call" | custom-call | flops 1073741824 | bytes 1024 | tf_op jit(solution)/shard_map/pallas_call | solution.py:164
  7.9 1.1 %collective-permute-done.3 = s32[320]{0:T(512)S(1)} collective-permute-done((s32[320]{0:T(512)}, s32[320]{0:T(512)S(1)}, u32[]{:S(2)}, u32[]{:S(2)}) %collective-permute-start.3) | collective-permute-done | bytes 1312 | tf_op jit(solution)/shard_map/ppermute | solution.py:181
  8.9 0.0 collective-permute-done.2.refs_4_.refs_2_
  9.0 0.0 collective-permute-start.4
  9.0 0.0 copy-done.5
  9.0 0.5 %collective-permute-start.5 = (s32[320]{0:T(512)S(1)}, s32[320]{0:T(512)S(1)}, u32[]{:S(2)}, u32[]{:S(2)}) collective-permute-start(s32[320]{0:T(512)S(1)} %copy-done.5), channel_id=1, source_target_pairs={{0,8},{8,0},{16,24},{24,16},{1,9},{9,1},{17,25},{25,17},{2,10},{10... | collective-permute-start | bytes 3848 | tf_op jit(solution)/shard_map/ppermute | solution.py:181
  9.5 0.1 collective-permute-start.6
  9.5 0.8 %collective-permute-done.5 = s32[320]{0:T(512)S(1)} collective-permute-done((s32[320]{0:T(512)S(1)}, s32[320]{0:T(512)S(1)}, u32[]{:S(2)}, u32[]{:S(2)}) %collective-permute-start.5) | collective-permute-done | bytes 1312 | tf_op jit(solution)/shard_map/ppermute | solution.py:181
  10.4 0.3 collective-permute-done.6
  10.6 0.0 copy-start.2
  10.6 0.0 copy-start.3
  10.6 0.3 shard_map.103.refs_6_
  10.9 0.7 %collective-permute-done.refs_1_ = bf16[320,256]{1,0:T(8,128)(2,1)S(1)} collective-permute-done((bf16[320,256]{1,0:T(8,128)(2,1)}, bf16[320,256]{1,0:T(8,128)(2,1)S(1)}, u32[]{:S(2)}, u32[]{:S(2)}) %collective-permute-start) | collective-permute-done | bytes 163872 | tf_op jit(solution)/shard_map/ppermute | solution.py:181
  11.6 0.0 collective-permute-done.1.refs_3_.refs_1_
  11.6 0.0 collective-permute-done.4.refs_5_.refs_3_
  11.6 0.0 copy-done.2
  11.6 0.0 copy-done.3
  11.7 2.3 %shard_map.104 = (f32[320,256]{1,0:T(8,128)S(1)}, f32[320,256]{1,0:T(8,128)S(1)}, f32[320]{0:T(512)}, bf16[4,320,320]{2,1,0:T(8,128)(2,1)S(1)}) custom-call(bf16[320,256]{1,0:T(8,128)(2,1)S(1)} %copy-done.2, bf16[320,256]{1,0:T(8,128)(2,1)S(1)} %collective-permute-done.refs_1_, bf16[320,256]{1,0:T(8,128)(2,1)S(1)} %copy-done.3, ...), custom_call_target="tpu_custom_call" | custom-call | bytes 1024 | tf_op jit(solution)/shard_map/pallas_call | solution.py:164
  13.9 0.1 collective-permute-start.7
  14.1 1.3 %shard_map.105 = f32[320,256]{1,0:T(8,128)} custom-call(bf16[4,320,320]{2,1,0:T(8,128)(2,1)S(1)} %get-tuple-element.30.weights_ref, bf16[320,256]{1,0:T(8,128)(2,1)S(1)} %copy-done.3, bf16[320,256]{1,0:T(8,128)(2,1)S(1)} %collective-permute-done.1.refs_3_.refs_1_, bf16[320,256]{1,0:T(8,128)(2,1)S(1)} %collective-permute-done.2.refs_4_.refs_2_, ...), custom_call_target="tpu_custom_call" | custom-call | flops 1073741824 | bytes 1024 | tf_op jit(solution)/shard_map/pallas_call | solution.py:164
  15.4 0.0 copy-start
  15.4 0.2 collective-permute-done.7.other_ref
  15.6 0.4 %shard_map.106 = (bf16[88,256]{1,0:T(8,128)(2,1)S(1)}, bf16[88,256]{1,0:T(8,128)(2,1)S(1)}, bf16[88,256]{1,0:T(8,128)(2,1)S(1)}, bf16[88,256]{1,0:T(8,128)(2,1)S...) custom-call(bf16[640,320]{1,0:T(8,128)(2,1)S(1)} %get-tuple-element., ...), custom_call_target="tpu_custom_call" | custom-call | bytes 1024 | tf_op jit(solution)/shard_map/pallas_call | solution.py:164
  16.0 3.1 %collective-permute-start.8 = (bf16[88,256]{1,0:T(8,128)(2,1)S(1)}, bf16[88,256]{1,0:T(8,128)(2,1)S(1)}, u32[]{:S(2)}, u32[]{:S(2)}) collective-permute-start(bf16[88,256]{1,0:T(8,128)(2,1)S(1)} %get-tuple-element.37), channel_id=1, source_target_pairs={{0,4},{1,5},{2,6},{3,7},{4,0},{5,1},{6,2},{7,3},{8,12},{9,13},{10,... | collective-permute-start | bytes 135176 | tf_op jit(solution)/shard_map/ppermute | solution.py:181
  19.1 1.3 %collective-permute-start.9 = (bf16[88,256]{1,0:T(8,128)(2,1)S(1)}, bf16[88,256]{1,0:T(8,128)(2,1)S(1)}, u32[]{:S(2)}, u32[]{:S(2)}) collective-permute-start(bf16[88,256]{1,0:T(8,128)(2,1)S(1)} %get-tuple-element.38), channel_id=1, source_target_pairs={{0,6},{1,7},{2,4},{3,5},{4,2},{5,3},{6,0},{7,1},{8,14},{9,15},{10,... | collective-permute-start | bytes 135176 | tf_op jit(solution)/shard_map/ppermute | solution.py:181
  20.4 2.6 %collective-permute-start.10 = (bf16[88,256]{1,0:T(8,128)(2,1)S(1)}, bf16[88,256]{1,0:T(8,128)(2,1)S(1)}, u32[]{:S(2)}, u32[]{:S(2)}) collective-permute-start(bf16[88,256]{1,0:T(8,128)(2,1)S(1)} %get-tuple-element.39), channel_id=1, source_target_pairs={{0,5},{1,4},{2,7},{3,6},{4,1},{5,0},{6,3},{7,2},{8,13},{9,12},{10,... | collective-permute-start | bytes 135176 | tf_op jit(solution)/shard_map/ppermute | solution.py:181
  23.0 0.9 %collective-permute-start.11 = (bf16[88,256]{1,0:T(8,128)(2,1)S(1)}, bf16[88,256]{1,0:T(8,128)(2,1)S(1)}, u32[]{:S(2)}, u32[]{:S(2)}) collective-permute-start(bf16[88,256]{1,0:T(8,128)(2,1)S(1)} %get-tuple-element.40), channel_id=1, source_target_pairs={{0,7},{1,6},{2,5},{3,4},{4,3},{5,2},{6,1},{7,0},{8,15},{9,14},{10,... | collective-permute-start | bytes 135176 | tf_op jit(solution)/shard_map/ppermute | solution.py:181
  23.9 0.9 %collective-permute-start.12 = (bf16[88,256]{1,0:T(8,128)(2,1)S(1)}, bf16[88,256]{1,0:T(8,128)(2,1)S(1)}, u32[]{:S(2)}, u32[]{:S(2)}) collective-permute-start(bf16[88,256]{1,0:T(8,128)(2,1)S(1)} %get-tuple-element.41), channel_id=1, source_target_pairs={{0,2},{1,3},{2,0},{3,1},{4,6},{5,7},{6,4},{7,5},{8,10},{9,11},{10,... | collective-permute-start | bytes 135176 | tf_op jit(solution)/shard_map/ppermute | solution.py:181
  24.8 0.0 collective-permute-done.8.refs_1_
  24.8 1.5 %collective-permute-start.13 = (bf16[88,256]{1,0:T(8,128)(2,1)S(1)}, bf16[88,256]{1,0:T(8,128)(2,1)S(1)}, u32[]{:S(2)}, u32[]{:S(2)}) collective-permute-start(bf16[88,256]{1,0:T(8,128)(2,1)S(1)} %get-tuple-element.42), channel_id=1, source_target_pairs={{0,1},{1,0},{2,3},{3,2},{4,5},{5,4},{6,7},{7,6},{8,9},{9,8},{10,11... | collective-permute-start | bytes 135176 | tf_op jit(solution)/shard_map/ppermute | solution.py:181
  26.3 0.0 collective-permute-done.9.refs_2_
  26.3 1.4 %collective-permute-start.14 = (bf16[88,256]{1,0:T(8,128)(2,1)S(1)}, bf16[88,256]{1,0:T(8,128)(2,1)S(1)}, u32[]{:S(2)}, u32[]{:S(2)}) collective-permute-start(bf16[88,256]{1,0:T(8,128)(2,1)S(1)} %get-tuple-element.43), channel_id=1, source_target_pairs={{0,3},{1,2},{2,1},{3,0},{4,7},{5,6},{6,5},{7,4},{8,11},{9,10},{10,... | collective-permute-start | bytes 135176 | tf_op jit(solution)/shard_map/ppermute | solution.py:181
  27.7 0.9 %collective-permute-done.10.refs_3_ = bf16[88,256]{1,0:T(8,128)(2,1)S(1)} collective-permute-done((bf16[88,256]{1,0:T(8,128)(2,1)S(1)}, bf16[88,256]{1,0:T(8,128)(2,1)S(1)}, u32[]{:S(2)}, u32[]{:S(2)}) %collective-permute-start.10) | collective-permute-done | bytes 45088 | tf_op jit(solution)/shard_map/ppermute | solution.py:181
  28.6 1.3 %collective-permute-done.11.refs_4_ = bf16[88,256]{1,0:T(8,128)(2,1)S(1)} collective-permute-done((bf16[88,256]{1,0:T(8,128)(2,1)S(1)}, bf16[88,256]{1,0:T(8,128)(2,1)S(1)}, u32[]{:S(2)}, u32[]{:S(2)}) %collective-permute-start.11) | collective-permute-done | bytes 45088 | tf_op jit(solution)/shard_map/ppermute | solution.py:181
  29.9 0.0 collective-permute-done.12.refs_5_
  29.9 0.0 collective-permute-done.13.refs_6_
  29.9 1.3 %collective-permute-done.14.refs_7_ = bf16[88,256]{1,0:T(8,128)(2,1)S(1)} collective-permute-done((bf16[88,256]{1,0:T(8,128)(2,1)S(1)}, bf16[88,256]{1,0:T(8,128)(2,1)S(1)}, u32[]{:S(2)}, u32[]{:S(2)}) %collective-permute-start.14) | collective-permute-done | bytes 45088 | tf_op jit(solution)/shard_map/ppermute | solution.py:181
  31.2 0.0 copy-done.1
  31.2 0.0 copy-done
  31.2 2.1 %shard_map.107 = (f32[640,256]{1,0:T(8,128)}, f32[640,256]{1,0:T(8,128)}) custom-call(bf16[88,256]{1,0:T(8,128)(2,1)S(1)} %get-tuple-element.36.refs_0_, bf16[88,256]{1,0:T(8,128)(2,1)S(1)} %collective-permute-done.8.refs_1_, bf16[88,256]{1,0:T(8,128)(2,1)S(1)} %collective-permute-done.9.refs_2_, bf16[88,256]{1,0:T(8,128)(2,1)S(1)} %collective-permute-done.10.refs_3_, ...), custom_call_target="tpu_custom_call" | custom-call | tf_op jit(solution)/shard_map/pallas_call | solution.py:252
  (9 shorter events, 0.0 us)
Async XLA Ops:
  0.6 8.3 %collective-permute-start.2 = (bf16[320,256]{1,0:T(8,128)(2,1)}, bf16[320,256]{1,0:T(8,128)(2,1)S(1)}, u32[]{:S(2)}, u32[]{:S(2)}) collective-permute-start(bf16[320,256]{1,0:T(8,128)(2,1)} %refs_0_.3), channel_id=1, source_target_pairs={{0,16},{8,24},{16,0},{24,8},{1,17},{9,25},{17,1},{25,9},{2,18},{10... | collective-permute-start | bytes 491528 | tf_op jit(solution)/shard_map/ppermute | solution.py:181
  3.7 8.0 %collective-permute-start.1 = (bf16[320,256]{1,0:T(8,128)(2,1)}, bf16[320,256]{1,0:T(8,128)(2,1)S(1)}, u32[]{:S(2)}, u32[]{:S(2)}) collective-permute-start(bf16[320,256]{1,0:T(8,128)(2,1)} %refs_0_.3), channel_id=1, source_target_pairs={{0,8},{8,0},{16,24},{24,16},{1,9},{9,1},{17,25},{25,17},{2,10},{10... | collective-permute-start | bytes 491528 | tf_op jit(solution)/shard_map/ppermute | solution.py:181
  3.7 5.3 %collective-permute-start.3 = (s32[320]{0:T(512)}, s32[320]{0:T(512)S(1)}, u32[]{:S(2)}, u32[]{:S(2)}) collective-permute-start(s32[320]{0:T(512)} %param.11), channel_id=1, source_target_pairs={{0,16},{8,24},{16,0},{24,8},{1,17},{9,25},{17,1},{25,9},{2,18},{10... | collective-permute-start | bytes 3848 | tf_op jit(solution)/shard_map/ppermute | solution.py:181
  3.8 7.8 %collective-permute-start = (bf16[320,256]{1,0:T(8,128)(2,1)}, bf16[320,256]{1,0:T(8,128)(2,1)S(1)}, u32[]{:S(2)}, u32[]{:S(2)}) collective-permute-start(bf16[320,256]{1,0:T(8,128)(2,1)} %refs_0_.2), channel_id=1, source_target_pairs={{0,16},{8,24},{16,0},{24,8},{1,17},{9,25},{17,1},{25,9},{2,18},{10... | collective-permute-start | bytes 491528 | tf_op jit(solution)/shard_map/ppermute | solution.py:181
  5.7 0.7 %copy-start.6 = (s32[320,1]{0,1:T(1,128)S(1)}, s32[320,1]{0,1:T(1,128)}, u32[]{:S(2)}) copy-start(s32[320,1]{0,1:T(1,128)} %param.9) | copy-start | bytes 3844
  6.4 0.7 %copy-start.4 = (s32[320]{0:T(512)S(1)}, s32[320]{0:T(512)}, u32[]{:S(2)}) copy-start(s32[320]{0:T(512)} %param.10) | copy-start | bytes 3844
  7.1 1.9 %copy-start.5 = (s32[320]{0:T(512)S(1)}, s32[320]{0:T(512)}, u32[]{:S(2)}) copy-start(s32[320]{0:T(512)} %param.11) | copy-start | bytes 3844
  9.0 2.7 %collective-permute-start.4 = (bf16[320,256]{1,0:T(8,128)(2,1)S(1)}, bf16[320,256]{1,0:T(8,128)(2,1)S(1)}, u32[]{:S(2)}, u32[]{:S(2)}) collective-permute-start(bf16[320,256]{1,0:T(8,128)(2,1)S(1)} %collective-permute-done.2.refs_4_.refs_2_), channel_id=1, source_target_pairs={{0,8},{8,0},{16,24},{24,16},{1,9},{9,1},{17,25},{25,17},{2,10},{10... | collective-permute-start | bytes 491528 | tf_op jit(solution)/shard_map/ppermute | solution.py:181
  9.0 1.4 %collective-permute-start.5 = (s32[320]{0:T(512)S(1)}, s32[320]{0:T(512)S(1)}, u32[]{:S(2)}, u32[]{:S(2)}) collective-permute-start(s32[320]{0:T(512)S(1)} %copy-done.5), channel_id=1, source_target_pairs={{0,8},{8,0},{16,24},{24,16},{1,9},{9,1},{17,25},{25,17},{2,10},{10... | collective-permute-start | bytes 3848 | tf_op jit(solution)/shard_map/ppermute | solution.py:181
  9.5 1.2 %collective-permute-start.6 = (s32[320]{0:T(512)S(1)}, s32[320]{0:T(512)S(1)}, u32[]{:S(2)}, u32[]{:S(2)}) collective-permute-start(s32[320]{0:T(512)S(1)} %collective-permute-done.3), channel_id=1, source_target_pairs={{0,8},{8,0},{16,24},{24,16},{1,9},{9,1},{17,25},{25,17},{2,10},{10... | collective-permute-start | bytes 3848 | tf_op jit(solution)/shard_map/ppermute | solution.py:181
  10.6 1.0 %copy-start.2 = (bf16[320,256]{1,0:T(8,128)(2,1)S(1)}, bf16[320,256]{1,0:T(8,128)(2,1)}, u32[]{:S(2)}) copy-start(bf16[320,256]{1,0:T(8,128)(2,1)} %refs_0_.2) | copy-start | bytes 491524
  10.6 1.0 %copy-start.3 = (bf16[320,256]{1,0:T(8,128)(2,1)S(1)}, bf16[320,256]{1,0:T(8,128)(2,1)}, u32[]{:S(2)}) copy-start(bf16[320,256]{1,0:T(8,128)(2,1)} %refs_0_.3) | copy-start | bytes 491524
  13.9 1.6 %collective-permute-start.7 = (f32[320,256]{1,0:T(8,128)S(1)}, f32[320,256]{1,0:T(8,128)S(1)}, u32[]{:S(2)}, u32[]{:S(2)}) collective-permute-start(f32[320,256]{1,0:T(8,128)S(1)} %get-tuple-element.29), channel_id=1, source_target_pairs={{0,8},{8,0},{16,24},{24,16},{1,9},{9,1},{17,25},{25,17},{2,10},{10... | collective-permute-start | bytes 983048 | tf_op jit(solution)/shard_map/ppermute | solution.py:181
  14.1 17.2 %copy-start.1 = (f32[640,256]{1,0:T(8,128)S(1)}, f32[640,256]{1,0:T(8,128)}, u32[]{:S(2)}) copy-start(f32[640,256]{1,0:T(8,128)} %refs_9_.1) | copy-start | bytes 1966084
  15.4 15.9 %copy-start = (f32[640,256]{1,0:T(8,128)S(1)}, f32[640,256]{1,0:T(8,128)}, u32[]{:S(2)}) copy-start(f32[640,256]{1,0:T(8,128)} %refs_8_.1) | copy-start | bytes 1966084
  16.0 8.8 %collective-permute-start.8 = (bf16[88,256]{1,0:T(8,128)(2,1)S(1)}, bf16[88,256]{1,0:T(8,128)(2,1)S(1)}, u32[]{:S(2)}, u32[]{:S(2)}) collective-permute-start(bf16[88,256]{1,0:T(8,128)(2,1)S(1)} %get-tuple-element.37), channel_id=1, source_target_pairs={{0,4},{1,5},{2,6},{3,7},{4,0},{5,1},{6,2},{7,3},{8,12},{9,13},{10,... | collective-permute-start | bytes 135176 | tf_op jit(solution)/shard_map/ppermute | solution.py:181
  19.1 7.2 %collective-permute-start.9 = (bf16[88,256]{1,0:T(8,128)(2,1)S(1)}, bf16[88,256]{1,0:T(8,128)(2,1)S(1)}, u32[]{:S(2)}, u32[]{:S(2)}) collective-permute-start(bf16[88,256]{1,0:T(8,128)(2,1)S(1)} %get-tuple-element.38), channel_id=1, source_target_pairs={{0,6},{1,7},{2,4},{3,5},{4,2},{5,3},{6,0},{7,1},{8,14},{9,15},{10,... | collective-permute-start | bytes 135176 | tf_op jit(solution)/shard_map/ppermute | solution.py:181
  20.4 8.2 %collective-permute-start.10 = (bf16[88,256]{1,0:T(8,128)(2,1)S(1)}, bf16[88,256]{1,0:T(8,128)(2,1)S(1)}, u32[]{:S(2)}, u32[]{:S(2)}) collective-permute-start(bf16[88,256]{1,0:T(8,128)(2,1)S(1)} %get-tuple-element.39), channel_id=1, source_target_pairs={{0,5},{1,4},{2,7},{3,6},{4,1},{5,0},{6,3},{7,2},{8,13},{9,12},{10,... | collective-permute-start | bytes 135176 | tf_op jit(solution)/shard_map/ppermute | solution.py:181
  23.0 6.9 %collective-permute-start.11 = (bf16[88,256]{1,0:T(8,128)(2,1)S(1)}, bf16[88,256]{1,0:T(8,128)(2,1)S(1)}, u32[]{:S(2)}, u32[]{:S(2)}) collective-permute-start(bf16[88,256]{1,0:T(8,128)(2,1)S(1)} %get-tuple-element.40), channel_id=1, source_target_pairs={{0,7},{1,6},{2,5},{3,4},{4,3},{5,2},{6,1},{7,0},{8,15},{9,14},{10,... | collective-permute-start | bytes 135176 | tf_op jit(solution)/shard_map/ppermute | solution.py:181
  23.9 6.0 %collective-permute-start.12 = (bf16[88,256]{1,0:T(8,128)(2,1)S(1)}, bf16[88,256]{1,0:T(8,128)(2,1)S(1)}, u32[]{:S(2)}, u32[]{:S(2)}) collective-permute-start(bf16[88,256]{1,0:T(8,128)(2,1)S(1)} %get-tuple-element.41), channel_id=1, source_target_pairs={{0,2},{1,3},{2,0},{3,1},{4,6},{5,7},{6,4},{7,5},{8,10},{9,11},{10,... | collective-permute-start | bytes 135176 | tf_op jit(solution)/shard_map/ppermute | solution.py:181
  24.8 5.1 %collective-permute-start.13 = (bf16[88,256]{1,0:T(8,128)(2,1)S(1)}, bf16[88,256]{1,0:T(8,128)(2,1)S(1)}, u32[]{:S(2)}, u32[]{:S(2)}) collective-permute-start(bf16[88,256]{1,0:T(8,128)(2,1)S(1)} %get-tuple-element.42), channel_id=1, source_target_pairs={{0,1},{1,0},{2,3},{3,2},{4,5},{5,4},{6,7},{7,6},{8,9},{9,8},{10,11... | collective-permute-start | bytes 135176 | tf_op jit(solution)/shard_map/ppermute | solution.py:181
  26.3 4.9 %collective-permute-start.14 = (bf16[88,256]{1,0:T(8,128)(2,1)S(1)}, bf16[88,256]{1,0:T(8,128)(2,1)S(1)}, u32[]{:S(2)}, u32[]{:S(2)}) collective-permute-start(bf16[88,256]{1,0:T(8,128)(2,1)S(1)} %get-tuple-element.43), channel_id=1, source_target_pairs={{0,3},{1,2},{2,1},{3,0},{4,7},{5,6},{6,5},{7,4},{8,11},{9,10},{10,... | collective-permute-start | bytes 135176 | tf_op jit(solution)/shard_map/ppermute | solution.py:181

commit v4 on v3

v4 whole, which is shorter than its diff:
```python
import functools
import math

import jax
import jax.numpy as jnp
from jax import lax
from jax.experimental import pallas as pl
from jax.experimental.pallas import tpu as pltpu
from jax.sharding import PartitionSpec as P

D = 256
SCALE = 3.0 / math.sqrt(D)
LOG2E = math.log2(math.e)
LANES = 128
TAIL = 8
ROW_CODES = 1 << 16
MIB = 1 << 20
NT = (((1,), (1,)), ((), ()))
TN = (((0,), (0,)), ((), ()))
F32 = jnp.float32
BF16 = jnp.bfloat16


def dot(a, b, dims=(((1,), (0,)), ((), ()))):
    return lax.dot_general(a, b, dims, preferred_element_type=F32)


def spread(column, width):
    pieces = [column] * (width // LANES)
    if width % LANES:
        pieces.append(column[:, : width % LANES])
    return jnp.concatenate(pieces, axis=1)


def code(x):
    y = x * x
    return jnp.where(x < 0, -y, y) * y


def decode(u):
    root = lax.rsqrt(lax.rsqrt(jnp.abs(u)))
    return jnp.where(u < 0, -root, root)


def diagonal(block):
    return lax.broadcasted_iota(jnp.int32, (block, block), 0) == lax.broadcasted_iota(
        jnp.int32, (block, block), 1
    )


def local_kernel(groups, slots, code_ref, pick_ref, tail_ref):
    block = code_ref.shape[1]
    owner = code_ref[...] // ROW_CODES
    offset = code_ref[...] % ROW_CODES
    member = lax.broadcasted_iota(jnp.int32, (groups, block), 0) == owner
    before = lax.broadcasted_iota(jnp.int32, (block, block), 0) < lax.broadcasted_iota(
        jnp.int32, (block, block), 1
    )
    ranks = dot(member.astype(BF16), before.astype(BF16))
    rank = jnp.sum(jnp.where(member, ranks, 0.0), axis=0, keepdims=True).astype(jnp.int32)
    high = jnp.broadcast_to((offset // LANES).astype(F32), (TAIL, block)).astype(BF16)
    low = jnp.broadcast_to((offset % LANES).astype(F32), (TAIL, block)).astype(BF16)
    here = lax.broadcasted_iota(jnp.int32, (LANES, block), 0) == rank
    for g in range(groups):
        pick = (here & (owner == g)).astype(F32).astype(BF16)
        pick_ref[g * slots : (g + 1) * slots] = pick[:slots]
        tail_ref[g] = jnp.concatenate([dot(high, pick, NT), dot(low, pick, NT)], axis=1).astype(BF16)


def bias_kernel(n, *refs):
    for b in range(n):
        block = refs[b].shape[1]
        row = jnp.log(refs[b][...].astype(F32)) * LOG2E
        refs[n][b] = jnp.transpose(jnp.broadcast_to(row, (LANES, block)))


def fill_logits(q, item_refs, bias_ref, first, out_ref):
    top = None
    for b, item_ref in enumerate(item_refs):
        logits = dot(item_ref[...], q, NT) * (SCALE * LOG2E)
        logits -= spread(bias_ref[first + b], q.shape[0])
        out_ref[b] = logits
        high = jnp.max(logits, axis=0, keepdims=True)
        top = high if top is None else jnp.maximum(top, high)
    return top


def to_powers(ref, top):
    total = jnp.zeros(top.shape, F32)
    for b in range(ref.shape[0]):
        e = jnp.exp2(ref[b] - top)
        ref[b] = e
        total += jnp.sum(e, axis=0, keepdims=True)
    return total


def diagonal(block):
    return lax.broadcasted_iota(jnp.int32, (block, block), 0) == lax.broadcasted_iota(
        jnp.int32, (block, block), 1
    )


def early_kernel(n, q_ref, *refs):
    item_refs, (bias_ref, e_ref, stats_ref) = refs[:n], refs[n:]
    block = q_ref.shape[0]
    top = fill_logits(q_ref[...], item_refs, bias_ref, 0, e_ref)
    chosen = jnp.sum(jnp.where(diagonal(block), e_ref[0], 0.0), axis=0, keepdims=True)
    stats_ref[0:1] = top
    stats_ref[1:2] = to_powers(e_ref, top)
    stats_ref[2:3] = chosen


def main_kernel(early, late, *refs):
    n = early + late
    q_ref, far_ref, item_refs, refs = refs[0], refs[1], refs[2 : 2 + n], refs[2 + n :]
    bias_ref, e_ref, stats_ref, mine_out, mate_out, loss_ref, late_ref, factor_ref, far_e_ref = refs
    block = q_ref.shape[0]
    q, far = q_ref[...], far_ref[...]
    far_top = fill_logits(far, item_refs, bias_ref, 0, far_e_ref)
    early_top, early_total, chosen = stats_ref[0:1], stats_ref[1:2], stats_ref[2:3]
    top = fill_logits(q, item_refs[early:], bias_ref, early, late_ref)
    top = jnp.maximum(top, early_top)
    far_inverse = 1.0 / to_powers(far_e_ref, far_top)
    shrink = jnp.exp2(early_top - top)
    total = to_powers(late_ref, top) + early_total * shrink
    inverse = 1.0 / total
    factor = shrink * inverse
    mate = dot((e_ref[1] * factor).astype(BF16), q)
    mate_out[...] = mate + dot((far_e_ref[1] * far_inverse).astype(BF16), far)
    weights = e_ref[0] * factor
    weights = jnp.where(diagonal(block), weights - 1.0, weights)
    mine = dot(weights.astype(BF16), q)
    mine_out[...] = mine + dot((far_e_ref[0] * far_inverse).astype(BF16), far)
    loss_ref[...] = ((top + jnp.log2(total) - chosen) * (1.0 / LOG2E))[0]
    factor_ref[0:1] = factor
    factor_ref[1:2] = inverse


def more_kernel(n, q_ref, *refs):
    item_refs, refs = refs[:n], refs[n:]
    bias_ref, mine_ref, mate_ref, mine_out, mate_out, e_ref = refs
    q = q_ref[...]
    inverse = 1.0 / to_powers(e_ref, fill_logits(q, item_refs, bias_ref, 0, e_ref))
    mate_out[...] = mate_ref[...] + dot((e_ref[1] * inverse).astype(BF16), q)
    mine_out[...] = mine_ref[...] + dot((e_ref[0] * inverse).astype(BF16), q)


def query_kernel(early, late, e_ref, late_ref, factor_ref, *refs):
    item_refs, out_ref = refs[:-1], refs[-1]
    total = None
    for b, item_ref in enumerate(item_refs):
        if b < early:
            weights = e_ref[b] * factor_ref[0:1]
        else:
            weights = late_ref[b - early] * factor_ref[1:2]
        if b == 0:
            weights = jnp.where(diagonal(weights.shape[0]), weights - 1.0, weights)
        part = dot(weights.astype(BF16), item_ref[...], TN)
        total = part if total is None else total + part
    out_ref[...] = total * SCALE


def pack_kernel(groups, slots, pick_ref, tail_ref, mine_ref, other_ref, *out_refs):
    grad = code((mine_ref[...] + other_ref[...]) * SCALE).astype(BF16)
    picked = dot(pick_ref[...], grad).astype(BF16)
    for g in range(groups):
        out = out_refs[g] if len(out_refs) == groups else out_refs[0].at[g]
        out[:slots] = picked[g * slots : (g + 1) * slots]
        out[slots:] = tail_ref[g]


def scatter(slots, got_refs, values_ref, ids_ref, rows):
    packets = got_refs
    if len(got_refs[0].shape) == 3:
        packets = [got_refs[0].at[g] for g in range(got_refs[0].shape[0])]
    half = len(packets) * slots
    for g, got in enumerate(packets):
        tail = got[slots : slots + TAIL].astype(F32)
        ids = tail[:, :slots] * LANES + tail[:, LANES : LANES + slots]
        ids_ref[:, g * slots : (g + 1) * slots] = ids
        values = decode(got[:slots].astype(F32))
        high = values.astype(BF16)
        values_ref[g * slots : (g + 1) * slots] = high
        low = (values - high.astype(F32)).astype(BF16)
        values_ref[half + g * slots : half + (g + 1) * slots] = low
    index = lax.broadcasted_iota(jnp.int32, (rows, half), 0).astype(F32)
    put = (index == ids_ref[:1]).astype(F32).astype(BF16)
    return dot(jnp.concatenate([put, put], axis=1), values_ref[...])


def first_kernel(slots, *refs):
    got_refs, (out_ref, values_ref, ids_ref) = refs[:-3], refs[-3:]
    out_ref[...] = scatter(slots, got_refs, values_ref, ids_ref, out_ref.shape[0])


def update_kernel(slots, partial, *refs):
    inputs, refs = refs[:-8], refs[-8:]
    table_ref, accum_ref, table_out, accum_out, values_ref, ids_ref, new_ref, sems = refs
    got_refs = inputs[1:] if partial else inputs
    rows = table_ref.shape[0]
    grad = scatter(slots, got_refs, values_ref, ids_ref, rows)
    if partial:
        grad += inputs[0][...]
    accum_new = accum_ref[...] + grad * grad
    new_ref[1] = accum_new
    first = pltpu.make_async_copy(new_ref.at[1], accum_out, sems.at[1])
    first.start()
    new_ref[0] = table_ref[...] - 0.1 * grad / (jnp.sqrt(accum_new) + 1e-08)
    second = pltpu.make_async_copy(new_ref.at[0], table_out, sems.at[0])
    second.start()
    first.wait()
    second.wait()


def call(kernel, outs, *args, scratch=(), limit=16, flops=0):
    return pl.pallas_call(
        kernel,
        out_shape=[jax.ShapeDtypeStruct(s, t) for s, t in outs],
        scratch_shapes=list(scratch),
        compiler_params=pltpu.CompilerParams(vmem_limit_bytes=limit * MIB),
        cost_estimate=pl.CostEstimate(flops=flops, bytes_accessed=1024, transcendentals=0),
    )(*args)


def shards(queries, items, item_owner, item_offset, sample_counts, table, accum):
    block = queries.shape[0]
    n, groups = lax.axis_size("wide"), lax.axis_size("group")
    capacity = 2 * block // groups
    slots = -(-capacity // TAIL) * TAIL
    paired = groups <= 8

    def swap(x, k, axis="wide"):
        return lax.ppermute(x, axis, [(i, i ^ k) for i in range(lax.axis_size(axis))])

    far_items = [swap(items, k) for k in range(2, n, 2)]
    far_queries = [swap(queries, k) for k in range(2, n, 2)]

    owner = item_owner.reshape(1, block)
    if paired:
        owner = owner ^ lax.axis_index("group")
    pick, tail = call(
        functools.partial(local_kernel, groups, slots),
        [((groups * slots, block), BF16), ((groups, TAIL, D), BF16)],
        owner * ROW_CODES + item_offset.reshape(1, block),
        flops=1 << 30,
    )
    own_counts, tail = lax.optimization_barrier((sample_counts, tail))
    counts = [swap(own_counts, k) for k in range(1, n)]
    far_items, counts, tail = lax.optimization_barrier((far_items, counts, tail))
    item_blocks = [items, swap(items, 1)] + far_items
    early = len(item_blocks)
    item_blocks += [swap(x, 1) for x in far_items]
    late = n - early
    count_blocks = [sample_counts, counts[0]] + counts[1::2] + counts[2::2]
    (bias,) = call(
        functools.partial(bias_kernel, n),
        [((n, block, LANES), F32)],
        *[x.reshape(1, block) for x in count_blocks],
    )

    part = ((block, D), F32)
    square = (block, block)
    powers, stats = call(
        functools.partial(early_kernel, early),
        [((early, *square), F32), ((8, block), F32)],
        queries,
        *item_blocks[:early],
        bias,
        limit=8 + 2 * n,
    )
    mine, mate, loss, late_powers, factors = call(
        functools.partial(main_kernel, early, late),
        [part, part, ((block,), F32), ((late, *square), F32), ((8, block), F32)],
        queries,
        far_queries[0],
        *item_blocks,
        bias,
        powers,
        stats,
        scratch=[pltpu.VMEM((n, *square), F32)],
        limit=8 + 4 * n,
    )
    for far in far_queries[1:]:
        mine, mate = call(
            functools.partial(more_kernel, n),
            [part, part],
            far,
            *item_blocks,
            bias,
            mine,
            mate,
            scratch=[pltpu.VMEM((n, *square), F32)],
            limit=8 + 4 * n,
        )
    other = swap(mate, 1)
    (query_grad,) = call(
        functools.partial(query_kernel, early, late),
        [part],
        powers,
        late_powers,
        factors,
        *item_blocks,
        limit=8 + 2 * n,
        flops=1 << 30,
    )
    other, query_grad = lax.optimization_barrier((other, query_grad))
    if paired:
        packets = [((slots + TAIL, D), BF16)] * groups
    else:
        packets = [((groups, slots + TAIL, D), BF16)]
    packed = call(
        functools.partial(pack_kernel, groups, slots), packets, pick, tail, mine, other
    )
    if paired:
        order = sorted(range(1, groups), key=lambda k: (k < groups // 2, k % 2, k))
        got = [packed[0]] + [swap(packed[k], k, "group") for k in order]
    else:
        got = [lax.all_to_all(packed[0], "group", split_axis=0, concat_axis=0, tiled=True)]
    rows = table.shape[0]

    def scratch(packets):
        return [
            pltpu.VMEM((2 * packets * slots, D), BF16),
            pltpu.VMEM((TAIL, packets * slots), F32),
        ]

    half = groups // 2
    before = []
    if paired:
        before = call(
            functools.partial(first_kernel, slots),
            [((rows, D), F32)],
            *got[:half],
            scratch=scratch(half),
            flops=1 << 28,
        )
        got = got[half:]
    table_new, accum_new = pl.pallas_call(
        functools.partial(update_kernel, slots, paired),
        out_shape=[jax.ShapeDtypeStruct(table.shape, F32)] * 2,
        out_specs=[pl.BlockSpec(memory_space=pl.ANY)] * 2,
        scratch_shapes=[
            *scratch(half if paired else groups),
            pltpu.VMEM((2, rows, D), F32),
            pltpu.SemaphoreType.DMA((2,)),
        ],
        compiler_params=pltpu.CompilerParams(vmem_limit_bytes=32 * MIB),
    )(*before, *got, table, accum)
    return (loss, query_grad, table_new, accum_new)


def solution(mesh):
    placed = (
        P(("wide", "group"), None),
        P(("wide", "group"), None),
        P(("wide", "group"), None),
        P(("wide", "group")),
        P(("wide", "group")),
        P(("wide", "group"), None),
        P(("wide", "group"), None),
    )
    return jax.shard_map(
        shards,
        mesh=mesh,
        in_specs=placed,
        out_specs=(
            P(("wide", "group")),
            P(("wide", "group"), None),
            P(("wide", "group"), None),
            P(("wide", "group"), None),
        ),
        check_vma=False,
    )
```

time: 33.5 us -> 35.2 us (1.051)
  waiting for transfers between devices: 6.59 us -> 8.81 us
  other arithmetic: 0.02 us -> 1.38 us
  local copies, waits for them, and re-layouts: 1.37 us -> 0.03 us
  starting transfers between devices: 17.5 us -> 16.5 us
  Pallas kernels: 7.11 us -> 7.51 us
    ppermute x15, waiting for transfers between devices: 6.59 us -> 8.81 us  [swap(): lax.ppermute(x, axis, [(i, i ^ k) for i in range(lax.axis_size(axis))])]
    unnamed x14 -> x10, local copies, waits for them, and re-layouts: 1.36 us -> 0.02 us
    ppermute x15, starting transfers between devices: 17.5 us -> 16.5 us  [swap(): lax.ppermute(x, axis, [(i, i ^ k) for i in range(lax.axis_size(axis))])]
    add x1, other arithmetic: 0.01 us -> 0.68 us  [shards(): owner * ROW_CODES + item_offset.reshape(1, block)]
    mul x1, other arithmetic: 0.02 us -> 0.7 us  [shards(): owner * ROW_CODES + item_offset.reshape(1, block)]
    pallas_call x5 -> x7, Pallas kernels: 5.02 us -> 5.69 us  [call(): pl.pallas_call(kernel, out_shape=[jax.ShapeDtypeStruct(s, t) for s, t in...]
  transfers between devices with their start and end apart: 15 -> 15, of which waited for: 8 -> 7; matrix products, arithmetic and copies ran while one was open for 0% -> 4% of each run, Pallas kernels for 7% -> 10%
where the time goes in v4:
time: 35.2 us; the launch traced here: 35 us
  starting transfers between devices  16.5 us (47%)
  waiting for transfers between devices  8.81 us (25%)
  Pallas kernels  7.51 us (21%)
  other arithmetic  1.38 us (4%)
  between operations  0.7 us (2%)
    ppermute x15, starting transfers between devices, swap(): lax.ppermute(x, axis, [(i, i ^ k) for i in range(lax.axis_size(axis))])  16.5 us
    ppermute x15, waiting for transfers between devices, swap(): lax.ppermute(x, axis, [(i, i ^ k) for i in range(lax.axis_size(axis))])  8.81 us
    pallas_call x7, Pallas kernels, call(): pl.pallas_call(kernel, out_shape=[jax.ShapeDtypeStruct(s, t) for s, t in...  5.69 us
    pallas_call x1, Pallas kernels, shards(): pl.pallas_call(functools.partial(update_kernel, slots, paired), out_shape...  1.81 us
  transfers between devices with their start and end apart: 15, of which 7 were waited for; matrix products, arithmetic and copies ran while one was open for 4% of the time, Pallas kernels for 10%

profile of v4, /device:TPU:0, one launch (start us, length us, event | category | flops | bytes accessed | tf_op | source)
XLA Modules:
  0.0 35.0 jit_solution(8716757948115987226)
XLA Ops:
  0.6 3.0 %collective-permute-start.2 = (bf16[320,256]{1,0:T(8,128)(2,1)}, bf16[320,256]{1,0:T(8,128)(2,1)S(1)}, u32[]{:S(2)}, u32[]{:S(2)}) collective-permute-start(bf16[320,256]{1,0:T(8,128)(2,1)} %refs_0_.5), channel_id=1, source_target_pairs={{0,16},{8,24},{16,0},{24,8},{1,17},{9,25},{17,1},{25,9},{2,18},{10... | collective-permute-start | bytes 491528 | tf_op jit(solution)/shard_map/ppermute | solution.py:233
  3.7 0.7 %multiply_reduce_fusion = s32[320]{0:T(512)S(1)} fusion(s32[320,1]{0,1:T(1,128)} %param.9, s32[]{:T(128)S(6)} %axis_index.12), kind=kLoop, calls=%fused_computation | loop fusion | flops 640 | bytes 2564 | tf_op jit(solution)/shard_map/mul | solution.py:244
  4.4 0.7 %add.5 = s32[320]{0:T(512)S(1)} add(s32[320]{0:T(512)S(1)} %multiply_reduce_fusion, s32[320]{0:T(512)} %param.10) | non-fusion elementwise | flops 320 | bytes 3840 | tf_op jit(solution)/shard_map/add | solution.py:244
  5.1 0.0 copy-start.4
  5.1 0.0 copy-start.1
  5.1 0.0 copy-start
  5.1 0.8 %shard_map.102 = (bf16[640,320]{1,0:T(8,128)(2,1)S(1)}, bf16[8,8,256]{2,1,0:T(8,128)(2,1)S(1)}) custom-call(s32[1,320]{1,0:T(1,128)S(1)} %add.6.code_ref), custom_call_target="tpu_custom_call" | custom-call | flops 1073741824 | bytes 1024 | tf_op jit(solution)/shard_map/pallas_call | solution.py:216
  5.9 0.0 copy-done.4
  5.9 0.0 collective-permute-start.5
  5.9 1.2 %collective-permute-start.4 = (s32[320]{0:T(512)S(1)}, s32[320]{0:T(512)S(1)}, u32[]{:S(2)}, u32[]{:S(2)}) collective-permute-start(s32[320]{0:T(512)S(1)} %copy-done.4), channel_id=1, source_target_pairs={{0,16},{8,24},{16,0},{24,8},{1,17},{9,25},{17,1},{25,9},{2,18},{10... | collective-permute-start | bytes 3848 | tf_op jit(solution)/shard_map/ppermute | solution.py:233
  7.1 0.7 %collective-permute-start.3 = (s32[320]{0:T(512)S(1)}, s32[320]{0:T(512)S(1)}, u32[]{:S(2)}, u32[]{:S(2)}) collective-permute-start(s32[320]{0:T(512)S(1)} %copy-done.4), channel_id=1, source_target_pairs={{0,8},{8,0},{16,24},{24,16},{1,9},{9,1},{17,25},{25,17},{2,10},{10... | collective-permute-start | bytes 3848 | tf_op jit(solution)/shard_map/ppermute | solution.py:233
  7.8 0.0 copy-done.1
  7.8 0.0 collective-permute-start.1
  7.8 1.1 %collective-permute-done.5 = s32[320]{0:T(512)S(1)} collective-permute-done((s32[320]{0:T(512)S(1)}, s32[320]{0:T(512)S(1)}, u32[]{:S(2)}, u32[]{:S(2)}) %collective-permute-start.5) | collective-permute-done | bytes 1312 | tf_op jit(solution)/shard_map/ppermute | solution.py:233
  8.9 0.0 copy-done
  8.9 0.1 collective-permute-start
  9.0 0.5 %collective-permute-done.4 = s32[320]{0:T(512)S(1)} collective-permute-done((s32[320]{0:T(512)S(1)}, s32[320]{0:T(512)S(1)}, u32[]{:S(2)}, u32[]{:S(2)}) %collective-permute-start.4) | collective-permute-done | bytes 1312 | tf_op jit(solution)/shard_map/ppermute | solution.py:233
  9.6 0.0 collective-permute-done.3
  9.6 0.0 collective-permute-done.2.refs_2_.refs_4_
  9.6 0.2 collective-permute-start.6
  9.8 0.3 shard_map.103.refs_3_.refs_6_
  10.0 0.0 collective-permute-done.1.refs_1_.refs_3_
  10.1 0.6 %shard_map.104 = (f32[3,320,320]{2,1,0:T(8,128)S(1)}, f32[8,320]{1,0:T(8,128)S(1)}) custom-call(bf16[320,256]{1,0:T(8,128)(2,1)S(1)} %copy-done, bf16[320,256]{1,0:T(8,128)(2,1)S(1)} %copy-done.1, bf16[320,256]{1,0:T(8,128)(2,1)S(1)} %collective-permute-done.1.refs_1_.refs_3_, bf16[320,256]{1,0:T(8,128)(2,1)S(1)} %collective-permute-done.2.refs_2_.refs_4_, ...), custom_call_target="tpu_custom_call" | custom-call | bytes 1024 | tf_op jit(solution)/shard_map/pallas_call | solution.py:216
  10.7 3.9 %collective-permute-done.refs_1_ = bf16[320,256]{1,0:T(8,128)(2,1)S(1)} collective-permute-done((bf16[320,256]{1,0:T(8,128)(2,1)S(1)}, bf16[320,256]{1,0:T(8,128)(2,1)S(1)}, u32[]{:S(2)}, u32[]{:S(2)}) %collective-permute-start) | collective-permute-done | bytes 163872 | tf_op jit(solution)/shard_map/ppermute | solution.py:233
  14.6 0.0 collective-permute-done.6.refs_5_.refs_3_
  14.6 1.7 %shard_map.105 = (f32[320,256]{1,0:T(8,128)S(1)}, f32[320,256]{1,0:T(8,128)S(1)}, f32[320]{0:T(512)}, f32[1,320,320]{2,1,0:T(8,128)S(1)}, f32[8,320]{1,0:T(8,128)S(1)}) custom-call(bf16[320,256]{1,0:T(8,128)(2,1)S(1)} %copy-done, bf16[320,256]{1,0:T(8,128)(2,1)S(1)} %collective-permute-done.refs_1_, bf16[320,256]{1,0:T(8,128)(2,1)S(1)} %copy-done.1, ...), custom_call_target="tpu_custom_call" | custom-call | bytes 1024 | tf_op jit(solution)/shard_map/pallas_call | solution.py:216
  16.3 0.0 collective-permute-start.7
  16.3 1.3 %shard_map.106 = f32[320,256]{1,0:T(8,128)} custom-call(f32[3,320,320]{2,1,0:T(8,128)S(1)} %get-tuple-element.39.refs_7_.e_ref, f32[1,320,320]{2,1,0:T(8,128)S(1)} %get-tuple-element.43.late_ref, f32[8,320]{1,0:T(8,128)S(1)} %get-tuple-element.44.factor_ref, bf16[320,256]{1,0:T(8,128)(2,1)S(1)} %copy-done.1, ...), custom_call_target="tpu_custom_call" | custom-call | flops 1073741824 | bytes 1024 | tf_op jit(solution)/shard_map/pallas_call | solution.py:216
  17.6 0.3 collective-permute-done.7.other_ref
  17.9 0.4 %shard_map.107 = (bf16[88,256]{1,0:T(8,128)(2,1)S(1)}, bf16[88,256]{1,0:T(8,128)(2,1)S(1)}, bf16[88,256]{1,0:T(8,128)(2,1)S(1)}, bf16[88,256]{1,0:T(8,128)(2,1)S...) custom-call(bf16[640,320]{1,0:T(8,128)(2,1)S(1)} %get-tuple-element., ...), custom_call_target="tpu_custom_call" | custom-call | bytes 1024 | tf_op jit(solution)/shard_map/pallas_call | solution.py:216
  18.3 2.7 %collective-permute-start.8 = (bf16[88,256]{1,0:T(8,128)(2,1)S(1)}, bf16[88,256]{1,0:T(8,128)(2,1)S(1)}, u32[]{:S(2)}, u32[]{:S(2)}) collective-permute-start(bf16[88,256]{1,0:T(8,128)(2,1)S(1)} %get-tuple-element.51), channel_id=1, source_target_pairs={{0,4},{1,5},{2,6},{3,7},{4,0},{5,1},{6,2},{7,3},{8,12},{9,13},{10,... | collective-permute-start | bytes 135176 | tf_op jit(solution)/shard_map/ppermute | solution.py:233
  21.0 1.3 %collective-permute-start.9 = (bf16[88,256]{1,0:T(8,128)(2,1)S(1)}, bf16[88,256]{1,0:T(8,128)(2,1)S(1)}, u32[]{:S(2)}, u32[]{:S(2)}) collective-permute-start(bf16[88,256]{1,0:T(8,128)(2,1)S(1)} %get-tuple-element.52), channel_id=1, source_target_pairs={{0,6},{1,7},{2,4},{3,5},{4,2},{5,3},{6,0},{7,1},{8,14},{9,15},{10,... | collective-permute-start | bytes 135176 | tf_op jit(solution)/shard_map/ppermute | solution.py:233
  22.3 2.6 %collective-permute-start.10 = (bf16[88,256]{1,0:T(8,128)(2,1)S(1)}, bf16[88,256]{1,0:T(8,128)(2,1)S(1)}, u32[]{:S(2)}, u32[]{:S(2)}) collective-permute-start(bf16[88,256]{1,0:T(8,128)(2,1)S(1)} %get-tuple-element.53), channel_id=1, source_target_pairs={{0,5},{1,4},{2,7},{3,6},{4,1},{5,0},{6,3},{7,2},{8,13},{9,12},{10,... | collective-permute-start | bytes 135176 | tf_op jit(solution)/shard_map/ppermute | solution.py:233
  24.9 0.9 %collective-permute-start.11 = (bf16[88,256]{1,0:T(8,128)(2,1)S(1)}, bf16[88,256]{1,0:T(8,128)(2,1)S(1)}, u32[]{:S(2)}, u32[]{:S(2)}) collective-permute-start(bf16[88,256]{1,0:T(8,128)(2,1)S(1)} %get-tuple-element.54), channel_id=1, source_target_pairs={{0,7},{1,6},{2,5},{3,4},{4,3},{5,2},{6,1},{7,0},{8,15},{9,14},{10,... | collective-permute-start | bytes 135176 | tf_op jit(solution)/shard_map/ppermute | solution.py:233
  25.8 0.9 %collective-permute-start.12 = (bf16[88,256]{1,0:T(8,128)(2,1)S(1)}, bf16[88,256]{1,0:T(8,128)(2,1)S(1)}, u32[]{:S(2)}, u32[]{:S(2)}) collective-permute-start(bf16[88,256]{1,0:T(8,128)(2,1)S(1)} %get-tuple-element.55), channel_id=1, source_target_pairs={{0,2},{1,3},{2,0},{3,1},{4,6},{5,7},{6,4},{7,5},{8,10},{9,11},{10,... | collective-permute-start | bytes 135176 | tf_op jit(solution)/shard_map/ppermute | solution.py:233
  26.7 0.0 collective-permute-done.8.refs_1_
  26.7 1.5 %collective-permute-start.13 = (bf16[88,256]{1,0:T(8,128)(2,1)S(1)}, bf16[88,256]{1,0:T(8,128)(2,1)S(1)}, u32[]{:S(2)}, u32[]{:S(2)}) collective-permute-start(bf16[88,256]{1,0:T(8,128)(2,1)S(1)} %get-tuple-element.56), channel_id=1, source_target_pairs={{0,1},{1,0},{2,3},{3,2},{4,5},{5,4},{6,7},{7,6},{8,9},{9,8},{10,11... | collective-permute-start | bytes 135176 | tf_op jit(solution)/shard_map/ppermute | solution.py:233
  28.2 0.0 collective-permute-done.9.refs_2_
  28.2 1.4 %collective-permute-start.14 = (bf16[88,256]{1,0:T(8,128)(2,1)S(1)}, bf16[88,256]{1,0:T(8,128)(2,1)S(1)}, u32[]{:S(2)}, u32[]{:S(2)}) collective-permute-start(bf16[88,256]{1,0:T(8,128)(2,1)S(1)} %get-tuple-element.57), channel_id=1, source_target_pairs={{0,3},{1,2},{2,1},{3,0},{4,7},{5,6},{6,5},{7,4},{8,11},{9,10},{10,... | collective-permute-start | bytes 135176 | tf_op jit(solution)/shard_map/ppermute | solution.py:233
  29.6 0.9 %collective-permute-done.10.refs_3_ = bf16[88,256]{1,0:T(8,128)(2,1)S(1)} collective-permute-done((bf16[88,256]{1,0:T(8,128)(2,1)S(1)}, bf16[88,256]{1,0:T(8,128)(2,1)S(1)}, u32[]{:S(2)}, u32[]{:S(2)}) %collective-permute-start.10) | collective-permute-done | bytes 45088 | tf_op jit(solution)/shard_map/ppermute | solution.py:233
  30.5 0.6 %shard_map.108.refs_0_ = f32[640,256]{1,0:T(8,128)S(1)} custom-call(bf16[88,256]{1,0:T(8,128)(2,1)S(1)} %get-tuple-element.50.refs_0_, bf16[88,256]{1,0:T(8,128)(2,1)S(1)} %collective-permute-done.8.refs_1_, bf16[88,256]{1,0:T(8,128)(2,1)S(1)} %collective-permute-done.9.refs_2_, bf16[88,256]{1,0:T(8,128)(2,1)S(1)} %collective-permute-done.10.refs_3_), custom_call_target="tpu_custom_call" | custom-call | flops 268435456 | bytes 1024 | tf_op jit(solution)/shard_map/pallas_call | solution.py:216
  31.1 0.7 %collective-permute-done.11.refs_1_ = bf16[88,256]{1,0:T(8,128)(2,1)S(1)} collective-permute-done((bf16[88,256]{1,0:T(8,128)(2,1)S(1)}, bf16[88,256]{1,0:T(8,128)(2,1)S(1)}, u32[]{:S(2)}, u32[]{:S(2)}) %collective-permute-start.11) | collective-permute-done | bytes 45088 | tf_op jit(solution)/shard_map/ppermute | solution.py:233
  31.8 0.0 collective-permute-done.12.refs_2_
  31.8 0.0 collective-permute-done.13.refs_3_
  31.8 1.3 %collective-permute-done.14.refs_4_ = bf16[88,256]{1,0:T(8,128)(2,1)S(1)} collective-permute-done((bf16[88,256]{1,0:T(8,128)(2,1)S(1)}, bf16[88,256]{1,0:T(8,128)(2,1)S(1)}, u32[]{:S(2)}, u32[]{:S(2)}) %collective-permute-start.14) | collective-permute-done | bytes 45088 | tf_op jit(solution)/shard_map/ppermute | solution.py:233
  33.2 0.0 copy-done.2
  33.2 0.0 copy-done.3
  33.2 1.8 %shard_map.109 = (f32[640,256]{1,0:T(8,128)}, f32[640,256]{1,0:T(8,128)}) custom-call(f32[640,256]{1,0:T(8,128)S(1)} %shard_map.108.refs_0_, bf16[88,256]{1,0:T(8,128)(2,1)S(1)} %collective-permute-done.11.refs_1_, bf16[88,256]{1,0:T(8,128)(2,1)S(1)} %collective-permute-done.12.refs_2_, bf16[88,256]{1,0:T(8,128)(2,1)S(1)} %collective-permute-done.13.refs_3_, ...), custom_call_target="tpu_custom_call" | custom-call | tf_op jit(solution)/shard_map/pallas_call | solution.py:338
  (7 shorter events, 0.0 us)
Async XLA Ops:
  0.6 8.9 %collective-permute-start.2 = (bf16[320,256]{1,0:T(8,128)(2,1)}, bf16[320,256]{1,0:T(8,128)(2,1)S(1)}, u32[]{:S(2)}, u32[]{:S(2)}) collective-permute-start(bf16[320,256]{1,0:T(8,128)(2,1)} %refs_0_.5), channel_id=1, source_target_pairs={{0,16},{8,24},{16,0},{24,8},{1,17},{9,25},{17,1},{25,9},{2,18},{10... | collective-permute-start | bytes 491528 | tf_op jit(solution)/shard_map/ppermute | solution.py:233
  5.1 0.8 %copy-start.4 = (s32[320]{0:T(512)S(1)}, s32[320]{0:T(512)}, u32[]{:S(2)}) copy-start(s32[320]{0:T(512)} %param.11) | copy-start | bytes 3844
  5.1 2.7 %copy-start.1 = (bf16[320,256]{1,0:T(8,128)(2,1)S(1)}, bf16[320,256]{1,0:T(8,128)(2,1)}, u32[]{:S(2)}) copy-start(bf16[320,256]{1,0:T(8,128)(2,1)} %refs_0_.5) | copy-start | bytes 491524
  5.1 3.9 %copy-start = (bf16[320,256]{1,0:T(8,128)(2,1)S(1)}, bf16[320,256]{1,0:T(8,128)(2,1)}, u32[]{:S(2)}) copy-start(bf16[320,256]{1,0:T(8,128)(2,1)} %refs_0_.4) | copy-start | bytes 491524
  5.9 3.0 %collective-permute-start.5 = (s32[320]{0:T(512)S(1)}, s32[320]{0:T(512)S(1)}, u32[]{:S(2)}, u32[]{:S(2)}) collective-permute-start(s32[320]{0:T(512)S(1)} %copy-done.4), channel_id=1, source_target_pairs={{0,24},{8,16},{16,8},{24,0},{1,25},{9,17},{17,9},{25,1},{2,26},{10... | collective-permute-start | bytes 3848 | tf_op jit(solution)/shard_map/ppermute | solution.py:233
  5.9 3.7 %collective-permute-start.4 = (s32[320]{0:T(512)S(1)}, s32[320]{0:T(512)S(1)}, u32[]{:S(2)}, u32[]{:S(2)}) collective-permute-start(s32[320]{0:T(512)S(1)} %copy-done.4), channel_id=1, source_target_pairs={{0,16},{8,24},{16,0},{24,8},{1,17},{9,25},{17,1},{25,9},{2,18},{10... | collective-permute-start | bytes 3848 | tf_op jit(solution)/shard_map/ppermute | solution.py:233
  7.1 2.5 %collective-permute-start.3 = (s32[320]{0:T(512)S(1)}, s32[320]{0:T(512)S(1)}, u32[]{:S(2)}, u32[]{:S(2)}) collective-permute-start(s32[320]{0:T(512)S(1)} %copy-done.4), channel_id=1, source_target_pairs={{0,8},{8,0},{16,24},{24,16},{1,9},{9,1},{17,25},{25,17},{2,10},{10... | collective-permute-start | bytes 3848 | tf_op jit(solution)/shard_map/ppermute | solution.py:233
  7.8 2.3 %collective-permute-start.1 = (bf16[320,256]{1,0:T(8,128)(2,1)S(1)}, bf16[320,256]{1,0:T(8,128)(2,1)S(1)}, u32[]{:S(2)}, u32[]{:S(2)}) collective-permute-start(bf16[320,256]{1,0:T(8,128)(2,1)S(1)} %copy-done.1), channel_id=1, source_target_pairs={{0,8},{8,0},{16,24},{24,16},{1,9},{9,1},{17,25},{25,17},{2,10},{10... | collective-permute-start | bytes 491528 | tf_op jit(solution)/shard_map/ppermute | solution.py:233
  8.9 5.7 %collective-permute-start = (bf16[320,256]{1,0:T(8,128)(2,1)S(1)}, bf16[320,256]{1,0:T(8,128)(2,1)S(1)}, u32[]{:S(2)}, u32[]{:S(2)}) collective-permute-start(bf16[320,256]{1,0:T(8,128)(2,1)S(1)} %copy-done), channel_id=1, source_target_pairs={{0,16},{8,24},{16,0},{24,8},{1,17},{9,25},{17,1},{25,9},{2,18},{10... | collective-permute-start | bytes 491528 | tf_op jit(solution)/shard_map/ppermute | solution.py:233
  9.6 5.0 %collective-permute-start.6 = (bf16[320,256]{1,0:T(8,128)(2,1)S(1)}, bf16[320,256]{1,0:T(8,128)(2,1)S(1)}, u32[]{:S(2)}, u32[]{:S(2)}) collective-permute-start(bf16[320,256]{1,0:T(8,128)(2,1)S(1)} %collective-permute-done.2.refs_2_.refs_4_), channel_id=1, source_target_pairs={{0,8},{8,0},{16,24},{24,16},{1,9},{9,1},{17,25},{25,17},{2,10},{10... | collective-permute-start | bytes 491528 | tf_op jit(solution)/shard_map/ppermute | solution.py:233
  16.3 1.6 %collective-permute-start.7 = (f32[320,256]{1,0:T(8,128)S(1)}, f32[320,256]{1,0:T(8,128)S(1)}, u32[]{:S(2)}, u32[]{:S(2)}) collective-permute-start(f32[320,256]{1,0:T(8,128)S(1)} %get-tuple-element.42), channel_id=1, source_target_pairs={{0,8},{8,0},{16,24},{24,16},{1,9},{9,1},{17,25},{25,17},{2,10},{10... | collective-permute-start | bytes 983048 | tf_op jit(solution)/shard_map/ppermute | solution.py:233
  17.6 15.6 %copy-start.2 = (f32[640,256]{1,0:T(8,128)S(1)}, f32[640,256]{1,0:T(8,128)}, u32[]{:S(2)}) copy-start(f32[640,256]{1,0:T(8,128)} %refs_5_.1) | copy-start | bytes 1966084
  17.6 15.6 %copy-start.3 = (f32[640,256]{1,0:T(8,128)S(1)}, f32[640,256]{1,0:T(8,128)}, u32[]{:S(2)}) copy-start(f32[640,256]{1,0:T(8,128)} %refs_6_.1) | copy-start | bytes 1966084
  18.3 8.4 %collective-permute-start.8 = (bf16[88,256]{1,0:T(8,128)(2,1)S(1)}, bf16[88,256]{1,0:T(8,128)(2,1)S(1)}, u32[]{:S(2)}, u32[]{:S(2)}) collective-permute-start(bf16[88,256]{1,0:T(8,128)(2,1)S(1)} %get-tuple-element.51), channel_id=1, source_target_pairs={{0,4},{1,5},{2,6},{3,7},{4,0},{5,1},{6,2},{7,3},{8,12},{9,13},{10,... | collective-permute-start | bytes 135176 | tf_op jit(solution)/shard_map/ppermute | solution.py:233
  21.0 7.2 %collective-permute-start.9 = (bf16[88,256]{1,0:T(8,128)(2,1)S(1)}, bf16[88,256]{1,0:T(8,128)(2,1)S(1)}, u32[]{:S(2)}, u32[]{:S(2)}) collective-permute-start(bf16[88,256]{1,0:T(8,128)(2,1)S(1)} %get-tuple-element.52), channel_id=1, source_target_pairs={{0,6},{1,7},{2,4},{3,5},{4,2},{5,3},{6,0},{7,1},{8,14},{9,15},{10,... | collective-permute-start | bytes 135176 | tf_op jit(solution)/shard_map/ppermute | solution.py:233
  22.3 8.2 %collective-permute-start.10 = (bf16[88,256]{1,0:T(8,128)(2,1)S(1)}, bf16[88,256]{1,0:T(8,128)(2,1)S(1)}, u32[]{:S(2)}, u32[]{:S(2)}) collective-permute-start(bf16[88,256]{1,0:T(8,128)(2,1)S(1)} %get-tuple-element.53), channel_id=1, source_target_pairs={{0,5},{1,4},{2,7},{3,6},{4,1},{5,0},{6,3},{7,2},{8,13},{9,12},{10,... | collective-permute-start | bytes 135176 | tf_op jit(solution)/shard_map/ppermute | solution.py:233
  24.9 6.9 %collective-permute-start.11 = (bf16[88,256]{1,0:T(8,128)(2,1)S(1)}, bf16[88,256]{1,0:T(8,128)(2,1)S(1)}, u32[]{:S(2)}, u32[]{:S(2)}) collective-permute-start(bf16[88,256]{1,0:T(8,128)(2,1)S(1)} %get-tuple-element.54), channel_id=1, source_target_pairs={{0,7},{1,6},{2,5},{3,4},{4,3},{5,2},{6,1},{7,0},{8,15},{9,14},{10,... | collective-permute-start | bytes 135176 | tf_op jit(solution)/shard_map/ppermute | solution.py:233
  25.8 6.0 %collective-permute-start.12 = (bf16[88,256]{1,0:T(8,128)(2,1)S(1)}, bf16[88,256]{1,0:T(8,128)(2,1)S(1)}, u32[]{:S(2)}, u32[]{:S(2)}) collective-permute-start(bf16[88,256]{1,0:T(8,128)(2,1)S(1)} %get-tuple-element.55), channel_id=1, source_target_pairs={{0,2},{1,3},{2,0},{3,1},{4,6},{5,7},{6,4},{7,5},{8,10},{9,11},{10,... | collective-permute-start | bytes 135176 | tf_op jit(solution)/shard_map/ppermute | solution.py:233
  26.7 5.1 %collective-permute-start.13 = (bf16[88,256]{1,0:T(8,128)(2,1)S(1)}, bf16[88,256]{1,0:T(8,128)(2,1)S(1)}, u32[]{:S(2)}, u32[]{:S(2)}) collective-permute-start(bf16[88,256]{1,0:T(8,128)(2,1)S(1)} %get-tuple-element.56), channel_id=1, source_target_pairs={{0,1},{1,0},{2,3},{3,2},{4,5},{5,4},{6,7},{7,6},{8,9},{9,8},{10,11... | collective-permute-start | bytes 135176 | tf_op jit(solution)/shard_map/ppermute | solution.py:233
  28.2 4.9 %collective-permute-start.14 = (bf16[88,256]{1,0:T(8,128)(2,1)S(1)}, bf16[88,256]{1,0:T(8,128)(2,1)S(1)}, u32[]{:S(2)}, u32[]{:S(2)}) collective-permute-start(bf16[88,256]{1,0:T(8,128)(2,1)S(1)} %get-tuple-element.57), channel_id=1, source_target_pairs={{0,3},{1,2},{2,1},{3,0},{4,7},{5,6},{6,5},{7,4},{8,11},{9,10},{10,... | collective-permute-start | bytes 135176 | tf_op jit(solution)/shard_map/ppermute | solution.py:233

commit v5 on v4

--- a/solution.py
+++ b/solution.py
@@ -232,6 +232,7 @@
     def swap(x, k, axis="wide"):
         return lax.ppermute(x, axis, [(i, i ^ k) for i in range(lax.axis_size(axis))])
 
+    far_counts = [swap(sample_counts, k) for k in range(2, n, 2)]
     far_items = [swap(items, k) for k in range(2, n, 2)]
     far_queries = [swap(queries, k) for k in range(2, n, 2)]
 
@@ -244,14 +245,13 @@
         owner * ROW_CODES + item_offset.reshape(1, block),
         flops=1 << 30,
     )
-    own_counts, tail = lax.optimization_barrier((sample_counts, tail))
-    counts = [swap(own_counts, k) for k in range(1, n)]
-    far_items, counts, tail = lax.optimization_barrier((far_items, counts, tail))
+    far_items, far_counts, tail = lax.optimization_barrier((far_items, far_counts, tail))
     item_blocks = [items, swap(items, 1)] + far_items
     early = len(item_blocks)
     item_blocks += [swap(x, 1) for x in far_items]
     late = n - early
-    count_blocks = [sample_counts, counts[0]] + counts[1::2] + counts[2::2]
+    count_blocks = [sample_counts, swap(sample_counts, 1)] + far_counts
+    count_blocks += [swap(x, 1) for x in far_counts]
     (bias,) = call(
         functools.partial(bias_kernel, n),
         [((n, block, LANES), F32)],

time: 35.2 us -> 32.7 us (0.929)
  waiting for transfers between devices: 8.81 us -> 5.29 us
  starting transfers between devices: 16.5 us -> 17.5 us
    ppermute x15, waiting for transfers between devices: 8.81 us -> 5.29 us  [swap(): lax.ppermute(x, axis, [(i, i ^ k) for i in range(lax.axis_size(axis))])]
    ppermute x15, starting transfers between devices: 16.5 us -> 17.5 us  [swap(): lax.ppermute(x, axis, [(i, i ^ k) for i in range(lax.axis_size(axis))])]
  transfers between devices with their start and end apart: 15 -> 15, of which waited for: 7 -> 8; matrix products, arithmetic and copies ran while one was open for 4% -> 4% of each run, Pallas kernels for 10% -> 11%
where the time goes in v5:
time: 32.7 us; the launch traced here: 32.5 us
  starting transfers between devices  17.5 us (54%)
  Pallas kernels  7.51 us (23%)
  waiting for transfers between devices  5.29 us (16%)
  other arithmetic  1.38 us (4%)
  between operations  0.71 us (2%)
    ppermute x15, starting transfers between devices, swap(): lax.ppermute(x, axis, [(i, i ^ k) for i in range(lax.axis_size(axis))])  17.5 us
    pallas_call x7, Pallas kernels, call(): pl.pallas_call(kernel, out_shape=[jax.ShapeDtypeStruct(s, t) for s, t in...  5.69 us
    ppermute x15, waiting for transfers between devices, swap(): lax.ppermute(x, axis, [(i, i ^ k) for i in range(lax.axis_size(axis))])  5.29 us
    pallas_call x1, Pallas kernels, shards(): pl.pallas_call(functools.partial(update_kernel, slots, paired), out_shape...  1.81 us
    mul x1, other arithmetic, shards(): owner * ROW_CODES + item_offset.reshape(1, block)  0.7 us
    add x1, other arithmetic, shards(): owner * ROW_CODES + item_offset.reshape(1, block)  0.68 us
  transfers between devices with their start and end apart: 15, of which 8 were waited for; matrix products, arithmetic and copies ran while one was open for 4% of the time, Pallas kernels for 11%

profile of v5, /device:TPU:0, one launch (start us, length us, event | category | flops | bytes accessed | tf_op | source)
XLA Modules:
  0.0 32.5 jit_solution(11807317543637285533)
XLA Ops:
  0.6 3.0 %collective-permute-start.2 = (bf16[320,256]{1,0:T(8,128)(2,1)}, bf16[320,256]{1,0:T(8,128)(2,1)S(1)}, u32[]{:S(2)}, u32[]{:S(2)}) collective-permute-start(bf16[320,256]{1,0:T(8,128)(2,1)} %refs_0_.5), channel_id=1, source_target_pairs={{0,16},{8,24},{16,0},{24,8},{1,17},{9,25},{17,1},{25,9},{2,18},{10... | collective-permute-start | bytes 491528 | tf_op jit(solution)/shard_map/ppermute | solution.py:233
  3.7 0.0 collective-permute-start.1
  3.7 0.2 collective-permute-start.3
  3.8 1.9 %collective-permute-start = (bf16[320,256]{1,0:T(8,128)(2,1)}, bf16[320,256]{1,0:T(8,128)(2,1)S(1)}, u32[]{:S(2)}, u32[]{:S(2)}) collective-permute-start(bf16[320,256]{1,0:T(8,128)(2,1)} %refs_0_.4), channel_id=1, source_target_pairs={{0,16},{8,24},{16,0},{24,8},{1,17},{9,25},{17,1},{25,9},{2,18},{10... | collective-permute-start | bytes 491528 | tf_op jit(solution)/shard_map/ppermute | solution.py:233
  5.7 0.7 %multiply_reduce_fusion = s32[320]{0:T(512)S(1)} fusion(s32[320,1]{0,1:T(1,128)} %param.9, s32[]{:T(128)S(6)} %axis_index.12), kind=kLoop, calls=%fused_computation | loop fusion | flops 640 | bytes 2564 | tf_op jit(solution)/shard_map/mul | solution.py:245
  6.4 0.7 %add.5 = s32[320]{0:T(512)S(1)} add(s32[320]{0:T(512)S(1)} %multiply_reduce_fusion, s32[320]{0:T(512)} %param.10) | non-fusion elementwise | flops 320 | bytes 3840 | tf_op jit(solution)/shard_map/add | solution.py:245
  7.1 0.0 copy-start
  7.1 0.0 copy-start.1
  7.1 0.8 %shard_map.102 = (bf16[640,320]{1,0:T(8,128)(2,1)S(1)}, bf16[8,8,256]{2,1,0:T(8,128)(2,1)S(1)}) custom-call(s32[1,320]{1,0:T(1,128)S(1)} %add.6.code_ref), custom_call_target="tpu_custom_call" | custom-call | flops 1073741824 | bytes 1024 | tf_op jit(solution)/shard_map/pallas_call | solution.py:216
  7.9 1.0 %collective-permute-done.3 = s32[320]{0:T(512)S(1)} collective-permute-done((s32[320]{0:T(512)}, s32[320]{0:T(512)S(1)}, u32[]{:S(2)}, u32[]{:S(2)}) %collective-permute-start.3) | collective-permute-done | bytes 1312 | tf_op jit(solution)/shard_map/ppermute | solution.py:233
  8.9 0.0 collective-permute-done.2.refs_2_.refs_4_
  8.9 0.0 collective-permute-start.4
  9.0 0.0 copy-done.4
  9.0 0.5 %collective-permute-start.5 = (s32[320]{0:T(512)S(1)}, s32[320]{0:T(512)S(1)}, u32[]{:S(2)}, u32[]{:S(2)}) collective-permute-start(s32[320]{0:T(512)S(1)} %copy-done.4), channel_id=1, source_target_pairs={{0,8},{8,0},{16,24},{24,16},{1,9},{9,1},{17,25},{25,17},{2,10},{10... | collective-permute-start | bytes 3848 | tf_op jit(solution)/shard_map/ppermute | solution.py:233
  9.5 0.1 collective-permute-start.6
  9.5 0.8 %collective-permute-done.5 = s32[320]{0:T(512)S(1)} collective-permute-done((s32[320]{0:T(512)S(1)}, s32[320]{0:T(512)S(1)}, u32[]{:S(2)}, u32[]{:S(2)}) %collective-permute-start.5) | collective-permute-done | bytes 1312 | tf_op jit(solution)/shard_map/ppermute | solution.py:233
  10.4 0.3 collective-permute-done.6
  10.6 0.3 shard_map.103.refs_3_.refs_6_
  10.9 0.0 collective-permute-done.1.refs_1_.refs_3_
  10.9 0.0 copy-done
  10.9 0.0 copy-done.1
  10.9 0.6 %shard_map.104 = (f32[3,320,320]{2,1,0:T(8,128)S(1)}, f32[8,320]{1,0:T(8,128)S(1)}) custom-call(bf16[320,256]{1,0:T(8,128)(2,1)S(1)} %copy-done, bf16[320,256]{1,0:T(8,128)(2,1)S(1)} %copy-done.1, bf16[320,256]{1,0:T(8,128)(2,1)S(1)} %collective-permute-done.1.refs_1_.refs_3_, bf16[320,256]{1,0:T(8,128)(2,1)S(1)} %collective-permute-done.2.refs_2_.refs_4_, ...), custom_call_target="tpu_custom_call" | custom-call | bytes 1024 | tf_op jit(solution)/shard_map/pallas_call | solution.py:216
  11.6 0.1 collective-permute-done.refs_1_
  11.6 0.0 collective-permute-done.4.refs_5_.refs_3_
  11.6 1.7 %shard_map.105 = (f32[320,256]{1,0:T(8,128)S(1)}, f32[320,256]{1,0:T(8,128)S(1)}, f32[320]{0:T(512)}, f32[1,320,320]{2,1,0:T(8,128)S(1)}, f32[8,320]{1,0:T(8,128)S(1)}) custom-call(bf16[320,256]{1,0:T(8,128)(2,1)S(1)} %copy-done, bf16[320,256]{1,0:T(8,128)(2,1)S(1)} %collective-permute-done.refs_1_, bf16[320,256]{1,0:T(8,128)(2,1)S(1)} %copy-done.1, ...), custom_call_target="tpu_custom_call" | custom-call | bytes 1024 | tf_op jit(solution)/shard_map/pallas_call | solution.py:216
  13.3 0.1 collective-permute-start.7
  13.5 1.3 %shard_map.106 = f32[320,256]{1,0:T(8,128)} custom-call(f32[3,320,320]{2,1,0:T(8,128)S(1)} %get-tuple-element.31.refs_7_.e_ref, f32[1,320,320]{2,1,0:T(8,128)S(1)} %get-tuple-element.35.late_ref, f32[8,320]{1,0:T(8,128)S(1)} %get-tuple-element.36.factor_ref, bf16[320,256]{1,0:T(8,128)(2,1)S(1)} %copy-done.1, ...), custom_call_target="tpu_custom_call" | custom-call | flops 1073741824 | bytes 1024 | tf_op jit(solution)/shard_map/pallas_call | solution.py:216
  14.8 0.0 copy-start.2
  14.8 0.2 collective-permute-done.7.other_ref
  15.0 0.4 %shard_map.107 = (bf16[88,256]{1,0:T(8,128)(2,1)S(1)}, bf16[88,256]{1,0:T(8,128)(2,1)S(1)}, bf16[88,256]{1,0:T(8,128)(2,1)S(1)}, bf16[88,256]{1,0:T(8,128)(2,1)S...) custom-call(bf16[640,320]{1,0:T(8,128)(2,1)S(1)} %get-tuple-element., ...), custom_call_target="tpu_custom_call" | custom-call | bytes 1024 | tf_op jit(solution)/shard_map/pallas_call | solution.py:216
  15.4 3.1 %collective-permute-start.8 = (bf16[88,256]{1,0:T(8,128)(2,1)S(1)}, bf16[88,256]{1,0:T(8,128)(2,1)S(1)}, u32[]{:S(2)}, u32[]{:S(2)}) collective-permute-start(bf16[88,256]{1,0:T(8,128)(2,1)S(1)} %get-tuple-element.43), channel_id=1, source_target_pairs={{0,4},{1,5},{2,6},{3,7},{4,0},{5,1},{6,2},{7,3},{8,12},{9,13},{10,... | collective-permute-start | bytes 135176 | tf_op jit(solution)/shard_map/ppermute | solution.py:233
  18.5 1.3 %collective-permute-start.9 = (bf16[88,256]{1,0:T(8,128)(2,1)S(1)}, bf16[88,256]{1,0:T(8,128)(2,1)S(1)}, u32[]{:S(2)}, u32[]{:S(2)}) collective-permute-start(bf16[88,256]{1,0:T(8,128)(2,1)S(1)} %get-tuple-element.44), channel_id=1, source_target_pairs={{0,6},{1,7},{2,4},{3,5},{4,2},{5,3},{6,0},{7,1},{8,14},{9,15},{10,... | collective-permute-start | bytes 135176 | tf_op jit(solution)/shard_map/ppermute | solution.py:233
  19.8 2.6 %collective-permute-start.10 = (bf16[88,256]{1,0:T(8,128)(2,1)S(1)}, bf16[88,256]{1,0:T(8,128)(2,1)S(1)}, u32[]{:S(2)}, u32[]{:S(2)}) collective-permute-start(bf16[88,256]{1,0:T(8,128)(2,1)S(1)} %get-tuple-element.45), channel_id=1, source_target_pairs={{0,5},{1,4},{2,7},{3,6},{4,1},{5,0},{6,3},{7,2},{8,13},{9,12},{10,... | collective-permute-start | bytes 135176 | tf_op jit(solution)/shard_map/ppermute | solution.py:233
  22.4 0.9 %collective-permute-start.11 = (bf16[88,256]{1,0:T(8,128)(2,1)S(1)}, bf16[88,256]{1,0:T(8,128)(2,1)S(1)}, u32[]{:S(2)}, u32[]{:S(2)}) collective-permute-start(bf16[88,256]{1,0:T(8,128)(2,1)S(1)} %get-tuple-element.46), channel_id=1, source_target_pairs={{0,7},{1,6},{2,5},{3,4},{4,3},{5,2},{6,1},{7,0},{8,15},{9,14},{10,... | collective-permute-start | bytes 135176 | tf_op jit(solution)/shard_map/ppermute | solution.py:233
  23.3 0.9 %collective-permute-start.12 = (bf16[88,256]{1,0:T(8,128)(2,1)S(1)}, bf16[88,256]{1,0:T(8,128)(2,1)S(1)}, u32[]{:S(2)}, u32[]{:S(2)}) collective-permute-start(bf16[88,256]{1,0:T(8,128)(2,1)S(1)} %get-tuple-element.47), channel_id=1, source_target_pairs={{0,2},{1,3},{2,0},{3,1},{4,6},{5,7},{6,4},{7,5},{8,10},{9,11},{10,... | collective-permute-start | bytes 135176 | tf_op jit(solution)/shard_map/ppermute | solution.py:233
  24.2 0.0 collective-permute-done.8.refs_1_
  24.2 1.5 %collective-permute-start.13 = (bf16[88,256]{1,0:T(8,128)(2,1)S(1)}, bf16[88,256]{1,0:T(8,128)(2,1)S(1)}, u32[]{:S(2)}, u32[]{:S(2)}) collective-permute-start(bf16[88,256]{1,0:T(8,128)(2,1)S(1)} %get-tuple-element.48), channel_id=1, source_target_pairs={{0,1},{1,0},{2,3},{3,2},{4,5},{5,4},{6,7},{7,6},{8,9},{9,8},{10,11... | collective-permute-start | bytes 135176 | tf_op jit(solution)/shard_map/ppermute | solution.py:233
  25.7 0.0 collective-permute-done.9.refs_2_
  25.7 1.4 %collective-permute-start.14 = (bf16[88,256]{1,0:T(8,128)(2,1)S(1)}, bf16[88,256]{1,0:T(8,128)(2,1)S(1)}, u32[]{:S(2)}, u32[]{:S(2)}) collective-permute-start(bf16[88,256]{1,0:T(8,128)(2,1)S(1)} %get-tuple-element.49), channel_id=1, source_target_pairs={{0,3},{1,2},{2,1},{3,0},{4,7},{5,6},{6,5},{7,4},{8,11},{9,10},{10,... | collective-permute-start | bytes 135176 | tf_op jit(solution)/shard_map/ppermute | solution.py:233
  27.1 0.9 %collective-permute-done.10.refs_3_ = bf16[88,256]{1,0:T(8,128)(2,1)S(1)} collective-permute-done((bf16[88,256]{1,0:T(8,128)(2,1)S(1)}, bf16[88,256]{1,0:T(8,128)(2,1)S(1)}, u32[]{:S(2)}, u32[]{:S(2)}) %collective-permute-start.10) | collective-permute-done | bytes 45088 | tf_op jit(solution)/shard_map/ppermute | solution.py:233
  28.0 0.6 %shard_map.108.refs_0_ = f32[640,256]{1,0:T(8,128)S(1)} custom-call(bf16[88,256]{1,0:T(8,128)(2,1)S(1)} %get-tuple-element.42.refs_0_, bf16[88,256]{1,0:T(8,128)(2,1)S(1)} %collective-permute-done.8.refs_1_, bf16[88,256]{1,0:T(8,128)(2,1)S(1)} %collective-permute-done.9.refs_2_, bf16[88,256]{1,0:T(8,128)(2,1)S(1)} %collective-permute-done.10.refs_3_), custom_call_target="tpu_custom_call" | custom-call | flops 268435456 | bytes 1024 | tf_op jit(solution)/shard_map/pallas_call | solution.py:216
  28.6 0.7 %collective-permute-done.11.refs_1_ = bf16[88,256]{1,0:T(8,128)(2,1)S(1)} collective-permute-done((bf16[88,256]{1,0:T(8,128)(2,1)S(1)}, bf16[88,256]{1,0:T(8,128)(2,1)S(1)}, u32[]{:S(2)}, u32[]{:S(2)}) %collective-permute-start.11) | collective-permute-done | bytes 45088 | tf_op jit(solution)/shard_map/ppermute | solution.py:233
  29.3 0.0 collective-permute-done.12.refs_2_
  29.3 0.0 collective-permute-done.13.refs_3_
  29.3 1.3 %collective-permute-done.14.refs_4_ = bf16[88,256]{1,0:T(8,128)(2,1)S(1)} collective-permute-done((bf16[88,256]{1,0:T(8,128)(2,1)S(1)}, bf16[88,256]{1,0:T(8,128)(2,1)S(1)}, u32[]{:S(2)}, u32[]{:S(2)}) %collective-permute-start.14) | collective-permute-done | bytes 45088 | tf_op jit(solution)/shard_map/ppermute | solution.py:233
  30.6 0.0 copy-done.2
  30.7 0.0 copy-done.3
  30.7 1.8 %shard_map.109 = (f32[640,256]{1,0:T(8,128)}, f32[640,256]{1,0:T(8,128)}) custom-call(f32[640,256]{1,0:T(8,128)S(1)} %shard_map.108.refs_0_, bf16[88,256]{1,0:T(8,128)(2,1)S(1)} %collective-permute-done.11.refs_1_, bf16[88,256]{1,0:T(8,128)(2,1)S(1)} %collective-permute-done.12.refs_2_, bf16[88,256]{1,0:T(8,128)(2,1)S(1)} %collective-permute-done.13.refs_3_, ...), custom_call_target="tpu_custom_call" | custom-call | tf_op jit(solution)/shard_map/pallas_call | solution.py:338
  (7 shorter events, 0.0 us)
Async XLA Ops:
  0.6 8.3 %collective-permute-start.2 = (bf16[320,256]{1,0:T(8,128)(2,1)}, bf16[320,256]{1,0:T(8,128)(2,1)S(1)}, u32[]{:S(2)}, u32[]{:S(2)}) collective-permute-start(bf16[320,256]{1,0:T(8,128)(2,1)} %refs_0_.5), channel_id=1, source_target_pairs={{0,16},{8,24},{16,0},{24,8},{1,17},{9,25},{17,1},{25,9},{2,18},{10... | collective-permute-start | bytes 491528 | tf_op jit(solution)/shard_map/ppermute | solution.py:233
  3.7 7.2 %collective-permute-start.1 = (bf16[320,256]{1,0:T(8,128)(2,1)}, bf16[320,256]{1,0:T(8,128)(2,1)S(1)}, u32[]{:S(2)}, u32[]{:S(2)}) collective-permute-start(bf16[320,256]{1,0:T(8,128)(2,1)} %refs_0_.5), channel_id=1, source_target_pairs={{0,8},{8,0},{16,24},{24,16},{1,9},{9,1},{17,25},{25,17},{2,10},{10... | collective-permute-start | bytes 491528 | tf_op jit(solution)/shard_map/ppermute | solution.py:233
  3.7 5.3 %collective-permute-start.3 = (s32[320]{0:T(512)}, s32[320]{0:T(512)S(1)}, u32[]{:S(2)}, u32[]{:S(2)}) collective-permute-start(s32[320]{0:T(512)} %param.11), channel_id=1, source_target_pairs={{0,16},{8,24},{16,0},{24,8},{1,17},{9,25},{17,1},{25,9},{2,18},{10... | collective-permute-start | bytes 3848 | tf_op jit(solution)/shard_map/ppermute | solution.py:233
  3.8 7.8 %collective-permute-start = (bf16[320,256]{1,0:T(8,128)(2,1)}, bf16[320,256]{1,0:T(8,128)(2,1)S(1)}, u32[]{:S(2)}, u32[]{:S(2)}) collective-permute-start(bf16[320,256]{1,0:T(8,128)(2,1)} %refs_0_.4), channel_id=1, source_target_pairs={{0,16},{8,24},{16,0},{24,8},{1,17},{9,25},{17,1},{25,9},{2,18},{10... | collective-permute-start | bytes 491528 | tf_op jit(solution)/shard_map/ppermute | solution.py:233
  7.1 1.9 %copy-start.4 = (s32[320]{0:T(512)S(1)}, s32[320]{0:T(512)}, u32[]{:S(2)}) copy-start(s32[320]{0:T(512)} %param.11) | copy-start | bytes 3844
  7.1 3.8 %copy-start = (bf16[320,256]{1,0:T(8,128)(2,1)S(1)}, bf16[320,256]{1,0:T(8,128)(2,1)}, u32[]{:S(2)}) copy-start(bf16[320,256]{1,0:T(8,128)(2,1)} %refs_0_.4) | copy-start | bytes 491524
  7.1 3.8 %copy-start.1 = (bf16[320,256]{1,0:T(8,128)(2,1)S(1)}, bf16[320,256]{1,0:T(8,128)(2,1)}, u32[]{:S(2)}) copy-start(bf16[320,256]{1,0:T(8,128)(2,1)} %refs_0_.5) | copy-start | bytes 491524
  8.9 2.7 %collective-permute-start.4 = (bf16[320,256]{1,0:T(8,128)(2,1)S(1)}, bf16[320,256]{1,0:T(8,128)(2,1)S(1)}, u32[]{:S(2)}, u32[]{:S(2)}) collective-permute-start(bf16[320,256]{1,0:T(8,128)(2,1)S(1)} %collective-permute-done.2.refs_2_.refs_4_), channel_id=1, source_target_pairs={{0,8},{8,0},{16,24},{24,16},{1,9},{9,1},{17,25},{25,17},{2,10},{10... | collective-permute-start | bytes 491528 | tf_op jit(solution)/shard_map/ppermute | solution.py:233
  9.0 1.4 %collective-permute-start.5 = (s32[320]{0:T(512)S(1)}, s32[320]{0:T(512)S(1)}, u32[]{:S(2)}, u32[]{:S(2)}) collective-permute-start(s32[320]{0:T(512)S(1)} %copy-done.4), channel_id=1, source_target_pairs={{0,8},{8,0},{16,24},{24,16},{1,9},{9,1},{17,25},{25,17},{2,10},{10... | collective-permute-start | bytes 3848 | tf_op jit(solution)/shard_map/ppermute | solution.py:233
  9.5 1.2 %collective-permute-start.6 = (s32[320]{0:T(512)S(1)}, s32[320]{0:T(512)S(1)}, u32[]{:S(2)}, u32[]{:S(2)}) collective-permute-start(s32[320]{0:T(512)S(1)} %collective-permute-done.3), channel_id=1, source_target_pairs={{0,8},{8,0},{16,24},{24,16},{1,9},{9,1},{17,25},{25,17},{2,10},{10... | collective-permute-start | bytes 3848 | tf_op jit(solution)/shard_map/ppermute | solution.py:233
  13.3 1.6 %collective-permute-start.7 = (f32[320,256]{1,0:T(8,128)S(1)}, f32[320,256]{1,0:T(8,128)S(1)}, u32[]{:S(2)}, u32[]{:S(2)}) collective-permute-start(f32[320,256]{1,0:T(8,128)S(1)} %get-tuple-element.34), channel_id=1, source_target_pairs={{0,8},{8,0},{16,24},{24,16},{1,9},{9,1},{17,25},{25,17},{2,10},{10... | collective-permute-start | bytes 983048 | tf_op jit(solution)/shard_map/ppermute | solution.py:233
  14.8 15.9 %copy-start.2 = (f32[640,256]{1,0:T(8,128)S(1)}, f32[640,256]{1,0:T(8,128)}, u32[]{:S(2)}) copy-start(f32[640,256]{1,0:T(8,128)} %refs_5_.1) | copy-start | bytes 1966084
  14.8 15.9 %copy-start.3 = (f32[640,256]{1,0:T(8,128)S(1)}, f32[640,256]{1,0:T(8,128)}, u32[]{:S(2)}) copy-start(f32[640,256]{1,0:T(8,128)} %refs_6_.1) | copy-start | bytes 1966084
  15.4 8.8 %collective-permute-start.8 = (bf16[88,256]{1,0:T(8,128)(2,1)S(1)}, bf16[88,256]{1,0:T(8,128)(2,1)S(1)}, u32[]{:S(2)}, u32[]{:S(2)}) collective-permute-start(bf16[88,256]{1,0:T(8,128)(2,1)S(1)} %get-tuple-element.43), channel_id=1, source_target_pairs={{0,4},{1,5},{2,6},{3,7},{4,0},{5,1},{6,2},{7,3},{8,12},{9,13},{10,... | collective-permute-start | bytes 135176 | tf_op jit(solution)/shard_map/ppermute | solution.py:233
  18.5 7.2 %collective-permute-start.9 = (bf16[88,256]{1,0:T(8,128)(2,1)S(1)}, bf16[88,256]{1,0:T(8,128)(2,1)S(1)}, u32[]{:S(2)}, u32[]{:S(2)}) collective-permute-start(bf16[88,256]{1,0:T(8,128)(2,1)S(1)} %get-tuple-element.44), channel_id=1, source_target_pairs={{0,6},{1,7},{2,4},{3,5},{4,2},{5,3},{6,0},{7,1},{8,14},{9,15},{10,... | collective-permute-start | bytes 135176 | tf_op jit(solution)/shard_map/ppermute | solution.py:233
  19.8 8.2 %collective-permute-start.10 = (bf16[88,256]{1,0:T(8,128)(2,1)S(1)}, bf16[88,256]{1,0:T(8,128)(2,1)S(1)}, u32[]{:S(2)}, u32[]{:S(2)}) collective-permute-start(bf16[88,256]{1,0:T(8,128)(2,1)S(1)} %get-tuple-element.45), channel_id=1, source_target_pairs={{0,5},{1,4},{2,7},{3,6},{4,1},{5,0},{6,3},{7,2},{8,13},{9,12},{10,... | collective-permute-start | bytes 135176 | tf_op jit(solution)/shard_map/ppermute | solution.py:233
  22.4 6.9 %collective-permute-start.11 = (bf16[88,256]{1,0:T(8,128)(2,1)S(1)}, bf16[88,256]{1,0:T(8,128)(2,1)S(1)}, u32[]{:S(2)}, u32[]{:S(2)}) collective-permute-start(bf16[88,256]{1,0:T(8,128)(2,1)S(1)} %get-tuple-element.46), channel_id=1, source_target_pairs={{0,7},{1,6},{2,5},{3,4},{4,3},{5,2},{6,1},{7,0},{8,15},{9,14},{10,... | collective-permute-start | bytes 135176 | tf_op jit(solution)/shard_map/ppermute | solution.py:233
  23.3 6.0 %collective-permute-start.12 = (bf16[88,256]{1,0:T(8,128)(2,1)S(1)}, bf16[88,256]{1,0:T(8,128)(2,1)S(1)}, u32[]{:S(2)}, u32[]{:S(2)}) collective-permute-start(bf16[88,256]{1,0:T(8,128)(2,1)S(1)} %get-tuple-element.47), channel_id=1, source_target_pairs={{0,2},{1,3},{2,0},{3,1},{4,6},{5,7},{6,4},{7,5},{8,10},{9,11},{10,... | collective-permute-start | bytes 135176 | tf_op jit(solution)/shard_map/ppermute | solution.py:233
  24.2 5.1 %collective-permute-start.13 = (bf16[88,256]{1,0:T(8,128)(2,1)S(1)}, bf16[88,256]{1,0:T(8,128)(2,1)S(1)}, u32[]{:S(2)}, u32[]{:S(2)}) collective-permute-start(bf16[88,256]{1,0:T(8,128)(2,1)S(1)} %get-tuple-element.48), channel_id=1, source_target_pairs={{0,1},{1,0},{2,3},{3,2},{4,5},{5,4},{6,7},{7,6},{8,9},{9,8},{10,11... | collective-permute-start | bytes 135176 | tf_op jit(solution)/shard_map/ppermute | solution.py:233
  25.7 4.9 %collective-permute-start.14 = (bf16[88,256]{1,0:T(8,128)(2,1)S(1)}, bf16[88,256]{1,0:T(8,128)(2,1)S(1)}, u32[]{:S(2)}, u32[]{:S(2)}) collective-permute-start(bf16[88,256]{1,0:T(8,128)(2,1)S(1)} %get-tuple-element.49), channel_id=1, source_target_pairs={{0,3},{1,2},{2,1},{3,0},{4,7},{5,6},{6,5},{7,4},{8,11},{9,10},{10,... | collective-permute-start | bytes 135176 | tf_op jit(solution)/shard_map/ppermute | solution.py:233

commit v6 on v5

--- a/solution.py
+++ b/solution.py
@@ -169,7 +169,7 @@
         out[slots:] = tail_ref[g]
 
 
-def scatter(slots, got_refs, values_ref, ids_ref, rows):
+def unpack(slots, got_refs, values_ref, ids_ref):
     packets = got_refs
     if len(got_refs[0].shape) == 3:
         packets = [got_refs[0].at[g] for g in range(got_refs[0].shape[0])]
@@ -183,33 +183,41 @@
         values_ref[g * slots : (g + 1) * slots] = high
         low = (values - high.astype(F32)).astype(BF16)
         values_ref[half + g * slots : half + (g + 1) * slots] = low
-    index = lax.broadcasted_iota(jnp.int32, (rows, half), 0).astype(F32)
-    put = (index == ids_ref[:1]).astype(F32).astype(BF16)
+
+
+def scatter(values_ref, ids_ref, first, rows):
+    index = lax.broadcasted_iota(jnp.int32, (rows, ids_ref.shape[1]), 0) + first
+    put = (index.astype(F32) == ids_ref[:1]).astype(F32).astype(BF16)
     return dot(jnp.concatenate([put, put], axis=1), values_ref[...])
 
 
 def first_kernel(slots, *refs):
     got_refs, (out_ref, values_ref, ids_ref) = refs[:-3], refs[-3:]
-    out_ref[...] = scatter(slots, got_refs, values_ref, ids_ref, out_ref.shape[0])
+    unpack(slots, got_refs, values_ref, ids_ref)
+    out_ref[...] = scatter(values_ref, ids_ref, 0, out_ref.shape[0])
 
 
 def update_kernel(slots, partial, *refs):
     inputs, refs = refs[:-8], refs[-8:]
     table_ref, accum_ref, table_out, accum_out, values_ref, ids_ref, new_ref, sems = refs
-    got_refs = inputs[1:] if partial else inputs
-    rows = table_ref.shape[0]
-    grad = scatter(slots, got_refs, values_ref, ids_ref, rows)
-    if partial:
-        grad += inputs[0][...]
-    accum_new = accum_ref[...] + grad * grad
-    new_ref[1] = accum_new
-    first = pltpu.make_async_copy(new_ref.at[1], accum_out, sems.at[1])
-    first.start()
-    new_ref[0] = table_ref[...] - 0.1 * grad / (jnp.sqrt(accum_new) + 1e-08)
-    second = pltpu.make_async_copy(new_ref.at[0], table_out, sems.at[0])
-    second.start()
-    first.wait()
-    second.wait()
+    unpack(slots, inputs[1:] if partial else inputs, values_ref, ids_ref)
+    chunks = sems.shape[1]
+    rows = table_ref.shape[0] // chunks
+    copies = []
+    for c in range(chunks):
+        here = slice(c * rows, (c + 1) * rows)
+        grad = scatter(values_ref, ids_ref, c * rows, rows)
+        if partial:
+            grad += inputs[0][here]
+        accum_new = accum_ref[here] + grad * grad
+        new_ref[1, here] = accum_new
+        copies.append(pltpu.make_async_copy(new_ref.at[1, here], accum_out.at[here], sems.at[1, c]))
+        copies[-1].start()
+        new_ref[0, here] = table_ref[here] - 0.1 * grad / (jnp.sqrt(accum_new) + 1e-08)
+        copies.append(pltpu.make_async_copy(new_ref.at[0, here], table_out.at[here], sems.at[0, c]))
+        copies[-1].start()
+    for copy in copies:
+        copy.wait()
 
 
 def call(kernel, outs, *args, scratch=(), limit=16, flops=0):
@@ -312,7 +320,9 @@
         functools.partial(pack_kernel, groups, slots), packets, pick, tail, mine, other
     )
     if paired:
-        order = sorted(range(1, groups), key=lambda k: (k < groups // 2, k % 2, k))
+        half = groups // 2
+        far = sorted(range(half, groups), key=lambda k: (k % 2, k))
+        order = far + sorted(range(1, half), key=lambda k: (1 - k % 2, -k))
         got = [packed[0]] + [swap(packed[k], k, "group") for k in order]
     else:
         got = [lax.all_to_all(packed[0], "group", split_axis=0, concat_axis=0, tiled=True)]
@@ -324,25 +334,25 @@
             pltpu.VMEM((TAIL, packets * slots), F32),
         ]
 
-    half = groups // 2
+    count = groups - 1
     before = []
     if paired:
         before = call(
             functools.partial(first_kernel, slots),
             [((rows, D), F32)],
-            *got[:half],
-            scratch=scratch(half),
+            *got[:count],
+            scratch=scratch(count),
             flops=1 << 28,
         )
-        got = got[half:]
+        got = got[count:]
     table_new, accum_new = pl.pallas_call(
         functools.partial(update_kernel, slots, paired),
         out_shape=[jax.ShapeDtypeStruct(table.shape, F32)] * 2,
         out_specs=[pl.BlockSpec(memory_space=pl.ANY)] * 2,
         scratch_shapes=[
-            *scratch(half if paired else groups),
+            *scratch(len(got) if paired else groups),
             pltpu.VMEM((2, rows, D), F32),
-            pltpu.SemaphoreType.DMA((2,)),
+            pltpu.SemaphoreType.DMA((2, 4)),
         ],
         compiler_params=pltpu.CompilerParams(vmem_limit_bytes=32 * MIB),
     )(*before, *got, table, accum)

time: 32.7 us -> 32.3 us (0.988)
    pallas_call x1, Pallas kernels: 1.81 us -> 1.46 us  [shards(): pl.pallas_call(functools.partial(update_kernel, slots, paired), out_shape...]
    ppermute x15, starting transfers between devices: 17.5 us -> 17.2 us  [swap(): lax.ppermute(x, axis, [(i, i ^ k) for i in range(lax.axis_size(axis))])]
  transfers between devices with their start and end apart: 15 -> 15, of which waited for: 8 -> 8; matrix products, arithmetic and copies ran while one was open for 4% -> 4% of each run, Pallas kernels for 11% -> 12%
where the time goes in v6:
time: 32.3 us; the launch traced here: 32.1 us
  starting transfers between devices  17.2 us (53%)
  Pallas kernels  7.39 us (23%)
  waiting for transfers between devices  5.33 us (17%)
  other arithmetic  1.38 us (4%)
  between operations  0.73 us (2%)
    ppermute x15, starting transfers between devices, swap(): lax.ppermute(x, axis, [(i, i ^ k) for i in range(lax.axis_size(axis))])  17.2 us
    pallas_call x7, Pallas kernels, call(): pl.pallas_call(kernel, out_shape=[jax.ShapeDtypeStruct(s, t) for s, t in...  5.93 us
    ppermute x15, waiting for transfers between devices, swap(): lax.ppermute(x, axis, [(i, i ^ k) for i in range(lax.axis_size(axis))])  5.33 us
    pallas_call x1, Pallas kernels, shards(): pl.pallas_call(functools.partial(update_kernel, slots, paired), out_shape...  1.46 us
    mul x1, other arithmetic, shards(): owner * ROW_CODES + item_offset.reshape(1, block)  0.7 us
    add x1, other arithmetic, shards(): owner * ROW_CODES + item_offset.reshape(1, block)  0.68 us
  transfers between devices with their start and end apart: 15, of which 8 were waited for; matrix products, arithmetic and copies ran while one was open for 4% of the time, Pallas kernels for 12%

profile of v6, /device:TPU:0, one launch (start us, length us, event | category | flops | bytes accessed | tf_op | source)
XLA Modules:
  0.0 32.1 jit_solution(17620125184322937447)
XLA Ops:
  0.6 3.0 %collective-permute-start.2 = (bf16[320,256]{1,0:T(8,128)(2,1)}, bf16[320,256]{1,0:T(8,128)(2,1)S(1)}, u32[]{:S(2)}, u32[]{:S(2)}) collective-permute-start(bf16[320,256]{1,0:T(8,128)(2,1)} %refs_0_.5), channel_id=1, source_target_pairs={{0,16},{8,24},{16,0},{24,8},{1,17},{9,25},{17,1},{25,9},{2,18},{10... | collective-permute-start | bytes 491528 | tf_op jit(solution)/shard_map/ppermute | solution.py:241
  3.7 0.0 collective-permute-start.1
  3.7 0.2 collective-permute-start.3
  3.8 1.9 %collective-permute-start = (bf16[320,256]{1,0:T(8,128)(2,1)}, bf16[320,256]{1,0:T(8,128)(2,1)S(1)}, u32[]{:S(2)}, u32[]{:S(2)}) collective-permute-start(bf16[320,256]{1,0:T(8,128)(2,1)} %refs_0_.4), channel_id=1, source_target_pairs={{0,16},{8,24},{16,0},{24,8},{1,17},{9,25},{17,1},{25,9},{2,18},{10... | collective-permute-start | bytes 491528 | tf_op jit(solution)/shard_map/ppermute | solution.py:241
  5.7 0.7 %multiply_reduce_fusion = s32[320]{0:T(512)S(1)} fusion(s32[320,1]{0,1:T(1,128)} %param.9, s32[]{:T(128)S(6)} %axis_index.12), kind=kLoop, calls=%fused_computation | loop fusion | flops 640 | bytes 2564 | tf_op jit(solution)/shard_map/mul | solution.py:253
  6.4 0.7 %add.5 = s32[320]{0:T(512)S(1)} add(s32[320]{0:T(512)S(1)} %multiply_reduce_fusion, s32[320]{0:T(512)} %param.10) | non-fusion elementwise | flops 320 | bytes 3840 | tf_op jit(solution)/shard_map/add | solution.py:253
  7.1 0.0 copy-start.4
  7.1 0.0 copy-start
  7.1 0.0 copy-start.1
  7.1 0.8 %shard_map.102 = (bf16[640,320]{1,0:T(8,128)(2,1)S(1)}, bf16[8,8,256]{2,1,0:T(8,128)(2,1)S(1)}) custom-call(s32[1,320]{1,0:T(1,128)S(1)} %add.6.code_ref), custom_call_target="tpu_custom_call" | custom-call | flops 1073741824 | bytes 1024 | tf_op jit(solution)/shard_map/pallas_call | solution.py:224
  7.9 1.0 %collective-permute-done.3 = s32[320]{0:T(512)S(1)} collective-permute-done((s32[320]{0:T(512)}, s32[320]{0:T(512)S(1)}, u32[]{:S(2)}, u32[]{:S(2)}) %collective-permute-start.3) | collective-permute-done | bytes 1312 | tf_op jit(solution)/shard_map/ppermute | solution.py:241
  8.9 0.0 collective-permute-done.2.refs_2_.refs_4_
  8.9 0.0 collective-permute-start.4
  9.0 0.0 copy-done.4
  9.0 0.5 %collective-permute-start.5 = (s32[320]{0:T(512)S(1)}, s32[320]{0:T(512)S(1)}, u32[]{:S(2)}, u32[]{:S(2)}) collective-permute-start(s32[320]{0:T(512)S(1)} %copy-done.4), channel_id=1, source_target_pairs={{0,8},{8,0},{16,24},{24,16},{1,9},{9,1},{17,25},{25,17},{2,10},{10... | collective-permute-start | bytes 3848 | tf_op jit(solution)/shard_map/ppermute | solution.py:241
  9.5 0.1 collective-permute-start.6
  9.5 0.8 %collective-permute-done.5 = s32[320]{0:T(512)S(1)} collective-permute-done((s32[320]{0:T(512)S(1)}, s32[320]{0:T(512)S(1)}, u32[]{:S(2)}, u32[]{:S(2)}) %collective-permute-start.5) | collective-permute-done | bytes 1312 | tf_op jit(solution)/shard_map/ppermute | solution.py:241
  10.4 0.3 collective-permute-done.6
  10.6 0.3 shard_map.103.refs_3_.refs_6_
  10.9 0.0 collective-permute-done.1.refs_1_.refs_3_
  10.9 0.0 copy-done
  10.9 0.0 copy-done.1
  10.9 0.6 %shard_map.104 = (f32[3,320,320]{2,1,0:T(8,128)S(1)}, f32[8,320]{1,0:T(8,128)S(1)}) custom-call(bf16[320,256]{1,0:T(8,128)(2,1)S(1)} %copy-done, bf16[320,256]{1,0:T(8,128)(2,1)S(1)} %copy-done.1, bf16[320,256]{1,0:T(8,128)(2,1)S(1)} %collective-permute-done.1.refs_1_.refs_3_, bf16[320,256]{1,0:T(8,128)(2,1)S(1)} %collective-permute-done.2.refs_2_.refs_4_, ...), custom_call_target="tpu_custom_call" | custom-call | bytes 1024 | tf_op jit(solution)/shard_map/pallas_call | solution.py:224
  11.6 0.1 collective-permute-done.refs_1_
  11.6 0.0 collective-permute-done.4.refs_5_.refs_3_
  11.6 1.7 %shard_map.105 = (f32[320,256]{1,0:T(8,128)S(1)}, f32[320,256]{1,0:T(8,128)S(1)}, f32[320]{0:T(512)}, f32[1,320,320]{2,1,0:T(8,128)S(1)}, f32[8,320]{1,0:T(8,128)S(1)}) custom-call(bf16[320,256]{1,0:T(8,128)(2,1)S(1)} %copy-done, bf16[320,256]{1,0:T(8,128)(2,1)S(1)} %collective-permute-done.refs_1_, bf16[320,256]{1,0:T(8,128)(2,1)S(1)} %copy-done.1, ...), custom_call_target="tpu_custom_call" | custom-call | bytes 1024 | tf_op jit(solution)/shard_map/pallas_call | solution.py:224
  13.3 0.1 collective-permute-start.7
  13.5 1.3 %shard_map.106 = f32[320,256]{1,0:T(8,128)} custom-call(f32[3,320,320]{2,1,0:T(8,128)S(1)} %get-tuple-element.31.refs_7_.e_ref, f32[1,320,320]{2,1,0:T(8,128)S(1)} %get-tuple-element.35.late_ref, f32[8,320]{1,0:T(8,128)S(1)} %get-tuple-element.36.factor_ref, bf16[320,256]{1,0:T(8,128)(2,1)S(1)} %copy-done.1, ...), custom_call_target="tpu_custom_call" | custom-call | flops 1073741824 | bytes 1024 | tf_op jit(solution)/shard_map/pallas_call | solution.py:224
  14.8 0.2 collective-permute-done.7.other_ref
  15.0 0.4 %shard_map.107 = (bf16[88,256]{1,0:T(8,128)(2,1)S(1)}, bf16[88,256]{1,0:T(8,128)(2,1)S(1)}, bf16[88,256]{1,0:T(8,128)(2,1)S(1)}, bf16[88,256]{1,0:T(8,128)(2,1)S...) custom-call(bf16[640,320]{1,0:T(8,128)(2,1)S(1)} %get-tuple-element., ...), custom_call_target="tpu_custom_call" | custom-call | bytes 1024 | tf_op jit(solution)/shard_map/pallas_call | solution.py:224
  15.4 3.1 %collective-permute-start.8 = (bf16[88,256]{1,0:T(8,128)(2,1)S(1)}, bf16[88,256]{1,0:T(8,128)(2,1)S(1)}, u32[]{:S(2)}, u32[]{:S(2)}) collective-permute-start(bf16[88,256]{1,0:T(8,128)(2,1)S(1)} %get-tuple-element.43), channel_id=1, source_target_pairs={{0,4},{1,5},{2,6},{3,7},{4,0},{5,1},{6,2},{7,3},{8,12},{9,13},{10,... | collective-permute-start | bytes 135176 | tf_op jit(solution)/shard_map/ppermute | solution.py:241
  18.5 1.3 %collective-permute-start.9 = (bf16[88,256]{1,0:T(8,128)(2,1)S(1)}, bf16[88,256]{1,0:T(8,128)(2,1)S(1)}, u32[]{:S(2)}, u32[]{:S(2)}) collective-permute-start(bf16[88,256]{1,0:T(8,128)(2,1)S(1)} %get-tuple-element.44), channel_id=1, source_target_pairs={{0,6},{1,7},{2,4},{3,5},{4,2},{5,3},{6,0},{7,1},{8,14},{9,15},{10,... | collective-permute-start | bytes 135176 | tf_op jit(solution)/shard_map/ppermute | solution.py:241
  19.8 2.6 %collective-permute-start.10 = (bf16[88,256]{1,0:T(8,128)(2,1)S(1)}, bf16[88,256]{1,0:T(8,128)(2,1)S(1)}, u32[]{:S(2)}, u32[]{:S(2)}) collective-permute-start(bf16[88,256]{1,0:T(8,128)(2,1)S(1)} %get-tuple-element.45), channel_id=1, source_target_pairs={{0,5},{1,4},{2,7},{3,6},{4,1},{5,0},{6,3},{7,2},{8,13},{9,12},{10,... | collective-permute-start | bytes 135176 | tf_op jit(solution)/shard_map/ppermute | solution.py:241
  22.4 0.9 %collective-permute-start.11 = (bf16[88,256]{1,0:T(8,128)(2,1)S(1)}, bf16[88,256]{1,0:T(8,128)(2,1)S(1)}, u32[]{:S(2)}, u32[]{:S(2)}) collective-permute-start(bf16[88,256]{1,0:T(8,128)(2,1)S(1)} %get-tuple-element.46), channel_id=1, source_target_pairs={{0,7},{1,6},{2,5},{3,4},{4,3},{5,2},{6,1},{7,0},{8,15},{9,14},{10,... | collective-permute-start | bytes 135176 | tf_op jit(solution)/shard_map/ppermute | solution.py:241
  23.3 1.8 %collective-permute-start.12 = (bf16[88,256]{1,0:T(8,128)(2,1)S(1)}, bf16[88,256]{1,0:T(8,128)(2,1)S(1)}, u32[]{:S(2)}, u32[]{:S(2)}) collective-permute-start(bf16[88,256]{1,0:T(8,128)(2,1)S(1)} %get-tuple-element.47), channel_id=1, source_target_pairs={{0,3},{1,2},{2,1},{3,0},{4,7},{5,6},{6,5},{7,4},{8,11},{9,10},{10,... | collective-permute-start | bytes 135176 | tf_op jit(solution)/shard_map/ppermute | solution.py:241
  25.1 0.0 collective-permute-done.8.refs_1_
  25.1 0.5 %collective-permute-start.13 = (bf16[88,256]{1,0:T(8,128)(2,1)S(1)}, bf16[88,256]{1,0:T(8,128)(2,1)S(1)}, u32[]{:S(2)}, u32[]{:S(2)}) collective-permute-start(bf16[88,256]{1,0:T(8,128)(2,1)S(1)} %get-tuple-element.48), channel_id=1, source_target_pairs={{0,1},{1,0},{2,3},{3,2},{4,5},{5,4},{6,7},{7,6},{8,9},{9,8},{10,11... | collective-permute-start | bytes 135176 | tf_op jit(solution)/shard_map/ppermute | solution.py:241
  25.7 0.0 collective-permute-done.9.refs_2_
  25.7 1.1 %collective-permute-start.14 = (bf16[88,256]{1,0:T(8,128)(2,1)S(1)}, bf16[88,256]{1,0:T(8,128)(2,1)S(1)}, u32[]{:S(2)}, u32[]{:S(2)}) collective-permute-start(bf16[88,256]{1,0:T(8,128)(2,1)S(1)} %get-tuple-element.49), channel_id=1, source_target_pairs={{0,2},{1,3},{2,0},{3,1},{4,6},{5,7},{6,4},{7,5},{8,10},{9,11},{10,... | collective-permute-start | bytes 135176 | tf_op jit(solution)/shard_map/ppermute | solution.py:241
  26.8 1.2 %collective-permute-done.10.refs_3_ = bf16[88,256]{1,0:T(8,128)(2,1)S(1)} collective-permute-done((bf16[88,256]{1,0:T(8,128)(2,1)S(1)}, bf16[88,256]{1,0:T(8,128)(2,1)S(1)}, u32[]{:S(2)}, u32[]{:S(2)}) %collective-permute-start.10) | collective-permute-done | bytes 45088 | tf_op jit(solution)/shard_map/ppermute | solution.py:241
  28.0 1.3 %collective-permute-done.11.refs_4_ = bf16[88,256]{1,0:T(8,128)(2,1)S(1)} collective-permute-done((bf16[88,256]{1,0:T(8,128)(2,1)S(1)}, bf16[88,256]{1,0:T(8,128)(2,1)S(1)}, u32[]{:S(2)}, u32[]{:S(2)}) %collective-permute-start.11) | collective-permute-done | bytes 45088 | tf_op jit(solution)/shard_map/ppermute | solution.py:241
  29.3 0.0 collective-permute-done.12.refs_5_
  29.4 0.4 %collective-permute-done.13.refs_6_ = bf16[88,256]{1,0:T(8,128)(2,1)S(1)} collective-permute-done((bf16[88,256]{1,0:T(8,128)(2,1)S(1)}, bf16[88,256]{1,0:T(8,128)(2,1)S(1)}, u32[]{:S(2)}, u32[]{:S(2)}) %collective-permute-start.13) | collective-permute-done | bytes 45088 | tf_op jit(solution)/shard_map/ppermute | solution.py:241
  29.7 0.8 %shard_map.108.refs_0_ = f32[640,256]{1,0:T(8,128)S(1)} custom-call(bf16[88,256]{1,0:T(8,128)(2,1)S(1)} %get-tuple-element.42.refs_0_, bf16[88,256]{1,0:T(8,128)(2,1)S(1)} %collective-permute-done.8.refs_1_, bf16[88,256]{1,0:T(8,128)(2,1)S(1)} %collective-permute-done.9.refs_2_, bf16[88,256]{1,0:T(8,128)(2,1)S(1)} %collective-permute-done.10.refs_3_, ...), custom_call_target="tpu_custom_call" | custom-call | flops 268435456 | bytes 1024 | tf_op jit(solution)/shard_map/pallas_call | solution.py:224
  30.6 0.0 collective-permute-done.14.refs_1_
  30.6 0.0 copy-done.2
  30.6 0.0 copy-done.3
  30.6 1.5 %shard_map.109 = (f32[640,256]{1,0:T(8,128)}, f32[640,256]{1,0:T(8,128)}) custom-call(f32[640,256]{1,0:T(8,128)S(1)} %shard_map.108.refs_0_, bf16[88,256]{1,0:T(8,128)(2,1)S(1)} %collective-permute-done.14.refs_1_, f32[640,256]{1,0:T(8,128)S(1)} %copy-done.2, f32[640,256]{1,0:T(8,128)S(1)} %copy-done.3), custom_call_target="tpu_custom_call" | custom-call | tf_op jit(solution)/shard_map/pallas_call | solution.py:348
  (7 shorter events, 0.0 us)
Async XLA Ops:
  0.6 8.3 %collective-permute-start.2 = (bf16[320,256]{1,0:T(8,128)(2,1)}, bf16[320,256]{1,0:T(8,128)(2,1)S(1)}, u32[]{:S(2)}, u32[]{:S(2)}) collective-permute-start(bf16[320,256]{1,0:T(8,128)(2,1)} %refs_0_.5), channel_id=1, source_target_pairs={{0,16},{8,24},{16,0},{24,8},{1,17},{9,25},{17,1},{25,9},{2,18},{10... | collective-permute-start | bytes 491528 | tf_op jit(solution)/shard_map/ppermute | solution.py:241
  3.7 7.2 %collective-permute-start.1 = (bf16[320,256]{1,0:T(8,128)(2,1)}, bf16[320,256]{1,0:T(8,128)(2,1)S(1)}, u32[]{:S(2)}, u32[]{:S(2)}) collective-permute-start(bf16[320,256]{1,0:T(8,128)(2,1)} %refs_0_.5), channel_id=1, source_target_pairs={{0,8},{8,0},{16,24},{24,16},{1,9},{9,1},{17,25},{25,17},{2,10},{10... | collective-permute-start | bytes 491528 | tf_op jit(solution)/shard_map/ppermute | solution.py:241
  3.7 5.3 %collective-permute-start.3 = (s32[320]{0:T(512)}, s32[320]{0:T(512)S(1)}, u32[]{:S(2)}, u32[]{:S(2)}) collective-permute-start(s32[320]{0:T(512)} %param.11), channel_id=1, source_target_pairs={{0,16},{8,24},{16,0},{24,8},{1,17},{9,25},{17,1},{25,9},{2,18},{10... | collective-permute-start | bytes 3848 | tf_op jit(solution)/shard_map/ppermute | solution.py:241
  3.8 7.8 %collective-permute-start = (bf16[320,256]{1,0:T(8,128)(2,1)}, bf16[320,256]{1,0:T(8,128)(2,1)S(1)}, u32[]{:S(2)}, u32[]{:S(2)}) collective-permute-start(bf16[320,256]{1,0:T(8,128)(2,1)} %refs_0_.4), channel_id=1, source_target_pairs={{0,16},{8,24},{16,0},{24,8},{1,17},{9,25},{17,1},{25,9},{2,18},{10... | collective-permute-start | bytes 491528 | tf_op jit(solution)/shard_map/ppermute | solution.py:241
  7.1 1.9 %copy-start.4 = (s32[320]{0:T(512)S(1)}, s32[320]{0:T(512)}, u32[]{:S(2)}) copy-start(s32[320]{0:T(512)} %param.11) | copy-start | bytes 3844
  7.1 3.8 %copy-start = (bf16[320,256]{1,0:T(8,128)(2,1)S(1)}, bf16[320,256]{1,0:T(8,128)(2,1)}, u32[]{:S(2)}) copy-start(bf16[320,256]{1,0:T(8,128)(2,1)} %refs_0_.4) | copy-start | bytes 491524
  7.1 3.8 %copy-start.1 = (bf16[320,256]{1,0:T(8,128)(2,1)S(1)}, bf16[320,256]{1,0:T(8,128)(2,1)}, u32[]{:S(2)}) copy-start(bf16[320,256]{1,0:T(8,128)(2,1)} %refs_0_.5) | copy-start | bytes 491524
  8.9 2.7 %collective-permute-start.4 = (bf16[320,256]{1,0:T(8,128)(2,1)S(1)}, bf16[320,256]{1,0:T(8,128)(2,1)S(1)}, u32[]{:S(2)}, u32[]{:S(2)}) collective-permute-start(bf16[320,256]{1,0:T(8,128)(2,1)S(1)} %collective-permute-done.2.refs_2_.refs_4_), channel_id=1, source_target_pairs={{0,8},{8,0},{16,24},{24,16},{1,9},{9,1},{17,25},{25,17},{2,10},{10... | collective-permute-start | bytes 491528 | tf_op jit(solution)/shard_map/ppermute | solution.py:241
  9.0 1.4 %collective-permute-start.5 = (s32[320]{0:T(512)S(1)}, s32[320]{0:T(512)S(1)}, u32[]{:S(2)}, u32[]{:S(2)}) collective-permute-start(s32[320]{0:T(512)S(1)} %copy-done.4), channel_id=1, source_target_pairs={{0,8},{8,0},{16,24},{24,16},{1,9},{9,1},{17,25},{25,17},{2,10},{10... | collective-permute-start | bytes 3848 | tf_op jit(solution)/shard_map/ppermute | solution.py:241
  9.5 1.2 %collective-permute-start.6 = (s32[320]{0:T(512)S(1)}, s32[320]{0:T(512)S(1)}, u32[]{:S(2)}, u32[]{:S(2)}) collective-permute-start(s32[320]{0:T(512)S(1)} %collective-permute-done.3), channel_id=1, source_target_pairs={{0,8},{8,0},{16,24},{24,16},{1,9},{9,1},{17,25},{25,17},{2,10},{10... | collective-permute-start | bytes 3848 | tf_op jit(solution)/shard_map/ppermute | solution.py:241
  13.3 1.6 %collective-permute-start.7 = (f32[320,256]{1,0:T(8,128)S(1)}, f32[320,256]{1,0:T(8,128)S(1)}, u32[]{:S(2)}, u32[]{:S(2)}) collective-permute-start(f32[320,256]{1,0:T(8,128)S(1)} %get-tuple-element.34), channel_id=1, source_target_pairs={{0,8},{8,0},{16,24},{24,16},{1,9},{9,1},{17,25},{25,17},{2,10},{10... | collective-permute-start | bytes 983048 | tf_op jit(solution)/shard_map/ppermute | solution.py:241
  14.8 15.8 %copy-start.2 = (f32[640,256]{1,0:T(8,128)S(1)}, f32[640,256]{1,0:T(8,128)}, u32[]{:S(2)}) copy-start(f32[640,256]{1,0:T(8,128)} %refs_2_.3) | copy-start | bytes 1966084
  14.8 15.8 %copy-start.3 = (f32[640,256]{1,0:T(8,128)S(1)}, f32[640,256]{1,0:T(8,128)}, u32[]{:S(2)}) copy-start(f32[640,256]{1,0:T(8,128)} %refs_3_.1) | copy-start | bytes 1966084
  15.4 9.8 %collective-permute-start.8 = (bf16[88,256]{1,0:T(8,128)(2,1)S(1)}, bf16[88,256]{1,0:T(8,128)(2,1)S(1)}, u32[]{:S(2)}, u32[]{:S(2)}) collective-permute-start(bf16[88,256]{1,0:T(8,128)(2,1)S(1)} %get-tuple-element.43), channel_id=1, source_target_pairs={{0,4},{1,5},{2,6},{3,7},{4,0},{5,1},{6,2},{7,3},{8,12},{9,13},{10,... | collective-permute-start | bytes 135176 | tf_op jit(solution)/shard_map/ppermute | solution.py:241
  18.5 7.2 %collective-permute-start.9 = (bf16[88,256]{1,0:T(8,128)(2,1)S(1)}, bf16[88,256]{1,0:T(8,128)(2,1)S(1)}, u32[]{:S(2)}, u32[]{:S(2)}) collective-permute-start(bf16[88,256]{1,0:T(8,128)(2,1)S(1)} %get-tuple-element.44), channel_id=1, source_target_pairs={{0,6},{1,7},{2,4},{3,5},{4,2},{5,3},{6,0},{7,1},{8,14},{9,15},{10,... | collective-permute-start | bytes 135176 | tf_op jit(solution)/shard_map/ppermute | solution.py:241
  19.8 8.2 %collective-permute-start.10 = (bf16[88,256]{1,0:T(8,128)(2,1)S(1)}, bf16[88,256]{1,0:T(8,128)(2,1)S(1)}, u32[]{:S(2)}, u32[]{:S(2)}) collective-permute-start(bf16[88,256]{1,0:T(8,128)(2,1)S(1)} %get-tuple-element.45), channel_id=1, source_target_pairs={{0,5},{1,4},{2,7},{3,6},{4,1},{5,0},{6,3},{7,2},{8,13},{9,12},{10,... | collective-permute-start | bytes 135176 | tf_op jit(solution)/shard_map/ppermute | solution.py:241
  22.4 6.9 %collective-permute-start.11 = (bf16[88,256]{1,0:T(8,128)(2,1)S(1)}, bf16[88,256]{1,0:T(8,128)(2,1)S(1)}, u32[]{:S(2)}, u32[]{:S(2)}) collective-permute-start(bf16[88,256]{1,0:T(8,128)(2,1)S(1)} %get-tuple-element.46), channel_id=1, source_target_pairs={{0,7},{1,6},{2,5},{3,4},{4,3},{5,2},{6,1},{7,0},{8,15},{9,14},{10,... | collective-permute-start | bytes 135176 | tf_op jit(solution)/shard_map/ppermute | solution.py:241
  23.3 6.1 %collective-permute-start.12 = (bf16[88,256]{1,0:T(8,128)(2,1)S(1)}, bf16[88,256]{1,0:T(8,128)(2,1)S(1)}, u32[]{:S(2)}, u32[]{:S(2)}) collective-permute-start(bf16[88,256]{1,0:T(8,128)(2,1)S(1)} %get-tuple-element.47), channel_id=1, source_target_pairs={{0,3},{1,2},{2,1},{3,0},{4,7},{5,6},{6,5},{7,4},{8,11},{9,10},{10,... | collective-permute-start | bytes 135176 | tf_op jit(solution)/shard_map/ppermute | solution.py:241
  25.1 4.6 %collective-permute-start.13 = (bf16[88,256]{1,0:T(8,128)(2,1)S(1)}, bf16[88,256]{1,0:T(8,128)(2,1)S(1)}, u32[]{:S(2)}, u32[]{:S(2)}) collective-permute-start(bf16[88,256]{1,0:T(8,128)(2,1)S(1)} %get-tuple-element.48), channel_id=1, source_target_pairs={{0,1},{1,0},{2,3},{3,2},{4,5},{5,4},{6,7},{7,6},{8,9},{9,8},{10,11... | collective-permute-start | bytes 135176 | tf_op jit(solution)/shard_map/ppermute | solution.py:241
  25.7 4.9 %collective-permute-start.14 = (bf16[88,256]{1,0:T(8,128)(2,1)S(1)}, bf16[88,256]{1,0:T(8,128)(2,1)S(1)}, u32[]{:S(2)}, u32[]{:S(2)}) collective-permute-start(bf16[88,256]{1,0:T(8,128)(2,1)S(1)} %get-tuple-element.49), channel_id=1, source_target_pairs={{0,2},{1,3},{2,0},{3,1},{4,6},{5,7},{6,4},{7,5},{8,10},{9,11},{10,... | collective-permute-start | bytes 135176 | tf_op jit(solution)/shard_map/ppermute | solution.py:241

commit v7 on v6

--- a/solution.py
+++ b/solution.py
@@ -67,28 +67,20 @@
         tail_ref[g] = jnp.concatenate([dot(high, pick, NT), dot(low, pick, NT)], axis=1).astype(BF16)
 
 
-def bias_kernel(n, *refs):
-    for b in range(n):
-        block = refs[b].shape[1]
-        row = jnp.log(refs[b][...].astype(F32)) * LOG2E
-        refs[n][b] = jnp.transpose(jnp.broadcast_to(row, (LANES, block)))
-
-
-def fill_logits(q, item_refs, bias_ref, first, out_ref):
+def fill_logits(q, item_refs, out_ref):
     top = None
     for b, item_ref in enumerate(item_refs):
         logits = dot(item_ref[...], q, NT) * (SCALE * LOG2E)
-        logits -= spread(bias_ref[first + b], q.shape[0])
         out_ref[b] = logits
         high = jnp.max(logits, axis=0, keepdims=True)
         top = high if top is None else jnp.maximum(top, high)
     return top
 
 
-def to_powers(ref, top):
+def to_powers(ref, top, rate_ref, first):
     total = jnp.zeros(top.shape, F32)
     for b in range(ref.shape[0]):
-        e = jnp.exp2(ref[b] - top)
+        e = jnp.exp2(ref[b] - top) * spread(rate_ref[first + b], top.shape[1])
         ref[b] = e
         total += jnp.sum(e, axis=0, keepdims=True)
     return total
@@ -101,28 +93,45 @@
 
 
 def early_kernel(n, q_ref, *refs):
-    item_refs, (bias_ref, e_ref, stats_ref) = refs[:n], refs[n:]
-    block = q_ref.shape[0]
-    top = fill_logits(q_ref[...], item_refs, bias_ref, 0, e_ref)
-    chosen = jnp.sum(jnp.where(diagonal(block), e_ref[0], 0.0), axis=0, keepdims=True)
+    item_refs, (e_ref, stats_ref) = refs[:n], refs[n:]
+    top = fill_logits(q_ref[...], item_refs, e_ref)
+    chosen = jnp.where(diagonal(q_ref.shape[0]), e_ref[0], 0.0)
     stats_ref[0:1] = top
-    stats_ref[1:2] = to_powers(e_ref, top)
-    stats_ref[2:3] = chosen
+    stats_ref[1:2] = jnp.sum(chosen, axis=0, keepdims=True)
+    for b in range(n):
+        e_ref[b] = jnp.exp2(e_ref[b] - top)
+
+
+def rate_kernel(n, early, e_ref, near_ref, mate_ref, rate_ref, out_ref, total_ref):
+    block = e_ref.shape[1]
+    near = [near_ref[:, k * block : (k + 1) * block].astype(F32) for k in range(n // 2)]
+    mate = [mate_ref[:, k * block : (k + 1) * block].astype(F32) for k in range(n // 2)]
+    counts = [near[0], mate[0]] + near[1:] + mate[1:]
+    total = jnp.zeros((1, block), F32)
+    for b in range(n):
+        rate = jnp.transpose(jnp.broadcast_to(1.0 / counts[b], (LANES, block)))
+        rate_ref[b] = rate
+        if b < early:
+            e = e_ref[b] * spread(rate, block)
+            out_ref[b] = e
+            total += jnp.sum(e, axis=0, keepdims=True)
+    total_ref[0:1] = total
+    total_ref[1:2] = jnp.log(counts[0]) * LOG2E
 
 
 def main_kernel(early, late, *refs):
     n = early + late
     q_ref, far_ref, item_refs, refs = refs[0], refs[1], refs[2 : 2 + n], refs[2 + n :]
-    bias_ref, e_ref, stats_ref, mine_out, mate_out, loss_ref, late_ref, factor_ref, far_e_ref = refs
+    rate_ref, e_ref, stats_ref, total_ref, mine_out, mate_out, *refs = refs
+    loss_ref, late_ref, factor_ref, far_e_ref = refs
     block = q_ref.shape[0]
     q, far = q_ref[...], far_ref[...]
-    far_top = fill_logits(far, item_refs, bias_ref, 0, far_e_ref)
-    early_top, early_total, chosen = stats_ref[0:1], stats_ref[1:2], stats_ref[2:3]
-    top = fill_logits(q, item_refs[early:], bias_ref, early, late_ref)
-    top = jnp.maximum(top, early_top)
-    far_inverse = 1.0 / to_powers(far_e_ref, far_top)
+    far_top = fill_logits(far, item_refs, far_e_ref)
+    early_top, early_total = stats_ref[0:1], total_ref[0:1]
+    top = jnp.maximum(fill_logits(q, item_refs[early:], late_ref), early_top)
+    far_inverse = 1.0 / to_powers(far_e_ref, far_top, rate_ref, 0)
     shrink = jnp.exp2(early_top - top)
-    total = to_powers(late_ref, top) + early_total * shrink
+    total = to_powers(late_ref, top, rate_ref, early) + early_total * shrink
     inverse = 1.0 / total
     factor = shrink * inverse
     mate = dot((e_ref[1] * factor).astype(BF16), q)
@@ -131,6 +140,7 @@
     weights = jnp.where(diagonal(block), weights - 1.0, weights)
     mine = dot(weights.astype(BF16), q)
     mine_out[...] = mine + dot((far_e_ref[0] * far_inverse).astype(BF16), far)
+    chosen = stats_ref[1:2] - total_ref[1:2]
     loss_ref[...] = ((top + jnp.log2(total) - chosen) * (1.0 / LOG2E))[0]
     factor_ref[0:1] = factor
     factor_ref[1:2] = inverse
@@ -138,9 +148,9 @@
 
 def more_kernel(n, q_ref, *refs):
     item_refs, refs = refs[:n], refs[n:]
-    bias_ref, mine_ref, mate_ref, mine_out, mate_out, e_ref = refs
+    rate_ref, mine_ref, mate_ref, mine_out, mate_out, e_ref = refs
     q = q_ref[...]
-    inverse = 1.0 / to_powers(e_ref, fill_logits(q, item_refs, bias_ref, 0, e_ref))
+    inverse = 1.0 / to_powers(e_ref, fill_logits(q, item_refs, e_ref), rate_ref, 0)
     mate_out[...] = mate_ref[...] + dot((e_ref[1] * inverse).astype(BF16), q)
     mine_out[...] = mine_ref[...] + dot((e_ref[0] * inverse).astype(BF16), q)
 
@@ -258,14 +268,8 @@
     early = len(item_blocks)
     item_blocks += [swap(x, 1) for x in far_items]
     late = n - early
-    count_blocks = [sample_counts, swap(sample_counts, 1)] + far_counts
-    count_blocks += [swap(x, 1) for x in far_counts]
-    (bias,) = call(
-        functools.partial(bias_kernel, n),
-        [((n, block, LANES), F32)],
-        *[x.reshape(1, block) for x in count_blocks],
-    )
-
+    near_counts = jnp.concatenate([sample_counts, *far_counts])
+    mate_counts = swap(near_counts, 1)
     part = ((block, D), F32)
     square = (block, block)
     powers, stats = call(
@@ -273,8 +277,16 @@
         [((early, *square), F32), ((8, block), F32)],
         queries,
         *item_blocks[:early],
-        bias,
         limit=8 + 2 * n,
+        flops=1 << 29,
+    )
+    rates, powers, totals = call(
+        functools.partial(rate_kernel, n, early),
+        [((n, block, LANES), F32), ((early, *square), F32), ((8, block), F32)],
+        powers,
+        near_counts.reshape(1, -1),
+        mate_counts.reshape(1, -1),
+        limit=8 + 4 * n,
     )
     mine, mate, loss, late_powers, factors = call(
         functools.partial(main_kernel, early, late),
@@ -282,9 +294,10 @@
         queries,
         far_queries[0],
         *item_blocks,
-        bias,
+        rates,
         powers,
         stats,
+        totals,
         scratch=[pltpu.VMEM((n, *square), F32)],
         limit=8 + 4 * n,
     )
@@ -294,7 +307,7 @@
             [part, part],
             far,
             *item_blocks,
-            bias,
+            rates,
             mine,
             mate,
             scratch=[pltpu.VMEM((n, *square), F32)],
@@ -334,7 +347,7 @@
             pltpu.VMEM((TAIL, packets * slots), F32),
         ]
 
-    count = groups - 1
+    count = groups // 2
     before = []
     if paired:
         before = call(

time: 32.3 us -> 31.5 us (0.975)
  waiting for transfers between devices: 5.33 us -> 4.79 us
  starting transfers between devices: 17.2 us -> 16.8 us
    ppermute x15 -> x14, waiting for transfers between devices: 5.33 us -> 4.79 us  [swap(): lax.ppermute(x, axis, [(i, i ^ k) for i in range(lax.axis_size(axis))])]
    ppermute x15 -> x14, starting transfers between devices: 17.2 us -> 16.8 us  [swap(): lax.ppermute(x, axis, [(i, i ^ k) for i in range(lax.axis_size(axis))])]
  transfers between devices with their start and end apart: 15 -> 14, of which waited for: 8 -> 7; matrix products, arithmetic and copies ran while one was open for 4% -> 5% of each run, Pallas kernels for 12% -> 12%
where the time goes in v7:
time: 31.5 us; the launch traced here: 31.3 us
  starting transfers between devices  16.8 us (53%)
  Pallas kernels  7.56 us (24%)
  waiting for transfers between devices  4.79 us (15%)
  other arithmetic  1.46 us (5%)
  between operations  0.71 us (2%)
    ppermute x14, starting transfers between devices, swap(): lax.ppermute(x, axis, [(i, i ^ k) for i in range(lax.axis_size(axis))])  16.8 us
    pallas_call x7, Pallas kernels, call(): pl.pallas_call(kernel, out_shape=[jax.ShapeDtypeStruct(s, t) for s, t in...  5.9 us
    ppermute x14, waiting for transfers between devices, swap(): lax.ppermute(x, axis, [(i, i ^ k) for i in range(lax.axis_size(axis))])  4.79 us
    pallas_call x1, Pallas kernels, shards(): pl.pallas_call(functools.partial(update_kernel, slots, paired), out_shape...  1.67 us
    mul x1, other arithmetic, shards(): owner * ROW_CODES + item_offset.reshape(1, block)  0.7 us
    add x1, other arithmetic, shards(): owner * ROW_CODES + item_offset.reshape(1, block)  0.68 us
  transfers between devices with their start and end apart: 14, of which 7 were waited for; matrix products, arithmetic and copies ran while one was open for 5% of the time, Pallas kernels for 12%

profile of v7, /device:TPU:0, one launch (start us, length us, event | category | flops | bytes accessed | tf_op | source)
XLA Modules:
  0.0 31.3 jit_solution(47599705882579213)
XLA Ops:
  0.6 3.0 %collective-permute-start.2 = (bf16[320,256]{1,0:T(8,128)(2,1)}, bf16[320,256]{1,0:T(8,128)(2,1)S(1)}, u32[]{:S(2)}, u32[]{:S(2)}) collective-permute-start(bf16[320,256]{1,0:T(8,128)(2,1)} %refs_0_.5), channel_id=1, source_target_pairs={{0,16},{8,24},{16,0},{24,8},{1,17},{9,25},{17,1},{25,9},{2,18},{10... | collective-permute-start | bytes 491528 | tf_op jit(solution)/shard_map/ppermute | solution.py:251
  3.7 0.0 collective-permute-start.1
  3.7 0.2 collective-permute-start.3
  3.8 1.9 %collective-permute-start = (bf16[320,256]{1,0:T(8,128)(2,1)}, bf16[320,256]{1,0:T(8,128)(2,1)S(1)}, u32[]{:S(2)}, u32[]{:S(2)}) collective-permute-start(bf16[320,256]{1,0:T(8,128)(2,1)} %refs_0_.4), channel_id=1, source_target_pairs={{0,16},{8,24},{16,0},{24,8},{1,17},{9,25},{17,1},{25,9},{2,18},{10... | collective-permute-start | bytes 491528 | tf_op jit(solution)/shard_map/ppermute | solution.py:251
  5.7 0.7 %multiply_reduce_fusion = s32[320]{0:T(512)S(1)} fusion(s32[320,1]{0,1:T(1,128)} %param.9, s32[]{:T(128)S(6)} %axis_index.12), kind=kLoop, calls=%fused_computation.1 | loop fusion | flops 640 | bytes 2564 | tf_op jit(solution)/shard_map/mul | solution.py:263
  6.4 0.7 %add.5 = s32[320]{0:T(512)S(1)} add(s32[320]{0:T(512)S(1)} %multiply_reduce_fusion, s32[320]{0:T(512)} %param.10) | non-fusion elementwise | flops 320 | bytes 3840 | tf_op jit(solution)/shard_map/add | solution.py:263
  7.1 0.0 copy-start.4
  7.1 0.0 copy-start.2
  7.1 0.0 copy-start.3
  7.1 0.8 %shard_map.102 = (bf16[640,320]{1,0:T(8,128)(2,1)S(1)}, bf16[8,8,256]{2,1,0:T(8,128)(2,1)S(1)}) custom-call(s32[1,320]{1,0:T(1,128)S(1)} %add.6.code_ref), custom_call_target="tpu_custom_call" | custom-call | flops 1073741824 | bytes 1024 | tf_op jit(solution)/shard_map/pallas_call | solution.py:234
  7.9 1.0 %collective-permute-done.3 = s32[320]{0:T(512)S(1)} collective-permute-done((s32[320]{0:T(512)}, s32[320]{0:T(512)S(1)}, u32[]{:S(2)}, u32[]{:S(2)}) %collective-permute-start.3) | collective-permute-done | bytes 1312 | tf_op jit(solution)/shard_map/ppermute | solution.py:251
  8.9 0.0 collective-permute-done.2.refs_2_.refs_4_
  8.9 0.0 collective-permute-start.4
  9.0 0.0 copy-done.4
  9.0 0.1 pad_add_fusion
  9.0 0.5 %collective-permute-start.5 = (s32[640]{0:T(1024)S(1)}, s32[640]{0:T(1024)S(1)}, u32[]{:S(2)}, u32[]{:S(2)}) collective-permute-start(s32[640]{0:T(1024)S(1)} %pad_add_fusion), channel_id=1, source_target_pairs={{0,8},{8,0},{16,24},{24,16},{1,9},{9,1},{17,25},{25,17},{2,10},{10... | collective-permute-start | bytes 7688 | tf_op jit(solution)/shard_map/ppermute | solution.py:251
  9.5 0.0 collective-permute-done.1.refs_1_.refs_3_
  9.5 0.0 copy-done.2
  9.5 0.0 copy-done.3
  9.6 0.6 %shard_map.103 = (f32[3,320,320]{2,1,0:T(8,128)S(1)}, f32[8,320]{1,0:T(8,128)S(1)}) custom-call(bf16[320,256]{1,0:T(8,128)(2,1)S(1)} %copy-done.2, bf16[320,256]{1,0:T(8,128)(2,1)S(1)} %copy-done.3, bf16[320,256]{1,0:T(8,128)(2,1)S(1)} %collective-permute-done.1.refs_1_.refs_3_, bf16[320,256]{1,0:T(8,128)(2,1)S(1)} %collective-permute-done.2.refs_2_.refs_4_), custom_call_target="tpu_custom_call" | custom-call | flops 536870912 | bytes 1024 | tf_op jit(solution)/shard_map/pallas_call | solution.py:234
  10.2 0.2 collective-permute-done.5
  10.4 0.4 %shard_map.104 = (f32[4,320,128]{2,1,0:T(8,128)S(1)}, f32[3,320,320]{2,1,0:T(8,128)S(1)}, f32[8,320]{1,0:T(8,128)S(1)}) custom-call(f32[3,320,320]{2,1,0:T(8,128)S(1)} %get-tuple-element.33.e_ref, s32[1,640]{1,0:T(1,128)S(1)} %reshape.24.near_ref, s32[1,640]{1,0:T(1,128)S(1)} %reshape.25.mate_ref), custom_call_target="tpu_custom_call" | custom-call | bytes 1024 | tf_op jit(solution)/shard_map/pallas_call | solution.py:234
  10.7 0.9 %collective-permute-done.refs_1_ = bf16[320,256]{1,0:T(8,128)(2,1)S(1)} collective-permute-done((bf16[320,256]{1,0:T(8,128)(2,1)}, bf16[320,256]{1,0:T(8,128)(2,1)S(1)}, u32[]{:S(2)}, u32[]{:S(2)}) %collective-permute-start) | collective-permute-done | bytes 163872 | tf_op jit(solution)/shard_map/ppermute | solution.py:251
  11.6 0.0 collective-permute-done.4.refs_5_.refs_3_
  11.6 1.8 %shard_map.105 = (f32[320,256]{1,0:T(8,128)S(1)}, f32[320,256]{1,0:T(8,128)S(1)}, f32[320]{0:T(512)}, f32[1,320,320]{2,1,0:T(8,128)S(1)}, f32[8,320]{1,0:T(8,128)S(1)}) custom-call(bf16[320,256]{1,0:T(8,128)(2,1)S(1)} %copy-done.2, bf16[320,256]{1,0:T(8,128)(2,1)S(1)} %collective-permute-done.refs_1_, bf16[320,256]{1,0:T(8,128)(2,1)S(1)} %copy-done.3, ...), custom_call_target="tpu_custom_call" | custom-call | bytes 1024 | tf_op jit(solution)/shard_map/pallas_call | solution.py:234
  13.5 0.0 collective-permute-start.6
  13.5 1.3 %shard_map.106 = f32[320,256]{1,0:T(8,128)} custom-call(f32[3,320,320]{2,1,0:T(8,128)S(1)} %get-tuple-element.36.refs_7_.e_ref, f32[1,320,320]{2,1,0:T(8,128)S(1)} %get-tuple-element.41.late_ref, f32[8,320]{1,0:T(8,128)S(1)} %get-tuple-element.42.factor_ref, bf16[320,256]{1,0:T(8,128)(2,1)S(1)} %copy-done.3, ...), custom_call_target="tpu_custom_call" | custom-call | flops 1073741824 | bytes 1024 | tf_op jit(solution)/shard_map/pallas_call | solution.py:234
  14.8 0.0 copy-start
  14.8 0.3 %collective-permute-done.6.other_ref = f32[320,256]{1,0:T(8,128)S(1)} collective-permute-done((f32[320,256]{1,0:T(8,128)S(1)}, f32[320,256]{1,0:T(8,128)S(1)}, u32[]{:S(2)}, u32[]{:S(2)}) %collective-permute-start.6) | collective-permute-done | bytes 327712 | tf_op jit(solution)/shard_map/ppermute | solution.py:251
  15.1 0.4 %shard_map.107 = (bf16[88,256]{1,0:T(8,128)(2,1)S(1)}, bf16[88,256]{1,0:T(8,128)(2,1)S(1)}, bf16[88,256]{1,0:T(8,128)(2,1)S(1)}, bf16[88,256]{1,0:T(8,128)(2,1)S...) custom-call(bf16[640,320]{1,0:T(8,128)(2,1)S(1)} %get-tuple-element., ...), custom_call_target="tpu_custom_call" | custom-call | bytes 1024 | tf_op jit(solution)/shard_map/pallas_call | solution.py:234
  15.5 2.9 %collective-permute-start.7 = (bf16[88,256]{1,0:T(8,128)(2,1)S(1)}, bf16[88,256]{1,0:T(8,128)(2,1)S(1)}, u32[]{:S(2)}, u32[]{:S(2)}) collective-permute-start(bf16[88,256]{1,0:T(8,128)(2,1)S(1)} %get-tuple-element.49), channel_id=1, source_target_pairs={{0,4},{1,5},{2,6},{3,7},{4,0},{5,1},{6,2},{7,3},{8,12},{9,13},{10,... | collective-permute-start | bytes 135176 | tf_op jit(solution)/shard_map/ppermute | solution.py:251
  18.4 1.3 %collective-permute-start.8 = (bf16[88,256]{1,0:T(8,128)(2,1)S(1)}, bf16[88,256]{1,0:T(8,128)(2,1)S(1)}, u32[]{:S(2)}, u32[]{:S(2)}) collective-permute-start(bf16[88,256]{1,0:T(8,128)(2,1)S(1)} %get-tuple-element.50), channel_id=1, source_target_pairs={{0,6},{1,7},{2,4},{3,5},{4,2},{5,3},{6,0},{7,1},{8,14},{9,15},{10,... | collective-permute-start | bytes 135176 | tf_op jit(solution)/shard_map/ppermute | solution.py:251
  19.7 2.6 %collective-permute-start.9 = (bf16[88,256]{1,0:T(8,128)(2,1)S(1)}, bf16[88,256]{1,0:T(8,128)(2,1)S(1)}, u32[]{:S(2)}, u32[]{:S(2)}) collective-permute-start(bf16[88,256]{1,0:T(8,128)(2,1)S(1)} %get-tuple-element.51), channel_id=1, source_target_pairs={{0,5},{1,4},{2,7},{3,6},{4,1},{5,0},{6,3},{7,2},{8,13},{9,12},{10,... | collective-permute-start | bytes 135176 | tf_op jit(solution)/shard_map/ppermute | solution.py:251
  22.3 0.9 %collective-permute-start.10 = (bf16[88,256]{1,0:T(8,128)(2,1)S(1)}, bf16[88,256]{1,0:T(8,128)(2,1)S(1)}, u32[]{:S(2)}, u32[]{:S(2)}) collective-permute-start(bf16[88,256]{1,0:T(8,128)(2,1)S(1)} %get-tuple-element.52), channel_id=1, source_target_pairs={{0,7},{1,6},{2,5},{3,4},{4,3},{5,2},{6,1},{7,0},{8,15},{9,14},{10,... | collective-permute-start | bytes 135176 | tf_op jit(solution)/shard_map/ppermute | solution.py:251
  23.2 1.8 %collective-permute-start.11 = (bf16[88,256]{1,0:T(8,128)(2,1)S(1)}, bf16[88,256]{1,0:T(8,128)(2,1)S(1)}, u32[]{:S(2)}, u32[]{:S(2)}) collective-permute-start(bf16[88,256]{1,0:T(8,128)(2,1)S(1)} %get-tuple-element.53), channel_id=1, source_target_pairs={{0,3},{1,2},{2,1},{3,0},{4,7},{5,6},{6,5},{7,4},{8,11},{9,10},{10,... | collective-permute-start | bytes 135176 | tf_op jit(solution)/shard_map/ppermute | solution.py:251
  25.0 0.0 collective-permute-done.7.refs_1_
  25.0 0.5 %collective-permute-start.12 = (bf16[88,256]{1,0:T(8,128)(2,1)S(1)}, bf16[88,256]{1,0:T(8,128)(2,1)S(1)}, u32[]{:S(2)}, u32[]{:S(2)}) collective-permute-start(bf16[88,256]{1,0:T(8,128)(2,1)S(1)} %get-tuple-element.54), channel_id=1, source_target_pairs={{0,1},{1,0},{2,3},{3,2},{4,5},{5,4},{6,7},{7,6},{8,9},{9,8},{10,11... | collective-permute-start | bytes 135176 | tf_op jit(solution)/shard_map/ppermute | solution.py:251
  25.6 0.0 collective-permute-done.8.refs_2_
  25.6 1.1 %collective-permute-start.13 = (bf16[88,256]{1,0:T(8,128)(2,1)S(1)}, bf16[88,256]{1,0:T(8,128)(2,1)S(1)}, u32[]{:S(2)}, u32[]{:S(2)}) collective-permute-start(bf16[88,256]{1,0:T(8,128)(2,1)S(1)} %get-tuple-element.55), channel_id=1, source_target_pairs={{0,2},{1,3},{2,0},{3,1},{4,6},{5,7},{6,4},{7,5},{8,10},{9,11},{10,... | collective-permute-start | bytes 135176 | tf_op jit(solution)/shard_map/ppermute | solution.py:251
  26.7 1.2 %collective-permute-done.9.refs_3_ = bf16[88,256]{1,0:T(8,128)(2,1)S(1)} collective-permute-done((bf16[88,256]{1,0:T(8,128)(2,1)S(1)}, bf16[88,256]{1,0:T(8,128)(2,1)S(1)}, u32[]{:S(2)}, u32[]{:S(2)}) %collective-permute-start.9) | collective-permute-done | bytes 45088 | tf_op jit(solution)/shard_map/ppermute | solution.py:251
  27.9 0.6 %shard_map.108.refs_0_ = f32[640,256]{1,0:T(8,128)S(1)} custom-call(bf16[88,256]{1,0:T(8,128)(2,1)S(1)} %get-tuple-element.48.refs_0_, bf16[88,256]{1,0:T(8,128)(2,1)S(1)} %collective-permute-done.7.refs_1_, bf16[88,256]{1,0:T(8,128)(2,1)S(1)} %collective-permute-done.8.refs_2_, bf16[88,256]{1,0:T(8,128)(2,1)S(1)} %collective-permute-done.9.refs_3_), custom_call_target="tpu_custom_call" | custom-call | flops 268435456 | bytes 1024 | tf_op jit(solution)/shard_map/pallas_call | solution.py:234
  28.5 0.7 %collective-permute-done.10.refs_1_ = bf16[88,256]{1,0:T(8,128)(2,1)S(1)} collective-permute-done((bf16[88,256]{1,0:T(8,128)(2,1)S(1)}, bf16[88,256]{1,0:T(8,128)(2,1)S(1)}, u32[]{:S(2)}, u32[]{:S(2)}) %collective-permute-start.10) | collective-permute-done | bytes 45088 | tf_op jit(solution)/shard_map/ppermute | solution.py:251
  29.2 0.0 collective-permute-done.11.refs_2_
  29.3 0.4 %collective-permute-done.12.refs_3_ = bf16[88,256]{1,0:T(8,128)(2,1)S(1)} collective-permute-done((bf16[88,256]{1,0:T(8,128)(2,1)S(1)}, bf16[88,256]{1,0:T(8,128)(2,1)S(1)}, u32[]{:S(2)}, u32[]{:S(2)}) %collective-permute-start.12) | collective-permute-done | bytes 45088 | tf_op jit(solution)/shard_map/ppermute | solution.py:251
  29.6 0.0 collective-permute-done.13.refs_4_
  29.6 0.0 copy-done
  29.6 0.0 copy-done.1
  29.7 1.7 %shard_map.109 = (f32[640,256]{1,0:T(8,128)}, f32[640,256]{1,0:T(8,128)}) custom-call(f32[640,256]{1,0:T(8,128)S(1)} %shard_map.108.refs_0_, bf16[88,256]{1,0:T(8,128)(2,1)S(1)} %collective-permute-done.10.refs_1_, bf16[88,256]{1,0:T(8,128)(2,1)S(1)} %collective-permute-done.11.refs_2_, bf16[88,256]{1,0:T(8,128)(2,1)S(1)} %collective-permute-done.12.refs_3_, ...), custom_call_target="tpu_custom_call" | custom-call | tf_op jit(solution)/shard_map/pallas_call | solution.py:361
  (4 shorter events, 0.0 us)
Async XLA Ops:
  0.6 8.3 %collective-permute-start.2 = (bf16[320,256]{1,0:T(8,128)(2,1)}, bf16[320,256]{1,0:T(8,128)(2,1)S(1)}, u32[]{:S(2)}, u32[]{:S(2)}) collective-permute-start(bf16[320,256]{1,0:T(8,128)(2,1)} %refs_0_.5), channel_id=1, source_target_pairs={{0,16},{8,24},{16,0},{24,8},{1,17},{9,25},{17,1},{25,9},{2,18},{10... | collective-permute-start | bytes 491528 | tf_op jit(solution)/shard_map/ppermute | solution.py:251
  3.7 5.9 %collective-permute-start.1 = (bf16[320,256]{1,0:T(8,128)(2,1)}, bf16[320,256]{1,0:T(8,128)(2,1)S(1)}, u32[]{:S(2)}, u32[]{:S(2)}) collective-permute-start(bf16[320,256]{1,0:T(8,128)(2,1)} %refs_0_.5), channel_id=1, source_target_pairs={{0,8},{8,0},{16,24},{24,16},{1,9},{9,1},{17,25},{25,17},{2,10},{10... | collective-permute-start | bytes 491528 | tf_op jit(solution)/shard_map/ppermute | solution.py:251
  3.7 5.3 %collective-permute-start.3 = (s32[320]{0:T(512)}, s32[320]{0:T(512)S(1)}, u32[]{:S(2)}, u32[]{:S(2)}) collective-permute-start(s32[320]{0:T(512)} %param.11), channel_id=1, source_target_pairs={{0,16},{8,24},{16,0},{24,8},{1,17},{9,25},{17,1},{25,9},{2,18},{10... | collective-permute-start | bytes 3848 | tf_op jit(solution)/shard_map/ppermute | solution.py:251
  3.8 7.8 %collective-permute-start = (bf16[320,256]{1,0:T(8,128)(2,1)}, bf16[320,256]{1,0:T(8,128)(2,1)S(1)}, u32[]{:S(2)}, u32[]{:S(2)}) collective-permute-start(bf16[320,256]{1,0:T(8,128)(2,1)} %refs_0_.4), channel_id=1, source_target_pairs={{0,16},{8,24},{16,0},{24,8},{1,17},{9,25},{17,1},{25,9},{2,18},{10... | collective-permute-start | bytes 491528 | tf_op jit(solution)/shard_map/ppermute | solution.py:251
  7.1 1.9 %copy-start.4 = (s32[320]{0:T(512)S(1)}, s32[320]{0:T(512)}, u32[]{:S(2)}) copy-start(s32[320]{0:T(512)} %param.11) | copy-start | bytes 3844
  7.1 2.5 %copy-start.2 = (bf16[320,256]{1,0:T(8,128)(2,1)S(1)}, bf16[320,256]{1,0:T(8,128)(2,1)}, u32[]{:S(2)}) copy-start(bf16[320,256]{1,0:T(8,128)(2,1)} %refs_0_.4) | copy-start | bytes 491524
  7.1 2.5 %copy-start.3 = (bf16[320,256]{1,0:T(8,128)(2,1)S(1)}, bf16[320,256]{1,0:T(8,128)(2,1)}, u32[]{:S(2)}) copy-start(bf16[320,256]{1,0:T(8,128)(2,1)} %refs_0_.5) | copy-start | bytes 491524
  8.9 2.7 %collective-permute-start.4 = (bf16[320,256]{1,0:T(8,128)(2,1)S(1)}, bf16[320,256]{1,0:T(8,128)(2,1)S(1)}, u32[]{:S(2)}, u32[]{:S(2)}) collective-permute-start(bf16[320,256]{1,0:T(8,128)(2,1)S(1)} %collective-permute-done.2.refs_2_.refs_4_), channel_id=1, source_target_pairs={{0,8},{8,0},{16,24},{24,16},{1,9},{9,1},{17,25},{25,17},{2,10},{10... | collective-permute-start | bytes 491528 | tf_op jit(solution)/shard_map/ppermute | solution.py:251
  9.0 1.3 %collective-permute-start.5 = (s32[640]{0:T(1024)S(1)}, s32[640]{0:T(1024)S(1)}, u32[]{:S(2)}, u32[]{:S(2)}) collective-permute-start(s32[640]{0:T(1024)S(1)} %pad_add_fusion), channel_id=1, source_target_pairs={{0,8},{8,0},{16,24},{24,16},{1,9},{9,1},{17,25},{25,17},{2,10},{10... | collective-permute-start | bytes 7688 | tf_op jit(solution)/shard_map/ppermute | solution.py:251
  13.5 1.6 %collective-permute-start.6 = (f32[320,256]{1,0:T(8,128)S(1)}, f32[320,256]{1,0:T(8,128)S(1)}, u32[]{:S(2)}, u32[]{:S(2)}) collective-permute-start(f32[320,256]{1,0:T(8,128)S(1)} %get-tuple-element.40), channel_id=1, source_target_pairs={{0,8},{8,0},{16,24},{24,16},{1,9},{9,1},{17,25},{25,17},{2,10},{10... | collective-permute-start | bytes 983048 | tf_op jit(solution)/shard_map/ppermute | solution.py:251
  14.8 14.9 %copy-start = (f32[640,256]{1,0:T(8,128)S(1)}, f32[640,256]{1,0:T(8,128)}, u32[]{:S(2)}) copy-start(f32[640,256]{1,0:T(8,128)} %refs_5_.1) | copy-start | bytes 1966084
  14.8 14.9 %copy-start.1 = (f32[640,256]{1,0:T(8,128)S(1)}, f32[640,256]{1,0:T(8,128)}, u32[]{:S(2)}) copy-start(f32[640,256]{1,0:T(8,128)} %refs_6_.1) | copy-start | bytes 1966084
  15.5 9.5 %collective-permute-start.7 = (bf16[88,256]{1,0:T(8,128)(2,1)S(1)}, bf16[88,256]{1,0:T(8,128)(2,1)S(1)}, u32[]{:S(2)}, u32[]{:S(2)}) collective-permute-start(bf16[88,256]{1,0:T(8,128)(2,1)S(1)} %get-tuple-element.49), channel_id=1, source_target_pairs={{0,4},{1,5},{2,6},{3,7},{4,0},{5,1},{6,2},{7,3},{8,12},{9,13},{10,... | collective-permute-start | bytes 135176 | tf_op jit(solution)/shard_map/ppermute | solution.py:251
  18.4 7.2 %collective-permute-start.8 = (bf16[88,256]{1,0:T(8,128)(2,1)S(1)}, bf16[88,256]{1,0:T(8,128)(2,1)S(1)}, u32[]{:S(2)}, u32[]{:S(2)}) collective-permute-start(bf16[88,256]{1,0:T(8,128)(2,1)S(1)} %get-tuple-element.50), channel_id=1, source_target_pairs={{0,6},{1,7},{2,4},{3,5},{4,2},{5,3},{6,0},{7,1},{8,14},{9,15},{10,... | collective-permute-start | bytes 135176 | tf_op jit(solution)/shard_map/ppermute | solution.py:251
  19.7 8.2 %collective-permute-start.9 = (bf16[88,256]{1,0:T(8,128)(2,1)S(1)}, bf16[88,256]{1,0:T(8,128)(2,1)S(1)}, u32[]{:S(2)}, u32[]{:S(2)}) collective-permute-start(bf16[88,256]{1,0:T(8,128)(2,1)S(1)} %get-tuple-element.51), channel_id=1, source_target_pairs={{0,5},{1,4},{2,7},{3,6},{4,1},{5,0},{6,3},{7,2},{8,13},{9,12},{10,... | collective-permute-start | bytes 135176 | tf_op jit(solution)/shard_map/ppermute | solution.py:251
  22.3 6.9 %collective-permute-start.10 = (bf16[88,256]{1,0:T(8,128)(2,1)S(1)}, bf16[88,256]{1,0:T(8,128)(2,1)S(1)}, u32[]{:S(2)}, u32[]{:S(2)}) collective-permute-start(bf16[88,256]{1,0:T(8,128)(2,1)S(1)} %get-tuple-element.52), channel_id=1, source_target_pairs={{0,7},{1,6},{2,5},{3,4},{4,3},{5,2},{6,1},{7,0},{8,15},{9,14},{10,... | collective-permute-start | bytes 135176 | tf_op jit(solution)/shard_map/ppermute | solution.py:251
  23.2 6.1 %collective-permute-start.11 = (bf16[88,256]{1,0:T(8,128)(2,1)S(1)}, bf16[88,256]{1,0:T(8,128)(2,1)S(1)}, u32[]{:S(2)}, u32[]{:S(2)}) collective-permute-start(bf16[88,256]{1,0:T(8,128)(2,1)S(1)} %get-tuple-element.53), channel_id=1, source_target_pairs={{0,3},{1,2},{2,1},{3,0},{4,7},{5,6},{6,5},{7,4},{8,11},{9,10},{10,... | collective-permute-start | bytes 135176 | tf_op jit(solution)/shard_map/ppermute | solution.py:251
  25.0 4.6 %collective-permute-start.12 = (bf16[88,256]{1,0:T(8,128)(2,1)S(1)}, bf16[88,256]{1,0:T(8,128)(2,1)S(1)}, u32[]{:S(2)}, u32[]{:S(2)}) collective-permute-start(bf16[88,256]{1,0:T(8,128)(2,1)S(1)} %get-tuple-element.54), channel_id=1, source_target_pairs={{0,1},{1,0},{2,3},{3,2},{4,5},{5,4},{6,7},{7,6},{8,9},{9,8},{10,11... | collective-permute-start | bytes 135176 | tf_op jit(solution)/shard_map/ppermute | solution.py:251
  25.6 4.1 %collective-permute-start.13 = (bf16[88,256]{1,0:T(8,128)(2,1)S(1)}, bf16[88,256]{1,0:T(8,128)(2,1)S(1)}, u32[]{:S(2)}, u32[]{:S(2)}) collective-permute-start(bf16[88,256]{1,0:T(8,128)(2,1)S(1)} %get-tuple-element.55), channel_id=1, source_target_pairs={{0,2},{1,3},{2,0},{3,1},{4,6},{5,7},{6,4},{7,5},{8,10},{9,11},{10,... | collective-permute-start | bytes 135176 | tf_op jit(solution)/shard_map/ppermute | solution.py:251

commit v8 on v7

--- a/solution.py
+++ b/solution.py
@@ -14,6 +14,7 @@
 LANES = 128
 TAIL = 8
 ROW_CODES = 1 << 16
+ROUNDS = ((4, 5), (6, 7), (1, 2), (0, 3))
 MIB = 1 << 20
 NT = (((1,), (1,)), ((), ()))
 TN = (((0,), (0,)), ((), ()))
@@ -48,9 +49,9 @@
     )
 
 
-def local_kernel(groups, slots, code_ref, pick_ref, tail_ref):
+def local_kernel(groups, slots, flip, code_ref, pick_ref, tail_ref):
     block = code_ref.shape[1]
-    owner = code_ref[...] // ROW_CODES
+    owner = (code_ref[...] // ROW_CODES) ^ flip
     offset = code_ref[...] % ROW_CODES
     member = lax.broadcasted_iota(jnp.int32, (groups, block), 0) == owner
     before = lax.broadcasted_iota(jnp.int32, (block, block), 0) < lax.broadcasted_iota(
@@ -64,7 +65,10 @@
     for g in range(groups):
         pick = (here & (owner == g)).astype(F32).astype(BF16)
         pick_ref[g * slots : (g + 1) * slots] = pick[:slots]
-        tail_ref[g] = jnp.concatenate([dot(high, pick, NT), dot(low, pick, NT)], axis=1).astype(BF16)
+        if g < tail_ref.shape[0]:
+            tail_ref[g] = jnp.concatenate(
+                [dot(high, pick, NT), dot(low, pick, NT)], axis=1
+            ).astype(BF16)
 
 
 def fill_logits(q, item_refs, out_ref):
@@ -170,19 +174,52 @@
     out_ref[...] = total * SCALE
 
 
-def pack_kernel(groups, slots, pick_ref, tail_ref, mine_ref, other_ref, *out_refs):
+def split(x):
+    high = x.astype(BF16)
+    return jnp.concatenate([high, (x - high.astype(F32)).astype(BF16)], axis=1)
+
+
+def give_kernel(pick_ref, mate_pick_ref, mine_ref, mate_ref, out_ref):
+    half = pick_ref.shape[0] // 2
+    for here, (pick, value) in enumerate(((pick_ref, mine_ref), (mate_pick_ref, mate_ref))):
+        values = code(value[...] * SCALE).astype(BF16)
+        out_ref[here * half : (here + 1) * half] = dot(pick[half:], values).astype(BF16)
+
+
+def keep_kernel(pick_ref, mate_pick_ref, mine_ref, mate_ref, out_ref):
+    half = pick_ref.shape[0] // 2
+    for here, (pick, value) in enumerate(((pick_ref, mine_ref), (mate_pick_ref, mate_ref))):
+        both = dot(pick[:half], split(value[...] * SCALE))
+        out_ref[here * half : (here + 1) * half] = both[:, :D] + both[:, D:]
+
+
+def pack_kernel(slots, keep_ref, given_ref, tail_ref, mate_tail_ref, *out_refs):
+    half = keep_ref.shape[0] // 2
+    tails = (tail_ref, mate_tail_ref)
+    for p, out in enumerate(out_refs):
+        for here in range(2):
+            start = here * half + p * slots
+            other = (1 - here) * half + p * slots
+            given = decode(given_ref[other : other + slots].astype(F32))
+            out[here, :slots] = code(keep_ref[start : start + slots] + given).astype(BF16)
+            out[here, slots:] = tails[here][p]
+
+
+def plain_pack_kernel(groups, slots, pick_ref, tail_ref, mine_ref, other_ref, out_ref):
     grad = code((mine_ref[...] + other_ref[...]) * SCALE).astype(BF16)
     picked = dot(pick_ref[...], grad).astype(BF16)
     for g in range(groups):
-        out = out_refs[g] if len(out_refs) == groups else out_refs[0].at[g]
-        out[:slots] = picked[g * slots : (g + 1) * slots]
-        out[slots:] = tail_ref[g]
-
-
-def unpack(slots, got_refs, values_ref, ids_ref):
-    packets = got_refs
-    if len(got_refs[0].shape) == 3:
-        packets = [got_refs[0].at[g] for g in range(got_refs[0].shape[0])]
+        out_ref[g, :slots] = picked[g * slots : (g + 1) * slots]
+        out_ref[g, slots:] = tail_ref[g]
+
+
+def unpack(slots, paired, got_refs, values_ref, ids_ref):
+    packets = []
+    for ref in got_refs:
+        if len(ref.shape) == 2:
+            packets.append(ref)
+        else:
+            packets += [ref.at[g] for g in range(1 if paired else ref.shape[0])]
     half = len(packets) * slots
     for g, got in enumerate(packets):
         tail = got[slots : slots + TAIL].astype(F32)
@@ -201,16 +238,17 @@
     return dot(jnp.concatenate([put, put], axis=1), values_ref[...])
 
 
-def first_kernel(slots, *refs):
-    got_refs, (out_ref, values_ref, ids_ref) = refs[:-3], refs[-3:]
-    unpack(slots, got_refs, values_ref, ids_ref)
-    out_ref[...] = scatter(values_ref, ids_ref, 0, out_ref.shape[0])
+def first_kernel(slots, partial, *refs):
+    inputs, (out_ref, values_ref, ids_ref) = refs[:-3], refs[-3:]
+    unpack(slots, True, inputs[partial:], values_ref, ids_ref)
+    sums = scatter(values_ref, ids_ref, 0, out_ref.shape[0])
+    out_ref[...] = sums + inputs[0][...] if partial else sums
 
 
 def update_kernel(slots, partial, *refs):
     inputs, refs = refs[:-8], refs[-8:]
     table_ref, accum_ref, table_out, accum_out, values_ref, ids_ref, new_ref, sems = refs
-    unpack(slots, inputs[1:] if partial else inputs, values_ref, ids_ref)
+    unpack(slots, partial, inputs[1:] if partial else inputs, values_ref, ids_ref)
     chunks = sems.shape[1]
     rows = table_ref.shape[0] // chunks
     copies = []
@@ -245,7 +283,7 @@
     n, groups = lax.axis_size("wide"), lax.axis_size("group")
     capacity = 2 * block // groups
     slots = -(-capacity // TAIL) * TAIL
-    paired = groups <= 8
+    paired = groups == 2 * len(ROUNDS)
 
     def swap(x, k, axis="wide"):
         return lax.ppermute(x, axis, [(i, i ^ k) for i in range(lax.axis_size(axis))])
@@ -256,15 +294,34 @@
 
     owner = item_owner.reshape(1, block)
     if paired:
-        owner = owner ^ lax.axis_index("group")
-    pick, tail = call(
-        functools.partial(local_kernel, groups, slots),
-        [((groups * slots, block), BF16), ((groups, TAIL, D), BF16)],
-        owner * ROW_CODES + item_offset.reshape(1, block),
-        flops=1 << 30,
-    )
-    far_items, far_counts, tail = lax.optimization_barrier((far_items, far_counts, tail))
-    item_blocks = [items, swap(items, 1)] + far_items
+        partner = owner ^ lax.axis_index("group")
+        owner = jnp.zeros_like(partner)
+        for core in range(2):
+            for k in range(len(ROUNDS)):
+                place = core * len(ROUNDS) + k
+                owner = jnp.where(partner == ROUNDS[k][core], place, owner)
+        owner = owner ^ (lax.axis_index("wide") % 2 * len(ROUNDS))
+    codes = owner * ROW_CODES + item_offset.reshape(1, block)
+
+    def route(codes, flip, flops):
+        return call(
+            functools.partial(local_kernel, groups, slots, flip),
+            [
+                ((groups * slots, block), BF16),
+                ((len(ROUNDS) if paired else groups, TAIL, D), BF16),
+            ],
+            codes,
+            flops=flops,
+        )
+
+    pick, tail = route(codes, 0, 0)
+    tails, own_items = [tail], items
+    if paired:
+        mate_codes, own_items = lax.optimization_barrier((swap(codes, 1), items))
+        mate_pick, mate_tail = route(mate_codes, len(ROUNDS), 1 << 30)
+        tails.append(mate_tail)
+    far_items, far_counts, tails = lax.optimization_barrier((far_items, far_counts, tails))
+    item_blocks = [items, swap(own_items, 1)] + far_items
     early = len(item_blocks)
     item_blocks += [swap(x, 1) for x in far_items]
     late = n - early
@@ -313,32 +370,67 @@
             scratch=[pltpu.VMEM((n, *square), F32)],
             limit=8 + 4 * n,
         )
-    other = swap(mate, 1)
-    (query_grad,) = call(
-        functools.partial(query_kernel, early, late),
-        [part],
-        powers,
-        late_powers,
-        factors,
-        *item_blocks,
-        limit=8 + 2 * n,
-        flops=1 << 30,
-    )
-    other, query_grad = lax.optimization_barrier((other, query_grad))
     if paired:
-        packets = [((slots + TAIL, D), BF16)] * groups
+        parts = [((groups * slots, D), BF16)]
+        (give,) = call(give_kernel, parts, pick, mate_pick, mine, mate)
+        given = swap(give, 1)
+        (query_grad,) = call(
+            functools.partial(query_kernel, early, late),
+            [part],
+            powers,
+            late_powers,
+            factors,
+            *item_blocks,
+            limit=8 + 2 * n,
+            flops=1 << 30,
+        )
+        given, query_grad = lax.optimization_barrier((given, query_grad))
+        (keep,) = call(
+            keep_kernel,
+            [((groups * slots, D), F32)],
+            pick,
+            mate_pick,
+            mine,
+            mate,
+            flops=1 << 29,
+        )
+        packed = call(
+            functools.partial(pack_kernel, slots),
+            [((2, slots + TAIL, D), BF16)] * len(ROUNDS),
+            keep,
+            given,
+            *tails,
+        )
+        got = []
+        for partners, packet in zip(ROUNDS, packed):
+            pairs = [
+                (w * groups + g, w * groups + (g ^ partners[w % 2]))
+                for w in range(n)
+                for g in range(groups)
+            ]
+            got.append(lax.ppermute(packet, ("wide", "group"), pairs))
+        forwarded = [swap(x[1], 1) for x in got]
     else:
-        packets = [((groups, slots + TAIL, D), BF16)]
-    packed = call(
-        functools.partial(pack_kernel, groups, slots), packets, pick, tail, mine, other
-    )
-    if paired:
-        half = groups // 2
-        far = sorted(range(half, groups), key=lambda k: (k % 2, k))
-        order = far + sorted(range(1, half), key=lambda k: (1 - k % 2, -k))
-        got = [packed[0]] + [swap(packed[k], k, "group") for k in order]
-    else:
-        got = [lax.all_to_all(packed[0], "group", split_axis=0, concat_axis=0, tiled=True)]
+        (query_grad,) = call(
+            functools.partial(query_kernel, early, late),
+            [part],
+            powers,
+            late_powers,
+            factors,
+            *item_blocks,
+            limit=8 + 2 * n,
+            flops=1 << 30,
+        )
+        (packed,) = call(
+            functools.partial(plain_pack_kernel, groups, slots),
+            [((groups, slots + TAIL, D), BF16)],
+            pick,
+            *tails,
+            mine,
+            swap(mate, 1),
+        )
+        got = [lax.all_to_all(packed, "group", split_axis=0, concat_axis=0, tiled=True)]
+
     rows = table.shape[0]
 
     def scratch(packets):
@@ -347,17 +439,18 @@
             pltpu.VMEM((TAIL, packets * slots), F32),
         ]
 
-    count = groups // 2
     before = []
     if paired:
-        before = call(
-            functools.partial(first_kernel, slots),
-            [((rows, D), F32)],
-            *got[:count],
-            scratch=scratch(count),
-            flops=1 << 28,
-        )
-        got = got[count:]
+        for pair in (got[:2], got[2:]):
+            before = call(
+                functools.partial(first_kernel, slots, len(before)),
+                [((rows, D), F32)],
+                *before,
+                *pair,
+                scratch=scratch(2),
+                flops=1 << 28,
+            )
+        got = forwarded
     table_new, accum_new = pl.pallas_call(
         functools.partial(update_kernel, slots, paired),
         out_shape=[jax.ShapeDtypeStruct(table.shape, F32)] * 2,

time: 31.5 us -> 32 us (1.016)
  Pallas kernels: 7.56 us -> 9.08 us
  starting transfers between devices: 16.8 us -> 16.1 us
  waiting for transfers between devices: 4.79 us -> 4.36 us
    ppermute x14 -> x12, starting transfers between devices: 16.8 us -> 9.74 us  [swap(): lax.ppermute(x, axis, [(i, i ^ k) for i in range(lax.axis_size(axis))])]
    ppermute x0 -> x4, starting transfers between devices: none -> 6.34 us  [shards(): got.append(lax.ppermute(packet, ('wide', 'group'), pairs))]
    ppermute x14 -> x12, waiting for transfers between devices: 4.79 us -> 2.08 us  [swap(): lax.ppermute(x, axis, [(i, i ^ k) for i in range(lax.axis_size(axis))])]
    ppermute x0 -> x4, waiting for transfers between devices: none -> 2.28 us  [shards(): got.append(lax.ppermute(packet, ('wide', 'group'), pairs))]
    pallas_call x7 -> x11, Pallas kernels: 5.9 us -> 7.41 us  [call(): pl.pallas_call(kernel, out_shape=[jax.ShapeDtypeStruct(s, t) for s, t in...]
  transfers between devices with their start and end apart: 14 -> 16, of which waited for: 7 -> 5; matrix products, arithmetic and copies ran while one was open for 5% -> 5% of each run, Pallas kernels for 12% -> 15%
where the time goes in v8:
time: 32 us; the launch traced here: 31.9 us
  starting transfers between devices  16.1 us (50%)
  Pallas kernels  9.08 us (28%)
  waiting for transfers between devices  4.36 us (14%)
  other arithmetic  1.47 us (5%)
  between operations  0.81 us (3%)
    ppermute x12, starting transfers between devices, swap(): lax.ppermute(x, axis, [(i, i ^ k) for i in range(lax.axis_size(axis))])  9.74 us
    pallas_call x11, Pallas kernels, call(): pl.pallas_call(kernel, out_shape=[jax.ShapeDtypeStruct(s, t) for s, t in...  7.41 us
    ppermute x4, starting transfers between devices, shards(): got.append(lax.ppermute(packet, ('wide', 'group'), pairs))  6.34 us
    ppermute x4, waiting for transfers between devices, shards(): got.append(lax.ppermute(packet, ('wide', 'group'), pairs))  2.28 us
    ppermute x12, waiting for transfers between devices, swap(): lax.ppermute(x, axis, [(i, i ^ k) for i in range(lax.axis_size(axis))])  2.08 us
    pallas_call x1, Pallas kernels, shards(): pl.pallas_call(functools.partial(update_kernel, slots, paired), out_shape...  1.67 us
    mul x1, other arithmetic, shards(): codes = owner * ROW_CODES + item_offset.reshape(1, block)  0.71 us
    add x1, other arithmetic, shards(): codes = owner * ROW_CODES + item_offset.reshape(1, block)  0.68 us
  transfers between devices with their start and end apart: 16, of which 5 were waited for; matrix products, arithmetic and copies ran while one was open for 5% of the time, Pallas kernels for 15%

profile of v8, /device:TPU:0, one launch (start us, length us, event | category | flops | bytes accessed | tf_op | source)
XLA Modules:
  0.0 31.9 jit_solution(734642410327515014)
XLA Ops:
  0.6 3.0 %collective-permute-start.3 = (bf16[320,256]{1,0:T(8,128)(2,1)}, bf16[320,256]{1,0:T(8,128)(2,1)S(1)}, u32[]{:S(2)}, u32[]{:S(2)}) collective-permute-start(bf16[320,256]{1,0:T(8,128)(2,1)} %refs_0_.5), channel_id=1, source_target_pairs={{0,16},{8,24},{16,0},{24,8},{1,17},{9,25},{17,1},{25,9},{2,18},{10... | collective-permute-start | bytes 491528 | tf_op jit(solution)/shard_map/ppermute | solution.py:289
  3.7 0.7 %fusion.2 = s32[320]{0:T(512)S(1)} fusion(s32[320,1]{0,1:T(1,128)} %param.9, s32[]{:T(128)S(6)} %mul.10, s32[]{:T(128)S(6)} %axis_index.22), kind=kLoop, calls=%fused_computation.14 | loop fusion | flops 5440 | bytes 2568 | tf_op jit(solution)/shard_map/mul | solution.py:304
  4.4 0.7 %add.10 = s32[320]{0:T(512)S(1)} add(s32[320]{0:T(512)S(1)} %fusion.2, s32[320]{0:T(512)} %param.10) | non-fusion elementwise | flops 320 | bytes 3840 | tf_op jit(solution)/shard_map/add | solution.py:304
  5.1 0.0 collective-permute-start.1
  5.1 0.0 collective-permute-start.4
  5.1 2.0 %collective-permute-start = (bf16[320,256]{1,0:T(8,128)(2,1)}, bf16[320,256]{1,0:T(8,128)(2,1)S(1)}, u32[]{:S(2)}, u32[]{:S(2)}) collective-permute-start(bf16[320,256]{1,0:T(8,128)(2,1)} %refs_0_.4), channel_id=1, source_target_pairs={{0,16},{8,24},{16,0},{24,8},{1,17},{9,25},{17,1},{25,9},{2,18},{10... | collective-permute-start | bytes 491528 | tf_op jit(solution)/shard_map/ppermute | solution.py:289
  7.1 0.5 %shard_map.102 = (bf16[640,320]{1,0:T(8,128)(2,1)S(1)}, bf16[4,8,256]{2,1,0:T(8,128)(2,1)S(1)}) custom-call(s32[1,320]{1,0:T(1,128)S(1)} %add.11.code_ref), custom_call_target="tpu_custom_call" | custom-call | bytes 1024 | tf_op jit(solution)/shard_map/pallas_call | solution.py:272
  7.6 0.0 collective-permute-done.1.code_ref
  7.7 0.1 collective-permute-start.2
  7.8 0.5 %shard_map.103 = (bf16[640,320]{1,0:T(8,128)(2,1)S(1)}, bf16[4,8,256]{2,1,0:T(8,128)(2,1)S(1)}) custom-call(s32[1,320]{1,0:T(1,128)S(1)} %collective-permute-done.1.code_ref), custom_call_target="tpu_custom_call" | custom-call | flops 1073741824 | bytes 1024 | tf_op jit(solution)/shard_map/pallas_call | solution.py:272
  8.3 0.6 %collective-permute-done.4 = s32[320]{0:T(512)S(1)} collective-permute-done((s32[320]{0:T(512)}, s32[320]{0:T(512)S(1)}, u32[]{:S(2)}, u32[]{:S(2)}) %collective-permute-start.4) | collective-permute-done | bytes 1312 | tf_op jit(solution)/shard_map/ppermute | solution.py:289
  8.9 0.0 collective-permute-done.3.refs_2_.refs_4_
  8.9 0.0 collective-permute-start.5
  8.9 0.1 pad_add_fusion
  8.9 0.5 %collective-permute-start.6 = (s32[640]{0:T(1024)S(1)}, s32[640]{0:T(1024)S(1)}, u32[]{:S(2)}, u32[]{:S(2)}) collective-permute-start(s32[640]{0:T(1024)S(1)} %pad_add_fusion), channel_id=1, source_target_pairs={{0,8},{8,0},{16,24},{24,16},{1,9},{9,1},{17,25},{25,17},{2,10},{10... | collective-permute-start | bytes 7688 | tf_op jit(solution)/shard_map/ppermute | solution.py:289
  9.5 0.0 collective-permute-done.2.refs_1_.refs_3_
  9.5 0.6 %shard_map.104 = (f32[3,320,320]{2,1,0:T(8,128)S(1)}, f32[8,320]{1,0:T(8,128)S(1)}) custom-call(bf16[320,256]{1,0:T(8,128)(2,1)S(1)} %copy-done.2, bf16[320,256]{1,0:T(8,128)(2,1)S(1)} %copy-done.3, bf16[320,256]{1,0:T(8,128)(2,1)S(1)} %collective-permute-done.2.refs_1_.refs_3_, bf16[320,256]{1,0:T(8,128)(2,1)S(1)} %collective-permute-done.3.refs_2_.refs_4_), custom_call_target="tpu_custom_call" | custom-call | flops 536870912 | bytes 1024 | tf_op jit(solution)/shard_map/pallas_call | solution.py:272
  10.1 0.2 collective-permute-done.6
  10.3 0.4 %shard_map.105 = (f32[4,320,128]{2,1,0:T(8,128)S(1)}, f32[3,320,320]{2,1,0:T(8,128)S(1)}, f32[8,320]{1,0:T(8,128)S(1)}) custom-call(f32[3,320,320]{2,1,0:T(8,128)S(1)} %get-tuple-element.37.e_ref, s32[1,640]{1,0:T(1,128)S(1)} %reshape.56.near_ref, s32[1,640]{1,0:T(1,128)S(1)} %reshape.57.mate_ref), custom_call_target="tpu_custom_call" | custom-call | bytes 1024 | tf_op jit(solution)/shard_map/pallas_call | solution.py:272
  10.7 1.3 %collective-permute-done.refs_1_ = bf16[320,256]{1,0:T(8,128)(2,1)S(1)} collective-permute-done((bf16[320,256]{1,0:T(8,128)(2,1)}, bf16[320,256]{1,0:T(8,128)(2,1)S(1)}, u32[]{:S(2)}, u32[]{:S(2)}) %collective-permute-start) | collective-permute-done | bytes 163872 | tf_op jit(solution)/shard_map/ppermute | solution.py:289
  11.9 0.0 collective-permute-done.5.refs_5_.refs_3_
  11.9 1.8 %shard_map.106 = (f32[320,256]{1,0:T(8,128)S(1)}, f32[320,256]{1,0:T(8,128)S(1)}, f32[320]{0:T(512)}, f32[1,320,320]{2,1,0:T(8,128)S(1)}, f32[8,320]{1,0:T(8,128)S(1)}) custom-call(bf16[320,256]{1,0:T(8,128)(2,1)S(1)} %copy-done.2, bf16[320,256]{1,0:T(8,128)(2,1)S(1)} %collective-permute-done.refs_1_, bf16[320,256]{1,0:T(8,128)(2,1)S(1)} %copy-done.3, ...), custom_call_target="tpu_custom_call" | custom-call | bytes 1024 | tf_op jit(solution)/shard_map/pallas_call | solution.py:272
  13.8 0.4 %shard_map.107 = bf16[640,256]{1,0:T(8,128)(2,1)S(1)} custom-call(bf16[640,320]{1,0:T(8,128)(2,1)S(1)} %get-tuple-element.44.pick_ref, bf16[640,320]{1,0:T(8,128)(2,1)S(1)} %get-tuple-element.45.mate_pick_ref, f32[320,256]{1,0:T(8,128)S(1)} %get-tuple-element.46.mine_ref, f32[320,256]{1,0:T(8,128)S(1)} %get-tuple-element.47.mate_ref), custom_call_target="tpu_custom_call" | custom-call | bytes 1024 | tf_op jit(solution)/shard_map/pallas_call | solution.py:272
  14.2 0.1 collective-permute-start.7
  14.3 0.5 %shard_map.109.keep_ref = f32[640,256]{1,0:T(8,128)S(1)} custom-call(bf16[640,320]{1,0:T(8,128)(2,1)S(1)} %get-tuple-element.44.pick_ref, bf16[640,320]{1,0:T(8,128)(2,1)S(1)} %get-tuple-element.45.mate_pick_ref, f32[320,256]{1,0:T(8,128)S(1)} %get-tuple-element.46.mine_ref, f32[320,256]{1,0:T(8,128)S(1)} %get-tuple-element.47.mate_ref), custom_call_target="tpu_custom_call" | custom-call | flops 536870912 | bytes 1024 | tf_op jit(solution)/shard_map/pallas_call | solution.py:272
  14.8 1.3 %shard_map.108 = f32[320,256]{1,0:T(8,128)} custom-call(f32[3,320,320]{2,1,0:T(8,128)S(1)} %get-tuple-element.40.refs_7_.e_ref, f32[1,320,320]{2,1,0:T(8,128)S(1)} %get-tuple-element.48.late_ref, f32[8,320]{1,0:T(8,128)S(1)} %get-tuple-element.49.factor_ref, bf16[320,256]{1,0:T(8,128)(2,1)S(1)} %copy-done.3, ...), custom_call_target="tpu_custom_call" | custom-call | flops 1073741824 | bytes 1024 | tf_op jit(solution)/shard_map/pallas_call | solution.py:272
  16.1 0.0 collective-permute-done.7.given_ref
  16.1 0.3 shard_map.110
  16.4 0.0 copy-start
  16.4 0.0 copy-start.1
  16.5 2.8 %collective-permute-start.8 = (bf16[2,88,256]{2,1,0:T(8,128)(2,1)S(1)}, bf16[2,88,256]{2,1,0:T(8,128)(2,1)S(1)}, u32[]{:S(2)}, u32[]{:S(2)}) collective-permute-start(bf16[2,88,256]{2,1,0:T(8,128)(2,1)S(1)} %get-tuple-element.54), channel_id=1, source_target_pairs={{0,4},{1,5},{2,6},{3,7},{4,0},{5,1},{6,2},{7,3},{8,13},{9,12},{10,... | collective-permute-start | bytes 270344 | tf_op jit(solution)/shard_map/ppermute | solution.py:411
  19.3 1.3 %collective-permute-start.9 = (bf16[2,88,256]{2,1,0:T(8,128)(2,1)S(1)}, bf16[2,88,256]{2,1,0:T(8,128)(2,1)S(1)}, u32[]{:S(2)}, u32[]{:S(2)}) collective-permute-start(bf16[2,88,256]{2,1,0:T(8,128)(2,1)S(1)} %get-tuple-element.55), channel_id=1, source_target_pairs={{0,6},{1,7},{2,4},{3,5},{4,2},{5,3},{6,0},{7,1},{8,15},{9,14},{10,... | collective-permute-start | bytes 270344 | tf_op jit(solution)/shard_map/ppermute | solution.py:411
  20.6 1.5 %collective-permute-start.10 = (bf16[2,88,256]{2,1,0:T(8,128)(2,1)S(1)}, bf16[2,88,256]{2,1,0:T(8,128)(2,1)S(1)}, u32[]{:S(2)}, u32[]{:S(2)}) collective-permute-start(bf16[2,88,256]{2,1,0:T(8,128)(2,1)S(1)} %get-tuple-element.56), channel_id=1, source_target_pairs={{0,1},{1,0},{2,3},{3,2},{4,5},{5,4},{6,7},{7,6},{8,10},{9,11},{10,... | collective-permute-start | bytes 270344 | tf_op jit(solution)/shard_map/ppermute | solution.py:411
  22.1 0.7 %collective-permute-start.11 = (bf16[2,88,256]{2,1,0:T(8,128)(2,1)S(1)}, bf16[2,88,256]{2,1,0:T(8,128)(2,1)S(1)}, u32[]{:S(2)}, u32[]{:S(2)}) collective-permute-start(bf16[2,88,256]{2,1,0:T(8,128)(2,1)S(1)} %get-tuple-element.57), channel_id=1, source_target_pairs={{0,0},{1,1},{2,2},{3,3},{4,4},{5,5},{6,6},{7,7},{8,11},{9,10},{10,... | collective-permute-start | bytes 270344 | tf_op jit(solution)/shard_map/ppermute | solution.py:411
  22.8 1.5 %collective-permute-done.8.refs_0_ = bf16[2,88,256]{2,1,0:T(8,128)(2,1)S(1)} collective-permute-done((bf16[2,88,256]{2,1,0:T(8,128)(2,1)S(1)}, bf16[2,88,256]{2,1,0:T(8,128)(2,1)S(1)}, u32[]{:S(2)}, u32[]{:S(2)}) %collective-permute-start.8) | collective-permute-done | bytes 90144 | tf_op jit(solution)/shard_map/ppermute | solution.py:411
  24.4 1.5 %collective-permute-start.12 = (bf16[88,256]{1,0:T(8,128)(2,1)S(1)}, bf16[88,256]{1,0:T(8,128)(2,1)S(1)}, u32[]{:S(2)}, u32[]{:S(2)}) collective-permute-start(bf16[88,256]{1,0:T(8,128)(2,1)S(1)} %slice_bitcast_fusion.3), channel_id=1, source_target_pairs={{0,8},{8,0},{16,24},{24,16},{1,9},{9,1},{17,25},{25,17},{2,10},{10... | collective-permute-start | bytes 135176 | tf_op jit(solution)/shard_map/ppermute | solution.py:289
  25.9 0.7 %collective-permute-done.9.refs_1_ = bf16[2,88,256]{2,1,0:T(8,128)(2,1)S(1)} collective-permute-done((bf16[2,88,256]{2,1,0:T(8,128)(2,1)S(1)}, bf16[2,88,256]{2,1,0:T(8,128)(2,1)S(1)}, u32[]{:S(2)}, u32[]{:S(2)}) %collective-permute-start.9) | collective-permute-done | bytes 90144 | tf_op jit(solution)/shard_map/ppermute | solution.py:411
  26.6 0.9 %collective-permute-start.13 = (bf16[88,256]{1,0:T(8,128)(2,1)S(1)}, bf16[88,256]{1,0:T(8,128)(2,1)S(1)}, u32[]{:S(2)}, u32[]{:S(2)}) collective-permute-start(bf16[88,256]{1,0:T(8,128)(2,1)S(1)} %slice_bitcast_fusion.2), channel_id=1, source_target_pairs={{0,8},{8,0},{16,24},{24,16},{1,9},{9,1},{17,25},{25,17},{2,10},{10... | collective-permute-start | bytes 135176 | tf_op jit(solution)/shard_map/ppermute | solution.py:289
  27.5 0.0 collective-permute-done.10.refs_1_
  27.5 0.1 collective-permute-start.14
  27.6 0.0 collective-permute-done.11.refs_2_
  27.6 1.5 %collective-permute-start.15 = (bf16[88,256]{1,0:T(8,128)(2,1)S(1)}, bf16[88,256]{1,0:T(8,128)(2,1)S(1)}, u32[]{:S(2)}, u32[]{:S(2)}) collective-permute-start(bf16[88,256]{1,0:T(8,128)(2,1)S(1)} %slice_bitcast_fusion), channel_id=1, source_target_pairs={{0,8},{8,0},{16,24},{24,16},{1,9},{9,1},{17,25},{25,17},{2,10},{10... | collective-permute-start | bytes 135176 | tf_op jit(solution)/shard_map/ppermute | solution.py:289
  29.1 0.5 %shard_map.111.refs_0_ = f32[640,256]{1,0:T(8,128)S(1)} custom-call(bf16[2,88,256]{2,1,0:T(8,128)(2,1)S(1)} %collective-permute-done.8.refs_0_, bf16[2,88,256]{2,1,0:T(8,128)(2,1)S(1)} %collective-permute-done.9.refs_1_), custom_call_target="tpu_custom_call" | custom-call | flops 268435456 | bytes 1024 | tf_op jit(solution)/shard_map/pallas_call | solution.py:272
  29.6 0.5 %shard_map.112.refs_0_ = f32[640,256]{1,0:T(8,128)S(1)} custom-call(f32[640,256]{1,0:T(8,128)S(1)} %shard_map.111.refs_0_, bf16[2,88,256]{2,1,0:T(8,128)(2,1)S(1)} %collective-permute-done.10.refs_1_, bf16[2,88,256]{2,1,0:T(8,128)(2,1)S(1)} %collective-permute-done.11.refs_2_), custom_call_target="tpu_custom_call" | custom-call | flops 268435456 | bytes 1024 | tf_op jit(solution)/shard_map/pallas_call | solution.py:272
  30.1 0.0 collective-permute-done.12.refs_1_
  30.1 0.0 collective-permute-done.14.refs_3_
  30.2 0.0 collective-permute-done.15.refs_4_
  30.2 1.7 %shard_map.113 = (f32[640,256]{1,0:T(8,128)}, f32[640,256]{1,0:T(8,128)}) custom-call(f32[640,256]{1,0:T(8,128)S(1)} %shard_map.112.refs_0_, bf16[88,256]{1,0:T(8,128)(2,1)S(1)} %collective-permute-done.12.refs_1_, bf16[88,256]{1,0:T(8,128)(2,1)S(1)} %collective-permute-done.13.refs_2_, bf16[88,256]{1,0:T(8,128)(2,1)S(1)} %collective-permute-done.14.refs_3_, ...), custom_call_target="tpu_custom_call" | custom-call | tf_op jit(solution)/shard_map/pallas_call | solution.py:454
  (16 shorter events, 0.0 us)
Async XLA Ops:
  0.6 8.2 %collective-permute-start.3 = (bf16[320,256]{1,0:T(8,128)(2,1)}, bf16[320,256]{1,0:T(8,128)(2,1)S(1)}, u32[]{:S(2)}, u32[]{:S(2)}) collective-permute-start(bf16[320,256]{1,0:T(8,128)(2,1)} %refs_0_.5), channel_id=1, source_target_pairs={{0,16},{8,24},{16,0},{24,8},{1,17},{9,25},{17,1},{25,9},{2,18},{10... | collective-permute-start | bytes 491528 | tf_op jit(solution)/shard_map/ppermute | solution.py:289
  5.1 2.6 %collective-permute-start.1 = (s32[1,320]{1,0:T(1,128)S(1)}, s32[1,320]{1,0:T(1,128)S(1)}, u32[]{:S(2)}, u32[]{:S(2)}) collective-permute-start(s32[1,320]{1,0:T(1,128)S(1)} %add.11.code_ref), channel_id=1, source_target_pairs={{0,8},{8,0},{16,24},{24,16},{1,9},{9,1},{17,25},{25,17},{2,10},{10... | collective-permute-start | bytes 3848 | tf_op jit(solution)/shard_map/ppermute | solution.py:289
  5.1 3.8 %collective-permute-start.4 = (s32[320]{0:T(512)}, s32[320]{0:T(512)S(1)}, u32[]{:S(2)}, u32[]{:S(2)}) collective-permute-start(s32[320]{0:T(512)} %param.11), channel_id=1, source_target_pairs={{0,16},{8,24},{16,0},{24,8},{1,17},{9,25},{17,1},{25,9},{2,18},{10... | collective-permute-start | bytes 3848 | tf_op jit(solution)/shard_map/ppermute | solution.py:289
  5.1 6.9 %collective-permute-start = (bf16[320,256]{1,0:T(8,128)(2,1)}, bf16[320,256]{1,0:T(8,128)(2,1)S(1)}, u32[]{:S(2)}, u32[]{:S(2)}) collective-permute-start(bf16[320,256]{1,0:T(8,128)(2,1)} %refs_0_.4), channel_id=1, source_target_pairs={{0,16},{8,24},{16,0},{24,8},{1,17},{9,25},{17,1},{25,9},{2,18},{10... | collective-permute-start | bytes 491528 | tf_op jit(solution)/shard_map/ppermute | solution.py:289
  7.6 1.2 %copy-start.4 = (s32[320]{0:T(512)S(1)}, s32[320]{0:T(512)}, u32[]{:S(2)}) copy-start(s32[320]{0:T(512)} %param.11) | copy-start | bytes 3844
  7.6 1.8 %copy-start.2 = (bf16[320,256]{1,0:T(8,128)(2,1)S(1)}, bf16[320,256]{1,0:T(8,128)(2,1)}, u32[]{:S(2)}) copy-start(bf16[320,256]{1,0:T(8,128)(2,1)} %refs_0_.4) | copy-start | bytes 491524
  7.6 1.8 %copy-start.3 = (bf16[320,256]{1,0:T(8,128)(2,1)S(1)}, bf16[320,256]{1,0:T(8,128)(2,1)}, u32[]{:S(2)}) copy-start(bf16[320,256]{1,0:T(8,128)(2,1)} %refs_0_.5) | copy-start | bytes 491524
  7.7 1.8 %collective-permute-start.2 = (bf16[320,256]{1,0:T(8,128)(2,1)}, bf16[320,256]{1,0:T(8,128)(2,1)S(1)}, u32[]{:S(2)}, u32[]{:S(2)}) collective-permute-start(bf16[320,256]{1,0:T(8,128)(2,1)} %refs_0_.5), channel_id=1, source_target_pairs={{0,8},{8,0},{16,24},{24,16},{1,9},{9,1},{17,25},{25,17},{2,10},{10... | collective-permute-start | bytes 491528 | tf_op jit(solution)/shard_map/ppermute | solution.py:289
  8.9 3.1 %collective-permute-start.5 = (bf16[320,256]{1,0:T(8,128)(2,1)S(1)}, bf16[320,256]{1,0:T(8,128)(2,1)S(1)}, u32[]{:S(2)}, u32[]{:S(2)}) collective-permute-start(bf16[320,256]{1,0:T(8,128)(2,1)S(1)} %collective-permute-done.3.refs_2_.refs_4_), channel_id=1, source_target_pairs={{0,8},{8,0},{16,24},{24,16},{1,9},{9,1},{17,25},{25,17},{2,10},{10... | collective-permute-start | bytes 491528 | tf_op jit(solution)/shard_map/ppermute | solution.py:289
  8.9 1.3 %collective-permute-start.6 = (s32[640]{0:T(1024)S(1)}, s32[640]{0:T(1024)S(1)}, u32[]{:S(2)}, u32[]{:S(2)}) collective-permute-start(s32[640]{0:T(1024)S(1)} %pad_add_fusion), channel_id=1, source_target_pairs={{0,8},{8,0},{16,24},{24,16},{1,9},{9,1},{17,25},{25,17},{2,10},{10... | collective-permute-start | bytes 7688 | tf_op jit(solution)/shard_map/ppermute | solution.py:289
  14.2 1.9 %collective-permute-start.7 = (bf16[640,256]{1,0:T(8,128)(2,1)S(1)}, bf16[640,256]{1,0:T(8,128)(2,1)S(1)}, u32[]{:S(2)}, u32[]{:S(2)}) collective-permute-start(bf16[640,256]{1,0:T(8,128)(2,1)S(1)} %shard_map.107), channel_id=1, source_target_pairs={{0,8},{8,0},{16,24},{24,16},{1,9},{9,1},{17,25},{25,17},{2,10},{10... | collective-permute-start | bytes 983048 | tf_op jit(solution)/shard_map/ppermute | solution.py:289
  16.4 13.7 %copy-start = (f32[640,256]{1,0:T(8,128)S(1)}, f32[640,256]{1,0:T(8,128)}, u32[]{:S(2)}) copy-start(f32[640,256]{1,0:T(8,128)} %refs_5_.1) | copy-start | bytes 1966084
  16.4 13.7 %copy-start.1 = (f32[640,256]{1,0:T(8,128)S(1)}, f32[640,256]{1,0:T(8,128)}, u32[]{:S(2)}) copy-start(f32[640,256]{1,0:T(8,128)} %refs_6_.1) | copy-start | bytes 1966084
  16.5 7.9 %collective-permute-start.8 = (bf16[2,88,256]{2,1,0:T(8,128)(2,1)S(1)}, bf16[2,88,256]{2,1,0:T(8,128)(2,1)S(1)}, u32[]{:S(2)}, u32[]{:S(2)}) collective-permute-start(bf16[2,88,256]{2,1,0:T(8,128)(2,1)S(1)} %get-tuple-element.54), channel_id=1, source_target_pairs={{0,4},{1,5},{2,6},{3,7},{4,0},{5,1},{6,2},{7,3},{8,13},{9,12},{10,... | collective-permute-start | bytes 270344 | tf_op jit(solution)/shard_map/ppermute | solution.py:411
  19.3 7.3 %collective-permute-start.9 = (bf16[2,88,256]{2,1,0:T(8,128)(2,1)S(1)}, bf16[2,88,256]{2,1,0:T(8,128)(2,1)S(1)}, u32[]{:S(2)}, u32[]{:S(2)}) collective-permute-start(bf16[2,88,256]{2,1,0:T(8,128)(2,1)S(1)} %get-tuple-element.55), channel_id=1, source_target_pairs={{0,6},{1,7},{2,4},{3,5},{4,2},{5,3},{6,0},{7,1},{8,15},{9,14},{10,... | collective-permute-start | bytes 270344 | tf_op jit(solution)/shard_map/ppermute | solution.py:411
  20.6 6.9 %collective-permute-start.10 = (bf16[2,88,256]{2,1,0:T(8,128)(2,1)S(1)}, bf16[2,88,256]{2,1,0:T(8,128)(2,1)S(1)}, u32[]{:S(2)}, u32[]{:S(2)}) collective-permute-start(bf16[2,88,256]{2,1,0:T(8,128)(2,1)S(1)} %get-tuple-element.56), channel_id=1, source_target_pairs={{0,1},{1,0},{2,3},{3,2},{4,5},{5,4},{6,7},{7,6},{8,10},{9,11},{10,... | collective-permute-start | bytes 270344 | tf_op jit(solution)/shard_map/ppermute | solution.py:411
  22.1 5.5 %collective-permute-start.11 = (bf16[2,88,256]{2,1,0:T(8,128)(2,1)S(1)}, bf16[2,88,256]{2,1,0:T(8,128)(2,1)S(1)}, u32[]{:S(2)}, u32[]{:S(2)}) collective-permute-start(bf16[2,88,256]{2,1,0:T(8,128)(2,1)S(1)} %get-tuple-element.57), channel_id=1, source_target_pairs={{0,0},{1,1},{2,2},{3,3},{4,4},{5,5},{6,6},{7,7},{8,11},{9,10},{10,... | collective-permute-start | bytes 270344 | tf_op jit(solution)/shard_map/ppermute | solution.py:411
  24.4 5.8 %collective-permute-start.12 = (bf16[88,256]{1,0:T(8,128)(2,1)S(1)}, bf16[88,256]{1,0:T(8,128)(2,1)S(1)}, u32[]{:S(2)}, u32[]{:S(2)}) collective-permute-start(bf16[88,256]{1,0:T(8,128)(2,1)S(1)} %slice_bitcast_fusion.3), channel_id=1, source_target_pairs={{0,8},{8,0},{16,24},{24,16},{1,9},{9,1},{17,25},{25,17},{2,10},{10... | collective-permute-start | bytes 135176 | tf_op jit(solution)/shard_map/ppermute | solution.py:289
  26.6 3.5 %collective-permute-start.13 = (bf16[88,256]{1,0:T(8,128)(2,1)S(1)}, bf16[88,256]{1,0:T(8,128)(2,1)S(1)}, u32[]{:S(2)}, u32[]{:S(2)}) collective-permute-start(bf16[88,256]{1,0:T(8,128)(2,1)S(1)} %slice_bitcast_fusion.2), channel_id=1, source_target_pairs={{0,8},{8,0},{16,24},{24,16},{1,9},{9,1},{17,25},{25,17},{2,10},{10... | collective-permute-start | bytes 135176 | tf_op jit(solution)/shard_map/ppermute | solution.py:289
  27.5 2.6 %collective-permute-start.14 = (bf16[88,256]{1,0:T(8,128)(2,1)S(1)}, bf16[88,256]{1,0:T(8,128)(2,1)S(1)}, u32[]{:S(2)}, u32[]{:S(2)}) collective-permute-start(bf16[88,256]{1,0:T(8,128)(2,1)S(1)} %slice_bitcast_fusion.1), channel_id=1, source_target_pairs={{0,8},{8,0},{16,24},{24,16},{1,9},{9,1},{17,25},{25,17},{2,10},{10... | collective-permute-start | bytes 135176 | tf_op jit(solution)/shard_map/ppermute | solution.py:289
  27.6 2.6 %collective-permute-start.15 = (bf16[88,256]{1,0:T(8,128)(2,1)S(1)}, bf16[88,256]{1,0:T(8,128)(2,1)S(1)}, u32[]{:S(2)}, u32[]{:S(2)}) collective-permute-start(bf16[88,256]{1,0:T(8,128)(2,1)S(1)} %slice_bitcast_fusion), channel_id=1, source_target_pairs={{0,8},{8,0},{16,24},{24,16},{1,9},{9,1},{17,25},{25,17},{2,10},{10... | collective-permute-start | bytes 135176 | tf_op jit(solution)/shard_map/ppermute | solution.py:289

commit v9 on v7

--- a/solution.py
+++ b/solution.py
@@ -122,9 +122,8 @@
 def main_kernel(early, late, *refs):
     n = early + late
     q_ref, far_ref, item_refs, refs = refs[0], refs[1], refs[2 : 2 + n], refs[2 + n :]
-    rate_ref, e_ref, stats_ref, total_ref, mine_out, mate_out, *refs = refs
+    rate_ref, e_ref, stats_ref, total_ref, mate_out, weights_ref, *refs = refs
     loss_ref, late_ref, factor_ref, far_e_ref = refs
-    block = q_ref.shape[0]
     q, far = q_ref[...], far_ref[...]
     far_top = fill_logits(far, item_refs, far_e_ref)
     early_top, early_total = stats_ref[0:1], total_ref[0:1]
@@ -135,43 +134,55 @@
     inverse = 1.0 / total
     factor = shrink * inverse
     mate = dot((e_ref[1] * factor).astype(BF16), q)
-    mate_out[...] = mate + dot((far_e_ref[1] * far_inverse).astype(BF16), far)
-    weights = e_ref[0] * factor
-    weights = jnp.where(diagonal(block), weights - 1.0, weights)
-    mine = dot(weights.astype(BF16), q)
-    mine_out[...] = mine + dot((far_e_ref[0] * far_inverse).astype(BF16), far)
+    mate += dot((far_e_ref[1] * far_inverse).astype(BF16), far)
+    mate_out[...] = code(mate * SCALE).astype(BF16) if mate_out.dtype == BF16 else mate
+    weights_ref[...] = (far_e_ref[0] * far_inverse).astype(BF16)
     chosen = stats_ref[1:2] - total_ref[1:2]
     loss_ref[...] = ((top + jnp.log2(total) - chosen) * (1.0 / LOG2E))[0]
     factor_ref[0:1] = factor
     factor_ref[1:2] = inverse
 
 
-def more_kernel(n, q_ref, *refs):
+def mine_kernel(e_ref, factor_ref, weights_ref, q_ref, far_ref, out_ref):
+    weights = e_ref[0] * factor_ref[0:1]
+    weights = jnp.where(diagonal(weights.shape[0]), weights - 1.0, weights)
+    out_ref[...] = dot(weights.astype(BF16), q_ref[...]) + dot(weights_ref[...], far_ref[...])
+
+
+def more_kernel(n, last, q_ref, *refs):
     item_refs, refs = refs[:n], refs[n:]
     rate_ref, mine_ref, mate_ref, mine_out, mate_out, e_ref = refs
     q = q_ref[...]
     inverse = 1.0 / to_powers(e_ref, fill_logits(q, item_refs, e_ref), rate_ref, 0)
-    mate_out[...] = mate_ref[...] + dot((e_ref[1] * inverse).astype(BF16), q)
+    mate = mate_ref[...] + dot((e_ref[1] * inverse).astype(BF16), q)
+    mate_out[...] = code(mate * SCALE).astype(BF16) if last else mate
     mine_out[...] = mine_ref[...] + dot((e_ref[0] * inverse).astype(BF16), q)
 
 
-def query_kernel(early, late, e_ref, late_ref, factor_ref, *refs):
-    item_refs, out_ref = refs[:-1], refs[-1]
+def transpose_kernel(*refs):
+    for b, ref in enumerate(refs[:-1]):
+        refs[-1][b] = jnp.transpose(ref[...])
+
+
+def query_kernel(early, late, e_ref, late_ref, factor_ref, turned_ref, *refs):
+    late_items, out_ref = refs[:-1], refs[-1]
     total = None
-    for b, item_ref in enumerate(item_refs):
+    for b in range(early + late):
         if b < early:
-            weights = e_ref[b] * factor_ref[0:1]
+            weights, items = e_ref[b] * factor_ref[0:1], turned_ref[b]
         else:
             weights = late_ref[b - early] * factor_ref[1:2]
+            items = jnp.transpose(late_items[b - early][...])
         if b == 0:
             weights = jnp.where(diagonal(weights.shape[0]), weights - 1.0, weights)
-        part = dot(weights.astype(BF16), item_ref[...], TN)
+        part = dot(items, weights.astype(BF16))
         total = part if total is None else total + part
-    out_ref[...] = total * SCALE
+    out_ref[...] = jnp.transpose(total * SCALE)
 
 
 def pack_kernel(groups, slots, pick_ref, tail_ref, mine_ref, other_ref, *out_refs):
-    grad = code((mine_ref[...] + other_ref[...]) * SCALE).astype(BF16)
+    grad = mine_ref[...] * SCALE + decode(other_ref[...].astype(F32))
+    grad = code(grad).astype(BF16)
     picked = dot(pick_ref[...], grad).astype(BF16)
     for g in range(groups):
         out = out_refs[g] if len(out_refs) == groups else out_refs[0].at[g]
@@ -201,10 +212,11 @@
     return dot(jnp.concatenate([put, put], axis=1), values_ref[...])
 
 
-def first_kernel(slots, *refs):
-    got_refs, (out_ref, values_ref, ids_ref) = refs[:-3], refs[-3:]
-    unpack(slots, got_refs, values_ref, ids_ref)
-    out_ref[...] = scatter(values_ref, ids_ref, 0, out_ref.shape[0])
+def first_kernel(slots, partial, *refs):
+    inputs, (out_ref, values_ref, ids_ref) = refs[:-3], refs[-3:]
+    unpack(slots, inputs[partial:], values_ref, ids_ref)
+    sums = scatter(values_ref, ids_ref, 0, out_ref.shape[0])
+    out_ref[...] = sums + inputs[0][...] if partial else sums
 
 
 def update_kernel(slots, partial, *refs):
@@ -245,7 +257,7 @@
     n, groups = lax.axis_size("wide"), lax.axis_size("group")
     capacity = 2 * block // groups
     slots = -(-capacity // TAIL) * TAIL
-    paired = groups <= 8
+    paired = groups == 8
 
     def swap(x, k, axis="wide"):
         return lax.ppermute(x, axis, [(i, i ^ k) for i in range(lax.axis_size(axis))])
@@ -288,9 +300,19 @@
         mate_counts.reshape(1, -1),
         limit=8 + 4 * n,
     )
-    mine, mate, loss, late_powers, factors = call(
+    (turned,) = call(
+        transpose_kernel, [((early, D, block), BF16)], *item_blocks[:early], limit=8 + n
+    )
+    far_queries[0], turned, rates = lax.optimization_barrier((far_queries[0], turned, rates))
+    mate, weights, loss, late_powers, factors = call(
         functools.partial(main_kernel, early, late),
-        [part, part, ((block,), F32), ((late, *square), F32), ((8, block), F32)],
+        [
+            ((block, D), BF16 if len(far_queries) == 1 else F32),
+            (square, BF16),
+            ((block,), F32),
+            ((late, *square), F32),
+            ((8, block), F32),
+        ],
         queries,
         far_queries[0],
         *item_blocks,
@@ -301,26 +323,37 @@
         scratch=[pltpu.VMEM((n, *square), F32)],
         limit=8 + 4 * n,
     )
-    for far in far_queries[1:]:
-        mine, mate = call(
-            functools.partial(more_kernel, n),
-            [part, part],
-            far,
-            *item_blocks,
-            rates,
-            mine,
-            mate,
-            scratch=[pltpu.VMEM((n, *square), F32)],
-            limit=8 + 4 * n,
-        )
-    other = swap(mate, 1)
+
+    def sum_mine():
+        return call(mine_kernel, [part], powers, factors, weights, queries, far_queries[0])[0]
+
+    if len(far_queries) == 1:
+        other = swap(mate, 1)
+        mine = sum_mine()
+    else:
+        mine = sum_mine()
+        for k, far in enumerate(far_queries[1:]):
+            last = k == len(far_queries) - 2
+            mine, mate = call(
+                functools.partial(more_kernel, n, last),
+                [part, ((block, D), BF16 if last else F32)],
+                far,
+                *item_blocks,
+                rates,
+                mine,
+                mate,
+                scratch=[pltpu.VMEM((n, *square), F32)],
+                limit=8 + 4 * n,
+            )
+        other = swap(mate, 1)
     (query_grad,) = call(
         functools.partial(query_kernel, early, late),
         [part],
         powers,
         late_powers,
         factors,
-        *item_blocks,
+        turned,
+        *item_blocks[early:],
         limit=8 + 2 * n,
         flops=1 << 30,
     )
@@ -347,17 +380,18 @@
             pltpu.VMEM((TAIL, packets * slots), F32),
         ]
 
-    count = groups // 2
     before = []
     if paired:
-        before = call(
-            functools.partial(first_kernel, slots),
-            [((rows, D), F32)],
-            *got[:count],
-            scratch=scratch(count),
-            flops=1 << 28,
-        )
-        got = got[count:]
+        for part_of in (got[:4], got[4:6]):
+            before = call(
+                functools.partial(first_kernel, slots, len(before)),
+                [((rows, D), F32)],
+                *before,
+                *part_of,
+                scratch=scratch(len(part_of)),
+                flops=1 << 28,
+            )
+        got = got[6:]
     table_new, accum_new = pl.pallas_call(
         functools.partial(update_kernel, slots, paired),
         out_shape=[jax.ShapeDtypeStruct(table.shape, F32)] * 2,

time: 31.5 us -> 32.1 us (1.019)
  Pallas kernels: 7.56 us -> 8.82 us
  waiting for transfers between devices: 4.79 us -> 4.12 us
    pallas_call x7 -> x10, Pallas kernels: 5.9 us -> 7.17 us  [call(): pl.pallas_call(kernel, out_shape=[jax.ShapeDtypeStruct(s, t) for s, t in...]
    ppermute x14, waiting for transfers between devices: 4.79 us -> 4.12 us  [swap(): lax.ppermute(x, axis, [(i, i ^ k) for i in range(lax.axis_size(axis))])]
  transfers between devices with their start and end apart: 14 -> 14, of which waited for: 7 -> 6; matrix products, arithmetic and copies ran while one was open for 5% -> 5% of each run, Pallas kernels for 12% -> 15%
where the time goes in v9:
time: 32.1 us; the launch traced here: 31.9 us
  starting transfers between devices  16.8 us (52%)
  Pallas kernels  8.82 us (27%)
  waiting for transfers between devices  4.12 us (13%)
  other arithmetic  1.46 us (5%)
  between operations  0.74 us (2%)
    ppermute x14, starting transfers between devices, swap(): lax.ppermute(x, axis, [(i, i ^ k) for i in range(lax.axis_size(axis))])  16.8 us
    pallas_call x10, Pallas kernels, call(): pl.pallas_call(kernel, out_shape=[jax.ShapeDtypeStruct(s, t) for s, t in...  7.17 us
    ppermute x14, waiting for transfers between devices, swap(): lax.ppermute(x, axis, [(i, i ^ k) for i in range(lax.axis_size(axis))])  4.12 us
    pallas_call x1, Pallas kernels, shards(): pl.pallas_call(functools.partial(update_kernel, slots, paired), out_shape...  1.65 us
    mul x1, other arithmetic, shards(): owner * ROW_CODES + item_offset.reshape(1, block)  0.7 us
    add x1, other arithmetic, shards(): owner * ROW_CODES + item_offset.reshape(1, block)  0.68 us
  transfers between devices with their start and end apart: 14, of which 6 were waited for; matrix products, arithmetic and copies ran while one was open for 5% of the time, Pallas kernels for 15%

profile of v9, /device:TPU:0, one launch (start us, length us, event | category | flops | bytes accessed | tf_op | source)
XLA Modules:
  0.0 31.9 jit_solution(2613735867716593230)
XLA Ops:
  0.6 3.0 %collective-permute-start.2 = (bf16[320,256]{1,0:T(8,128)(2,1)}, bf16[320,256]{1,0:T(8,128)(2,1)S(1)}, u32[]{:S(2)}, u32[]{:S(2)}) collective-permute-start(bf16[320,256]{1,0:T(8,128)(2,1)} %refs_2_.1), channel_id=1, source_target_pairs={{0,16},{8,24},{16,0},{24,8},{1,17},{9,25},{17,1},{25,9},{2,18},{10... | collective-permute-start | bytes 491528 | tf_op jit(solution)/shard_map/ppermute | solution.py:263
  3.7 0.0 collective-permute-start.1
  3.7 0.2 collective-permute-start.3
  3.8 1.9 %collective-permute-start = (bf16[320,256]{1,0:T(8,128)(2,1)}, bf16[320,256]{1,0:T(8,128)(2,1)S(1)}, u32[]{:S(2)}, u32[]{:S(2)}) collective-permute-start(bf16[320,256]{1,0:T(8,128)(2,1)} %q_ref.3), channel_id=1, source_target_pairs={{0,16},{8,24},{16,0},{24,8},{1,17},{9,25},{17,1},{25,9},{2,18},{10... | collective-permute-start | bytes 491528 | tf_op jit(solution)/shard_map/ppermute | solution.py:263
  5.7 0.7 %multiply_reduce_fusion = s32[320]{0:T(512)S(1)} fusion(s32[320,1]{0,1:T(1,128)} %param.9, s32[]{:T(128)S(6)} %axis_index.12), kind=kLoop, calls=%fused_computation.1 | loop fusion | flops 640 | bytes 2564 | tf_op jit(solution)/shard_map/mul | solution.py:275
  6.4 0.7 %add.5 = s32[320]{0:T(512)S(1)} add(s32[320]{0:T(512)S(1)} %multiply_reduce_fusion, s32[320]{0:T(512)} %param.10) | non-fusion elementwise | flops 320 | bytes 3840 | tf_op jit(solution)/shard_map/add | solution.py:275
  7.1 0.0 copy-start.1
  7.1 0.8 %shard_map.102 = (bf16[640,320]{1,0:T(8,128)(2,1)S(1)}, bf16[8,8,256]{2,1,0:T(8,128)(2,1)S(1)}) custom-call(s32[1,320]{1,0:T(1,128)S(1)} %add.6.code_ref), custom_call_target="tpu_custom_call" | custom-call | flops 1073741824 | bytes 1024 | tf_op jit(solution)/shard_map/pallas_call | solution.py:246
  7.9 1.0 %collective-permute-done.3 = s32[320]{0:T(512)S(1)} collective-permute-done((s32[320]{0:T(512)}, s32[320]{0:T(512)S(1)}, u32[]{:S(2)}, u32[]{:S(2)}) %collective-permute-start.3) | collective-permute-done | bytes 1312 | tf_op jit(solution)/shard_map/ppermute | solution.py:263
  8.9 0.0 collective-permute-done.2.refs_2_.refs_4_
  8.9 0.0 collective-permute-start.5
  9.0 0.0 copy-done.4
  9.0 0.1 pad_add_fusion
  9.0 0.5 %collective-permute-start.4 = (s32[640]{0:T(1024)S(1)}, s32[640]{0:T(1024)S(1)}, u32[]{:S(2)}, u32[]{:S(2)}) collective-permute-start(s32[640]{0:T(1024)S(1)} %pad_add_fusion), channel_id=1, source_target_pairs={{0,8},{8,0},{16,24},{24,16},{1,9},{9,1},{17,25},{25,17},{2,10},{10... | collective-permute-start | bytes 7688 | tf_op jit(solution)/shard_map/ppermute | solution.py:263
  9.5 0.0 collective-permute-done.1.refs_1_.refs_3_
  9.5 0.0 copy-done
  9.5 0.0 copy-done.1
  9.6 0.6 %shard_map.104 = (f32[3,320,320]{2,1,0:T(8,128)S(1)}, f32[8,320]{1,0:T(8,128)S(1)}) custom-call(bf16[320,256]{1,0:T(8,128)(2,1)S(1)} %copy-done, bf16[320,256]{1,0:T(8,128)(2,1)S(1)} %copy-done.1, bf16[320,256]{1,0:T(8,128)(2,1)S(1)} %collective-permute-done.1.refs_1_.refs_3_, bf16[320,256]{1,0:T(8,128)(2,1)S(1)} %collective-permute-done.2.refs_2_.refs_4_), custom_call_target="tpu_custom_call" | custom-call | flops 536870912 | bytes 1024 | tf_op jit(solution)/shard_map/pallas_call | solution.py:246
  10.2 0.2 shard_map.103.turned_ref
  10.4 0.0 collective-permute-done.4
  10.4 0.4 %shard_map.105 = (f32[4,320,128]{2,1,0:T(8,128)S(1)}, f32[3,320,320]{2,1,0:T(8,128)S(1)}, f32[8,320]{1,0:T(8,128)S(1)}) custom-call(f32[3,320,320]{2,1,0:T(8,128)S(1)} %get-tuple-element.36.e_ref, s32[1,640]{1,0:T(1,128)S(1)} %reshape.24.near_ref, s32[1,640]{1,0:T(1,128)S(1)} %reshape.25.mate_ref), custom_call_target="tpu_custom_call" | custom-call | bytes 1024 | tf_op jit(solution)/shard_map/pallas_call | solution.py:246
  10.8 0.8 %collective-permute-done.refs_1_.far_ref = bf16[320,256]{1,0:T(8,128)(2,1)S(1)} collective-permute-done((bf16[320,256]{1,0:T(8,128)(2,1)}, bf16[320,256]{1,0:T(8,128)(2,1)S(1)}, u32[]{:S(2)}, u32[]{:S(2)}) %collective-permute-start) | collective-permute-done | bytes 163872 | tf_op jit(solution)/shard_map/ppermute | solution.py:263
  11.6 0.0 collective-permute-done.5.refs_5_.refs_0_
  11.6 1.8 %shard_map.106 = (bf16[320,256]{1,0:T(8,128)(2,1)S(1)}, bf16[320,320]{1,0:T(8,128)(2,1)S(1)}, f32[320]{0:T(512)}, f32[1,320,320]{2,1,0:T(8,128)S(1)}, f32[8,320]{1,0:T(8,128)S(1)}) custom-call(bf16[320,256]{1,0:T(8,128)(2,1)S(1)} %copy-done, bf16[320,256]{1,0:T(8,128)(2,1)S(1)} %collective-permute-done.refs_1_.far_ref, bf16[320,256]{1,0:T(8,128)(2,1)S(1)} %copy-done.1, ...), custom_call_target="tpu_custom_call" | custom-call | bytes 1024 | tf_op jit(solution)/shard_map/pallas_call | solution.py:246
  13.5 0.0 collective-permute-start.6
  13.5 0.3 %shard_map.108.mine_ref = f32[320,256]{1,0:T(8,128)S(1)} custom-call(f32[3,320,320]{2,1,0:T(8,128)S(1)} %get-tuple-element.41.refs_7_.e_ref, f32[8,320]{1,0:T(8,128)S(1)} %get-tuple-element.47.factor_ref, bf16[320,320]{1,0:T(8,128)(2,1)S(1)} %get-tuple-element.52.weights_ref, bf16[320,256]{1,0:T(8,128)(2,1)S(1)} %copy-done, ...), custom_call_target="tpu_custom_call" | custom-call | bytes 1024 | tf_op jit(solution)/shard_map/pallas_call | solution.py:246
  13.8 1.5 %shard_map.107 = f32[320,256]{1,0:T(8,128)} custom-call(f32[3,320,320]{2,1,0:T(8,128)S(1)} %get-tuple-element.41.refs_7_.e_ref, f32[1,320,320]{2,1,0:T(8,128)S(1)} %get-tuple-element.46.late_ref, f32[8,320]{1,0:T(8,128)S(1)} %get-tuple-element.47.factor_ref, bf16[3,256,320]{2,1,0:T(8,128)(2,1)S(1)} %shard_map.103.turned_ref, ...), custom_call_target="tpu_custom_call" | custom-call | flops 1073741824 | bytes 1024 | tf_op jit(solution)/shard_map/pallas_call | solution.py:246
  15.3 0.0 collective-permute-done.6.other_ref
  15.3 0.5 %shard_map.109 = (bf16[88,256]{1,0:T(8,128)(2,1)S(1)}, bf16[88,256]{1,0:T(8,128)(2,1)S(1)}, bf16[88,256]{1,0:T(8,128)(2,1)S(1)}, bf16[88,256]{1,0:T(8,128)(2,1)S...) custom-call(bf16[640,320]{1,0:T(8,128)(2,1)S(1)} %get-tuple-element., ...), custom_call_target="tpu_custom_call" | custom-call | bytes 1024 | tf_op jit(solution)/shard_map/pallas_call | solution.py:246
  15.8 2.9 %collective-permute-start.7 = (bf16[88,256]{1,0:T(8,128)(2,1)S(1)}, bf16[88,256]{1,0:T(8,128)(2,1)S(1)}, u32[]{:S(2)}, u32[]{:S(2)}) collective-permute-start(bf16[88,256]{1,0:T(8,128)(2,1)S(1)} %get-tuple-element.55), channel_id=1, source_target_pairs={{0,4},{1,5},{2,6},{3,7},{4,0},{5,1},{6,2},{7,3},{8,12},{9,13},{10,... | collective-permute-start | bytes 135176 | tf_op jit(solution)/shard_map/ppermute | solution.py:263
  18.6 1.3 %collective-permute-start.8 = (bf16[88,256]{1,0:T(8,128)(2,1)S(1)}, bf16[88,256]{1,0:T(8,128)(2,1)S(1)}, u32[]{:S(2)}, u32[]{:S(2)}) collective-permute-start(bf16[88,256]{1,0:T(8,128)(2,1)S(1)} %get-tuple-element.56), channel_id=1, source_target_pairs={{0,6},{1,7},{2,4},{3,5},{4,2},{5,3},{6,0},{7,1},{8,14},{9,15},{10,... | collective-permute-start | bytes 135176 | tf_op jit(solution)/shard_map/ppermute | solution.py:263
  20.0 2.6 %collective-permute-start.9 = (bf16[88,256]{1,0:T(8,128)(2,1)S(1)}, bf16[88,256]{1,0:T(8,128)(2,1)S(1)}, u32[]{:S(2)}, u32[]{:S(2)}) collective-permute-start(bf16[88,256]{1,0:T(8,128)(2,1)S(1)} %get-tuple-element.57), channel_id=1, source_target_pairs={{0,5},{1,4},{2,7},{3,6},{4,1},{5,0},{6,3},{7,2},{8,13},{9,12},{10,... | collective-permute-start | bytes 135176 | tf_op jit(solution)/shard_map/ppermute | solution.py:263
  22.6 0.9 %collective-permute-start.10 = (bf16[88,256]{1,0:T(8,128)(2,1)S(1)}, bf16[88,256]{1,0:T(8,128)(2,1)S(1)}, u32[]{:S(2)}, u32[]{:S(2)}) collective-permute-start(bf16[88,256]{1,0:T(8,128)(2,1)S(1)} %get-tuple-element.58), channel_id=1, source_target_pairs={{0,7},{1,6},{2,5},{3,4},{4,3},{5,2},{6,1},{7,0},{8,15},{9,14},{10,... | collective-permute-start | bytes 135176 | tf_op jit(solution)/shard_map/ppermute | solution.py:263
  23.5 1.8 %collective-permute-start.11 = (bf16[88,256]{1,0:T(8,128)(2,1)S(1)}, bf16[88,256]{1,0:T(8,128)(2,1)S(1)}, u32[]{:S(2)}, u32[]{:S(2)}) collective-permute-start(bf16[88,256]{1,0:T(8,128)(2,1)S(1)} %get-tuple-element.59), channel_id=1, source_target_pairs={{0,3},{1,2},{2,1},{3,0},{4,7},{5,6},{6,5},{7,4},{8,11},{9,10},{10,... | collective-permute-start | bytes 135176 | tf_op jit(solution)/shard_map/ppermute | solution.py:263
  25.3 0.0 collective-permute-done.7.refs_1_
  25.3 0.5 %collective-permute-start.12 = (bf16[88,256]{1,0:T(8,128)(2,1)S(1)}, bf16[88,256]{1,0:T(8,128)(2,1)S(1)}, u32[]{:S(2)}, u32[]{:S(2)}) collective-permute-start(bf16[88,256]{1,0:T(8,128)(2,1)S(1)} %get-tuple-element.60), channel_id=1, source_target_pairs={{0,1},{1,0},{2,3},{3,2},{4,5},{5,4},{6,7},{7,6},{8,9},{9,8},{10,11... | collective-permute-start | bytes 135176 | tf_op jit(solution)/shard_map/ppermute | solution.py:263
  25.8 0.0 collective-permute-done.8.refs_2_
  25.8 1.1 %collective-permute-start.13 = (bf16[88,256]{1,0:T(8,128)(2,1)S(1)}, bf16[88,256]{1,0:T(8,128)(2,1)S(1)}, u32[]{:S(2)}, u32[]{:S(2)}) collective-permute-start(bf16[88,256]{1,0:T(8,128)(2,1)S(1)} %get-tuple-element.61), channel_id=1, source_target_pairs={{0,2},{1,3},{2,0},{3,1},{4,6},{5,7},{6,4},{7,5},{8,10},{9,11},{10,... | collective-permute-start | bytes 135176 | tf_op jit(solution)/shard_map/ppermute | solution.py:263
  27.0 1.5 %collective-permute-done.9.refs_3_ = bf16[88,256]{1,0:T(8,128)(2,1)S(1)} collective-permute-done((bf16[88,256]{1,0:T(8,128)(2,1)S(1)}, bf16[88,256]{1,0:T(8,128)(2,1)S(1)}, u32[]{:S(2)}, u32[]{:S(2)}) %collective-permute-start.9) | collective-permute-done | bytes 45088 | tf_op jit(solution)/shard_map/ppermute | solution.py:263
  28.4 0.6 %shard_map.110.refs_0_ = f32[640,256]{1,0:T(8,128)S(1)} custom-call(bf16[88,256]{1,0:T(8,128)(2,1)S(1)} %get-tuple-element.54.refs_0_, bf16[88,256]{1,0:T(8,128)(2,1)S(1)} %collective-permute-done.7.refs_1_, bf16[88,256]{1,0:T(8,128)(2,1)S(1)} %collective-permute-done.8.refs_2_, bf16[88,256]{1,0:T(8,128)(2,1)S(1)} %collective-permute-done.9.refs_3_), custom_call_target="tpu_custom_call" | custom-call | flops 268435456 | bytes 1024 | tf_op jit(solution)/shard_map/pallas_call | solution.py:246
  29.0 0.5 %collective-permute-done.10.refs_1_ = bf16[88,256]{1,0:T(8,128)(2,1)S(1)} collective-permute-done((bf16[88,256]{1,0:T(8,128)(2,1)S(1)}, bf16[88,256]{1,0:T(8,128)(2,1)S(1)}, u32[]{:S(2)}, u32[]{:S(2)}) %collective-permute-start.10) | collective-permute-done | bytes 45088 | tf_op jit(solution)/shard_map/ppermute | solution.py:263
  29.5 0.2 collective-permute-done.11.refs_2_
  29.7 0.5 %shard_map.111.refs_0_ = f32[640,256]{1,0:T(8,128)S(1)} custom-call(f32[640,256]{1,0:T(8,128)S(1)} %shard_map.110.refs_0_, bf16[88,256]{1,0:T(8,128)(2,1)S(1)} %collective-permute-done.10.refs_1_, bf16[88,256]{1,0:T(8,128)(2,1)S(1)} %collective-permute-done.11.refs_2_), custom_call_target="tpu_custom_call" | custom-call | flops 268435456 | bytes 1024 | tf_op jit(solution)/shard_map/pallas_call | solution.py:246
  30.2 0.1 collective-permute-done.12.refs_1_
  30.3 0.0 collective-permute-done.13.refs_2_
  30.3 0.0 copy-done.2
  30.3 0.0 copy-done.3
  30.3 1.6 %shard_map.112 = (f32[640,256]{1,0:T(8,128)}, f32[640,256]{1,0:T(8,128)}) custom-call(f32[640,256]{1,0:T(8,128)S(1)} %shard_map.111.refs_0_, bf16[88,256]{1,0:T(8,128)(2,1)S(1)} %collective-permute-done.12.refs_1_, bf16[88,256]{1,0:T(8,128)(2,1)S(1)} %collective-permute-done.13.refs_2_, f32[640,256]{1,0:T(8,128)S(1)} %copy-done.2, f32[640,256]{1,0:T(8,128)S(1)} %copy-done.3), custom_call_target="tpu_custom_call" | custom-call | tf_op jit(solution)/shard_map/pallas_call | solution.py:395
  (7 shorter events, 0.0 us)
Async XLA Ops:
  0.6 8.3 %collective-permute-start.2 = (bf16[320,256]{1,0:T(8,128)(2,1)}, bf16[320,256]{1,0:T(8,128)(2,1)S(1)}, u32[]{:S(2)}, u32[]{:S(2)}) collective-permute-start(bf16[320,256]{1,0:T(8,128)(2,1)} %refs_2_.1), channel_id=1, source_target_pairs={{0,16},{8,24},{16,0},{24,8},{1,17},{9,25},{17,1},{25,9},{2,18},{10... | collective-permute-start | bytes 491528 | tf_op jit(solution)/shard_map/ppermute | solution.py:263
  3.7 5.9 %collective-permute-start.1 = (bf16[320,256]{1,0:T(8,128)(2,1)}, bf16[320,256]{1,0:T(8,128)(2,1)S(1)}, u32[]{:S(2)}, u32[]{:S(2)}) collective-permute-start(bf16[320,256]{1,0:T(8,128)(2,1)} %refs_2_.1), channel_id=1, source_target_pairs={{0,8},{8,0},{16,24},{24,16},{1,9},{9,1},{17,25},{25,17},{2,10},{10... | collective-permute-start | bytes 491528 | tf_op jit(solution)/shard_map/ppermute | solution.py:263
  3.7 5.3 %collective-permute-start.3 = (s32[320]{0:T(512)}, s32[320]{0:T(512)S(1)}, u32[]{:S(2)}, u32[]{:S(2)}) collective-permute-start(s32[320]{0:T(512)} %param.11), channel_id=1, source_target_pairs={{0,16},{8,24},{16,0},{24,8},{1,17},{9,25},{17,1},{25,9},{2,18},{10... | collective-permute-start | bytes 3848 | tf_op jit(solution)/shard_map/ppermute | solution.py:263
  3.8 7.8 %collective-permute-start = (bf16[320,256]{1,0:T(8,128)(2,1)}, bf16[320,256]{1,0:T(8,128)(2,1)S(1)}, u32[]{:S(2)}, u32[]{:S(2)}) collective-permute-start(bf16[320,256]{1,0:T(8,128)(2,1)} %q_ref.3), channel_id=1, source_target_pairs={{0,16},{8,24},{16,0},{24,8},{1,17},{9,25},{17,1},{25,9},{2,18},{10... | collective-permute-start | bytes 491528 | tf_op jit(solution)/shard_map/ppermute | solution.py:263
  7.1 1.9 %copy-start.4 = (s32[320]{0:T(512)S(1)}, s32[320]{0:T(512)}, u32[]{:S(2)}) copy-start(s32[320]{0:T(512)} %param.11) | copy-start | bytes 3844
  7.1 2.5 %copy-start = (bf16[320,256]{1,0:T(8,128)(2,1)S(1)}, bf16[320,256]{1,0:T(8,128)(2,1)}, u32[]{:S(2)}) copy-start(bf16[320,256]{1,0:T(8,128)(2,1)} %q_ref.3) | copy-start | bytes 491524
  7.1 2.5 %copy-start.1 = (bf16[320,256]{1,0:T(8,128)(2,1)S(1)}, bf16[320,256]{1,0:T(8,128)(2,1)}, u32[]{:S(2)}) copy-start(bf16[320,256]{1,0:T(8,128)(2,1)} %refs_2_.1) | copy-start | bytes 491524
  8.9 2.7 %collective-permute-start.5 = (bf16[320,256]{1,0:T(8,128)(2,1)S(1)}, bf16[320,256]{1,0:T(8,128)(2,1)S(1)}, u32[]{:S(2)}, u32[]{:S(2)}) collective-permute-start(bf16[320,256]{1,0:T(8,128)(2,1)S(1)} %collective-permute-done.2.refs_2_.refs_4_), channel_id=1, source_target_pairs={{0,8},{8,0},{16,24},{24,16},{1,9},{9,1},{17,25},{25,17},{2,10},{10... | collective-permute-start | bytes 491528 | tf_op jit(solution)/shard_map/ppermute | solution.py:263
  9.0 1.4 %collective-permute-start.4 = (s32[640]{0:T(1024)S(1)}, s32[640]{0:T(1024)S(1)}, u32[]{:S(2)}, u32[]{:S(2)}) collective-permute-start(s32[640]{0:T(1024)S(1)} %pad_add_fusion), channel_id=1, source_target_pairs={{0,8},{8,0},{16,24},{24,16},{1,9},{9,1},{17,25},{25,17},{2,10},{10... | collective-permute-start | bytes 7688 | tf_op jit(solution)/shard_map/ppermute | solution.py:263
  13.5 1.8 %collective-permute-start.6 = (bf16[320,256]{1,0:T(8,128)(2,1)S(1)}, bf16[320,256]{1,0:T(8,128)(2,1)S(1)}, u32[]{:S(2)}, u32[]{:S(2)}) collective-permute-start(bf16[320,256]{1,0:T(8,128)(2,1)S(1)} %get-tuple-element.45), channel_id=1, source_target_pairs={{0,8},{8,0},{16,24},{24,16},{1,9},{9,1},{17,25},{25,17},{2,10},{10... | collective-permute-start | bytes 491528 | tf_op jit(solution)/shard_map/ppermute | solution.py:263
  15.3 15.0 %copy-start.2 = (f32[640,256]{1,0:T(8,128)S(1)}, f32[640,256]{1,0:T(8,128)}, u32[]{:S(2)}) copy-start(f32[640,256]{1,0:T(8,128)} %refs_3_.1) | copy-start | bytes 1966084
  15.3 15.0 %copy-start.3 = (f32[640,256]{1,0:T(8,128)S(1)}, f32[640,256]{1,0:T(8,128)}, u32[]{:S(2)}) copy-start(f32[640,256]{1,0:T(8,128)} %refs_4_.1) | copy-start | bytes 1966084
  15.8 9.5 %collective-permute-start.7 = (bf16[88,256]{1,0:T(8,128)(2,1)S(1)}, bf16[88,256]{1,0:T(8,128)(2,1)S(1)}, u32[]{:S(2)}, u32[]{:S(2)}) collective-permute-start(bf16[88,256]{1,0:T(8,128)(2,1)S(1)} %get-tuple-element.55), channel_id=1, source_target_pairs={{0,4},{1,5},{2,6},{3,7},{4,0},{5,1},{6,2},{7,3},{8,12},{9,13},{10,... | collective-permute-start | bytes 135176 | tf_op jit(solution)/shard_map/ppermute | solution.py:263
  18.6 7.2 %collective-permute-start.8 = (bf16[88,256]{1,0:T(8,128)(2,1)S(1)}, bf16[88,256]{1,0:T(8,128)(2,1)S(1)}, u32[]{:S(2)}, u32[]{:S(2)}) collective-permute-start(bf16[88,256]{1,0:T(8,128)(2,1)S(1)} %get-tuple-element.56), channel_id=1, source_target_pairs={{0,6},{1,7},{2,4},{3,5},{4,2},{5,3},{6,0},{7,1},{8,14},{9,15},{10,... | collective-permute-start | bytes 135176 | tf_op jit(solution)/shard_map/ppermute | solution.py:263
  20.0 8.5 %collective-permute-start.9 = (bf16[88,256]{1,0:T(8,128)(2,1)S(1)}, bf16[88,256]{1,0:T(8,128)(2,1)S(1)}, u32[]{:S(2)}, u32[]{:S(2)}) collective-permute-start(bf16[88,256]{1,0:T(8,128)(2,1)S(1)} %get-tuple-element.57), channel_id=1, source_target_pairs={{0,5},{1,4},{2,7},{3,6},{4,1},{5,0},{6,3},{7,2},{8,13},{9,12},{10,... | collective-permute-start | bytes 135176 | tf_op jit(solution)/shard_map/ppermute | solution.py:263
  22.6 6.9 %collective-permute-start.10 = (bf16[88,256]{1,0:T(8,128)(2,1)S(1)}, bf16[88,256]{1,0:T(8,128)(2,1)S(1)}, u32[]{:S(2)}, u32[]{:S(2)}) collective-permute-start(bf16[88,256]{1,0:T(8,128)(2,1)S(1)} %get-tuple-element.58), channel_id=1, source_target_pairs={{0,7},{1,6},{2,5},{3,4},{4,3},{5,2},{6,1},{7,0},{8,15},{9,14},{10,... | collective-permute-start | bytes 135176 | tf_op jit(solution)/shard_map/ppermute | solution.py:263
  23.5 6.2 %collective-permute-start.11 = (bf16[88,256]{1,0:T(8,128)(2,1)S(1)}, bf16[88,256]{1,0:T(8,128)(2,1)S(1)}, u32[]{:S(2)}, u32[]{:S(2)}) collective-permute-start(bf16[88,256]{1,0:T(8,128)(2,1)S(1)} %get-tuple-element.59), channel_id=1, source_target_pairs={{0,3},{1,2},{2,1},{3,0},{4,7},{5,6},{6,5},{7,4},{8,11},{9,10},{10,... | collective-permute-start | bytes 135176 | tf_op jit(solution)/shard_map/ppermute | solution.py:263
  25.3 5.0 %collective-permute-start.12 = (bf16[88,256]{1,0:T(8,128)(2,1)S(1)}, bf16[88,256]{1,0:T(8,128)(2,1)S(1)}, u32[]{:S(2)}, u32[]{:S(2)}) collective-permute-start(bf16[88,256]{1,0:T(8,128)(2,1)S(1)} %get-tuple-element.60), channel_id=1, source_target_pairs={{0,1},{1,0},{2,3},{3,2},{4,5},{5,4},{6,7},{7,6},{8,9},{9,8},{10,11... | collective-permute-start | bytes 135176 | tf_op jit(solution)/shard_map/ppermute | solution.py:263
  25.8 4.4 %collective-permute-start.13 = (bf16[88,256]{1,0:T(8,128)(2,1)S(1)}, bf16[88,256]{1,0:T(8,128)(2,1)S(1)}, u32[]{:S(2)}, u32[]{:S(2)}) collective-permute-start(bf16[88,256]{1,0:T(8,128)(2,1)S(1)} %get-tuple-element.61), channel_id=1, source_target_pairs={{0,2},{1,3},{2,0},{3,1},{4,6},{5,7},{6,4},{7,5},{8,10},{9,11},{10,... | collective-permute-start | bytes 135176 | tf_op jit(solution)/shard_map/ppermute | solution.py:263

commit v10 on v7

--- a/solution.py
+++ b/solution.py
@@ -67,23 +67,23 @@
         tail_ref[g] = jnp.concatenate([dot(high, pick, NT), dot(low, pick, NT)], axis=1).astype(BF16)
 
 
-def fill_logits(q, item_refs, out_ref):
-    top = None
-    for b, item_ref in enumerate(item_refs):
-        logits = dot(item_ref[...], q, NT) * (SCALE * LOG2E)
-        out_ref[b] = logits
-        high = jnp.max(logits, axis=0, keepdims=True)
-        top = high if top is None else jnp.maximum(top, high)
-    return top
-
-
-def to_powers(ref, top, rate_ref, first):
-    total = jnp.zeros(top.shape, F32)
-    for b in range(ref.shape[0]):
-        e = jnp.exp2(ref[b] - top) * spread(rate_ref[first + b], top.shape[1])
-        ref[b] = e
-        total += jnp.sum(e, axis=0, keepdims=True)
-    return total
+def powers_of(q, item_ref, rate_ref=None):
+    logits = dot(item_ref[...], q, NT) * (SCALE * LOG2E)
+    top = jnp.max(logits, axis=0, keepdims=True)
+    e = jnp.exp2(logits - top)
+    return (e if rate_ref is None else e * spread(rate_ref[...], q.shape[0])), top, logits
+
+
+def column_sum(x):
+    return jnp.sum(x, axis=0, keepdims=True)
+
+
+def join(tops, sums):
+    top = functools.reduce(jnp.maximum, tops)
+    shrinks = [jnp.exp2(t - top) for t in tops]
+    total = sum(x * s for x, s in zip(sums, shrinks))
+    inverse = 1.0 / total
+    return top, total, [s * inverse for s in shrinks]
 
 
 def diagonal(block):
@@ -93,76 +93,85 @@
 
 
 def early_kernel(n, q_ref, *refs):
-    item_refs, (e_ref, stats_ref) = refs[:n], refs[n:]
-    top = fill_logits(q_ref[...], item_refs, e_ref)
-    chosen = jnp.where(diagonal(q_ref.shape[0]), e_ref[0], 0.0)
-    stats_ref[0:1] = top
-    stats_ref[1:2] = jnp.sum(chosen, axis=0, keepdims=True)
+    item_refs, (e_ref, tops_ref) = refs[:n], refs[n:]
+    q = q_ref[...]
     for b in range(n):
-        e_ref[b] = jnp.exp2(e_ref[b] - top)
-
-
-def rate_kernel(n, early, e_ref, near_ref, mate_ref, rate_ref, out_ref, total_ref):
+        e, tops_ref[b : b + 1], logits = powers_of(q, item_refs[b])
+        e_ref[b] = e
+        if b == 0:
+            tops_ref[n : n + 1] = column_sum(jnp.where(diagonal(q.shape[0]), logits, 0.0))
+
+
+def rate_kernel(n, early, e_ref, near_ref, mate_ref, rate_ref, out_ref, sums_ref):
     block = e_ref.shape[1]
     near = [near_ref[:, k * block : (k + 1) * block].astype(F32) for k in range(n // 2)]
     mate = [mate_ref[:, k * block : (k + 1) * block].astype(F32) for k in range(n // 2)]
     counts = [near[0], mate[0]] + near[1:] + mate[1:]
-    total = jnp.zeros((1, block), F32)
     for b in range(n):
         rate = jnp.transpose(jnp.broadcast_to(1.0 / counts[b], (LANES, block)))
         rate_ref[b] = rate
         if b < early:
             e = e_ref[b] * spread(rate, block)
             out_ref[b] = e
-            total += jnp.sum(e, axis=0, keepdims=True)
-    total_ref[0:1] = total
-    total_ref[1:2] = jnp.log(counts[0]) * LOG2E
+            sums_ref[b : b + 1] = column_sum(e)
+    sums_ref[early : early + 1] = jnp.log(counts[0]) * LOG2E
+
+
+def far_powers(n, q, item_refs, rate_ref, e_ref):
+    tops, sums = [], []
+    for b in range(n):
+        e, top, _ = powers_of(q, item_refs[b], rate_ref.at[b])
+        if b < 2:
+            e_ref[b] = e
+        tops.append(top)
+        sums.append(column_sum(e))
+    return join(tops, sums)[2]
 
 
 def main_kernel(early, late, *refs):
     n = early + late
     q_ref, far_ref, item_refs, refs = refs[0], refs[1], refs[2 : 2 + n], refs[2 + n :]
-    rate_ref, e_ref, stats_ref, total_ref, mine_out, mate_out, *refs = refs
+    rate_ref, e_ref, tops_ref, sums_ref, mine_out, mate_out, *refs = refs
     loss_ref, late_ref, factor_ref, far_e_ref = refs
-    block = q_ref.shape[0]
     q, far = q_ref[...], far_ref[...]
-    far_top = fill_logits(far, item_refs, far_e_ref)
-    early_top, early_total = stats_ref[0:1], total_ref[0:1]
-    top = jnp.maximum(fill_logits(q, item_refs[early:], late_ref), early_top)
-    far_inverse = 1.0 / to_powers(far_e_ref, far_top, rate_ref, 0)
-    shrink = jnp.exp2(early_top - top)
-    total = to_powers(late_ref, top, rate_ref, early) + early_total * shrink
-    inverse = 1.0 / total
-    factor = shrink * inverse
-    mate = dot((e_ref[1] * factor).astype(BF16), q)
-    mate_out[...] = mate + dot((far_e_ref[1] * far_inverse).astype(BF16), far)
-    weights = e_ref[0] * factor
-    weights = jnp.where(diagonal(block), weights - 1.0, weights)
+    tops = [tops_ref[b : b + 1] for b in range(early)]
+    sums = [sums_ref[b : b + 1] for b in range(early)]
+    for b in range(late):
+        e, top, _ = powers_of(q, item_refs[early + b], rate_ref.at[early + b])
+        late_ref[b] = e
+        tops.append(top)
+        sums.append(column_sum(e))
+    top, total, factors = join(tops, sums)
+    far_factors = far_powers(n, far, item_refs, rate_ref, far_e_ref)
+    mate = dot((e_ref[1] * factors[1]).astype(BF16), q)
+    mate += dot((far_e_ref[1] * far_factors[1]).astype(BF16), far)
+    mate_out[...] = code(mate * SCALE).astype(BF16) if mate_out.dtype == BF16 else mate
+    weights = e_ref[0] * factors[0]
+    weights = jnp.where(diagonal(q.shape[0]), weights - 1.0, weights)
     mine = dot(weights.astype(BF16), q)
-    mine_out[...] = mine + dot((far_e_ref[0] * far_inverse).astype(BF16), far)
-    chosen = stats_ref[1:2] - total_ref[1:2]
+    mine_out[...] = mine + dot((far_e_ref[0] * far_factors[0]).astype(BF16), far)
+    chosen = tops_ref[early : early + 1] - sums_ref[early : early + 1]
     loss_ref[...] = ((top + jnp.log2(total) - chosen) * (1.0 / LOG2E))[0]
-    factor_ref[0:1] = factor
-    factor_ref[1:2] = inverse
+    for b in range(n):
+        factor_ref[b : b + 1] = factors[b]
 
 
 def more_kernel(n, q_ref, *refs):
     item_refs, refs = refs[:n], refs[n:]
     rate_ref, mine_ref, mate_ref, mine_out, mate_out, e_ref = refs
     q = q_ref[...]
-    inverse = 1.0 / to_powers(e_ref, fill_logits(q, item_refs, e_ref), rate_ref, 0)
-    mate_out[...] = mate_ref[...] + dot((e_ref[1] * inverse).astype(BF16), q)
-    mine_out[...] = mine_ref[...] + dot((e_ref[0] * inverse).astype(BF16), q)
+    factors = far_powers(n, q, item_refs, rate_ref, e_ref)
+    mate = mate_ref[...] + dot((e_ref[1] * factors[1]).astype(BF16), q)
+    mate_out[...] = code(mate * SCALE).astype(BF16) if mate_out.dtype == BF16 else mate
+    mine_out[...] = mine_ref[...] + dot((e_ref[0] * factors[0]).astype(BF16), q)
 
 
 def query_kernel(early, late, e_ref, late_ref, factor_ref, *refs):
     item_refs, out_ref = refs[:-1], refs[-1]
     total = None
     for b, item_ref in enumerate(item_refs):
-        if b < early:
-            weights = e_ref[b] * factor_ref[0:1]
-        else:
-            weights = late_ref[b - early] * factor_ref[1:2]
+        e = e_ref[b] if b < early else late_ref[b - early]
+        weights = e * factor_ref[b : b + 1]
         if b == 0:
             weights = jnp.where(diagonal(weights.shape[0]), weights - 1.0, weights)
         part = dot(weights.astype(BF16), item_ref[...], TN)
@@ -171,7 +180,8 @@
 
 
 def pack_kernel(groups, slots, pick_ref, tail_ref, mine_ref, other_ref, *out_refs):
-    grad = code((mine_ref[...] + other_ref[...]) * SCALE).astype(BF16)
+    grad = mine_ref[...] * SCALE + decode(other_ref[...].astype(F32))
+    grad = code(grad).astype(BF16)
     picked = dot(pick_ref[...], grad).astype(BF16)
     for g in range(groups):
         out = out_refs[g] if len(out_refs) == groups else out_refs[0].at[g]
@@ -272,9 +282,11 @@
     mate_counts = swap(near_counts, 1)
     part = ((block, D), F32)
     square = (block, block)
+    rows_of = ((-(-(n + 1) // TAIL) * TAIL, block), F32)
+    sent = ((block, D), BF16)
     powers, stats = call(
         functools.partial(early_kernel, early),
-        [((early, *square), F32), ((8, block), F32)],
+        [((early, *square), F32), rows_of],
         queries,
         *item_blocks[:early],
         limit=8 + 2 * n,
@@ -282,7 +294,7 @@
     )
     rates, powers, totals = call(
         functools.partial(rate_kernel, n, early),
-        [((n, block, LANES), F32), ((early, *square), F32), ((8, block), F32)],
+        [((n, block, LANES), F32), ((early, *square), F32), rows_of],
         powers,
         near_counts.reshape(1, -1),
         mate_counts.reshape(1, -1),
@@ -290,7 +302,13 @@
     )
     mine, mate, loss, late_powers, factors = call(
         functools.partial(main_kernel, early, late),
-        [part, part, ((block,), F32), ((late, *square), F32), ((8, block), F32)],
+        [
+            part,
+            part if far_queries[1:] else sent,
+            ((block,), F32),
+            ((late, *square), F32),
+            rows_of,
+        ],
         queries,
         far_queries[0],
         *item_blocks,
@@ -298,19 +316,19 @@
         powers,
         stats,
         totals,
-        scratch=[pltpu.VMEM((n, *square), F32)],
+        scratch=[pltpu.VMEM((2, *square), F32)],
         limit=8 + 4 * n,
     )
-    for far in far_queries[1:]:
+    for k, far in enumerate(far_queries[1:], 2):
         mine, mate = call(
             functools.partial(more_kernel, n),
-            [part, part],
+            [part, part if k < len(far_queries) else sent],
             far,
             *item_blocks,
             rates,
             mine,
             mate,
-            scratch=[pltpu.VMEM((n, *square), F32)],
+            scratch=[pltpu.VMEM((2, *square), F32)],
             limit=8 + 4 * n,
         )
     other = swap(mate, 1)

time: 31.5 us -> 31.5 us (level)
  transfers between devices with their start and end apart: 14 -> 14, of which waited for: 7 -> 8; matrix products, arithmetic and copies ran while one was open for 5% -> 5% of each run, Pallas kernels for 12% -> 12%
where the time goes in v10:
time: 31.5 us; the launch traced here: 31.3 us
  starting transfers between devices  16.8 us (53%)
  Pallas kernels  7.45 us (24%)
  waiting for transfers between devices  4.88 us (15%)
  other arithmetic  1.46 us (5%)
  between operations  0.71 us (2%)
    ppermute x14, starting transfers between devices, swap(): lax.ppermute(x, axis, [(i, i ^ k) for i in range(lax.axis_size(axis))])  16.8 us
    pallas_call x7, Pallas kernels, call(): pl.pallas_call(kernel, out_shape=[jax.ShapeDtypeStruct(s, t) for s, t in...  5.78 us
    ppermute x14, waiting for transfers between devices, swap(): lax.ppermute(x, axis, [(i, i ^ k) for i in range(lax.axis_size(axis))])  4.88 us
    pallas_call x1, Pallas kernels, shards(): pl.pallas_call(functools.partial(update_kernel, slots, paired), out_shape...  1.67 us
    mul x1, other arithmetic, shards(): owner * ROW_CODES + item_offset.reshape(1, block)  0.7 us
    add x1, other arithmetic, shards(): owner * ROW_CODES + item_offset.reshape(1, block)  0.68 us
  transfers between devices with their start and end apart: 14, of which 8 were waited for; matrix products, arithmetic and copies ran while one was open for 5% of the time, Pallas kernels for 12%

profile of v10, /device:TPU:0, one launch (start us, length us, event | category | flops | bytes accessed | tf_op | source)
XLA Modules:
  0.0 31.3 jit_solution(2874183250239780065)
XLA Ops:
  0.6 3.0 %collective-permute-start.2 = (bf16[320,256]{1,0:T(8,128)(2,1)}, bf16[320,256]{1,0:T(8,128)(2,1)S(1)}, u32[]{:S(2)}, u32[]{:S(2)}) collective-permute-start(bf16[320,256]{1,0:T(8,128)(2,1)} %refs_0_.5), channel_id=1, source_target_pairs={{0,16},{8,24},{16,0},{24,8},{1,17},{9,25},{17,1},{25,9},{2,18},{10... | collective-permute-start | bytes 491528 | tf_op jit(solution)/shard_map/ppermute | solution.py:261
  3.7 0.0 collective-permute-start.1
  3.7 0.2 collective-permute-start.3
  3.8 1.9 %collective-permute-start = (bf16[320,256]{1,0:T(8,128)(2,1)}, bf16[320,256]{1,0:T(8,128)(2,1)S(1)}, u32[]{:S(2)}, u32[]{:S(2)}) collective-permute-start(bf16[320,256]{1,0:T(8,128)(2,1)} %refs_0_.4), channel_id=1, source_target_pairs={{0,16},{8,24},{16,0},{24,8},{1,17},{9,25},{17,1},{25,9},{2,18},{10... | collective-permute-start | bytes 491528 | tf_op jit(solution)/shard_map/ppermute | solution.py:261
  5.7 0.7 %multiply_reduce_fusion = s32[320]{0:T(512)S(1)} fusion(s32[320,1]{0,1:T(1,128)} %param.9, s32[]{:T(128)S(6)} %axis_index.12), kind=kLoop, calls=%fused_computation.1 | loop fusion | flops 640 | bytes 2564 | tf_op jit(solution)/shard_map/mul | solution.py:273
  6.4 0.7 %add.5 = s32[320]{0:T(512)S(1)} add(s32[320]{0:T(512)S(1)} %multiply_reduce_fusion, s32[320]{0:T(512)} %param.10) | non-fusion elementwise | flops 320 | bytes 3840 | tf_op jit(solution)/shard_map/add | solution.py:273
  7.1 0.0 copy-start.4
  7.1 0.0 copy-start.2
  7.1 0.0 copy-start.3
  7.1 0.8 %shard_map.102 = (bf16[640,320]{1,0:T(8,128)(2,1)S(1)}, bf16[8,8,256]{2,1,0:T(8,128)(2,1)S(1)}) custom-call(s32[1,320]{1,0:T(1,128)S(1)} %add.6.code_ref), custom_call_target="tpu_custom_call" | custom-call | flops 1073741824 | bytes 1024 | tf_op jit(solution)/shard_map/pallas_call | solution.py:244
  7.9 1.0 %collective-permute-done.3 = s32[320]{0:T(512)S(1)} collective-permute-done((s32[320]{0:T(512)}, s32[320]{0:T(512)S(1)}, u32[]{:S(2)}, u32[]{:S(2)}) %collective-permute-start.3) | collective-permute-done | bytes 1312 | tf_op jit(solution)/shard_map/ppermute | solution.py:261
  8.9 0.0 collective-permute-done.2.refs_2_.refs_4_
  8.9 0.0 collective-permute-start.4
  9.0 0.0 copy-done.4
  9.0 0.1 pad_add_fusion
  9.0 0.5 %collective-permute-start.5 = (s32[640]{0:T(1024)S(1)}, s32[640]{0:T(1024)S(1)}, u32[]{:S(2)}, u32[]{:S(2)}) collective-permute-start(s32[640]{0:T(1024)S(1)} %pad_add_fusion), channel_id=1, source_target_pairs={{0,8},{8,0},{16,24},{24,16},{1,9},{9,1},{17,25},{25,17},{2,10},{10... | collective-permute-start | bytes 7688 | tf_op jit(solution)/shard_map/ppermute | solution.py:261
  9.5 0.0 collective-permute-done.1.refs_1_.refs_3_
  9.5 0.0 copy-done.2
  9.5 0.0 copy-done.3
  9.6 0.5 %shard_map.103 = (f32[3,320,320]{2,1,0:T(8,128)S(1)}, f32[8,320]{1,0:T(8,128)S(1)}) custom-call(bf16[320,256]{1,0:T(8,128)(2,1)S(1)} %copy-done.2, bf16[320,256]{1,0:T(8,128)(2,1)S(1)} %copy-done.3, bf16[320,256]{1,0:T(8,128)(2,1)S(1)} %collective-permute-done.1.refs_1_.refs_3_, bf16[320,256]{1,0:T(8,128)(2,1)S(1)} %collective-permute-done.2.refs_2_.refs_4_), custom_call_target="tpu_custom_call" | custom-call | flops 536870912 | bytes 1024 | tf_op jit(solution)/shard_map/pallas_call | solution.py:244
  10.1 0.3 collective-permute-done.5
  10.4 0.4 %shard_map.104 = (f32[4,320,128]{2,1,0:T(8,128)S(1)}, f32[3,320,320]{2,1,0:T(8,128)S(1)}, f32[8,320]{1,0:T(8,128)S(1)}) custom-call(f32[3,320,320]{2,1,0:T(8,128)S(1)} %get-tuple-element.33.e_ref, s32[1,640]{1,0:T(1,128)S(1)} %reshape.24.near_ref, s32[1,640]{1,0:T(1,128)S(1)} %reshape.25.mate_ref), custom_call_target="tpu_custom_call" | custom-call | bytes 1024 | tf_op jit(solution)/shard_map/pallas_call | solution.py:244
  10.7 0.9 %collective-permute-done.refs_1_ = bf16[320,256]{1,0:T(8,128)(2,1)S(1)} collective-permute-done((bf16[320,256]{1,0:T(8,128)(2,1)}, bf16[320,256]{1,0:T(8,128)(2,1)S(1)}, u32[]{:S(2)}, u32[]{:S(2)}) %collective-permute-start) | collective-permute-done | bytes 163872 | tf_op jit(solution)/shard_map/ppermute | solution.py:261
  11.6 0.0 collective-permute-done.4.refs_5_.refs_3_
  11.6 1.7 %shard_map.105 = (f32[320,256]{1,0:T(8,128)S(1)}, bf16[320,256]{1,0:T(8,128)(2,1)S(1)}, f32[320]{0:T(512)}, f32[1,320,320]{2,1,0:T(8,128)S(1)}, f32[8,320]{1,0:T(8,128)S(1)}) custom-call(bf16[320,256]{1,0:T(8,128)(2,1)S(1)} %copy-done.2, bf16[320,256]{1,0:T(8,128)(2,1)S(1)} %collective-permute-done.refs_1_, bf16[320,256]{1,0:T(8,128)(2,1)S(1)} %copy-done.3, ...), custom_call_target="tpu_custom_call" | custom-call | bytes 1024 | tf_op jit(solution)/shard_map/pallas_call | solution.py:244
  13.4 0.0 collective-permute-start.6
  13.4 1.3 %shard_map.106 = f32[320,256]{1,0:T(8,128)} custom-call(f32[3,320,320]{2,1,0:T(8,128)S(1)} %get-tuple-element.36.refs_7_.e_ref, f32[1,320,320]{2,1,0:T(8,128)S(1)} %get-tuple-element.41.late_ref, f32[8,320]{1,0:T(8,128)S(1)} %get-tuple-element.42.factor_ref, bf16[320,256]{1,0:T(8,128)(2,1)S(1)} %copy-done.3, ...), custom_call_target="tpu_custom_call" | custom-call | flops 1073741824 | bytes 1024 | tf_op jit(solution)/shard_map/pallas_call | solution.py:244
  14.6 0.0 copy-start
  14.7 0.1 collective-permute-done.6.other_ref
  14.7 0.5 %shard_map.107 = (bf16[88,256]{1,0:T(8,128)(2,1)S(1)}, bf16[88,256]{1,0:T(8,128)(2,1)S(1)}, bf16[88,256]{1,0:T(8,128)(2,1)S(1)}, bf16[88,256]{1,0:T(8,128)(2,1)S...) custom-call(bf16[640,320]{1,0:T(8,128)(2,1)S(1)} %get-tuple-element., ...), custom_call_target="tpu_custom_call" | custom-call | bytes 1024 | tf_op jit(solution)/shard_map/pallas_call | solution.py:244
  15.2 2.9 %collective-permute-start.7 = (bf16[88,256]{1,0:T(8,128)(2,1)S(1)}, bf16[88,256]{1,0:T(8,128)(2,1)S(1)}, u32[]{:S(2)}, u32[]{:S(2)}) collective-permute-start(bf16[88,256]{1,0:T(8,128)(2,1)S(1)} %get-tuple-element.49), channel_id=1, source_target_pairs={{0,4},{1,5},{2,6},{3,7},{4,0},{5,1},{6,2},{7,3},{8,12},{9,13},{10,... | collective-permute-start | bytes 135176 | tf_op jit(solution)/shard_map/ppermute | solution.py:261
  18.1 1.4 %collective-permute-start.8 = (bf16[88,256]{1,0:T(8,128)(2,1)S(1)}, bf16[88,256]{1,0:T(8,128)(2,1)S(1)}, u32[]{:S(2)}, u32[]{:S(2)}) collective-permute-start(bf16[88,256]{1,0:T(8,128)(2,1)S(1)} %get-tuple-element.50), channel_id=1, source_target_pairs={{0,6},{1,7},{2,4},{3,5},{4,2},{5,3},{6,0},{7,1},{8,14},{9,15},{10,... | collective-permute-start | bytes 135176 | tf_op jit(solution)/shard_map/ppermute | solution.py:261
  19.4 2.6 %collective-permute-start.9 = (bf16[88,256]{1,0:T(8,128)(2,1)S(1)}, bf16[88,256]{1,0:T(8,128)(2,1)S(1)}, u32[]{:S(2)}, u32[]{:S(2)}) collective-permute-start(bf16[88,256]{1,0:T(8,128)(2,1)S(1)} %get-tuple-element.51), channel_id=1, source_target_pairs={{0,5},{1,4},{2,7},{3,6},{4,1},{5,0},{6,3},{7,2},{8,13},{9,12},{10,... | collective-permute-start | bytes 135176 | tf_op jit(solution)/shard_map/ppermute | solution.py:261
  22.1 0.9 %collective-permute-start.10 = (bf16[88,256]{1,0:T(8,128)(2,1)S(1)}, bf16[88,256]{1,0:T(8,128)(2,1)S(1)}, u32[]{:S(2)}, u32[]{:S(2)}) collective-permute-start(bf16[88,256]{1,0:T(8,128)(2,1)S(1)} %get-tuple-element.52), channel_id=1, source_target_pairs={{0,7},{1,6},{2,5},{3,4},{4,3},{5,2},{6,1},{7,0},{8,15},{9,14},{10,... | collective-permute-start | bytes 135176 | tf_op jit(solution)/shard_map/ppermute | solution.py:261
  22.9 1.8 %collective-permute-start.11 = (bf16[88,256]{1,0:T(8,128)(2,1)S(1)}, bf16[88,256]{1,0:T(8,128)(2,1)S(1)}, u32[]{:S(2)}, u32[]{:S(2)}) collective-permute-start(bf16[88,256]{1,0:T(8,128)(2,1)S(1)} %get-tuple-element.53), channel_id=1, source_target_pairs={{0,3},{1,2},{2,1},{3,0},{4,7},{5,6},{6,5},{7,4},{8,11},{9,10},{10,... | collective-permute-start | bytes 135176 | tf_op jit(solution)/shard_map/ppermute | solution.py:261
  24.8 0.0 collective-permute-done.7.refs_1_
  24.8 0.5 %collective-permute-start.12 = (bf16[88,256]{1,0:T(8,128)(2,1)S(1)}, bf16[88,256]{1,0:T(8,128)(2,1)S(1)}, u32[]{:S(2)}, u32[]{:S(2)}) collective-permute-start(bf16[88,256]{1,0:T(8,128)(2,1)S(1)} %get-tuple-element.54), channel_id=1, source_target_pairs={{0,1},{1,0},{2,3},{3,2},{4,5},{5,4},{6,7},{7,6},{8,9},{9,8},{10,11... | collective-permute-start | bytes 135176 | tf_op jit(solution)/shard_map/ppermute | solution.py:261
  25.3 0.0 collective-permute-done.8.refs_2_
  25.3 1.1 %collective-permute-start.13 = (bf16[88,256]{1,0:T(8,128)(2,1)S(1)}, bf16[88,256]{1,0:T(8,128)(2,1)S(1)}, u32[]{:S(2)}, u32[]{:S(2)}) collective-permute-start(bf16[88,256]{1,0:T(8,128)(2,1)S(1)} %get-tuple-element.55), channel_id=1, source_target_pairs={{0,2},{1,3},{2,0},{3,1},{4,6},{5,7},{6,4},{7,5},{8,10},{9,11},{10,... | collective-permute-start | bytes 135176 | tf_op jit(solution)/shard_map/ppermute | solution.py:261
  26.4 1.5 %collective-permute-done.9.refs_3_ = bf16[88,256]{1,0:T(8,128)(2,1)S(1)} collective-permute-done((bf16[88,256]{1,0:T(8,128)(2,1)S(1)}, bf16[88,256]{1,0:T(8,128)(2,1)S(1)}, u32[]{:S(2)}, u32[]{:S(2)}) %collective-permute-start.9) | collective-permute-done | bytes 45088 | tf_op jit(solution)/shard_map/ppermute | solution.py:261
  27.9 0.6 %shard_map.108.refs_0_ = f32[640,256]{1,0:T(8,128)S(1)} custom-call(bf16[88,256]{1,0:T(8,128)(2,1)S(1)} %get-tuple-element.48.refs_0_, bf16[88,256]{1,0:T(8,128)(2,1)S(1)} %collective-permute-done.7.refs_1_, bf16[88,256]{1,0:T(8,128)(2,1)S(1)} %collective-permute-done.8.refs_2_, bf16[88,256]{1,0:T(8,128)(2,1)S(1)} %collective-permute-done.9.refs_3_), custom_call_target="tpu_custom_call" | custom-call | flops 268435456 | bytes 1024 | tf_op jit(solution)/shard_map/pallas_call | solution.py:244
  28.5 0.4 %collective-permute-done.10.refs_1_ = bf16[88,256]{1,0:T(8,128)(2,1)S(1)} collective-permute-done((bf16[88,256]{1,0:T(8,128)(2,1)S(1)}, bf16[88,256]{1,0:T(8,128)(2,1)S(1)}, u32[]{:S(2)}, u32[]{:S(2)}) %collective-permute-start.10) | collective-permute-done | bytes 45088 | tf_op jit(solution)/shard_map/ppermute | solution.py:261
  28.9 0.2 collective-permute-done.11.refs_2_
  29.1 0.5 %collective-permute-done.12.refs_3_ = bf16[88,256]{1,0:T(8,128)(2,1)S(1)} collective-permute-done((bf16[88,256]{1,0:T(8,128)(2,1)S(1)}, bf16[88,256]{1,0:T(8,128)(2,1)S(1)}, u32[]{:S(2)}, u32[]{:S(2)}) %collective-permute-start.12) | collective-permute-done | bytes 45088 | tf_op jit(solution)/shard_map/ppermute | solution.py:261
  29.6 0.0 collective-permute-done.13.refs_4_
  29.6 0.0 copy-done
  29.6 0.0 copy-done.1
  29.6 1.7 %shard_map.109 = (f32[640,256]{1,0:T(8,128)}, f32[640,256]{1,0:T(8,128)}) custom-call(f32[640,256]{1,0:T(8,128)S(1)} %shard_map.108.refs_0_, bf16[88,256]{1,0:T(8,128)(2,1)S(1)} %collective-permute-done.10.refs_1_, bf16[88,256]{1,0:T(8,128)(2,1)S(1)} %collective-permute-done.11.refs_2_, bf16[88,256]{1,0:T(8,128)(2,1)S(1)} %collective-permute-done.12.refs_3_, ...), custom_call_target="tpu_custom_call" | custom-call | tf_op jit(solution)/shard_map/pallas_call | solution.py:379
  (4 shorter events, 0.0 us)
Async XLA Ops:
  0.6 8.3 %collective-permute-start.2 = (bf16[320,256]{1,0:T(8,128)(2,1)}, bf16[320,256]{1,0:T(8,128)(2,1)S(1)}, u32[]{:S(2)}, u32[]{:S(2)}) collective-permute-start(bf16[320,256]{1,0:T(8,128)(2,1)} %refs_0_.5), channel_id=1, source_target_pairs={{0,16},{8,24},{16,0},{24,8},{1,17},{9,25},{17,1},{25,9},{2,18},{10... | collective-permute-start | bytes 491528 | tf_op jit(solution)/shard_map/ppermute | solution.py:261
  3.7 5.9 %collective-permute-start.1 = (bf16[320,256]{1,0:T(8,128)(2,1)}, bf16[320,256]{1,0:T(8,128)(2,1)S(1)}, u32[]{:S(2)}, u32[]{:S(2)}) collective-permute-start(bf16[320,256]{1,0:T(8,128)(2,1)} %refs_0_.5), channel_id=1, source_target_pairs={{0,8},{8,0},{16,24},{24,16},{1,9},{9,1},{17,25},{25,17},{2,10},{10... | collective-permute-start | bytes 491528 | tf_op jit(solution)/shard_map/ppermute | solution.py:261
  3.7 5.3 %collective-permute-start.3 = (s32[320]{0:T(512)}, s32[320]{0:T(512)S(1)}, u32[]{:S(2)}, u32[]{:S(2)}) collective-permute-start(s32[320]{0:T(512)} %param.11), channel_id=1, source_target_pairs={{0,16},{8,24},{16,0},{24,8},{1,17},{9,25},{17,1},{25,9},{2,18},{10... | collective-permute-start | bytes 3848 | tf_op jit(solution)/shard_map/ppermute | solution.py:261
  3.8 7.8 %collective-permute-start = (bf16[320,256]{1,0:T(8,128)(2,1)}, bf16[320,256]{1,0:T(8,128)(2,1)S(1)}, u32[]{:S(2)}, u32[]{:S(2)}) collective-permute-start(bf16[320,256]{1,0:T(8,128)(2,1)} %refs_0_.4), channel_id=1, source_target_pairs={{0,16},{8,24},{16,0},{24,8},{1,17},{9,25},{17,1},{25,9},{2,18},{10... | collective-permute-start | bytes 491528 | tf_op jit(solution)/shard_map/ppermute | solution.py:261
  7.1 1.9 %copy-start.4 = (s32[320]{0:T(512)S(1)}, s32[320]{0:T(512)}, u32[]{:S(2)}) copy-start(s32[320]{0:T(512)} %param.11) | copy-start | bytes 3844
  7.1 2.5 %copy-start.2 = (bf16[320,256]{1,0:T(8,128)(2,1)S(1)}, bf16[320,256]{1,0:T(8,128)(2,1)}, u32[]{:S(2)}) copy-start(bf16[320,256]{1,0:T(8,128)(2,1)} %refs_0_.4) | copy-start | bytes 491524
  7.1 2.5 %copy-start.3 = (bf16[320,256]{1,0:T(8,128)(2,1)S(1)}, bf16[320,256]{1,0:T(8,128)(2,1)}, u32[]{:S(2)}) copy-start(bf16[320,256]{1,0:T(8,128)(2,1)} %refs_0_.5) | copy-start | bytes 491524
  8.9 2.7 %collective-permute-start.4 = (bf16[320,256]{1,0:T(8,128)(2,1)S(1)}, bf16[320,256]{1,0:T(8,128)(2,1)S(1)}, u32[]{:S(2)}, u32[]{:S(2)}) collective-permute-start(bf16[320,256]{1,0:T(8,128)(2,1)S(1)} %collective-permute-done.2.refs_2_.refs_4_), channel_id=1, source_target_pairs={{0,8},{8,0},{16,24},{24,16},{1,9},{9,1},{17,25},{25,17},{2,10},{10... | collective-permute-start | bytes 491528 | tf_op jit(solution)/shard_map/ppermute | solution.py:261
  9.0 1.3 %collective-permute-start.5 = (s32[640]{0:T(1024)S(1)}, s32[640]{0:T(1024)S(1)}, u32[]{:S(2)}, u32[]{:S(2)}) collective-permute-start(s32[640]{0:T(1024)S(1)} %pad_add_fusion), channel_id=1, source_target_pairs={{0,8},{8,0},{16,24},{24,16},{1,9},{9,1},{17,25},{25,17},{2,10},{10... | collective-permute-start | bytes 7688 | tf_op jit(solution)/shard_map/ppermute | solution.py:261
  13.4 1.4 %collective-permute-start.6 = (bf16[320,256]{1,0:T(8,128)(2,1)S(1)}, bf16[320,256]{1,0:T(8,128)(2,1)S(1)}, u32[]{:S(2)}, u32[]{:S(2)}) collective-permute-start(bf16[320,256]{1,0:T(8,128)(2,1)S(1)} %get-tuple-element.40), channel_id=1, source_target_pairs={{0,8},{8,0},{16,24},{24,16},{1,9},{9,1},{17,25},{25,17},{2,10},{10... | collective-permute-start | bytes 491528 | tf_op jit(solution)/shard_map/ppermute | solution.py:261
  14.6 15.0 %copy-start = (f32[640,256]{1,0:T(8,128)S(1)}, f32[640,256]{1,0:T(8,128)}, u32[]{:S(2)}) copy-start(f32[640,256]{1,0:T(8,128)} %refs_5_.1) | copy-start | bytes 1966084
  14.6 15.0 %copy-start.1 = (f32[640,256]{1,0:T(8,128)S(1)}, f32[640,256]{1,0:T(8,128)}, u32[]{:S(2)}) copy-start(f32[640,256]{1,0:T(8,128)} %refs_6_.1) | copy-start | bytes 1966084
  15.2 9.5 %collective-permute-start.7 = (bf16[88,256]{1,0:T(8,128)(2,1)S(1)}, bf16[88,256]{1,0:T(8,128)(2,1)S(1)}, u32[]{:S(2)}, u32[]{:S(2)}) collective-permute-start(bf16[88,256]{1,0:T(8,128)(2,1)S(1)} %get-tuple-element.49), channel_id=1, source_target_pairs={{0,4},{1,5},{2,6},{3,7},{4,0},{5,1},{6,2},{7,3},{8,12},{9,13},{10,... | collective-permute-start | bytes 135176 | tf_op jit(solution)/shard_map/ppermute | solution.py:261
  18.1 7.2 %collective-permute-start.8 = (bf16[88,256]{1,0:T(8,128)(2,1)S(1)}, bf16[88,256]{1,0:T(8,128)(2,1)S(1)}, u32[]{:S(2)}, u32[]{:S(2)}) collective-permute-start(bf16[88,256]{1,0:T(8,128)(2,1)S(1)} %get-tuple-element.50), channel_id=1, source_target_pairs={{0,6},{1,7},{2,4},{3,5},{4,2},{5,3},{6,0},{7,1},{8,14},{9,15},{10,... | collective-permute-start | bytes 135176 | tf_op jit(solution)/shard_map/ppermute | solution.py:261
  19.4 8.5 %collective-permute-start.9 = (bf16[88,256]{1,0:T(8,128)(2,1)S(1)}, bf16[88,256]{1,0:T(8,128)(2,1)S(1)}, u32[]{:S(2)}, u32[]{:S(2)}) collective-permute-start(bf16[88,256]{1,0:T(8,128)(2,1)S(1)} %get-tuple-element.51), channel_id=1, source_target_pairs={{0,5},{1,4},{2,7},{3,6},{4,1},{5,0},{6,3},{7,2},{8,13},{9,12},{10,... | collective-permute-start | bytes 135176 | tf_op jit(solution)/shard_map/ppermute | solution.py:261
  22.1 6.9 %collective-permute-start.10 = (bf16[88,256]{1,0:T(8,128)(2,1)S(1)}, bf16[88,256]{1,0:T(8,128)(2,1)S(1)}, u32[]{:S(2)}, u32[]{:S(2)}) collective-permute-start(bf16[88,256]{1,0:T(8,128)(2,1)S(1)} %get-tuple-element.52), channel_id=1, source_target_pairs={{0,7},{1,6},{2,5},{3,4},{4,3},{5,2},{6,1},{7,0},{8,15},{9,14},{10,... | collective-permute-start | bytes 135176 | tf_op jit(solution)/shard_map/ppermute | solution.py:261
  22.9 6.2 %collective-permute-start.11 = (bf16[88,256]{1,0:T(8,128)(2,1)S(1)}, bf16[88,256]{1,0:T(8,128)(2,1)S(1)}, u32[]{:S(2)}, u32[]{:S(2)}) collective-permute-start(bf16[88,256]{1,0:T(8,128)(2,1)S(1)} %get-tuple-element.53), channel_id=1, source_target_pairs={{0,3},{1,2},{2,1},{3,0},{4,7},{5,6},{6,5},{7,4},{8,11},{9,10},{10,... | collective-permute-start | bytes 135176 | tf_op jit(solution)/shard_map/ppermute | solution.py:261
  24.8 4.9 %collective-permute-start.12 = (bf16[88,256]{1,0:T(8,128)(2,1)S(1)}, bf16[88,256]{1,0:T(8,128)(2,1)S(1)}, u32[]{:S(2)}, u32[]{:S(2)}) collective-permute-start(bf16[88,256]{1,0:T(8,128)(2,1)S(1)} %get-tuple-element.54), channel_id=1, source_target_pairs={{0,1},{1,0},{2,3},{3,2},{4,5},{5,4},{6,7},{7,6},{8,9},{9,8},{10,11... | collective-permute-start | bytes 135176 | tf_op jit(solution)/shard_map/ppermute | solution.py:261
  25.3 4.3 %collective-permute-start.13 = (bf16[88,256]{1,0:T(8,128)(2,1)S(1)}, bf16[88,256]{1,0:T(8,128)(2,1)S(1)}, u32[]{:S(2)}, u32[]{:S(2)}) collective-permute-start(bf16[88,256]{1,0:T(8,128)(2,1)S(1)} %get-tuple-element.55), channel_id=1, source_target_pairs={{0,2},{1,3},{2,0},{3,1},{4,6},{5,7},{6,4},{7,5},{8,10},{9,11},{10,... | collective-permute-start | bytes 135176 | tf_op jit(solution)/shard_map/ppermute | solution.py:261

commit v11 on v10

--- a/solution.py
+++ b/solution.py
@@ -132,7 +132,7 @@
     n = early + late
     q_ref, far_ref, item_refs, refs = refs[0], refs[1], refs[2 : 2 + n], refs[2 + n :]
     rate_ref, e_ref, tops_ref, sums_ref, mine_out, mate_out, *refs = refs
-    loss_ref, late_ref, factor_ref, far_e_ref = refs
+    late_ref, factor_ref, far_e_ref = refs
     q, far = q_ref[...], far_ref[...]
     tops = [tops_ref[b : b + 1] for b in range(early)]
     sums = [sums_ref[b : b + 1] for b in range(early)]
@@ -151,7 +151,7 @@
     mine = dot(weights.astype(BF16), q)
     mine_out[...] = mine + dot((far_e_ref[0] * far_factors[0]).astype(BF16), far)
     chosen = tops_ref[early : early + 1] - sums_ref[early : early + 1]
-    loss_ref[...] = ((top + jnp.log2(total) - chosen) * (1.0 / LOG2E))[0]
+    factor_ref[n : n + 1] = (top + jnp.log2(total) - chosen) * (1.0 / LOG2E)
     for b in range(n):
         factor_ref[b : b + 1] = factors[b]
 
@@ -167,7 +167,8 @@
 
 
 def query_kernel(early, late, e_ref, late_ref, factor_ref, *refs):
-    item_refs, out_ref = refs[:-1], refs[-1]
+    item_refs, out_ref, loss_ref = refs[:-2], refs[-2], refs[-1]
+    loss_ref[...] = factor_ref[early + late]
     total = None
     for b, item_ref in enumerate(item_refs):
         e = e_ref[b] if b < early else late_ref[b - early]
@@ -300,12 +301,11 @@
         mate_counts.reshape(1, -1),
         limit=8 + 4 * n,
     )
-    mine, mate, loss, late_powers, factors = call(
+    mine, mate, late_powers, factors = call(
         functools.partial(main_kernel, early, late),
         [
             part,
             part if far_queries[1:] else sent,
-            ((block,), F32),
             ((late, *square), F32),
             rows_of,
         ],
@@ -332,9 +332,9 @@
             limit=8 + 4 * n,
         )
     other = swap(mate, 1)
-    (query_grad,) = call(
+    query_grad, loss = call(
         functools.partial(query_kernel, early, late),
-        [part],
+        [part, ((block,), F32)],
         powers,
         late_powers,
         factors,

time: 31.5 us -> 31.4 us (level)
  no operation moved by 1% of the time
where the time goes in v11:
time: 31.4 us; the launch traced here: 31.2 us
  starting transfers between devices  16.8 us (54%)
  Pallas kernels  7.25 us (23%)
  waiting for transfers between devices  4.87 us (16%)
  other arithmetic  1.46 us (5%)
  between operations  0.72 us (2%)
    ppermute x14, starting transfers between devices, swap(): lax.ppermute(x, axis, [(i, i ^ k) for i in range(lax.axis_size(axis))])  16.8 us
    pallas_call x7, Pallas kernels, call(): pl.pallas_call(kernel, out_shape=[jax.ShapeDtypeStruct(s, t) for s, t in...  5.58 us
    ppermute x14, waiting for transfers between devices, swap(): lax.ppermute(x, axis, [(i, i ^ k) for i in range(lax.axis_size(axis))])  4.87 us
    pallas_call x1, Pallas kernels, shards(): pl.pallas_call(functools.partial(update_kernel, slots, paired), out_shape...  1.67 us
    mul x1, other arithmetic, shards(): owner * ROW_CODES + item_offset.reshape(1, block)  0.7 us
    add x1, other arithmetic, shards(): owner * ROW_CODES + item_offset.reshape(1, block)  0.68 us
  transfers between devices with their start and end apart: 14, of which 8 were waited for; matrix products, arithmetic and copies ran while one was open for 5% of the time, Pallas kernels for 12%

profile of v11, /device:TPU:0, one launch (start us, length us, event | category | flops | bytes accessed | tf_op | source)
XLA Modules:
  0.0 31.2 jit_solution(353919283493433980)
XLA Ops:
  0.6 3.0 %collective-permute-start.1 = (bf16[320,256]{1,0:T(8,128)(2,1)}, bf16[320,256]{1,0:T(8,128)(2,1)S(1)}, u32[]{:S(2)}, u32[]{:S(2)}) collective-permute-start(bf16[320,256]{1,0:T(8,128)(2,1)} %refs_0_.5), channel_id=1, source_target_pairs={{0,16},{8,24},{16,0},{24,8},{1,17},{9,25},{17,1},{25,9},{2,18},{10... | collective-permute-start | bytes 491528 | tf_op jit(solution)/shard_map/ppermute | solution.py:262
  3.7 0.0 collective-permute-start
  3.7 0.2 collective-permute-start.2
  3.8 1.9 %collective-permute-start.4 = (bf16[320,256]{1,0:T(8,128)(2,1)}, bf16[320,256]{1,0:T(8,128)(2,1)S(1)}, u32[]{:S(2)}, u32[]{:S(2)}) collective-permute-start(bf16[320,256]{1,0:T(8,128)(2,1)} %refs_0_.4), channel_id=1, source_target_pairs={{0,16},{8,24},{16,0},{24,8},{1,17},{9,25},{17,1},{25,9},{2,18},{10... | collective-permute-start | bytes 491528 | tf_op jit(solution)/shard_map/ppermute | solution.py:262
  5.7 0.7 %multiply_reduce_fusion = s32[320]{0:T(512)S(1)} fusion(s32[320,1]{0,1:T(1,128)} %param.9, s32[]{:T(128)S(6)} %axis_index.12), kind=kLoop, calls=%fused_computation.1 | loop fusion | flops 640 | bytes 2564 | tf_op jit(solution)/shard_map/mul | solution.py:274
  6.4 0.7 %add.5 = s32[320]{0:T(512)S(1)} add(s32[320]{0:T(512)S(1)} %multiply_reduce_fusion, s32[320]{0:T(512)} %param.10) | non-fusion elementwise | flops 320 | bytes 3840 | tf_op jit(solution)/shard_map/add | solution.py:274
  7.1 0.0 copy-start.4
  7.1 0.0 copy-start.2
  7.1 0.0 copy-start.3
  7.1 0.8 %shard_map.102 = (bf16[640,320]{1,0:T(8,128)(2,1)S(1)}, bf16[8,8,256]{2,1,0:T(8,128)(2,1)S(1)}) custom-call(s32[1,320]{1,0:T(1,128)S(1)} %add.6.code_ref), custom_call_target="tpu_custom_call" | custom-call | flops 1073741824 | bytes 1024 | tf_op jit(solution)/shard_map/pallas_call | solution.py:245
  7.9 1.0 %collective-permute-done.2 = s32[320]{0:T(512)S(1)} collective-permute-done((s32[320]{0:T(512)}, s32[320]{0:T(512)S(1)}, u32[]{:S(2)}, u32[]{:S(2)}) %collective-permute-start.2) | collective-permute-done | bytes 1312 | tf_op jit(solution)/shard_map/ppermute | solution.py:262
  8.9 0.0 collective-permute-done.1.refs_2_.refs_4_
  8.9 0.0 collective-permute-start.5
  9.0 0.0 copy-done.4
  9.0 0.1 pad_add_fusion
  9.0 0.5 %collective-permute-start.3 = (s32[640]{0:T(1024)S(1)}, s32[640]{0:T(1024)S(1)}, u32[]{:S(2)}, u32[]{:S(2)}) collective-permute-start(s32[640]{0:T(1024)S(1)} %pad_add_fusion), channel_id=1, source_target_pairs={{0,8},{8,0},{16,24},{24,16},{1,9},{9,1},{17,25},{25,17},{2,10},{10... | collective-permute-start | bytes 7688 | tf_op jit(solution)/shard_map/ppermute | solution.py:262
  9.5 0.0 collective-permute-done.refs_1_.refs_3_
  9.5 0.0 copy-done.2
  9.5 0.0 copy-done.3
  9.6 0.5 %shard_map.103 = (f32[3,320,320]{2,1,0:T(8,128)S(1)}, f32[8,320]{1,0:T(8,128)S(1)}) custom-call(bf16[320,256]{1,0:T(8,128)(2,1)S(1)} %copy-done.2, bf16[320,256]{1,0:T(8,128)(2,1)S(1)} %copy-done.3, bf16[320,256]{1,0:T(8,128)(2,1)S(1)} %collective-permute-done.refs_1_.refs_3_, bf16[320,256]{1,0:T(8,128)(2,1)S(1)} %collective-permute-done.1.refs_2_.refs_4_), custom_call_target="tpu_custom_call" | custom-call | flops 536870912 | bytes 1024 | tf_op jit(solution)/shard_map/pallas_call | solution.py:245
  10.1 0.3 collective-permute-done.3
  10.4 0.4 %shard_map.104 = (f32[4,320,128]{2,1,0:T(8,128)S(1)}, f32[3,320,320]{2,1,0:T(8,128)S(1)}, f32[8,320]{1,0:T(8,128)S(1)}) custom-call(f32[3,320,320]{2,1,0:T(8,128)S(1)} %get-tuple-element.34.e_ref, s32[1,640]{1,0:T(1,128)S(1)} %reshape.24.near_ref, s32[1,640]{1,0:T(1,128)S(1)} %reshape.25.mate_ref), custom_call_target="tpu_custom_call" | custom-call | bytes 1024 | tf_op jit(solution)/shard_map/pallas_call | solution.py:245
  10.7 0.9 %collective-permute-done.4.refs_1_ = bf16[320,256]{1,0:T(8,128)(2,1)S(1)} collective-permute-done((bf16[320,256]{1,0:T(8,128)(2,1)}, bf16[320,256]{1,0:T(8,128)(2,1)S(1)}, u32[]{:S(2)}, u32[]{:S(2)}) %collective-permute-start.4) | collective-permute-done | bytes 163872 | tf_op jit(solution)/shard_map/ppermute | solution.py:262
  11.6 0.0 collective-permute-done.5.refs_5_.refs_3_
  11.6 1.5 %shard_map.105 = (f32[320,256]{1,0:T(8,128)S(1)}, bf16[320,256]{1,0:T(8,128)(2,1)S(1)}, f32[1,320,320]{2,1,0:T(8,128)S(1)}, f32[8,320]{1,0:T(8,128)S(1)}) custom-call(bf16[320,256]{1,0:T(8,128)(2,1)S(1)} %copy-done.2, bf16[320,256]{1,0:T(8,128)(2,1)S(1)} %collective-permute-done.4.refs_1_, bf16[320,256]{1,0:T(8,128)(2,1)S(1)} %copy-done.3, ...), custom_call_target="tpu_custom_call" | custom-call | bytes 1024 | tf_op jit(solution)/shard_map/pallas_call | solution.py:245
  13.1 0.1 collective-permute-start.6
  13.2 1.3 %shard_map.106 = (f32[320,256]{1,0:T(8,128)}, f32[320]{0:T(512)}) custom-call(f32[3,320,320]{2,1,0:T(8,128)S(1)} %get-tuple-element.36.refs_7_.e_ref, f32[1,320,320]{2,1,0:T(8,128)S(1)} %get-tuple-element.40.late_ref, f32[8,320]{1,0:T(8,128)S(1)} %get-tuple-element.41.factor_ref, bf16[320,256]{1,0:T(8,128)(2,1)S(1)} %copy-done.3, ...), custom_call_target="tpu_custom_call" | custom-call | flops 1073741824 | bytes 1024 | tf_op jit(solution)/shard_map/pallas_call | solution.py:245
  14.5 0.0 copy-start
  14.5 0.1 collective-permute-done.6.other_ref
  14.6 0.5 %shard_map.107 = (bf16[88,256]{1,0:T(8,128)(2,1)S(1)}, bf16[88,256]{1,0:T(8,128)(2,1)S(1)}, bf16[88,256]{1,0:T(8,128)(2,1)S(1)}, bf16[88,256]{1,0:T(8,128)(2,1)S...) custom-call(bf16[640,320]{1,0:T(8,128)(2,1)S(1)} %get-tuple-element., ...), custom_call_target="tpu_custom_call" | custom-call | bytes 1024 | tf_op jit(solution)/shard_map/pallas_call | solution.py:245
  15.1 2.9 %collective-permute-start.7 = (bf16[88,256]{1,0:T(8,128)(2,1)S(1)}, bf16[88,256]{1,0:T(8,128)(2,1)S(1)}, u32[]{:S(2)}, u32[]{:S(2)}) collective-permute-start(bf16[88,256]{1,0:T(8,128)(2,1)S(1)} %get-tuple-element.51), channel_id=1, source_target_pairs={{0,4},{1,5},{2,6},{3,7},{4,0},{5,1},{6,2},{7,3},{8,12},{9,13},{10,... | collective-permute-start | bytes 135176 | tf_op jit(solution)/shard_map/ppermute | solution.py:262
  17.9 1.4 %collective-permute-start.8 = (bf16[88,256]{1,0:T(8,128)(2,1)S(1)}, bf16[88,256]{1,0:T(8,128)(2,1)S(1)}, u32[]{:S(2)}, u32[]{:S(2)}) collective-permute-start(bf16[88,256]{1,0:T(8,128)(2,1)S(1)} %get-tuple-element.52), channel_id=1, source_target_pairs={{0,6},{1,7},{2,4},{3,5},{4,2},{5,3},{6,0},{7,1},{8,14},{9,15},{10,... | collective-permute-start | bytes 135176 | tf_op jit(solution)/shard_map/ppermute | solution.py:262
  19.3 2.6 %collective-permute-start.9 = (bf16[88,256]{1,0:T(8,128)(2,1)S(1)}, bf16[88,256]{1,0:T(8,128)(2,1)S(1)}, u32[]{:S(2)}, u32[]{:S(2)}) collective-permute-start(bf16[88,256]{1,0:T(8,128)(2,1)S(1)} %get-tuple-element.53), channel_id=1, source_target_pairs={{0,5},{1,4},{2,7},{3,6},{4,1},{5,0},{6,3},{7,2},{8,13},{9,12},{10,... | collective-permute-start | bytes 135176 | tf_op jit(solution)/shard_map/ppermute | solution.py:262
  21.9 0.9 %collective-permute-start.10 = (bf16[88,256]{1,0:T(8,128)(2,1)S(1)}, bf16[88,256]{1,0:T(8,128)(2,1)S(1)}, u32[]{:S(2)}, u32[]{:S(2)}) collective-permute-start(bf16[88,256]{1,0:T(8,128)(2,1)S(1)} %get-tuple-element.54), channel_id=1, source_target_pairs={{0,7},{1,6},{2,5},{3,4},{4,3},{5,2},{6,1},{7,0},{8,15},{9,14},{10,... | collective-permute-start | bytes 135176 | tf_op jit(solution)/shard_map/ppermute | solution.py:262
  22.8 1.8 %collective-permute-start.11 = (bf16[88,256]{1,0:T(8,128)(2,1)S(1)}, bf16[88,256]{1,0:T(8,128)(2,1)S(1)}, u32[]{:S(2)}, u32[]{:S(2)}) collective-permute-start(bf16[88,256]{1,0:T(8,128)(2,1)S(1)} %get-tuple-element.55), channel_id=1, source_target_pairs={{0,3},{1,2},{2,1},{3,0},{4,7},{5,6},{6,5},{7,4},{8,11},{9,10},{10,... | collective-permute-start | bytes 135176 | tf_op jit(solution)/shard_map/ppermute | solution.py:262
  24.6 0.0 collective-permute-done.7.refs_1_
  24.6 0.5 %collective-permute-start.12 = (bf16[88,256]{1,0:T(8,128)(2,1)S(1)}, bf16[88,256]{1,0:T(8,128)(2,1)S(1)}, u32[]{:S(2)}, u32[]{:S(2)}) collective-permute-start(bf16[88,256]{1,0:T(8,128)(2,1)S(1)} %get-tuple-element.56), channel_id=1, source_target_pairs={{0,1},{1,0},{2,3},{3,2},{4,5},{5,4},{6,7},{7,6},{8,9},{9,8},{10,11... | collective-permute-start | bytes 135176 | tf_op jit(solution)/shard_map/ppermute | solution.py:262
  25.2 0.0 collective-permute-done.8.refs_2_
  25.2 1.1 %collective-permute-start.13 = (bf16[88,256]{1,0:T(8,128)(2,1)S(1)}, bf16[88,256]{1,0:T(8,128)(2,1)S(1)}, u32[]{:S(2)}, u32[]{:S(2)}) collective-permute-start(bf16[88,256]{1,0:T(8,128)(2,1)S(1)} %get-tuple-element.57), channel_id=1, source_target_pairs={{0,2},{1,3},{2,0},{3,1},{4,6},{5,7},{6,4},{7,5},{8,10},{9,11},{10,... | collective-permute-start | bytes 135176 | tf_op jit(solution)/shard_map/ppermute | solution.py:262
  26.3 1.5 %collective-permute-done.9.refs_3_ = bf16[88,256]{1,0:T(8,128)(2,1)S(1)} collective-permute-done((bf16[88,256]{1,0:T(8,128)(2,1)S(1)}, bf16[88,256]{1,0:T(8,128)(2,1)S(1)}, u32[]{:S(2)}, u32[]{:S(2)}) %collective-permute-start.9) | collective-permute-done | bytes 45088 | tf_op jit(solution)/shard_map/ppermute | solution.py:262
  27.8 0.6 %shard_map.108.refs_0_ = f32[640,256]{1,0:T(8,128)S(1)} custom-call(bf16[88,256]{1,0:T(8,128)(2,1)S(1)} %get-tuple-element.50.refs_0_, bf16[88,256]{1,0:T(8,128)(2,1)S(1)} %collective-permute-done.7.refs_1_, bf16[88,256]{1,0:T(8,128)(2,1)S(1)} %collective-permute-done.8.refs_2_, bf16[88,256]{1,0:T(8,128)(2,1)S(1)} %collective-permute-done.9.refs_3_), custom_call_target="tpu_custom_call" | custom-call | flops 268435456 | bytes 1024 | tf_op jit(solution)/shard_map/pallas_call | solution.py:245
  28.4 0.4 %collective-permute-done.10.refs_1_ = bf16[88,256]{1,0:T(8,128)(2,1)S(1)} collective-permute-done((bf16[88,256]{1,0:T(8,128)(2,1)S(1)}, bf16[88,256]{1,0:T(8,128)(2,1)S(1)}, u32[]{:S(2)}, u32[]{:S(2)}) %collective-permute-start.10) | collective-permute-done | bytes 45088 | tf_op jit(solution)/shard_map/ppermute | solution.py:262
  28.8 0.2 collective-permute-done.11.refs_2_
  29.0 0.5 %collective-permute-done.12.refs_3_ = bf16[88,256]{1,0:T(8,128)(2,1)S(1)} collective-permute-done((bf16[88,256]{1,0:T(8,128)(2,1)S(1)}, bf16[88,256]{1,0:T(8,128)(2,1)S(1)}, u32[]{:S(2)}, u32[]{:S(2)}) %collective-permute-start.12) | collective-permute-done | bytes 45088 | tf_op jit(solution)/shard_map/ppermute | solution.py:262
  29.5 0.0 collective-permute-done.13.refs_4_
  29.5 0.0 copy-done
  29.5 0.0 copy-done.1
  29.5 1.7 %shard_map.109 = (f32[640,256]{1,0:T(8,128)}, f32[640,256]{1,0:T(8,128)}) custom-call(f32[640,256]{1,0:T(8,128)S(1)} %shard_map.108.refs_0_, bf16[88,256]{1,0:T(8,128)(2,1)S(1)} %collective-permute-done.10.refs_1_, bf16[88,256]{1,0:T(8,128)(2,1)S(1)} %collective-permute-done.11.refs_2_, bf16[88,256]{1,0:T(8,128)(2,1)S(1)} %collective-permute-done.12.refs_3_, ...), custom_call_target="tpu_custom_call" | custom-call | tf_op jit(solution)/shard_map/pallas_call | solution.py:379
  (4 shorter events, 0.0 us)
Async XLA Ops:
  0.6 8.3 %collective-permute-start.1 = (bf16[320,256]{1,0:T(8,128)(2,1)}, bf16[320,256]{1,0:T(8,128)(2,1)S(1)}, u32[]{:S(2)}, u32[]{:S(2)}) collective-permute-start(bf16[320,256]{1,0:T(8,128)(2,1)} %refs_0_.5), channel_id=1, source_target_pairs={{0,16},{8,24},{16,0},{24,8},{1,17},{9,25},{17,1},{25,9},{2,18},{10... | collective-permute-start | bytes 491528 | tf_op jit(solution)/shard_map/ppermute | solution.py:262
  3.7 5.9 %collective-permute-start = (bf16[320,256]{1,0:T(8,128)(2,1)}, bf16[320,256]{1,0:T(8,128)(2,1)S(1)}, u32[]{:S(2)}, u32[]{:S(2)}) collective-permute-start(bf16[320,256]{1,0:T(8,128)(2,1)} %refs_0_.5), channel_id=1, source_target_pairs={{0,8},{8,0},{16,24},{24,16},{1,9},{9,1},{17,25},{25,17},{2,10},{10... | collective-permute-start | bytes 491528 | tf_op jit(solution)/shard_map/ppermute | solution.py:262
  3.7 5.3 %collective-permute-start.2 = (s32[320]{0:T(512)}, s32[320]{0:T(512)S(1)}, u32[]{:S(2)}, u32[]{:S(2)}) collective-permute-start(s32[320]{0:T(512)} %param.11), channel_id=1, source_target_pairs={{0,16},{8,24},{16,0},{24,8},{1,17},{9,25},{17,1},{25,9},{2,18},{10... | collective-permute-start | bytes 3848 | tf_op jit(solution)/shard_map/ppermute | solution.py:262
  3.8 7.8 %collective-permute-start.4 = (bf16[320,256]{1,0:T(8,128)(2,1)}, bf16[320,256]{1,0:T(8,128)(2,1)S(1)}, u32[]{:S(2)}, u32[]{:S(2)}) collective-permute-start(bf16[320,256]{1,0:T(8,128)(2,1)} %refs_0_.4), channel_id=1, source_target_pairs={{0,16},{8,24},{16,0},{24,8},{1,17},{9,25},{17,1},{25,9},{2,18},{10... | collective-permute-start | bytes 491528 | tf_op jit(solution)/shard_map/ppermute | solution.py:262
  7.1 1.9 %copy-start.4 = (s32[320]{0:T(512)S(1)}, s32[320]{0:T(512)}, u32[]{:S(2)}) copy-start(s32[320]{0:T(512)} %param.11) | copy-start | bytes 3844
  7.1 2.5 %copy-start.2 = (bf16[320,256]{1,0:T(8,128)(2,1)S(1)}, bf16[320,256]{1,0:T(8,128)(2,1)}, u32[]{:S(2)}) copy-start(bf16[320,256]{1,0:T(8,128)(2,1)} %refs_0_.4) | copy-start | bytes 491524
  7.1 2.5 %copy-start.3 = (bf16[320,256]{1,0:T(8,128)(2,1)S(1)}, bf16[320,256]{1,0:T(8,128)(2,1)}, u32[]{:S(2)}) copy-start(bf16[320,256]{1,0:T(8,128)(2,1)} %refs_0_.5) | copy-start | bytes 491524
  8.9 2.7 %collective-permute-start.5 = (bf16[320,256]{1,0:T(8,128)(2,1)S(1)}, bf16[320,256]{1,0:T(8,128)(2,1)S(1)}, u32[]{:S(2)}, u32[]{:S(2)}) collective-permute-start(bf16[320,256]{1,0:T(8,128)(2,1)S(1)} %collective-permute-done.1.refs_2_.refs_4_), channel_id=1, source_target_pairs={{0,8},{8,0},{16,24},{24,16},{1,9},{9,1},{17,25},{25,17},{2,10},{10... | collective-permute-start | bytes 491528 | tf_op jit(solution)/shard_map/ppermute | solution.py:262
  9.0 1.3 %collective-permute-start.3 = (s32[640]{0:T(1024)S(1)}, s32[640]{0:T(1024)S(1)}, u32[]{:S(2)}, u32[]{:S(2)}) collective-permute-start(s32[640]{0:T(1024)S(1)} %pad_add_fusion), channel_id=1, source_target_pairs={{0,8},{8,0},{16,24},{24,16},{1,9},{9,1},{17,25},{25,17},{2,10},{10... | collective-permute-start | bytes 7688 | tf_op jit(solution)/shard_map/ppermute | solution.py:262
  13.1 1.5 %collective-permute-start.6 = (bf16[320,256]{1,0:T(8,128)(2,1)S(1)}, bf16[320,256]{1,0:T(8,128)(2,1)S(1)}, u32[]{:S(2)}, u32[]{:S(2)}) collective-permute-start(bf16[320,256]{1,0:T(8,128)(2,1)S(1)} %get-tuple-element.43), channel_id=1, source_target_pairs={{0,8},{8,0},{16,24},{24,16},{1,9},{9,1},{17,25},{25,17},{2,10},{10... | collective-permute-start | bytes 491528 | tf_op jit(solution)/shard_map/ppermute | solution.py:262
  14.5 15.0 %copy-start = (f32[640,256]{1,0:T(8,128)S(1)}, f32[640,256]{1,0:T(8,128)}, u32[]{:S(2)}) copy-start(f32[640,256]{1,0:T(8,128)} %refs_5_.1) | copy-start | bytes 1966084
  14.5 15.0 %copy-start.1 = (f32[640,256]{1,0:T(8,128)S(1)}, f32[640,256]{1,0:T(8,128)}, u32[]{:S(2)}) copy-start(f32[640,256]{1,0:T(8,128)} %refs_6_.1) | copy-start | bytes 1966084
  15.1 9.5 %collective-permute-start.7 = (bf16[88,256]{1,0:T(8,128)(2,1)S(1)}, bf16[88,256]{1,0:T(8,128)(2,1)S(1)}, u32[]{:S(2)}, u32[]{:S(2)}) collective-permute-start(bf16[88,256]{1,0:T(8,128)(2,1)S(1)} %get-tuple-element.51), channel_id=1, source_target_pairs={{0,4},{1,5},{2,6},{3,7},{4,0},{5,1},{6,2},{7,3},{8,12},{9,13},{10,... | collective-permute-start | bytes 135176 | tf_op jit(solution)/shard_map/ppermute | solution.py:262
  17.9 7.2 %collective-permute-start.8 = (bf16[88,256]{1,0:T(8,128)(2,1)S(1)}, bf16[88,256]{1,0:T(8,128)(2,1)S(1)}, u32[]{:S(2)}, u32[]{:S(2)}) collective-permute-start(bf16[88,256]{1,0:T(8,128)(2,1)S(1)} %get-tuple-element.52), channel_id=1, source_target_pairs={{0,6},{1,7},{2,4},{3,5},{4,2},{5,3},{6,0},{7,1},{8,14},{9,15},{10,... | collective-permute-start | bytes 135176 | tf_op jit(solution)/shard_map/ppermute | solution.py:262
  19.3 8.5 %collective-permute-start.9 = (bf16[88,256]{1,0:T(8,128)(2,1)S(1)}, bf16[88,256]{1,0:T(8,128)(2,1)S(1)}, u32[]{:S(2)}, u32[]{:S(2)}) collective-permute-start(bf16[88,256]{1,0:T(8,128)(2,1)S(1)} %get-tuple-element.53), channel_id=1, source_target_pairs={{0,5},{1,4},{2,7},{3,6},{4,1},{5,0},{6,3},{7,2},{8,13},{9,12},{10,... | collective-permute-start | bytes 135176 | tf_op jit(solution)/shard_map/ppermute | solution.py:262
  21.9 6.9 %collective-permute-start.10 = (bf16[88,256]{1,0:T(8,128)(2,1)S(1)}, bf16[88,256]{1,0:T(8,128)(2,1)S(1)}, u32[]{:S(2)}, u32[]{:S(2)}) collective-permute-start(bf16[88,256]{1,0:T(8,128)(2,1)S(1)} %get-tuple-element.54), channel_id=1, source_target_pairs={{0,7},{1,6},{2,5},{3,4},{4,3},{5,2},{6,1},{7,0},{8,15},{9,14},{10,... | collective-permute-start | bytes 135176 | tf_op jit(solution)/shard_map/ppermute | solution.py:262
  22.8 6.2 %collective-permute-start.11 = (bf16[88,256]{1,0:T(8,128)(2,1)S(1)}, bf16[88,256]{1,0:T(8,128)(2,1)S(1)}, u32[]{:S(2)}, u32[]{:S(2)}) collective-permute-start(bf16[88,256]{1,0:T(8,128)(2,1)S(1)} %get-tuple-element.55), channel_id=1, source_target_pairs={{0,3},{1,2},{2,1},{3,0},{4,7},{5,6},{6,5},{7,4},{8,11},{9,10},{10,... | collective-permute-start | bytes 135176 | tf_op jit(solution)/shard_map/ppermute | solution.py:262
  24.6 4.9 %collective-permute-start.12 = (bf16[88,256]{1,0:T(8,128)(2,1)S(1)}, bf16[88,256]{1,0:T(8,128)(2,1)S(1)}, u32[]{:S(2)}, u32[]{:S(2)}) collective-permute-start(bf16[88,256]{1,0:T(8,128)(2,1)S(1)} %get-tuple-element.56), channel_id=1, source_target_pairs={{0,1},{1,0},{2,3},{3,2},{4,5},{5,4},{6,7},{7,6},{8,9},{9,8},{10,11... | collective-permute-start | bytes 135176 | tf_op jit(solution)/shard_map/ppermute | solution.py:262
  25.2 4.3 %collective-permute-start.13 = (bf16[88,256]{1,0:T(8,128)(2,1)S(1)}, bf16[88,256]{1,0:T(8,128)(2,1)S(1)}, u32[]{:S(2)}, u32[]{:S(2)}) collective-permute-start(bf16[88,256]{1,0:T(8,128)(2,1)S(1)} %get-tuple-element.57), channel_id=1, source_target_pairs={{0,2},{1,3},{2,0},{3,1},{4,6},{5,7},{6,4},{7,5},{8,10},{9,11},{10,... | collective-permute-start | bytes 135176 | tf_op jit(solution)/shard_map/ppermute | solution.py:262

commit v12 on v11

--- a/solution.py
+++ b/solution.py
@@ -131,7 +131,7 @@
 def main_kernel(early, late, *refs):
     n = early + late
     q_ref, far_ref, item_refs, refs = refs[0], refs[1], refs[2 : 2 + n], refs[2 + n :]
-    rate_ref, e_ref, tops_ref, sums_ref, mine_out, mate_out, *refs = refs
+    rate_ref, e_ref, tops_ref, sums_ref, weights_ref, mate_out, *refs = refs
     late_ref, factor_ref, far_e_ref = refs
     q, far = q_ref[...], far_ref[...]
     tops = [tops_ref[b : b + 1] for b in range(early)]
@@ -146,14 +146,17 @@
     mate = dot((e_ref[1] * factors[1]).astype(BF16), q)
     mate += dot((far_e_ref[1] * far_factors[1]).astype(BF16), far)
     mate_out[...] = code(mate * SCALE).astype(BF16) if mate_out.dtype == BF16 else mate
-    weights = e_ref[0] * factors[0]
-    weights = jnp.where(diagonal(q.shape[0]), weights - 1.0, weights)
-    mine = dot(weights.astype(BF16), q)
-    mine_out[...] = mine + dot((far_e_ref[0] * far_factors[0]).astype(BF16), far)
+    weights_ref[...] = (far_e_ref[0] * far_factors[0]).astype(BF16)
     chosen = tops_ref[early : early + 1] - sums_ref[early : early + 1]
     factor_ref[n : n + 1] = (top + jnp.log2(total) - chosen) * (1.0 / LOG2E)
     for b in range(n):
         factor_ref[b : b + 1] = factors[b]
+
+
+def mine_kernel(e_ref, factor_ref, weights_ref, q_ref, far_ref, out_ref):
+    weights = e_ref[0] * factor_ref[0:1]
+    weights = jnp.where(diagonal(weights.shape[0]), weights - 1.0, weights)
+    out_ref[...] = dot(weights.astype(BF16), q_ref[...]) + dot(weights_ref[...], far_ref[...])
 
 
 def more_kernel(n, q_ref, *refs):
@@ -234,7 +237,7 @@
         new_ref[1, here] = accum_new
         copies.append(pltpu.make_async_copy(new_ref.at[1, here], accum_out.at[here], sems.at[1, c]))
         copies[-1].start()
-        new_ref[0, here] = table_ref[here] - 0.1 * grad / (jnp.sqrt(accum_new) + 1e-08)
+        new_ref[0, here] = table_ref[here] - 0.1 * grad / (accum_new * lax.rsqrt(accum_new) + 1e-08)
         copies.append(pltpu.make_async_copy(new_ref.at[0, here], table_out.at[here], sems.at[0, c]))
         copies[-1].start()
     for copy in copies:
@@ -301,10 +304,10 @@
         mate_counts.reshape(1, -1),
         limit=8 + 4 * n,
     )
-    mine, mate, late_powers, factors = call(
+    weights, mate, late_powers, factors = call(
         functools.partial(main_kernel, early, late),
         [
-            part,
+            (square, BF16),
             part if far_queries[1:] else sent,
             ((late, *square), F32),
             rows_of,
@@ -318,6 +321,9 @@
         totals,
         scratch=[pltpu.VMEM((2, *square), F32)],
         limit=8 + 4 * n,
+    )
+    (mine,) = call(
+        mine_kernel, [part], powers, factors, weights, queries, far_queries[0], flops=1 << 28
     )
     for k, far in enumerate(far_queries[1:], 2):
         mine, mate = call(
@@ -342,7 +348,6 @@
         limit=8 + 2 * n,
         flops=1 << 30,
     )
-    other, query_grad = lax.optimization_barrier((other, query_grad))
     if paired:
         packets = [((slots + TAIL, D), BF16)] * groups
     else:

time: 31.4 us -> 31.7 us (level)
    pallas_call x7 -> x8, Pallas kernels: 5.58 us -> 5.91 us  [call(): pl.pallas_call(kernel, out_shape=[jax.ShapeDtypeStruct(s, t) for s, t in...]
  transfers between devices with their start and end apart: 14 -> 14, of which waited for: 8 -> 6; matrix products, arithmetic and copies ran while one was open for 5% -> 5% of each run, Pallas kernels for 12% -> 13%
where the time goes in v12:
time: 31.7 us; the launch traced here: 31.5 us
  starting transfers between devices  16.9 us (53%)
  Pallas kernels  7.53 us (24%)
  waiting for transfers between devices  4.86 us (15%)
  other arithmetic  1.46 us (5%)
  between operations  0.73 us (2%)
    ppermute x14, starting transfers between devices, swap(): lax.ppermute(x, axis, [(i, i ^ k) for i in range(lax.axis_size(axis))])  16.9 us
    pallas_call x8, Pallas kernels, call(): pl.pallas_call(kernel, out_shape=[jax.ShapeDtypeStruct(s, t) for s, t in...  5.91 us
    ppermute x14, waiting for transfers between devices, swap(): lax.ppermute(x, axis, [(i, i ^ k) for i in range(lax.axis_size(axis))])  4.86 us
    pallas_call x1, Pallas kernels, shards(): pl.pallas_call(functools.partial(update_kernel, slots, paired), out_shape...  1.62 us
    mul x1, other arithmetic, shards(): owner * ROW_CODES + item_offset.reshape(1, block)  0.7 us
    add x1, other arithmetic, shards(): owner * ROW_CODES + item_offset.reshape(1, block)  0.68 us
  transfers between devices with their start and end apart: 14, of which 6 were waited for; matrix products, arithmetic and copies ran while one was open for 5% of the time, Pallas kernels for 13%

profile of v12, /device:TPU:0, one launch (start us, length us, event | category | flops | bytes accessed | tf_op | source)
XLA Modules:
  0.0 31.5 jit_solution(5708568118254185191)
XLA Ops:
  0.6 0.5 %collective-permute-start = (bf16[320,256]{1,0:T(8,128)(2,1)}, bf16[320,256]{1,0:T(8,128)(2,1)S(1)}, u32[]{:S(2)}, u32[]{:S(2)}) collective-permute-start(bf16[320,256]{1,0:T(8,128)(2,1)} %refs_0_.5), channel_id=1, source_target_pairs={{0,8},{8,0},{16,24},{24,16},{1,9},{9,1},{17,25},{25,17},{2,10},{10... | collective-permute-start | bytes 491528 | tf_op jit(solution)/shard_map/ppermute | solution.py:265
  1.1 2.6 %collective-permute-start.1 = (bf16[320,256]{1,0:T(8,128)(2,1)}, bf16[320,256]{1,0:T(8,128)(2,1)S(1)}, u32[]{:S(2)}, u32[]{:S(2)}) collective-permute-start(bf16[320,256]{1,0:T(8,128)(2,1)} %refs_0_.5), channel_id=1, source_target_pairs={{0,16},{8,24},{16,0},{24,8},{1,17},{9,25},{17,1},{25,9},{2,18},{10... | collective-permute-start | bytes 491528 | tf_op jit(solution)/shard_map/ppermute | solution.py:265
  3.7 0.1 collective-permute-start.2
  3.8 1.9 %collective-permute-start.4 = (bf16[320,256]{1,0:T(8,128)(2,1)}, bf16[320,256]{1,0:T(8,128)(2,1)S(1)}, u32[]{:S(2)}, u32[]{:S(2)}) collective-permute-start(bf16[320,256]{1,0:T(8,128)(2,1)} %q_ref.3), channel_id=1, source_target_pairs={{0,16},{8,24},{16,0},{24,8},{1,17},{9,25},{17,1},{25,9},{2,18},{10... | collective-permute-start | bytes 491528 | tf_op jit(solution)/shard_map/ppermute | solution.py:265
  5.8 0.7 %multiply_reduce_fusion = s32[320]{0:T(512)S(1)} fusion(s32[320,1]{0,1:T(1,128)} %param.9, s32[]{:T(128)S(6)} %axis_index.12), kind=kLoop, calls=%fused_computation.1 | loop fusion | flops 640 | bytes 2564 | tf_op jit(solution)/shard_map/mul | solution.py:277
  6.5 0.7 %add.5 = s32[320]{0:T(512)S(1)} add(s32[320]{0:T(512)S(1)} %multiply_reduce_fusion, s32[320]{0:T(512)} %param.10) | non-fusion elementwise | flops 320 | bytes 3840 | tf_op jit(solution)/shard_map/add | solution.py:277
  7.2 0.0 copy-start.4
  7.2 0.0 copy-start
  7.2 0.0 copy-start.3
  7.2 0.8 %shard_map.102 = (bf16[640,320]{1,0:T(8,128)(2,1)S(1)}, bf16[8,8,256]{2,1,0:T(8,128)(2,1)S(1)}) custom-call(s32[1,320]{1,0:T(1,128)S(1)} %add.6.code_ref), custom_call_target="tpu_custom_call" | custom-call | flops 1073741824 | bytes 1024 | tf_op jit(solution)/shard_map/pallas_call | solution.py:248
  8.0 1.1 %collective-permute-done.2 = s32[320]{0:T(512)S(1)} collective-permute-done((s32[320]{0:T(512)}, s32[320]{0:T(512)S(1)}, u32[]{:S(2)}, u32[]{:S(2)}) %collective-permute-start.2) | collective-permute-done | bytes 1312 | tf_op jit(solution)/shard_map/ppermute | solution.py:265
  9.1 0.0 collective-permute-done.1.refs_2_.refs_4_
  9.1 0.0 collective-permute-start.5
  9.1 0.0 copy-done.4
  9.1 0.1 pad_add_fusion
  9.1 0.5 %collective-permute-start.3 = (s32[640]{0:T(1024)S(1)}, s32[640]{0:T(1024)S(1)}, u32[]{:S(2)}, u32[]{:S(2)}) collective-permute-start(s32[640]{0:T(1024)S(1)} %pad_add_fusion), channel_id=1, source_target_pairs={{0,8},{8,0},{16,24},{24,16},{1,9},{9,1},{17,25},{25,17},{2,10},{10... | collective-permute-start | bytes 7688 | tf_op jit(solution)/shard_map/ppermute | solution.py:265
  9.6 0.0 collective-permute-done.refs_1_.refs_3_
  9.6 0.0 copy-done
  9.7 0.0 copy-done.3
  9.7 0.5 %shard_map.103 = (f32[3,320,320]{2,1,0:T(8,128)S(1)}, f32[8,320]{1,0:T(8,128)S(1)}) custom-call(bf16[320,256]{1,0:T(8,128)(2,1)S(1)} %copy-done, bf16[320,256]{1,0:T(8,128)(2,1)S(1)} %copy-done.3, bf16[320,256]{1,0:T(8,128)(2,1)S(1)} %collective-permute-done.refs_1_.refs_3_, bf16[320,256]{1,0:T(8,128)(2,1)S(1)} %collective-permute-done.1.refs_2_.refs_4_), custom_call_target="tpu_custom_call" | custom-call | flops 536870912 | bytes 1024 | tf_op jit(solution)/shard_map/pallas_call | solution.py:248
  10.2 0.3 collective-permute-done.3
  10.5 0.4 %shard_map.104 = (f32[4,320,128]{2,1,0:T(8,128)S(1)}, f32[3,320,320]{2,1,0:T(8,128)S(1)}, f32[8,320]{1,0:T(8,128)S(1)}) custom-call(f32[3,320,320]{2,1,0:T(8,128)S(1)} %get-tuple-element.32.e_ref, s32[1,640]{1,0:T(1,128)S(1)} %reshape.24.near_ref, s32[1,640]{1,0:T(1,128)S(1)} %reshape.25.mate_ref), custom_call_target="tpu_custom_call" | custom-call | bytes 1024 | tf_op jit(solution)/shard_map/pallas_call | solution.py:248
  10.8 1.5 %collective-permute-done.4.refs_1_.far_ref = bf16[320,256]{1,0:T(8,128)(2,1)S(1)} collective-permute-done((bf16[320,256]{1,0:T(8,128)(2,1)}, bf16[320,256]{1,0:T(8,128)(2,1)S(1)}, u32[]{:S(2)}, u32[]{:S(2)}) %collective-permute-start.4) | collective-permute-done | bytes 163872 | tf_op jit(solution)/shard_map/ppermute | solution.py:265
  12.3 0.0 collective-permute-done.5.refs_5_.refs_3_
  12.3 1.5 %shard_map.105 = (bf16[320,320]{1,0:T(8,128)(2,1)S(1)}, bf16[320,256]{1,0:T(8,128)(2,1)S(1)}, f32[1,320,320]{2,1,0:T(8,128)S(1)}, f32[8,320]{1,0:T(8,128)S(1)}) custom-call(bf16[320,256]{1,0:T(8,128)(2,1)S(1)} %copy-done, bf16[320,256]{1,0:T(8,128)(2,1)S(1)} %collective-permute-done.4.refs_1_.far_ref, bf16[320,256]{1,0:T(8,128)(2,1)S(1)} %copy-done.3, ...), custom_call_target="tpu_custom_call" | custom-call | bytes 1024 | tf_op jit(solution)/shard_map/pallas_call | solution.py:248
  13.8 0.1 collective-permute-start.6
  13.9 0.3 %shard_map.107.mine_ref = f32[320,256]{1,0:T(8,128)S(1)} custom-call(f32[3,320,320]{2,1,0:T(8,128)S(1)} %get-tuple-element.34.refs_7_.e_ref, f32[8,320]{1,0:T(8,128)S(1)} %get-tuple-element.39.factor_ref, bf16[320,320]{1,0:T(8,128)(2,1)S(1)} %get-tuple-element.44.weights_ref, bf16[320,256]{1,0:T(8,128)(2,1)S(1)} %copy-done, ...), custom_call_target="tpu_custom_call" | custom-call | flops 268435456 | bytes 1024 | tf_op jit(solution)/shard_map/pallas_call | solution.py:248
  14.2 1.1 %collective-permute-done.6.other_ref = bf16[320,256]{1,0:T(8,128)(2,1)S(1)} collective-permute-done((bf16[320,256]{1,0:T(8,128)(2,1)S(1)}, bf16[320,256]{1,0:T(8,128)(2,1)S(1)}, u32[]{:S(2)}, u32[]{:S(2)}) %collective-permute-start.6) | collective-permute-done | bytes 163872 | tf_op jit(solution)/shard_map/ppermute | solution.py:265
  15.3 0.5 %shard_map.108 = (bf16[88,256]{1,0:T(8,128)(2,1)S(1)}, bf16[88,256]{1,0:T(8,128)(2,1)S(1)}, bf16[88,256]{1,0:T(8,128)(2,1)S(1)}, bf16[88,256]{1,0:T(8,128)(2,1)S...) custom-call(bf16[640,320]{1,0:T(8,128)(2,1)S(1)} %get-tuple-element., ...), custom_call_target="tpu_custom_call" | custom-call | bytes 1024 | tf_op jit(solution)/shard_map/pallas_call | solution.py:248
  15.7 2.9 %collective-permute-start.7 = (bf16[88,256]{1,0:T(8,128)(2,1)S(1)}, bf16[88,256]{1,0:T(8,128)(2,1)S(1)}, u32[]{:S(2)}, u32[]{:S(2)}) collective-permute-start(bf16[88,256]{1,0:T(8,128)(2,1)S(1)} %get-tuple-element.47), channel_id=1, source_target_pairs={{0,4},{1,5},{2,6},{3,7},{4,0},{5,1},{6,2},{7,3},{8,12},{9,13},{10,... | collective-permute-start | bytes 135176 | tf_op jit(solution)/shard_map/ppermute | solution.py:265
  18.6 1.4 %collective-permute-start.8 = (bf16[88,256]{1,0:T(8,128)(2,1)S(1)}, bf16[88,256]{1,0:T(8,128)(2,1)S(1)}, u32[]{:S(2)}, u32[]{:S(2)}) collective-permute-start(bf16[88,256]{1,0:T(8,128)(2,1)S(1)} %get-tuple-element.48), channel_id=1, source_target_pairs={{0,6},{1,7},{2,4},{3,5},{4,2},{5,3},{6,0},{7,1},{8,14},{9,15},{10,... | collective-permute-start | bytes 135176 | tf_op jit(solution)/shard_map/ppermute | solution.py:265
  20.0 2.6 %collective-permute-start.9 = (bf16[88,256]{1,0:T(8,128)(2,1)S(1)}, bf16[88,256]{1,0:T(8,128)(2,1)S(1)}, u32[]{:S(2)}, u32[]{:S(2)}) collective-permute-start(bf16[88,256]{1,0:T(8,128)(2,1)S(1)} %get-tuple-element.49), channel_id=1, source_target_pairs={{0,5},{1,4},{2,7},{3,6},{4,1},{5,0},{6,3},{7,2},{8,13},{9,12},{10,... | collective-permute-start | bytes 135176 | tf_op jit(solution)/shard_map/ppermute | solution.py:265
  22.6 0.9 %collective-permute-start.10 = (bf16[88,256]{1,0:T(8,128)(2,1)S(1)}, bf16[88,256]{1,0:T(8,128)(2,1)S(1)}, u32[]{:S(2)}, u32[]{:S(2)}) collective-permute-start(bf16[88,256]{1,0:T(8,128)(2,1)S(1)} %get-tuple-element.50), channel_id=1, source_target_pairs={{0,7},{1,6},{2,5},{3,4},{4,3},{5,2},{6,1},{7,0},{8,15},{9,14},{10,... | collective-permute-start | bytes 135176 | tf_op jit(solution)/shard_map/ppermute | solution.py:265
  23.5 1.8 %collective-permute-start.11 = (bf16[88,256]{1,0:T(8,128)(2,1)S(1)}, bf16[88,256]{1,0:T(8,128)(2,1)S(1)}, u32[]{:S(2)}, u32[]{:S(2)}) collective-permute-start(bf16[88,256]{1,0:T(8,128)(2,1)S(1)} %get-tuple-element.51), channel_id=1, source_target_pairs={{0,3},{1,2},{2,1},{3,0},{4,7},{5,6},{6,5},{7,4},{8,11},{9,10},{10,... | collective-permute-start | bytes 135176 | tf_op jit(solution)/shard_map/ppermute | solution.py:265
  25.3 0.0 collective-permute-done.7.refs_1_
  25.3 0.5 %collective-permute-start.12 = (bf16[88,256]{1,0:T(8,128)(2,1)S(1)}, bf16[88,256]{1,0:T(8,128)(2,1)S(1)}, u32[]{:S(2)}, u32[]{:S(2)}) collective-permute-start(bf16[88,256]{1,0:T(8,128)(2,1)S(1)} %get-tuple-element.52), channel_id=1, source_target_pairs={{0,1},{1,0},{2,3},{3,2},{4,5},{5,4},{6,7},{7,6},{8,9},{9,8},{10,11... | collective-permute-start | bytes 135176 | tf_op jit(solution)/shard_map/ppermute | solution.py:265
  25.8 0.0 collective-permute-done.8.refs_2_
  25.9 1.1 %collective-permute-start.13 = (bf16[88,256]{1,0:T(8,128)(2,1)S(1)}, bf16[88,256]{1,0:T(8,128)(2,1)S(1)}, u32[]{:S(2)}, u32[]{:S(2)}) collective-permute-start(bf16[88,256]{1,0:T(8,128)(2,1)S(1)} %get-tuple-element.53), channel_id=1, source_target_pairs={{0,2},{1,3},{2,0},{3,1},{4,6},{5,7},{6,4},{7,5},{8,10},{9,11},{10,... | collective-permute-start | bytes 135176 | tf_op jit(solution)/shard_map/ppermute | solution.py:265
  27.0 1.3 %shard_map.106 = (f32[320,256]{1,0:T(8,128)}, f32[320]{0:T(512)}) custom-call(f32[3,320,320]{2,1,0:T(8,128)S(1)} %get-tuple-element.34.refs_7_.e_ref, f32[1,320,320]{2,1,0:T(8,128)S(1)} %get-tuple-element.38.late_ref, f32[8,320]{1,0:T(8,128)S(1)} %get-tuple-element.39.factor_ref, bf16[320,256]{1,0:T(8,128)(2,1)S(1)} %copy-done.3, ...), custom_call_target="tpu_custom_call" | custom-call | flops 1073741824 | bytes 1024 | tf_op jit(solution)/shard_map/pallas_call | solution.py:248
  28.3 0.0 collective-permute-done.9.refs_3_
  28.3 0.6 %shard_map.109.refs_0_ = f32[640,256]{1,0:T(8,128)S(1)} custom-call(bf16[88,256]{1,0:T(8,128)(2,1)S(1)} %get-tuple-element.46.refs_0_, bf16[88,256]{1,0:T(8,128)(2,1)S(1)} %collective-permute-done.7.refs_1_, bf16[88,256]{1,0:T(8,128)(2,1)S(1)} %collective-permute-done.8.refs_2_, bf16[88,256]{1,0:T(8,128)(2,1)S(1)} %collective-permute-done.9.refs_3_), custom_call_target="tpu_custom_call" | custom-call | flops 268435456 | bytes 1024 | tf_op jit(solution)/shard_map/pallas_call | solution.py:248
  28.9 0.6 %collective-permute-done.10.refs_1_ = bf16[88,256]{1,0:T(8,128)(2,1)S(1)} collective-permute-done((bf16[88,256]{1,0:T(8,128)(2,1)S(1)}, bf16[88,256]{1,0:T(8,128)(2,1)S(1)}, u32[]{:S(2)}, u32[]{:S(2)}) %collective-permute-start.10) | collective-permute-done | bytes 45088 | tf_op jit(solution)/shard_map/ppermute | solution.py:265
  29.5 0.0 collective-permute-done.11.refs_2_
  29.5 0.4 %collective-permute-done.12.refs_3_ = bf16[88,256]{1,0:T(8,128)(2,1)S(1)} collective-permute-done((bf16[88,256]{1,0:T(8,128)(2,1)S(1)}, bf16[88,256]{1,0:T(8,128)(2,1)S(1)}, u32[]{:S(2)}, u32[]{:S(2)}) %collective-permute-start.12) | collective-permute-done | bytes 45088 | tf_op jit(solution)/shard_map/ppermute | solution.py:265
  29.9 0.0 collective-permute-done.13.refs_4_
  29.9 0.0 copy-done.1
  29.9 0.0 copy-done.2
  29.9 1.6 %shard_map.110 = (f32[640,256]{1,0:T(8,128)}, f32[640,256]{1,0:T(8,128)}) custom-call(f32[640,256]{1,0:T(8,128)S(1)} %shard_map.109.refs_0_, bf16[88,256]{1,0:T(8,128)(2,1)S(1)} %collective-permute-done.10.refs_1_, bf16[88,256]{1,0:T(8,128)(2,1)S(1)} %collective-permute-done.11.refs_2_, bf16[88,256]{1,0:T(8,128)(2,1)S(1)} %collective-permute-done.12.refs_3_, ...), custom_call_target="tpu_custom_call" | custom-call | tf_op jit(solution)/shard_map/pallas_call | solution.py:384
  (5 shorter events, 0.0 us)
Async XLA Ops:
  0.6 9.0 %collective-permute-start = (bf16[320,256]{1,0:T(8,128)(2,1)}, bf16[320,256]{1,0:T(8,128)(2,1)S(1)}, u32[]{:S(2)}, u32[]{:S(2)}) collective-permute-start(bf16[320,256]{1,0:T(8,128)(2,1)} %refs_0_.5), channel_id=1, source_target_pairs={{0,8},{8,0},{16,24},{24,16},{1,9},{9,1},{17,25},{25,17},{2,10},{10... | collective-permute-start | bytes 491528 | tf_op jit(solution)/shard_map/ppermute | solution.py:265
  1.1 7.9 %collective-permute-start.1 = (bf16[320,256]{1,0:T(8,128)(2,1)}, bf16[320,256]{1,0:T(8,128)(2,1)S(1)}, u32[]{:S(2)}, u32[]{:S(2)}) collective-permute-start(bf16[320,256]{1,0:T(8,128)(2,1)} %refs_0_.5), channel_id=1, source_target_pairs={{0,16},{8,24},{16,0},{24,8},{1,17},{9,25},{17,1},{25,9},{2,18},{10... | collective-permute-start | bytes 491528 | tf_op jit(solution)/shard_map/ppermute | solution.py:265
  3.7 5.3 %collective-permute-start.2 = (s32[320]{0:T(512)}, s32[320]{0:T(512)S(1)}, u32[]{:S(2)}, u32[]{:S(2)}) collective-permute-start(s32[320]{0:T(512)} %param.11), channel_id=1, source_target_pairs={{0,16},{8,24},{16,0},{24,8},{1,17},{9,25},{17,1},{25,9},{2,18},{10... | collective-permute-start | bytes 3848 | tf_op jit(solution)/shard_map/ppermute | solution.py:265
  3.8 8.5 %collective-permute-start.4 = (bf16[320,256]{1,0:T(8,128)(2,1)}, bf16[320,256]{1,0:T(8,128)(2,1)S(1)}, u32[]{:S(2)}, u32[]{:S(2)}) collective-permute-start(bf16[320,256]{1,0:T(8,128)(2,1)} %q_ref.3), channel_id=1, source_target_pairs={{0,16},{8,24},{16,0},{24,8},{1,17},{9,25},{17,1},{25,9},{2,18},{10... | collective-permute-start | bytes 491528 | tf_op jit(solution)/shard_map/ppermute | solution.py:265
  7.2 1.9 %copy-start.4 = (s32[320]{0:T(512)S(1)}, s32[320]{0:T(512)}, u32[]{:S(2)}) copy-start(s32[320]{0:T(512)} %param.11) | copy-start | bytes 3844
  7.2 2.5 %copy-start = (bf16[320,256]{1,0:T(8,128)(2,1)S(1)}, bf16[320,256]{1,0:T(8,128)(2,1)}, u32[]{:S(2)}) copy-start(bf16[320,256]{1,0:T(8,128)(2,1)} %q_ref.3) | copy-start | bytes 491524
  7.2 2.5 %copy-start.3 = (bf16[320,256]{1,0:T(8,128)(2,1)S(1)}, bf16[320,256]{1,0:T(8,128)(2,1)}, u32[]{:S(2)}) copy-start(bf16[320,256]{1,0:T(8,128)(2,1)} %refs_0_.5) | copy-start | bytes 491524
  9.1 3.2 %collective-permute-start.5 = (bf16[320,256]{1,0:T(8,128)(2,1)S(1)}, bf16[320,256]{1,0:T(8,128)(2,1)S(1)}, u32[]{:S(2)}, u32[]{:S(2)}) collective-permute-start(bf16[320,256]{1,0:T(8,128)(2,1)S(1)} %collective-permute-done.1.refs_2_.refs_4_), channel_id=1, source_target_pairs={{0,8},{8,0},{16,24},{24,16},{1,9},{9,1},{17,25},{25,17},{2,10},{10... | collective-permute-start | bytes 491528 | tf_op jit(solution)/shard_map/ppermute | solution.py:265
  9.1 1.3 %collective-permute-start.3 = (s32[640]{0:T(1024)S(1)}, s32[640]{0:T(1024)S(1)}, u32[]{:S(2)}, u32[]{:S(2)}) collective-permute-start(s32[640]{0:T(1024)S(1)} %pad_add_fusion), channel_id=1, source_target_pairs={{0,8},{8,0},{16,24},{24,16},{1,9},{9,1},{17,25},{25,17},{2,10},{10... | collective-permute-start | bytes 7688 | tf_op jit(solution)/shard_map/ppermute | solution.py:265
  13.8 1.5 %collective-permute-start.6 = (bf16[320,256]{1,0:T(8,128)(2,1)S(1)}, bf16[320,256]{1,0:T(8,128)(2,1)S(1)}, u32[]{:S(2)}, u32[]{:S(2)}) collective-permute-start(bf16[320,256]{1,0:T(8,128)(2,1)S(1)} %get-tuple-element.45), channel_id=1, source_target_pairs={{0,8},{8,0},{16,24},{24,16},{1,9},{9,1},{17,25},{25,17},{2,10},{10... | collective-permute-start | bytes 491528 | tf_op jit(solution)/shard_map/ppermute | solution.py:265
  15.7 9.6 %collective-permute-start.7 = (bf16[88,256]{1,0:T(8,128)(2,1)S(1)}, bf16[88,256]{1,0:T(8,128)(2,1)S(1)}, u32[]{:S(2)}, u32[]{:S(2)}) collective-permute-start(bf16[88,256]{1,0:T(8,128)(2,1)S(1)} %get-tuple-element.47), channel_id=1, source_target_pairs={{0,4},{1,5},{2,6},{3,7},{4,0},{5,1},{6,2},{7,3},{8,12},{9,13},{10,... | collective-permute-start | bytes 135176 | tf_op jit(solution)/shard_map/ppermute | solution.py:265
  18.6 7.2 %collective-permute-start.8 = (bf16[88,256]{1,0:T(8,128)(2,1)S(1)}, bf16[88,256]{1,0:T(8,128)(2,1)S(1)}, u32[]{:S(2)}, u32[]{:S(2)}) collective-permute-start(bf16[88,256]{1,0:T(8,128)(2,1)S(1)} %get-tuple-element.48), channel_id=1, source_target_pairs={{0,6},{1,7},{2,4},{3,5},{4,2},{5,3},{6,0},{7,1},{8,14},{9,15},{10,... | collective-permute-start | bytes 135176 | tf_op jit(solution)/shard_map/ppermute | solution.py:265
  20.0 8.3 %collective-permute-start.9 = (bf16[88,256]{1,0:T(8,128)(2,1)S(1)}, bf16[88,256]{1,0:T(8,128)(2,1)S(1)}, u32[]{:S(2)}, u32[]{:S(2)}) collective-permute-start(bf16[88,256]{1,0:T(8,128)(2,1)S(1)} %get-tuple-element.49), channel_id=1, source_target_pairs={{0,5},{1,4},{2,7},{3,6},{4,1},{5,0},{6,3},{7,2},{8,13},{9,12},{10,... | collective-permute-start | bytes 135176 | tf_op jit(solution)/shard_map/ppermute | solution.py:265
  22.6 6.9 %collective-permute-start.10 = (bf16[88,256]{1,0:T(8,128)(2,1)S(1)}, bf16[88,256]{1,0:T(8,128)(2,1)S(1)}, u32[]{:S(2)}, u32[]{:S(2)}) collective-permute-start(bf16[88,256]{1,0:T(8,128)(2,1)S(1)} %get-tuple-element.50), channel_id=1, source_target_pairs={{0,7},{1,6},{2,5},{3,4},{4,3},{5,2},{6,1},{7,0},{8,15},{9,14},{10,... | collective-permute-start | bytes 135176 | tf_op jit(solution)/shard_map/ppermute | solution.py:265
  23.5 6.0 %collective-permute-start.11 = (bf16[88,256]{1,0:T(8,128)(2,1)S(1)}, bf16[88,256]{1,0:T(8,128)(2,1)S(1)}, u32[]{:S(2)}, u32[]{:S(2)}) collective-permute-start(bf16[88,256]{1,0:T(8,128)(2,1)S(1)} %get-tuple-element.51), channel_id=1, source_target_pairs={{0,3},{1,2},{2,1},{3,0},{4,7},{5,6},{6,5},{7,4},{8,11},{9,10},{10,... | collective-permute-start | bytes 135176 | tf_op jit(solution)/shard_map/ppermute | solution.py:265
  25.3 4.6 %collective-permute-start.12 = (bf16[88,256]{1,0:T(8,128)(2,1)S(1)}, bf16[88,256]{1,0:T(8,128)(2,1)S(1)}, u32[]{:S(2)}, u32[]{:S(2)}) collective-permute-start(bf16[88,256]{1,0:T(8,128)(2,1)S(1)} %get-tuple-element.52), channel_id=1, source_target_pairs={{0,1},{1,0},{2,3},{3,2},{4,5},{5,4},{6,7},{7,6},{8,9},{9,8},{10,11... | collective-permute-start | bytes 135176 | tf_op jit(solution)/shard_map/ppermute | solution.py:265
  25.9 4.1 %collective-permute-start.13 = (bf16[88,256]{1,0:T(8,128)(2,1)S(1)}, bf16[88,256]{1,0:T(8,128)(2,1)S(1)}, u32[]{:S(2)}, u32[]{:S(2)}) collective-permute-start(bf16[88,256]{1,0:T(8,128)(2,1)S(1)} %get-tuple-element.53), channel_id=1, source_target_pairs={{0,2},{1,3},{2,0},{3,1},{4,6},{5,7},{6,4},{7,5},{8,10},{9,11},{10,... | collective-permute-start | bytes 135176 | tf_op jit(solution)/shard_map/ppermute | solution.py:265
  27.0 2.9 %copy-start.1 = (f32[640,256]{1,0:T(8,128)S(1)}, f32[640,256]{1,0:T(8,128)}, u32[]{:S(2)}) copy-start(f32[640,256]{1,0:T(8,128)} %refs_5_.1) | copy-start | bytes 1966084
  27.0 2.9 %copy-start.2 = (f32[640,256]{1,0:T(8,128)S(1)}, f32[640,256]{1,0:T(8,128)}, u32[]{:S(2)}) copy-start(f32[640,256]{1,0:T(8,128)} %refs_6_.1) | copy-start | bytes 1966084

commit v13 on v11

--- a/solution.py
+++ b/solution.py
@@ -234,7 +234,7 @@
         new_ref[1, here] = accum_new
         copies.append(pltpu.make_async_copy(new_ref.at[1, here], accum_out.at[here], sems.at[1, c]))
         copies[-1].start()
-        new_ref[0, here] = table_ref[here] - 0.1 * grad / (jnp.sqrt(accum_new) + 1e-08)
+        new_ref[0, here] = table_ref[here] - 0.1 * grad / (accum_new * lax.rsqrt(accum_new) + 1e-08)
         copies.append(pltpu.make_async_copy(new_ref.at[0, here], table_out.at[here], sems.at[0, c]))
         copies[-1].start()
     for copy in copies:
@@ -268,14 +268,16 @@
     owner = item_owner.reshape(1, block)
     if paired:
         owner = owner ^ lax.axis_index("group")
+    codes = owner * ROW_CODES + item_offset.reshape(1, block)
+    codes, own_items = lax.optimization_barrier((codes, items))
     pick, tail = call(
         functools.partial(local_kernel, groups, slots),
         [((groups * slots, block), BF16), ((groups, TAIL, D), BF16)],
-        owner * ROW_CODES + item_offset.reshape(1, block),
+        codes,
         flops=1 << 30,
     )
     far_items, far_counts, tail = lax.optimization_barrier((far_items, far_counts, tail))
-    item_blocks = [items, swap(items, 1)] + far_items
+    item_blocks = [items, swap(own_items, 1)] + far_items
     early = len(item_blocks)
     item_blocks += [swap(x, 1) for x in far_items]
     late = n - early

time: 31.4 us -> 31.9 us (1.016)
  waiting for transfers between devices: 4.87 us -> 5.35 us
    ppermute x14, waiting for transfers between devices: 4.87 us -> 5.35 us  [swap(): lax.ppermute(x, axis, [(i, i ^ k) for i in range(lax.axis_size(axis))])]
  transfers between devices with their start and end apart: 14 -> 14, of which waited for: 8 -> 8; matrix products, arithmetic and copies ran while one was open for 5% -> 5% of each run, Pallas kernels for 12% -> 11%
where the time goes in v13:
time: 31.9 us; the launch traced here: 31.8 us
  starting transfers between devices  17 us (53%)
  Pallas kernels  7.19 us (23%)
  waiting for transfers between devices  5.35 us (17%)
  other arithmetic  1.46 us (5%)
  between operations  0.72 us (2%)
    ppermute x14, starting transfers between devices, swap(): lax.ppermute(x, axis, [(i, i ^ k) for i in range(lax.axis_size(axis))])  17 us
    pallas_call x7, Pallas kernels, call(): pl.pallas_call(kernel, out_shape=[jax.ShapeDtypeStruct(s, t) for s, t in...  5.57 us
    ppermute x14, waiting for transfers between devices, swap(): lax.ppermute(x, axis, [(i, i ^ k) for i in range(lax.axis_size(axis))])  5.35 us
    pallas_call x1, Pallas kernels, shards(): pl.pallas_call(functools.partial(update_kernel, slots, paired), out_shape...  1.62 us
    mul x1, other arithmetic, shards(): codes = owner * ROW_CODES + item_offset.reshape(1, block)  0.7 us
    add x1, other arithmetic, shards(): codes = owner * ROW_CODES + item_offset.reshape(1, block)  0.68 us
  transfers between devices with their start and end apart: 14, of which 8 were waited for; matrix products, arithmetic and copies ran while one was open for 5% of the time, Pallas kernels for 11%

profile of v13, /device:TPU:0, one launch (start us, length us, event | category | flops | bytes accessed | tf_op | source)
XLA Modules:
  0.0 31.8 jit_solution(7830107290632087839)
XLA Ops:
  0.6 3.0 %collective-permute-start.1 = (bf16[320,256]{1,0:T(8,128)(2,1)}, bf16[320,256]{1,0:T(8,128)(2,1)S(1)}, u32[]{:S(2)}, u32[]{:S(2)}) collective-permute-start(bf16[320,256]{1,0:T(8,128)(2,1)} %refs_0_.5), channel_id=1, source_target_pairs={{0,16},{8,24},{16,0},{24,8},{1,17},{9,25},{17,1},{25,9},{2,18},{10... | collective-permute-start | bytes 491528 | tf_op jit(solution)/shard_map/ppermute | solution.py:262
  3.7 0.1 collective-permute-start.2
  3.7 0.7 %multiply_reduce_fusion = s32[320]{0:T(512)S(1)} fusion(s32[320,1]{0,1:T(1,128)} %param.9, s32[]{:T(128)S(6)} %axis_index.12), kind=kLoop, calls=%fused_computation.1 | loop fusion | flops 640 | bytes 2564 | tf_op jit(solution)/shard_map/mul | solution.py:271
  4.4 0.7 %add.6 = s32[320]{0:T(512)S(1)} add(s32[320]{0:T(512)S(1)} %multiply_reduce_fusion, s32[320]{0:T(512)} %param.10) | non-fusion elementwise | flops 320 | bytes 3840 | tf_op jit(solution)/shard_map/add | solution.py:271
  5.1 0.0 copy-start.4
  5.1 0.0 copy-start.2
  5.1 0.0 copy-start.3
  5.1 0.1 collective-permute-start
  5.2 2.0 %collective-permute-start.4 = (bf16[320,256]{1,0:T(8,128)(2,1)}, bf16[320,256]{1,0:T(8,128)(2,1)S(1)}, u32[]{:S(2)}, u32[]{:S(2)}) collective-permute-start(bf16[320,256]{1,0:T(8,128)(2,1)} %refs_0_.4), channel_id=1, source_target_pairs={{0,16},{8,24},{16,0},{24,8},{1,17},{9,25},{17,1},{25,9},{2,18},{10... | collective-permute-start | bytes 491528 | tf_op jit(solution)/shard_map/ppermute | solution.py:262
  7.2 0.8 %shard_map.102 = (bf16[640,320]{1,0:T(8,128)(2,1)S(1)}, bf16[8,8,256]{2,1,0:T(8,128)(2,1)S(1)}) custom-call(s32[1,320]{1,0:T(1,128)S(1)} %add.7.code_ref), custom_call_target="tpu_custom_call" | custom-call | flops 1073741824 | bytes 1024 | tf_op jit(solution)/shard_map/pallas_call | solution.py:245
  8.1 0.1 collective-permute-done.2
  8.1 0.0 collective-permute-done.1.refs_2_.refs_4_
  8.1 0.2 collective-permute-start.5
  8.3 0.0 copy-done.4
  8.3 0.1 pad_add_fusion
  8.4 0.3 %collective-permute-start.3 = (s32[640]{0:T(1024)S(1)}, s32[640]{0:T(1024)S(1)}, u32[]{:S(2)}, u32[]{:S(2)}) collective-permute-start(s32[640]{0:T(1024)S(1)} %pad_add_fusion), channel_id=1, source_target_pairs={{0,8},{8,0},{16,24},{24,16},{1,9},{9,1},{17,25},{25,17},{2,10},{10... | collective-permute-start | bytes 7688 | tf_op jit(solution)/shard_map/ppermute | solution.py:262
  8.7 0.0 collective-permute-done.refs_1_.refs_3_
  8.7 0.0 copy-done.2
  8.7 0.0 copy-done.3
  8.7 0.5 %shard_map.103 = (f32[3,320,320]{2,1,0:T(8,128)S(1)}, f32[8,320]{1,0:T(8,128)S(1)}) custom-call(bf16[320,256]{1,0:T(8,128)(2,1)S(1)} %copy-done.2, bf16[320,256]{1,0:T(8,128)(2,1)S(1)} %copy-done.3, bf16[320,256]{1,0:T(8,128)(2,1)S(1)} %collective-permute-done.refs_1_.refs_3_, bf16[320,256]{1,0:T(8,128)(2,1)S(1)} %collective-permute-done.1.refs_2_.refs_4_), custom_call_target="tpu_custom_call" | custom-call | flops 536870912 | bytes 1024 | tf_op jit(solution)/shard_map/pallas_call | solution.py:245
  9.3 0.3 collective-permute-done.3
  9.5 0.4 %shard_map.104 = (f32[4,320,128]{2,1,0:T(8,128)S(1)}, f32[3,320,320]{2,1,0:T(8,128)S(1)}, f32[8,320]{1,0:T(8,128)S(1)}) custom-call(f32[3,320,320]{2,1,0:T(8,128)S(1)} %get-tuple-element.38.e_ref, s32[1,640]{1,0:T(1,128)S(1)} %reshape.24.near_ref, s32[1,640]{1,0:T(1,128)S(1)} %reshape.25.mate_ref), custom_call_target="tpu_custom_call" | custom-call | bytes 1024 | tf_op jit(solution)/shard_map/pallas_call | solution.py:245
  9.9 2.3 %collective-permute-done.4.refs_1_ = bf16[320,256]{1,0:T(8,128)(2,1)S(1)} collective-permute-done((bf16[320,256]{1,0:T(8,128)(2,1)}, bf16[320,256]{1,0:T(8,128)(2,1)S(1)}, u32[]{:S(2)}, u32[]{:S(2)}) %collective-permute-start.4) | collective-permute-done | bytes 163872 | tf_op jit(solution)/shard_map/ppermute | solution.py:262
  12.2 0.0 collective-permute-done.5.refs_5_.refs_3_
  12.2 1.5 %shard_map.105 = (f32[320,256]{1,0:T(8,128)S(1)}, bf16[320,256]{1,0:T(8,128)(2,1)S(1)}, f32[1,320,320]{2,1,0:T(8,128)S(1)}, f32[8,320]{1,0:T(8,128)S(1)}) custom-call(bf16[320,256]{1,0:T(8,128)(2,1)S(1)} %copy-done.2, bf16[320,256]{1,0:T(8,128)(2,1)S(1)} %collective-permute-done.4.refs_1_, bf16[320,256]{1,0:T(8,128)(2,1)S(1)} %copy-done.3, ...), custom_call_target="tpu_custom_call" | custom-call | bytes 1024 | tf_op jit(solution)/shard_map/pallas_call | solution.py:245
  13.8 0.1 collective-permute-start.6
  13.8 1.3 %shard_map.106 = (f32[320,256]{1,0:T(8,128)}, f32[320]{0:T(512)}) custom-call(f32[3,320,320]{2,1,0:T(8,128)S(1)} %get-tuple-element.40.refs_7_.e_ref, f32[1,320,320]{2,1,0:T(8,128)S(1)} %get-tuple-element.44.late_ref, f32[8,320]{1,0:T(8,128)S(1)} %get-tuple-element.45.factor_ref, bf16[320,256]{1,0:T(8,128)(2,1)S(1)} %copy-done.3, ...), custom_call_target="tpu_custom_call" | custom-call | flops 1073741824 | bytes 1024 | tf_op jit(solution)/shard_map/pallas_call | solution.py:245
  15.1 0.0 copy-start
  15.1 0.1 collective-permute-done.6.other_ref
  15.2 0.5 %shard_map.107 = (bf16[88,256]{1,0:T(8,128)(2,1)S(1)}, bf16[88,256]{1,0:T(8,128)(2,1)S(1)}, bf16[88,256]{1,0:T(8,128)(2,1)S(1)}, bf16[88,256]{1,0:T(8,128)(2,1)S...) custom-call(bf16[640,320]{1,0:T(8,128)(2,1)S(1)} %get-tuple-element., ...), custom_call_target="tpu_custom_call" | custom-call | bytes 1024 | tf_op jit(solution)/shard_map/pallas_call | solution.py:245
  15.7 2.9 %collective-permute-start.7 = (bf16[88,256]{1,0:T(8,128)(2,1)S(1)}, bf16[88,256]{1,0:T(8,128)(2,1)S(1)}, u32[]{:S(2)}, u32[]{:S(2)}) collective-permute-start(bf16[88,256]{1,0:T(8,128)(2,1)S(1)} %get-tuple-element.55), channel_id=1, source_target_pairs={{0,4},{1,5},{2,6},{3,7},{4,0},{5,1},{6,2},{7,3},{8,12},{9,13},{10,... | collective-permute-start | bytes 135176 | tf_op jit(solution)/shard_map/ppermute | solution.py:262
  18.6 1.3 %collective-permute-start.8 = (bf16[88,256]{1,0:T(8,128)(2,1)S(1)}, bf16[88,256]{1,0:T(8,128)(2,1)S(1)}, u32[]{:S(2)}, u32[]{:S(2)}) collective-permute-start(bf16[88,256]{1,0:T(8,128)(2,1)S(1)} %get-tuple-element.56), channel_id=1, source_target_pairs={{0,6},{1,7},{2,4},{3,5},{4,2},{5,3},{6,0},{7,1},{8,14},{9,15},{10,... | collective-permute-start | bytes 135176 | tf_op jit(solution)/shard_map/ppermute | solution.py:262
  19.9 2.6 %collective-permute-start.9 = (bf16[88,256]{1,0:T(8,128)(2,1)S(1)}, bf16[88,256]{1,0:T(8,128)(2,1)S(1)}, u32[]{:S(2)}, u32[]{:S(2)}) collective-permute-start(bf16[88,256]{1,0:T(8,128)(2,1)S(1)} %get-tuple-element.57), channel_id=1, source_target_pairs={{0,5},{1,4},{2,7},{3,6},{4,1},{5,0},{6,3},{7,2},{8,13},{9,12},{10,... | collective-permute-start | bytes 135176 | tf_op jit(solution)/shard_map/ppermute | solution.py:262
  22.6 0.9 %collective-permute-start.10 = (bf16[88,256]{1,0:T(8,128)(2,1)S(1)}, bf16[88,256]{1,0:T(8,128)(2,1)S(1)}, u32[]{:S(2)}, u32[]{:S(2)}) collective-permute-start(bf16[88,256]{1,0:T(8,128)(2,1)S(1)} %get-tuple-element.58), channel_id=1, source_target_pairs={{0,7},{1,6},{2,5},{3,4},{4,3},{5,2},{6,1},{7,0},{8,15},{9,14},{10,... | collective-permute-start | bytes 135176 | tf_op jit(solution)/shard_map/ppermute | solution.py:262
  23.4 1.8 %collective-permute-start.11 = (bf16[88,256]{1,0:T(8,128)(2,1)S(1)}, bf16[88,256]{1,0:T(8,128)(2,1)S(1)}, u32[]{:S(2)}, u32[]{:S(2)}) collective-permute-start(bf16[88,256]{1,0:T(8,128)(2,1)S(1)} %get-tuple-element.59), channel_id=1, source_target_pairs={{0,3},{1,2},{2,1},{3,0},{4,7},{5,6},{6,5},{7,4},{8,11},{9,10},{10,... | collective-permute-start | bytes 135176 | tf_op jit(solution)/shard_map/ppermute | solution.py:262
  25.2 0.0 collective-permute-done.7.refs_1_
  25.3 0.5 %collective-permute-start.12 = (bf16[88,256]{1,0:T(8,128)(2,1)S(1)}, bf16[88,256]{1,0:T(8,128)(2,1)S(1)}, u32[]{:S(2)}, u32[]{:S(2)}) collective-permute-start(bf16[88,256]{1,0:T(8,128)(2,1)S(1)} %get-tuple-element.60), channel_id=1, source_target_pairs={{0,1},{1,0},{2,3},{3,2},{4,5},{5,4},{6,7},{7,6},{8,9},{9,8},{10,11... | collective-permute-start | bytes 135176 | tf_op jit(solution)/shard_map/ppermute | solution.py:262
  25.8 0.0 collective-permute-done.8.refs_2_
  25.8 1.1 %collective-permute-start.13 = (bf16[88,256]{1,0:T(8,128)(2,1)S(1)}, bf16[88,256]{1,0:T(8,128)(2,1)S(1)}, u32[]{:S(2)}, u32[]{:S(2)}) collective-permute-start(bf16[88,256]{1,0:T(8,128)(2,1)S(1)} %get-tuple-element.61), channel_id=1, source_target_pairs={{0,2},{1,3},{2,0},{3,1},{4,6},{5,7},{6,4},{7,5},{8,10},{9,11},{10,... | collective-permute-start | bytes 135176 | tf_op jit(solution)/shard_map/ppermute | solution.py:262
  26.9 1.5 %collective-permute-done.9.refs_3_ = bf16[88,256]{1,0:T(8,128)(2,1)S(1)} collective-permute-done((bf16[88,256]{1,0:T(8,128)(2,1)S(1)}, bf16[88,256]{1,0:T(8,128)(2,1)S(1)}, u32[]{:S(2)}, u32[]{:S(2)}) %collective-permute-start.9) | collective-permute-done | bytes 45088 | tf_op jit(solution)/shard_map/ppermute | solution.py:262
  28.4 0.6 %shard_map.108.refs_0_ = f32[640,256]{1,0:T(8,128)S(1)} custom-call(bf16[88,256]{1,0:T(8,128)(2,1)S(1)} %get-tuple-element.54.refs_0_, bf16[88,256]{1,0:T(8,128)(2,1)S(1)} %collective-permute-done.7.refs_1_, bf16[88,256]{1,0:T(8,128)(2,1)S(1)} %collective-permute-done.8.refs_2_, bf16[88,256]{1,0:T(8,128)(2,1)S(1)} %collective-permute-done.9.refs_3_), custom_call_target="tpu_custom_call" | custom-call | flops 268435456 | bytes 1024 | tf_op jit(solution)/shard_map/pallas_call | solution.py:245
  29.0 0.4 %collective-permute-done.10.refs_1_ = bf16[88,256]{1,0:T(8,128)(2,1)S(1)} collective-permute-done((bf16[88,256]{1,0:T(8,128)(2,1)S(1)}, bf16[88,256]{1,0:T(8,128)(2,1)S(1)}, u32[]{:S(2)}, u32[]{:S(2)}) %collective-permute-start.10) | collective-permute-done | bytes 45088 | tf_op jit(solution)/shard_map/ppermute | solution.py:262
  29.4 0.2 collective-permute-done.11.refs_2_
  29.6 0.5 %collective-permute-done.12.refs_3_ = bf16[88,256]{1,0:T(8,128)(2,1)S(1)} collective-permute-done((bf16[88,256]{1,0:T(8,128)(2,1)S(1)}, bf16[88,256]{1,0:T(8,128)(2,1)S(1)}, u32[]{:S(2)}, u32[]{:S(2)}) %collective-permute-start.12) | collective-permute-done | bytes 45088 | tf_op jit(solution)/shard_map/ppermute | solution.py:262
  30.1 0.0 collective-permute-done.13.refs_4_
  30.1 0.0 copy-done
  30.1 0.0 copy-done.1
  30.1 1.6 %shard_map.109 = (f32[640,256]{1,0:T(8,128)}, f32[640,256]{1,0:T(8,128)}) custom-call(f32[640,256]{1,0:T(8,128)S(1)} %shard_map.108.refs_0_, bf16[88,256]{1,0:T(8,128)(2,1)S(1)} %collective-permute-done.10.refs_1_, bf16[88,256]{1,0:T(8,128)(2,1)S(1)} %collective-permute-done.11.refs_2_, bf16[88,256]{1,0:T(8,128)(2,1)S(1)} %collective-permute-done.12.refs_3_, ...), custom_call_target="tpu_custom_call" | custom-call | tf_op jit(solution)/shard_map/pallas_call | solution.py:381
  (4 shorter events, 0.0 us)
Async XLA Ops:
  0.6 7.5 %collective-permute-start.1 = (bf16[320,256]{1,0:T(8,128)(2,1)}, bf16[320,256]{1,0:T(8,128)(2,1)S(1)}, u32[]{:S(2)}, u32[]{:S(2)}) collective-permute-start(bf16[320,256]{1,0:T(8,128)(2,1)} %refs_0_.5), channel_id=1, source_target_pairs={{0,16},{8,24},{16,0},{24,8},{1,17},{9,25},{17,1},{25,9},{2,18},{10... | collective-permute-start | bytes 491528 | tf_op jit(solution)/shard_map/ppermute | solution.py:262
  3.7 4.5 %collective-permute-start.2 = (s32[320]{0:T(512)}, s32[320]{0:T(512)S(1)}, u32[]{:S(2)}, u32[]{:S(2)}) collective-permute-start(s32[320]{0:T(512)} %param.11), channel_id=1, source_target_pairs={{0,16},{8,24},{16,0},{24,8},{1,17},{9,25},{17,1},{25,9},{2,18},{10... | collective-permute-start | bytes 3848 | tf_op jit(solution)/shard_map/ppermute | solution.py:262
  5.1 3.2 %copy-start.4 = (s32[320]{0:T(512)S(1)}, s32[320]{0:T(512)}, u32[]{:S(2)}) copy-start(s32[320]{0:T(512)} %param.11) | copy-start | bytes 3844
  5.1 3.6 %copy-start.2 = (bf16[320,256]{1,0:T(8,128)(2,1)S(1)}, bf16[320,256]{1,0:T(8,128)(2,1)}, u32[]{:S(2)}) copy-start(bf16[320,256]{1,0:T(8,128)(2,1)} %refs_0_.4) | copy-start | bytes 491524
  5.1 3.6 %copy-start.3 = (bf16[320,256]{1,0:T(8,128)(2,1)S(1)}, bf16[320,256]{1,0:T(8,128)(2,1)}, u32[]{:S(2)}) copy-start(bf16[320,256]{1,0:T(8,128)(2,1)} %refs_0_.5) | copy-start | bytes 491524
  5.1 3.6 %collective-permute-start = (bf16[320,256]{1,0:T(8,128)(2,1)}, bf16[320,256]{1,0:T(8,128)(2,1)S(1)}, u32[]{:S(2)}, u32[]{:S(2)}) collective-permute-start(bf16[320,256]{1,0:T(8,128)(2,1)} %refs_0_.5), channel_id=1, source_target_pairs={{0,8},{8,0},{16,24},{24,16},{1,9},{9,1},{17,25},{25,17},{2,10},{10... | collective-permute-start | bytes 491528 | tf_op jit(solution)/shard_map/ppermute | solution.py:262
  5.2 7.0 %collective-permute-start.4 = (bf16[320,256]{1,0:T(8,128)(2,1)}, bf16[320,256]{1,0:T(8,128)(2,1)S(1)}, u32[]{:S(2)}, u32[]{:S(2)}) collective-permute-start(bf16[320,256]{1,0:T(8,128)(2,1)} %refs_0_.4), channel_id=1, source_target_pairs={{0,16},{8,24},{16,0},{24,8},{1,17},{9,25},{17,1},{25,9},{2,18},{10... | collective-permute-start | bytes 491528 | tf_op jit(solution)/shard_map/ppermute | solution.py:262
  8.1 4.1 %collective-permute-start.5 = (bf16[320,256]{1,0:T(8,128)(2,1)S(1)}, bf16[320,256]{1,0:T(8,128)(2,1)S(1)}, u32[]{:S(2)}, u32[]{:S(2)}) collective-permute-start(bf16[320,256]{1,0:T(8,128)(2,1)S(1)} %collective-permute-done.1.refs_2_.refs_4_), channel_id=1, source_target_pairs={{0,8},{8,0},{16,24},{24,16},{1,9},{9,1},{17,25},{25,17},{2,10},{10... | collective-permute-start | bytes 491528 | tf_op jit(solution)/shard_map/ppermute | solution.py:262
  8.4 1.2 %collective-permute-start.3 = (s32[640]{0:T(1024)S(1)}, s32[640]{0:T(1024)S(1)}, u32[]{:S(2)}, u32[]{:S(2)}) collective-permute-start(s32[640]{0:T(1024)S(1)} %pad_add_fusion), channel_id=1, source_target_pairs={{0,8},{8,0},{16,24},{24,16},{1,9},{9,1},{17,25},{25,17},{2,10},{10... | collective-permute-start | bytes 7688 | tf_op jit(solution)/shard_map/ppermute | solution.py:262
  13.8 1.5 %collective-permute-start.6 = (bf16[320,256]{1,0:T(8,128)(2,1)S(1)}, bf16[320,256]{1,0:T(8,128)(2,1)S(1)}, u32[]{:S(2)}, u32[]{:S(2)}) collective-permute-start(bf16[320,256]{1,0:T(8,128)(2,1)S(1)} %get-tuple-element.47), channel_id=1, source_target_pairs={{0,8},{8,0},{16,24},{24,16},{1,9},{9,1},{17,25},{25,17},{2,10},{10... | collective-permute-start | bytes 491528 | tf_op jit(solution)/shard_map/ppermute | solution.py:262
  15.1 15.0 %copy-start = (f32[640,256]{1,0:T(8,128)S(1)}, f32[640,256]{1,0:T(8,128)}, u32[]{:S(2)}) copy-start(f32[640,256]{1,0:T(8,128)} %refs_5_.1) | copy-start | bytes 1966084
  15.1 15.0 %copy-start.1 = (f32[640,256]{1,0:T(8,128)S(1)}, f32[640,256]{1,0:T(8,128)}, u32[]{:S(2)}) copy-start(f32[640,256]{1,0:T(8,128)} %refs_6_.1) | copy-start | bytes 1966084
  15.7 9.6 %collective-permute-start.7 = (bf16[88,256]{1,0:T(8,128)(2,1)S(1)}, bf16[88,256]{1,0:T(8,128)(2,1)S(1)}, u32[]{:S(2)}, u32[]{:S(2)}) collective-permute-start(bf16[88,256]{1,0:T(8,128)(2,1)S(1)} %get-tuple-element.55), channel_id=1, source_target_pairs={{0,4},{1,5},{2,6},{3,7},{4,0},{5,1},{6,2},{7,3},{8,12},{9,13},{10,... | collective-permute-start | bytes 135176 | tf_op jit(solution)/shard_map/ppermute | solution.py:262
  18.6 7.2 %collective-permute-start.8 = (bf16[88,256]{1,0:T(8,128)(2,1)S(1)}, bf16[88,256]{1,0:T(8,128)(2,1)S(1)}, u32[]{:S(2)}, u32[]{:S(2)}) collective-permute-start(bf16[88,256]{1,0:T(8,128)(2,1)S(1)} %get-tuple-element.56), channel_id=1, source_target_pairs={{0,6},{1,7},{2,4},{3,5},{4,2},{5,3},{6,0},{7,1},{8,14},{9,15},{10,... | collective-permute-start | bytes 135176 | tf_op jit(solution)/shard_map/ppermute | solution.py:262
  19.9 8.5 %collective-permute-start.9 = (bf16[88,256]{1,0:T(8,128)(2,1)S(1)}, bf16[88,256]{1,0:T(8,128)(2,1)S(1)}, u32[]{:S(2)}, u32[]{:S(2)}) collective-permute-start(bf16[88,256]{1,0:T(8,128)(2,1)S(1)} %get-tuple-element.57), channel_id=1, source_target_pairs={{0,5},{1,4},{2,7},{3,6},{4,1},{5,0},{6,3},{7,2},{8,13},{9,12},{10,... | collective-permute-start | bytes 135176 | tf_op jit(solution)/shard_map/ppermute | solution.py:262
  22.6 6.9 %collective-permute-start.10 = (bf16[88,256]{1,0:T(8,128)(2,1)S(1)}, bf16[88,256]{1,0:T(8,128)(2,1)S(1)}, u32[]{:S(2)}, u32[]{:S(2)}) collective-permute-start(bf16[88,256]{1,0:T(8,128)(2,1)S(1)} %get-tuple-element.58), channel_id=1, source_target_pairs={{0,7},{1,6},{2,5},{3,4},{4,3},{5,2},{6,1},{7,0},{8,15},{9,14},{10,... | collective-permute-start | bytes 135176 | tf_op jit(solution)/shard_map/ppermute | solution.py:262
  23.4 6.2 %collective-permute-start.11 = (bf16[88,256]{1,0:T(8,128)(2,1)S(1)}, bf16[88,256]{1,0:T(8,128)(2,1)S(1)}, u32[]{:S(2)}, u32[]{:S(2)}) collective-permute-start(bf16[88,256]{1,0:T(8,128)(2,1)S(1)} %get-tuple-element.59), channel_id=1, source_target_pairs={{0,3},{1,2},{2,1},{3,0},{4,7},{5,6},{6,5},{7,4},{8,11},{9,10},{10,... | collective-permute-start | bytes 135176 | tf_op jit(solution)/shard_map/ppermute | solution.py:262
  25.3 4.9 %collective-permute-start.12 = (bf16[88,256]{1,0:T(8,128)(2,1)S(1)}, bf16[88,256]{1,0:T(8,128)(2,1)S(1)}, u32[]{:S(2)}, u32[]{:S(2)}) collective-permute-start(bf16[88,256]{1,0:T(8,128)(2,1)S(1)} %get-tuple-element.60), channel_id=1, source_target_pairs={{0,1},{1,0},{2,3},{3,2},{4,5},{5,4},{6,7},{7,6},{8,9},{9,8},{10,11... | collective-permute-start | bytes 135176 | tf_op jit(solution)/shard_map/ppermute | solution.py:262
  25.8 4.3 %collective-permute-start.13 = (bf16[88,256]{1,0:T(8,128)(2,1)S(1)}, bf16[88,256]{1,0:T(8,128)(2,1)S(1)}, u32[]{:S(2)}, u32[]{:S(2)}) collective-permute-start(bf16[88,256]{1,0:T(8,128)(2,1)S(1)} %get-tuple-element.61), channel_id=1, source_target_pairs={{0,2},{1,3},{2,0},{3,1},{4,6},{5,7},{6,4},{7,5},{8,10},{9,11},{10,... | collective-permute-start | bytes 135176 | tf_op jit(solution)/shard_map/ppermute | solution.py:262

commit v14 on v13

--- a/solution.py
+++ b/solution.py
@@ -14,6 +14,8 @@
 LANES = 128
 TAIL = 8
 ROW_CODES = 1 << 16
+FAR = ((4, 5), (6, 7))
+NEAR = (0, 3, 1, 2)
 MIB = 1 << 20
 NT = (((1,), (1,)), ((), ()))
 TN = (((0,), (0,)), ((), ()))
@@ -48,9 +50,10 @@
     )
 
 
-def local_kernel(groups, slots, code_ref, pick_ref, tail_ref):
+def local_kernel(groups, slots, flip, code_ref, pick_ref, tail_ref):
     block = code_ref.shape[1]
     owner = code_ref[...] // ROW_CODES
+    owner = jnp.where(owner < groups // 2, owner ^ flip, owner)
     offset = code_ref[...] % ROW_CODES
     member = lax.broadcasted_iota(jnp.int32, (groups, block), 0) == owner
     before = lax.broadcasted_iota(jnp.int32, (block, block), 0) < lax.broadcasted_iota(
@@ -180,20 +183,58 @@
     out_ref[...] = total * SCALE
 
 
-def pack_kernel(groups, slots, pick_ref, tail_ref, mine_ref, other_ref, *out_refs):
+def split(x):
+    high = x.astype(BF16)
+    return jnp.concatenate([high, (x - high.astype(F32)).astype(BF16)], axis=1)
+
+
+def give_kernel(slots, pick_ref, mate_pick_ref, mine_ref, mate_ref, out_ref):
+    mate = code(mate_ref[...] * SCALE).astype(BF16)
+    out_ref[: 6 * slots] = dot(mate_pick_ref[2 * slots :], mate).astype(BF16)
+    mine = code(mine_ref[...] * SCALE).astype(BF16)
+    out_ref[6 * slots :] = dot(pick_ref[2 * slots : 4 * slots], mine).astype(BF16)
+
+
+def keep_kernel(slots, pick_ref, mate_pick_ref, mine_ref, mate_ref, out_ref):
+    mine = split(mine_ref[...] * SCALE)
+    both = dot(pick_ref[: 2 * slots], mine)
+    out_ref[: 2 * slots] = both[:, :D] + both[:, D:]
+    both = dot(pick_ref[4 * slots :], mine)
+    out_ref[2 * slots : 6 * slots] = both[:, :D] + both[:, D:]
+    both = dot(mate_pick_ref[: 2 * slots], split(mate_ref[...] * SCALE))
+    out_ref[6 * slots :] = both[:, :D] + both[:, D:]
+
+
+def pack_kernel(slots, keep_ref, given_ref, tail_ref, mate_tail_ref, *out_refs):
+    def rows(k):
+        here = slice(k * slots, (k + 1) * slots)
+        return code(keep_ref[here] + decode(given_ref[here].astype(F32))).astype(BF16)
+
+    for p in range(2):
+        out_refs[p][0, :slots] = rows(p)
+        out_refs[p][0, slots:] = tail_ref[p]
+        out_refs[p][1, :slots] = rows(6 + p)
+        out_refs[p][1, slots:] = mate_tail_ref[p]
+    for p in range(4):
+        out_refs[2 + p][:slots] = rows(2 + p)
+        out_refs[2 + p][slots:] = tail_ref[4 + p]
+
+
+def plain_pack_kernel(groups, slots, pick_ref, tail_ref, mine_ref, other_ref, out_ref):
     grad = mine_ref[...] * SCALE + decode(other_ref[...].astype(F32))
-    grad = code(grad).astype(BF16)
-    picked = dot(pick_ref[...], grad).astype(BF16)
+    picked = dot(pick_ref[...], code(grad).astype(BF16)).astype(BF16)
     for g in range(groups):
-        out = out_refs[g] if len(out_refs) == groups else out_refs[0].at[g]
-        out[:slots] = picked[g * slots : (g + 1) * slots]
-        out[slots:] = tail_ref[g]
-
-
-def unpack(slots, got_refs, values_ref, ids_ref):
-    packets = got_refs
-    if len(got_refs[0].shape) == 3:
-        packets = [got_refs[0].at[g] for g in range(got_refs[0].shape[0])]
+        out_ref[g, :slots] = picked[g * slots : (g + 1) * slots]
+        out_ref[g, slots:] = tail_ref[g]
+
+
+def unpack(slots, paired, got_refs, values_ref, ids_ref):
+    packets = []
+    for ref in got_refs:
+        if len(ref.shape) == 2:
+            packets.append(ref)
+        else:
+            packets += [ref.at[g] for g in range(1 if paired else ref.shape[0])]
     half = len(packets) * slots
     for g, got in enumerate(packets):
         tail = got[slots : slots + TAIL].astype(F32)
@@ -214,14 +255,14 @@
 
 def first_kernel(slots, *refs):
     got_refs, (out_ref, values_ref, ids_ref) = refs[:-3], refs[-3:]
-    unpack(slots, got_refs, values_ref, ids_ref)
+    unpack(slots, True, got_refs, values_ref, ids_ref)
     out_ref[...] = scatter(values_ref, ids_ref, 0, out_ref.shape[0])
 
 
 def update_kernel(slots, partial, *refs):
     inputs, refs = refs[:-8], refs[-8:]
     table_ref, accum_ref, table_out, accum_out, values_ref, ids_ref, new_ref, sems = refs
-    unpack(slots, inputs[1:] if partial else inputs, values_ref, ids_ref)
+    unpack(slots, partial, inputs[1:] if partial else inputs, values_ref, ids_ref)
     chunks = sems.shape[1]
     rows = table_ref.shape[0] // chunks
     copies = []
@@ -234,7 +275,7 @@
         new_ref[1, here] = accum_new
         copies.append(pltpu.make_async_copy(new_ref.at[1, here], accum_out.at[here], sems.at[1, c]))
         copies[-1].start()
-        new_ref[0, here] = table_ref[here] - 0.1 * grad / (accum_new * lax.rsqrt(accum_new) + 1e-08)
+        new_ref[0, here] = table_ref[here] - 0.1 * grad / (jnp.sqrt(accum_new) + 1e-08)
         copies.append(pltpu.make_async_copy(new_ref.at[0, here], table_out.at[here], sems.at[0, c]))
         copies[-1].start()
     for copy in copies:
@@ -256,7 +297,7 @@
     n, groups = lax.axis_size("wide"), lax.axis_size("group")
     capacity = 2 * block // groups
     slots = -(-capacity // TAIL) * TAIL
-    paired = groups <= 8
+    paired = groups == 8 and n == 4
 
     def swap(x, k, axis="wide"):
         return lax.ppermute(x, axis, [(i, i ^ k) for i in range(lax.axis_size(axis))])
@@ -267,16 +308,32 @@
 
     owner = item_owner.reshape(1, block)
     if paired:
-        owner = owner ^ lax.axis_index("group")
+        partner = owner ^ lax.axis_index("group")
+        flip = lax.axis_index("wide") % 2 * 2
+        owner = jnp.zeros_like(partner)
+        for core in range(2):
+            for k in range(2):
+                place = (2 * core + k) ^ flip
+                owner = jnp.where(partner == FAR[k][core], place, owner)
+        for k in range(4):
+            owner = jnp.where(partner == NEAR[k], 4 + k, owner)
     codes = owner * ROW_CODES + item_offset.reshape(1, block)
-    codes, own_items = lax.optimization_barrier((codes, items))
-    pick, tail = call(
-        functools.partial(local_kernel, groups, slots),
-        [((groups * slots, block), BF16), ((groups, TAIL, D), BF16)],
-        codes,
-        flops=1 << 30,
-    )
-    far_items, far_counts, tail = lax.optimization_barrier((far_items, far_counts, tail))
+
+    def route(codes, flip, flops):
+        return call(
+            functools.partial(local_kernel, groups, slots, flip),
+            [((groups * slots, block), BF16), ((groups, TAIL, D), BF16)],
+            codes,
+            flops=flops,
+        )
+
+    pick, tail = route(codes, 0, 0)
+    tails, own_items = [tail], items
+    if paired:
+        mate_codes, own_items = lax.optimization_barrier((swap(codes, 1), items))
+        mate_pick, mate_tail = route(mate_codes, 2, 1 << 30)
+        tails.append(mate_tail)
+    far_items, far_counts, tails = lax.optimization_barrier((far_items, far_counts, tails))
     item_blocks = [items, swap(own_items, 1)] + far_items
     early = len(item_blocks)
     item_blocks += [swap(x, 1) for x in far_items]
@@ -307,7 +364,7 @@
         functools.partial(main_kernel, early, late),
         [
             part,
-            part if far_queries[1:] else sent,
+            part if paired or far_queries[1:] else sent,
             ((late, *square), F32),
             rows_of,
         ],
@@ -333,7 +390,6 @@
             scratch=[pltpu.VMEM((2, *square), F32)],
             limit=8 + 4 * n,
         )
-    other = swap(mate, 1)
     query_grad, loss = call(
         functools.partial(query_kernel, early, late),
         [part, ((block,), F32)],
@@ -344,21 +400,44 @@
         limit=8 + 2 * n,
         flops=1 << 30,
     )
-    other, query_grad = lax.optimization_barrier((other, query_grad))
     if paired:
-        packets = [((slots + TAIL, D), BF16)] * groups
+        sums = ((groups * slots, D), BF16)
+        partials = (pick, mate_pick, mine, mate)
+        (give,) = call(functools.partial(give_kernel, slots), [sums], *partials)
+        given = swap(give, 1)
+        (keep,) = call(
+            functools.partial(keep_kernel, slots), [(sums[0], F32)], *partials, flops=1 << 29
+        )
+        packet = (slots + TAIL, D)
+        packed = call(
+            functools.partial(pack_kernel, slots),
+            [((2, *packet), BF16)] * 2 + [(packet, BF16)] * 4,
+            keep,
+            given,
+            *tails,
+        )
+        far = []
+        for p in range(2):
+            pairs = [
+                (w * groups + g, w * groups + (g ^ FAR[p][w % 2]))
+                for w in range(n)
+                for g in range(groups)
+            ]
+            far.append(lax.ppermute(packed[p], ("wide", "group"), pairs))
+        near = [swap(packed[2 + k], NEAR[k], "group") for k in range(1, 4)]
+        forwarded = [swap(x[1], 1) for x in far]
+        got = [packed[2], *far, *near, *forwarded]
     else:
-        packets = [((groups, slots + TAIL, D), BF16)]
-    packed = call(
-        functools.partial(pack_kernel, groups, slots), packets, pick, tail, mine, other
-    )
-    if paired:
-        half = groups // 2
-        far = sorted(range(half, groups), key=lambda k: (k % 2, k))
-        order = far + sorted(range(1, half), key=lambda k: (1 - k % 2, -k))
-        got = [packed[0]] + [swap(packed[k], k, "group") for k in order]
-    else:
-        got = [lax.all_to_all(packed[0], "group", split_axis=0, concat_axis=0, tiled=True)]
+        (packed,) = call(
+            functools.partial(plain_pack_kernel, groups, slots),
+            [((groups, slots + TAIL, D), BF16)],
+            pick,
+            *tails,
+            mine,
+            swap(mate, 1),
+        )
+        got = [lax.all_to_all(packed, "group", split_axis=0, concat_axis=0, tiled=True)]
+
     rows = table.shape[0]
 
     def scratch(packets):
@@ -367,7 +446,7 @@
             pltpu.VMEM((TAIL, packets * slots), F32),
         ]
 
-    count = groups // 2
+    count = 6
     before = []
     if paired:
         before = call(

time: 31.9 us -> 31.5 us (0.987)
  the two profiles are of different devices: /device:TPU:0 before, /device:TPU:17 now
where the time goes in v14:
time: 31.5 us; the launch traced here: 31.3 us
  starting transfers between devices  12.9 us (41%)
  Pallas kernels  8.92 us (28%)
  waiting for transfers between devices  7.26 us (23%)
  other arithmetic  1.47 us (5%)
  between operations  0.75 us (2%)
    ppermute x13, starting transfers between devices, swap(): lax.ppermute(x, axis, [(i, i ^ k) for i in range(lax.axis_size(axis))])  9.42 us
    pallas_call x10, Pallas kernels, call(): pl.pallas_call(kernel, out_shape=[jax.ShapeDtypeStruct(s, t) for s, t in...  7.27 us
    ppermute x2, waiting for transfers between devices, shards(): far.append(lax.ppermute(packed[p], ('wide', 'group'), pairs))  5.86 us
    ppermute x2, starting transfers between devices, shards(): far.append(lax.ppermute(packed[p], ('wide', 'group'), pairs))  3.44 us
    pallas_call x1, Pallas kernels, shards(): pl.pallas_call(functools.partial(update_kernel, slots, paired), out_shape...  1.64 us
    ppermute x13, waiting for transfers between devices, swap(): lax.ppermute(x, axis, [(i, i ^ k) for i in range(lax.axis_size(axis))])  1.4 us
    mul x1, other arithmetic, shards(): codes = owner * ROW_CODES + item_offset.reshape(1, block)  0.71 us
    add x1, other arithmetic, shards(): codes = owner * ROW_CODES + item_offset.reshape(1, block)  0.68 us
  transfers between devices with their start and end apart: 15, of which 5 were waited for; matrix products, arithmetic and copies ran while one was open for 5% of the time, Pallas kernels for 16%

profile of v14, /device:TPU:17, one launch (start us, length us, event | category | flops | bytes accessed | tf_op | source)
XLA Modules:
  0.0 31.3 jit_solution(11427265476547262961)
XLA Ops:
  0.6 1.3 %collective-permute-start.2 = (bf16[320,256]{1,0:T(8,128)(2,1)}, bf16[320,256]{1,0:T(8,128)(2,1)S(1)}, u32[]{:S(2)}, u32[]{:S(2)}) collective-permute-start(bf16[320,256]{1,0:T(8,128)(2,1)} %refs_0_.5), channel_id=1, source_target_pairs={{0,16},{8,24},{16,0},{24,8},{1,17},{9,25},{17,1},{25,9},{2,18},{10... | collective-permute-start | bytes 491528 | tf_op jit(solution)/shard_map/ppermute | solution.py:303
  1.9 0.7 %fusion.1 = s32[320]{0:T(512)S(1)} fusion(s32[320,1]{0,1:T(1,128)} %param.9, s32[]{:T(128)S(6)} %xor.19, s32[]{:T(128)S(6)} %xor.20, s32[]{:T(128)S(6)} %mul.10, s32[]{:T(128)S(6)} %xor.21, s32[]{:T(128)S(6)} %axis_index.22), kind=kLoop, calls=%fused_computation.12 | loop fusion | flops 5760 | bytes 2580 | tf_op jit(solution)/shard_map/mul | solution.py:320
  2.6 0.7 %add.10 = s32[320]{0:T(512)S(1)} add(s32[320]{0:T(512)S(1)} %fusion.1, s32[320]{0:T(512)} %param.10) | non-fusion elementwise | flops 320 | bytes 3840 | tf_op jit(solution)/shard_map/add | solution.py:320
  3.3 1.0 %collective-permute-start = (s32[1,320]{1,0:T(1,128)S(1)}, s32[1,320]{1,0:T(1,128)S(1)}, u32[]{:S(2)}, u32[]{:S(2)}) collective-permute-start(s32[1,320]{1,0:T(1,128)S(1)} %add.11.code_ref), channel_id=1, source_target_pairs={{0,8},{8,0},{16,24},{24,16},{1,9},{9,1},{17,25},{25,17},{2,10},{10... | collective-permute-start | bytes 3848 | tf_op jit(solution)/shard_map/ppermute | solution.py:303
  4.3 0.2 collective-permute-start.3
  4.5 1.2 %collective-permute-start.5 = (bf16[320,256]{1,0:T(8,128)(2,1)}, bf16[320,256]{1,0:T(8,128)(2,1)S(1)}, u32[]{:S(2)}, u32[]{:S(2)}) collective-permute-start(bf16[320,256]{1,0:T(8,128)(2,1)} %refs_0_.4), channel_id=1, source_target_pairs={{0,16},{8,24},{16,0},{24,8},{1,17},{9,25},{17,1},{25,9},{2,18},{10... | collective-permute-start | bytes 491528 | tf_op jit(solution)/shard_map/ppermute | solution.py:303
  5.8 0.8 %shard_map.102 = (bf16[640,320]{1,0:T(8,128)(2,1)S(1)}, bf16[8,8,256]{2,1,0:T(8,128)(2,1)S(1)}) custom-call(s32[1,320]{1,0:T(1,128)S(1)} %add.11.code_ref), custom_call_target="tpu_custom_call" | custom-call | bytes 1024 | tf_op jit(solution)/shard_map/pallas_call | solution.py:286
  6.6 0.0 collective-permute-done.code_ref
  6.6 0.6 %collective-permute-start.1 = (bf16[320,256]{1,0:T(8,128)(2,1)}, bf16[320,256]{1,0:T(8,128)(2,1)S(1)}, u32[]{:S(2)}, u32[]{:S(2)}) collective-permute-start(bf16[320,256]{1,0:T(8,128)(2,1)} %refs_0_.5), channel_id=1, source_target_pairs={{0,8},{8,0},{16,24},{24,16},{1,9},{9,1},{17,25},{25,17},{2,10},{10... | collective-permute-start | bytes 491528 | tf_op jit(solution)/shard_map/ppermute | solution.py:303
  7.2 0.8 %shard_map.103 = (bf16[640,320]{1,0:T(8,128)(2,1)S(1)}, bf16[8,8,256]{2,1,0:T(8,128)(2,1)S(1)}) custom-call(s32[1,320]{1,0:T(1,128)S(1)} %collective-permute-done.code_ref), custom_call_target="tpu_custom_call" | custom-call | flops 1073741824 | bytes 1024 | tf_op jit(solution)/shard_map/pallas_call | solution.py:286
  8.1 0.0 collective-permute-done.3
  8.1 0.0 collective-permute-done.2.refs_2_.refs_4_
  8.1 0.1 collective-permute-start.6
  8.2 0.0 copy-done.4
  8.2 0.1 pad_add_fusion
  8.2 0.5 %collective-permute-start.4 = (s32[640]{0:T(1024)S(1)}, s32[640]{0:T(1024)S(1)}, u32[]{:S(2)}, u32[]{:S(2)}) collective-permute-start(s32[640]{0:T(1024)S(1)} %pad_add_fusion), channel_id=1, source_target_pairs={{0,8},{8,0},{16,24},{24,16},{1,9},{9,1},{17,25},{25,17},{2,10},{10... | collective-permute-start | bytes 7688 | tf_op jit(solution)/shard_map/ppermute | solution.py:303
  8.7 0.0 collective-permute-done.1.refs_1_.refs_3_
  8.7 0.0 copy-done.2
  8.8 0.5 %shard_map.104 = (f32[3,320,320]{2,1,0:T(8,128)S(1)}, f32[8,320]{1,0:T(8,128)S(1)}) custom-call(bf16[320,256]{1,0:T(8,128)(2,1)S(1)} %copy-done.2, bf16[320,256]{1,0:T(8,128)(2,1)S(1)} %copy-done.3, bf16[320,256]{1,0:T(8,128)(2,1)S(1)} %collective-permute-done.1.refs_1_.refs_3_, bf16[320,256]{1,0:T(8,128)(2,1)S(1)} %collective-permute-done.2.refs_2_.refs_4_), custom_call_target="tpu_custom_call" | custom-call | flops 536870912 | bytes 1024 | tf_op jit(solution)/shard_map/pallas_call | solution.py:286
  9.3 0.3 collective-permute-done.4
  9.6 0.4 %shard_map.105 = (f32[4,320,128]{2,1,0:T(8,128)S(1)}, f32[3,320,320]{2,1,0:T(8,128)S(1)}, f32[8,320]{1,0:T(8,128)S(1)}) custom-call(f32[3,320,320]{2,1,0:T(8,128)S(1)} %get-tuple-element.38.e_ref, s32[1,640]{1,0:T(1,128)S(1)} %reshape.59.near_ref, s32[1,640]{1,0:T(1,128)S(1)} %reshape.60.mate_ref), custom_call_target="tpu_custom_call" | custom-call | bytes 1024 | tf_op jit(solution)/shard_map/pallas_call | solution.py:286
  9.9 0.3 %collective-permute-done.5.refs_1_ = bf16[320,256]{1,0:T(8,128)(2,1)S(1)} collective-permute-done((bf16[320,256]{1,0:T(8,128)(2,1)}, bf16[320,256]{1,0:T(8,128)(2,1)S(1)}, u32[]{:S(2)}, u32[]{:S(2)}) %collective-permute-start.5) | collective-permute-done | bytes 163872 | tf_op jit(solution)/shard_map/ppermute | solution.py:303
  10.3 0.0 collective-permute-done.6.refs_5_.refs_3_
  10.3 1.5 %shard_map.106 = (f32[320,256]{1,0:T(8,128)S(1)}, f32[320,256]{1,0:T(8,128)S(1)}, f32[1,320,320]{2,1,0:T(8,128)S(1)}, f32[8,320]{1,0:T(8,128)S(1)}) custom-call(bf16[320,256]{1,0:T(8,128)(2,1)S(1)} %copy-done.2, bf16[320,256]{1,0:T(8,128)(2,1)S(1)} %collective-permute-done.5.refs_1_, bf16[320,256]{1,0:T(8,128)(2,1)S(1)} %copy-done.3, ...), custom_call_target="tpu_custom_call" | custom-call | bytes 1024 | tf_op jit(solution)/shard_map/pallas_call | solution.py:286
  11.8 0.4 %shard_map.109 = bf16[640,256]{1,0:T(8,128)(2,1)S(1)} custom-call(bf16[640,320]{1,0:T(8,128)(2,1)S(1)} %get-tuple-element.48.pick_ref, bf16[640,320]{1,0:T(8,128)(2,1)S(1)} %get-tuple-element.49.mate_pick_ref, f32[320,256]{1,0:T(8,128)S(1)} %get-tuple-element.50.mine_ref, f32[320,256]{1,0:T(8,128)S(1)} %get-tuple-element.51.mate_ref), custom_call_target="tpu_custom_call" | custom-call | bytes 1024 | tf_op jit(solution)/shard_map/pallas_call | solution.py:286
  12.2 1.1 %collective-permute-start.7 = (bf16[640,256]{1,0:T(8,128)(2,1)S(1)}, bf16[640,256]{1,0:T(8,128)(2,1)S(1)}, u32[]{:S(2)}, u32[]{:S(2)}) collective-permute-start(bf16[640,256]{1,0:T(8,128)(2,1)S(1)} %shard_map.109), channel_id=1, source_target_pairs={{0,8},{8,0},{16,24},{24,16},{1,9},{9,1},{17,25},{25,17},{2,10},{10... | collective-permute-start | bytes 983048 | tf_op jit(solution)/shard_map/ppermute | solution.py:303
  13.3 0.5 %shard_map.108.keep_ref = f32[640,256]{1,0:T(8,128)S(1)} custom-call(bf16[640,320]{1,0:T(8,128)(2,1)S(1)} %get-tuple-element.48.pick_ref, bf16[640,320]{1,0:T(8,128)(2,1)S(1)} %get-tuple-element.49.mate_pick_ref, f32[320,256]{1,0:T(8,128)S(1)} %get-tuple-element.50.mine_ref, f32[320,256]{1,0:T(8,128)S(1)} %get-tuple-element.51.mate_ref), custom_call_target="tpu_custom_call" | custom-call | flops 536870912 | bytes 1024 | tf_op jit(solution)/shard_map/pallas_call | solution.py:286
  13.8 0.7 %collective-permute-done.7.given_ref = bf16[640,256]{1,0:T(8,128)(2,1)S(1)} collective-permute-done((bf16[640,256]{1,0:T(8,128)(2,1)S(1)}, bf16[640,256]{1,0:T(8,128)(2,1)S(1)}, u32[]{:S(2)}, u32[]{:S(2)}) %collective-permute-start.7) | collective-permute-done | bytes 327712 | tf_op jit(solution)/shard_map/ppermute | solution.py:303
  14.6 0.3 shard_map.110
  14.9 1.1 %collective-permute-start.8 = (bf16[2,88,256]{2,1,0:T(8,128)(2,1)S(1)}, bf16[2,88,256]{2,1,0:T(8,128)(2,1)S(1)}, u32[]{:S(2)}, u32[]{:S(2)}) collective-permute-start(bf16[2,88,256]{2,1,0:T(8,128)(2,1)S(1)} %get-tuple-element.55), channel_id=1, source_target_pairs={{0,4},{1,5},{2,6},{3,7},{4,0},{5,1},{6,2},{7,3},{8,13},{9,12},{10,... | collective-permute-start | bytes 270344 | tf_op jit(solution)/shard_map/ppermute | solution.py:426
  15.9 2.4 %collective-permute-start.9 = (bf16[2,88,256]{2,1,0:T(8,128)(2,1)S(1)}, bf16[2,88,256]{2,1,0:T(8,128)(2,1)S(1)}, u32[]{:S(2)}, u32[]{:S(2)}) collective-permute-start(bf16[2,88,256]{2,1,0:T(8,128)(2,1)S(1)} %get-tuple-element.56), channel_id=1, source_target_pairs={{0,6},{1,7},{2,4},{3,5},{4,2},{5,3},{6,0},{7,1},{8,15},{9,14},{10,... | collective-permute-start | bytes 270344 | tf_op jit(solution)/shard_map/ppermute | solution.py:426
  18.3 2.0 %collective-permute-start.10 = (bf16[88,256]{1,0:T(8,128)(2,1)S(1)}, bf16[88,256]{1,0:T(8,128)(2,1)S(1)}, u32[]{:S(2)}, u32[]{:S(2)}) collective-permute-start(bf16[88,256]{1,0:T(8,128)(2,1)S(1)} %get-tuple-element.57), channel_id=1, source_target_pairs={{0,3},{1,2},{2,1},{3,0},{4,7},{5,6},{6,5},{7,4},{8,11},{9,10},{10,... | collective-permute-start | bytes 135176 | tf_op jit(solution)/shard_map/ppermute | solution.py:303
  20.3 0.2 collective-permute-start.11
  20.6 0.4 %collective-permute-start.12 = (bf16[88,256]{1,0:T(8,128)(2,1)S(1)}, bf16[88,256]{1,0:T(8,128)(2,1)S(1)}, u32[]{:S(2)}, u32[]{:S(2)}) collective-permute-start(bf16[88,256]{1,0:T(8,128)(2,1)S(1)} %get-tuple-element.59), channel_id=1, source_target_pairs={{0,2},{1,3},{2,0},{3,1},{4,6},{5,7},{6,4},{7,5},{8,10},{9,11},{10,... | collective-permute-start | bytes 135176 | tf_op jit(solution)/shard_map/ppermute | solution.py:303
  21.0 1.1 %collective-permute-done.8.refs_1_ = bf16[2,88,256]{2,1,0:T(8,128)(2,1)S(1)} collective-permute-done((bf16[2,88,256]{2,1,0:T(8,128)(2,1)S(1)}, bf16[2,88,256]{2,1,0:T(8,128)(2,1)S(1)}, u32[]{:S(2)}, u32[]{:S(2)}) %collective-permute-start.8) | collective-permute-done | bytes 90144 | tf_op jit(solution)/shard_map/ppermute | solution.py:426
  22.1 0.0 collective-permute-start.13
  22.1 4.7 %collective-permute-done.9.refs_2_ = bf16[2,88,256]{2,1,0:T(8,128)(2,1)S(1)} collective-permute-done((bf16[2,88,256]{2,1,0:T(8,128)(2,1)S(1)}, bf16[2,88,256]{2,1,0:T(8,128)(2,1)S(1)}, u32[]{:S(2)}, u32[]{:S(2)}) %collective-permute-start.9) | collective-permute-done | bytes 90144 | tf_op jit(solution)/shard_map/ppermute | solution.py:426
  26.8 0.7 %collective-permute-start.14 = (bf16[88,256]{1,0:T(8,128)(2,1)S(1)}, bf16[88,256]{1,0:T(8,128)(2,1)S(1)}, u32[]{:S(2)}, u32[]{:S(2)}) collective-permute-start(bf16[88,256]{1,0:T(8,128)(2,1)S(1)} %slice_bitcast_fusion), channel_id=1, source_target_pairs={{0,8},{8,0},{16,24},{24,16},{1,9},{9,1},{17,25},{25,17},{2,10},{10... | collective-permute-start | bytes 135176 | tf_op jit(solution)/shard_map/ppermute | solution.py:303
  27.5 1.3 %shard_map.107 = (f32[320,256]{1,0:T(8,128)}, f32[320]{0:T(512)}) custom-call(f32[3,320,320]{2,1,0:T(8,128)S(1)} %get-tuple-element.40.refs_7_.e_ref, f32[1,320,320]{2,1,0:T(8,128)S(1)} %get-tuple-element.44.late_ref, f32[8,320]{1,0:T(8,128)S(1)} %get-tuple-element.45.factor_ref, bf16[320,256]{1,0:T(8,128)(2,1)S(1)} %copy-done.3, ...), custom_call_target="tpu_custom_call" | custom-call | flops 1073741824 | bytes 1024 | tf_op jit(solution)/shard_map/pallas_call | solution.py:286
  28.8 0.0 collective-permute-done.10.refs_3_
  28.8 0.0 collective-permute-done.11.refs_4_
  28.8 0.0 collective-permute-done.12.refs_5_
  28.9 0.7 %shard_map.111.refs_0_ = f32[640,256]{1,0:T(8,128)S(1)} custom-call(bf16[88,256]{1,0:T(8,128)(2,1)S(1)} %get-tuple-element.54.refs_0_, bf16[2,88,256]{2,1,0:T(8,128)(2,1)S(1)} %collective-permute-done.8.refs_1_, bf16[2,88,256]{2,1,0:T(8,128)(2,1)S(1)} %collective-permute-done.9.refs_2_, bf16[88,256]{1,0:T(8,128)(2,1)S(1)} %collective-permute-done.10.refs_3_, ...), custom_call_target="tpu_custom_call" | custom-call | flops 268435456 | bytes 1024 | tf_op jit(solution)/shard_map/pallas_call | solution.py:286
  29.6 0.0 collective-permute-done.13.refs_1_
  29.6 0.0 collective-permute-done.14.refs_2_
  29.6 0.0 copy-done
  29.6 0.0 copy-done.1
  29.6 1.6 %shard_map.112 = (f32[640,256]{1,0:T(8,128)}, f32[640,256]{1,0:T(8,128)}) custom-call(f32[640,256]{1,0:T(8,128)S(1)} %shard_map.111.refs_0_, bf16[88,256]{1,0:T(8,128)(2,1)S(1)} %collective-permute-done.13.refs_1_, bf16[88,256]{1,0:T(8,128)(2,1)S(1)} %collective-permute-done.14.refs_2_, f32[640,256]{1,0:T(8,128)S(1)} %copy-done, f32[640,256]{1,0:T(8,128)S(1)} %copy-done.1), custom_call_target="tpu_custom_call" | custom-call | tf_op jit(solution)/shard_map/pallas_call | solution.py:460
  (11 shorter events, 0.0 us)
Async XLA Ops:
  0.6 7.4 %collective-permute-start.2 = (bf16[320,256]{1,0:T(8,128)(2,1)}, bf16[320,256]{1,0:T(8,128)(2,1)S(1)}, u32[]{:S(2)}, u32[]{:S(2)}) collective-permute-start(bf16[320,256]{1,0:T(8,128)(2,1)} %refs_0_.5), channel_id=1, source_target_pairs={{0,16},{8,24},{16,0},{24,8},{1,17},{9,25},{17,1},{25,9},{2,18},{10... | collective-permute-start | bytes 491528 | tf_op jit(solution)/shard_map/ppermute | solution.py:303
  3.3 3.3 %collective-permute-start = (s32[1,320]{1,0:T(1,128)S(1)}, s32[1,320]{1,0:T(1,128)S(1)}, u32[]{:S(2)}, u32[]{:S(2)}) collective-permute-start(s32[1,320]{1,0:T(1,128)S(1)} %add.11.code_ref), channel_id=1, source_target_pairs={{0,8},{8,0},{16,24},{24,16},{1,9},{9,1},{17,25},{25,17},{2,10},{10... | collective-permute-start | bytes 3848 | tf_op jit(solution)/shard_map/ppermute | solution.py:303
  4.3 3.8 %collective-permute-start.3 = (s32[320]{0:T(512)}, s32[320]{0:T(512)S(1)}, u32[]{:S(2)}, u32[]{:S(2)}) collective-permute-start(s32[320]{0:T(512)} %param.11), channel_id=1, source_target_pairs={{0,16},{8,24},{16,0},{24,8},{1,17},{9,25},{17,1},{25,9},{2,18},{10... | collective-permute-start | bytes 3848 | tf_op jit(solution)/shard_map/ppermute | solution.py:303
  4.5 5.8 %collective-permute-start.5 = (bf16[320,256]{1,0:T(8,128)(2,1)}, bf16[320,256]{1,0:T(8,128)(2,1)S(1)}, u32[]{:S(2)}, u32[]{:S(2)}) collective-permute-start(bf16[320,256]{1,0:T(8,128)(2,1)} %refs_0_.4), channel_id=1, source_target_pairs={{0,16},{8,24},{16,0},{24,8},{1,17},{9,25},{17,1},{25,9},{2,18},{10... | collective-permute-start | bytes 491528 | tf_op jit(solution)/shard_map/ppermute | solution.py:303
  6.6 1.6 %copy-start.4 = (s32[320]{0:T(512)S(1)}, s32[320]{0:T(512)}, u32[]{:S(2)}) copy-start(s32[320]{0:T(512)} %param.11) | copy-start | bytes 3844
  6.6 2.2 %copy-start.2 = (bf16[320,256]{1,0:T(8,128)(2,1)S(1)}, bf16[320,256]{1,0:T(8,128)(2,1)}, u32[]{:S(2)}) copy-start(bf16[320,256]{1,0:T(8,128)(2,1)} %refs_0_.4) | copy-start | bytes 491524
  6.6 2.2 %copy-start.3 = (bf16[320,256]{1,0:T(8,128)(2,1)S(1)}, bf16[320,256]{1,0:T(8,128)(2,1)}, u32[]{:S(2)}) copy-start(bf16[320,256]{1,0:T(8,128)(2,1)} %refs_0_.5) | copy-start | bytes 491524
  6.6 2.1 %collective-permute-start.1 = (bf16[320,256]{1,0:T(8,128)(2,1)}, bf16[320,256]{1,0:T(8,128)(2,1)S(1)}, u32[]{:S(2)}, u32[]{:S(2)}) collective-permute-start(bf16[320,256]{1,0:T(8,128)(2,1)} %refs_0_.5), channel_id=1, source_target_pairs={{0,8},{8,0},{16,24},{24,16},{1,9},{9,1},{17,25},{25,17},{2,10},{10... | collective-permute-start | bytes 491528 | tf_op jit(solution)/shard_map/ppermute | solution.py:303
  8.1 2.2 %collective-permute-start.6 = (bf16[320,256]{1,0:T(8,128)(2,1)S(1)}, bf16[320,256]{1,0:T(8,128)(2,1)S(1)}, u32[]{:S(2)}, u32[]{:S(2)}) collective-permute-start(bf16[320,256]{1,0:T(8,128)(2,1)S(1)} %collective-permute-done.2.refs_2_.refs_4_), channel_id=1, source_target_pairs={{0,8},{8,0},{16,24},{24,16},{1,9},{9,1},{17,25},{25,17},{2,10},{10... | collective-permute-start | bytes 491528 | tf_op jit(solution)/shard_map/ppermute | solution.py:303
  8.2 1.3 %collective-permute-start.4 = (s32[640]{0:T(1024)S(1)}, s32[640]{0:T(1024)S(1)}, u32[]{:S(2)}, u32[]{:S(2)}) collective-permute-start(s32[640]{0:T(1024)S(1)} %pad_add_fusion), channel_id=1, source_target_pairs={{0,8},{8,0},{16,24},{24,16},{1,9},{9,1},{17,25},{25,17},{2,10},{10... | collective-permute-start | bytes 7688 | tf_op jit(solution)/shard_map/ppermute | solution.py:303
  12.2 2.4 %collective-permute-start.7 = (bf16[640,256]{1,0:T(8,128)(2,1)S(1)}, bf16[640,256]{1,0:T(8,128)(2,1)S(1)}, u32[]{:S(2)}, u32[]{:S(2)}) collective-permute-start(bf16[640,256]{1,0:T(8,128)(2,1)S(1)} %shard_map.109), channel_id=1, source_target_pairs={{0,8},{8,0},{16,24},{24,16},{1,9},{9,1},{17,25},{25,17},{2,10},{10... | collective-permute-start | bytes 983048 | tf_op jit(solution)/shard_map/ppermute | solution.py:303
  14.9 7.2 %collective-permute-start.8 = (bf16[2,88,256]{2,1,0:T(8,128)(2,1)S(1)}, bf16[2,88,256]{2,1,0:T(8,128)(2,1)S(1)}, u32[]{:S(2)}, u32[]{:S(2)}) collective-permute-start(bf16[2,88,256]{2,1,0:T(8,128)(2,1)S(1)} %get-tuple-element.55), channel_id=1, source_target_pairs={{0,4},{1,5},{2,6},{3,7},{4,0},{5,1},{6,2},{7,3},{8,13},{9,12},{10,... | collective-permute-start | bytes 270344 | tf_op jit(solution)/shard_map/ppermute | solution.py:426
  15.9 10.9 %collective-permute-start.9 = (bf16[2,88,256]{2,1,0:T(8,128)(2,1)S(1)}, bf16[2,88,256]{2,1,0:T(8,128)(2,1)S(1)}, u32[]{:S(2)}, u32[]{:S(2)}) collective-permute-start(bf16[2,88,256]{2,1,0:T(8,128)(2,1)S(1)} %get-tuple-element.56), channel_id=1, source_target_pairs={{0,6},{1,7},{2,4},{3,5},{4,2},{5,3},{6,0},{7,1},{8,15},{9,14},{10,... | collective-permute-start | bytes 270344 | tf_op jit(solution)/shard_map/ppermute | solution.py:426
  18.3 10.5 %collective-permute-start.10 = (bf16[88,256]{1,0:T(8,128)(2,1)S(1)}, bf16[88,256]{1,0:T(8,128)(2,1)S(1)}, u32[]{:S(2)}, u32[]{:S(2)}) collective-permute-start(bf16[88,256]{1,0:T(8,128)(2,1)S(1)} %get-tuple-element.57), channel_id=1, source_target_pairs={{0,3},{1,2},{2,1},{3,0},{4,7},{5,6},{6,5},{7,4},{8,11},{9,10},{10,... | collective-permute-start | bytes 135176 | tf_op jit(solution)/shard_map/ppermute | solution.py:303
  20.3 8.5 %collective-permute-start.11 = (bf16[88,256]{1,0:T(8,128)(2,1)S(1)}, bf16[88,256]{1,0:T(8,128)(2,1)S(1)}, u32[]{:S(2)}, u32[]{:S(2)}) collective-permute-start(bf16[88,256]{1,0:T(8,128)(2,1)S(1)} %get-tuple-element.58), channel_id=1, source_target_pairs={{0,1},{1,0},{2,3},{3,2},{4,5},{5,4},{6,7},{7,6},{8,9},{9,8},{10,11... | collective-permute-start | bytes 135176 | tf_op jit(solution)/shard_map/ppermute | solution.py:303
  20.6 8.3 %collective-permute-start.12 = (bf16[88,256]{1,0:T(8,128)(2,1)S(1)}, bf16[88,256]{1,0:T(8,128)(2,1)S(1)}, u32[]{:S(2)}, u32[]{:S(2)}) collective-permute-start(bf16[88,256]{1,0:T(8,128)(2,1)S(1)} %get-tuple-element.59), channel_id=1, source_target_pairs={{0,2},{1,3},{2,0},{3,1},{4,6},{5,7},{6,4},{7,5},{8,10},{9,11},{10,... | collective-permute-start | bytes 135176 | tf_op jit(solution)/shard_map/ppermute | solution.py:303
  22.1 7.5 %collective-permute-start.13 = (bf16[88,256]{1,0:T(8,128)(2,1)S(1)}, bf16[88,256]{1,0:T(8,128)(2,1)S(1)}, u32[]{:S(2)}, u32[]{:S(2)}) collective-permute-start(bf16[88,256]{1,0:T(8,128)(2,1)S(1)} %slice_bitcast_fusion.1), channel_id=1, source_target_pairs={{0,8},{8,0},{16,24},{24,16},{1,9},{9,1},{17,25},{25,17},{2,10},{10... | collective-permute-start | bytes 135176 | tf_op jit(solution)/shard_map/ppermute | solution.py:303
  26.8 2.8 %collective-permute-start.14 = (bf16[88,256]{1,0:T(8,128)(2,1)S(1)}, bf16[88,256]{1,0:T(8,128)(2,1)S(1)}, u32[]{:S(2)}, u32[]{:S(2)}) collective-permute-start(bf16[88,256]{1,0:T(8,128)(2,1)S(1)} %slice_bitcast_fusion), channel_id=1, source_target_pairs={{0,8},{8,0},{16,24},{24,16},{1,9},{9,1},{17,25},{25,17},{2,10},{10... | collective-permute-start | bytes 135176 | tf_op jit(solution)/shard_map/ppermute | solution.py:303
  27.5 2.1 %copy-start = (f32[640,256]{1,0:T(8,128)S(1)}, f32[640,256]{1,0:T(8,128)}, u32[]{:S(2)}) copy-start(f32[640,256]{1,0:T(8,128)} %refs_3_.1) | copy-start | bytes 1966084
  27.5 2.1 %copy-start.1 = (f32[640,256]{1,0:T(8,128)S(1)}, f32[640,256]{1,0:T(8,128)}, u32[]{:S(2)}) copy-start(f32[640,256]{1,0:T(8,128)} %refs_4_.1) | copy-start | bytes 1966084

commit v15 on v14

--- a/solution.py
+++ b/solution.py
@@ -390,16 +390,6 @@
             scratch=[pltpu.VMEM((2, *square), F32)],
             limit=8 + 4 * n,
         )
-    query_grad, loss = call(
-        functools.partial(query_kernel, early, late),
-        [part, ((block,), F32)],
-        powers,
-        late_powers,
-        factors,
-        *item_blocks,
-        limit=8 + 2 * n,
-        flops=1 << 30,
-    )
     if paired:
         sums = ((groups * slots, D), BF16)
         partials = (pick, mate_pick, mine, mate)
@@ -408,6 +398,17 @@
         (keep,) = call(
             functools.partial(keep_kernel, slots), [(sums[0], F32)], *partials, flops=1 << 29
         )
+        query_grad, loss = call(
+            functools.partial(query_kernel, early, late),
+            [part, ((block,), F32)],
+            powers,
+            late_powers,
+            factors,
+            *item_blocks,
+            limit=8 + 2 * n,
+            flops=1 << 30,
+        )
+        given, query_grad = lax.optimization_barrier((given, query_grad))
         packet = (slots + TAIL, D)
         packed = call(
             functools.partial(pack_kernel, slots),
@@ -428,6 +429,16 @@
         forwarded = [swap(x[1], 1) for x in far]
         got = [packed[2], *far, *near, *forwarded]
     else:
+        query_grad, loss = call(
+            functools.partial(query_kernel, early, late),
+            [part, ((block,), F32)],
+            powers,
+            late_powers,
+            factors,
+            *item_blocks,
+            limit=8 + 2 * n,
+            flops=1 << 30,
+        )
         (packed,) = call(
             functools.partial(plain_pack_kernel, groups, slots),
             [((groups, slots + TAIL, D), BF16)],
@@ -446,7 +457,7 @@
             pltpu.VMEM((TAIL, packets * slots), F32),
         ]
 
-    count = 6
+    count = 3
     before = []
     if paired:
         before = call(

time: 31.5 us -> 30.8 us (0.978)
  the two profiles are of different devices: /device:TPU:17 before, /device:TPU:0 now
where the time goes in v15:
time: 30.8 us; the launch traced here: 30.5 us
  starting transfers between devices  15.2 us (49%)
  Pallas kernels  8.95 us (29%)
  waiting for transfers between devices  4.07 us (13%)
  other arithmetic  1.47 us (5%)
  between operations  0.74 us (2%)
    ppermute x13, starting transfers between devices, swap(): lax.ppermute(x, axis, [(i, i ^ k) for i in range(lax.axis_size(axis))])  11 us
    pallas_call x10, Pallas kernels, call(): pl.pallas_call(kernel, out_shape=[jax.ShapeDtypeStruct(s, t) for s, t in...  7.05 us
    ppermute x2, starting transfers between devices, shards(): far.append(lax.ppermute(packed[p], ('wide', 'group'), pairs))  4.2 us
    ppermute x13, waiting for transfers between devices, swap(): lax.ppermute(x, axis, [(i, i ^ k) for i in range(lax.axis_size(axis))])  2.41 us
    pallas_call x1, Pallas kernels, shards(): pl.pallas_call(functools.partial(update_kernel, slots, paired), out_shape...  1.91 us
    ppermute x2, waiting for transfers between devices, shards(): far.append(lax.ppermute(packed[p], ('wide', 'group'), pairs))  1.66 us
    mul x1, other arithmetic, shards(): codes = owner * ROW_CODES + item_offset.reshape(1, block)  0.71 us
    add x1, other arithmetic, shards(): codes = owner * ROW_CODES + item_offset.reshape(1, block)  0.68 us
  transfers between devices with their start and end apart: 15, of which 7 were waited for; matrix products, arithmetic and copies ran while one was open for 5% of the time, Pallas kernels for 16%

profile of v15, /device:TPU:0, one launch (start us, length us, event | category | flops | bytes accessed | tf_op | source)
XLA Modules:
  0.0 30.5 jit_solution(16332357717265922689)
XLA Ops:
  0.6 3.0 %collective-permute-start.2 = (bf16[320,256]{1,0:T(8,128)(2,1)}, bf16[320,256]{1,0:T(8,128)(2,1)S(1)}, u32[]{:S(2)}, u32[]{:S(2)}) collective-permute-start(bf16[320,256]{1,0:T(8,128)(2,1)} %refs_0_.5), channel_id=1, source_target_pairs={{0,16},{8,24},{16,0},{24,8},{1,17},{9,25},{17,1},{25,9},{2,18},{10... | collective-permute-start | bytes 491528 | tf_op jit(solution)/shard_map/ppermute | solution.py:303
  3.7 0.7 %fusion.1 = s32[320]{0:T(512)S(1)} fusion(s32[320,1]{0,1:T(1,128)} %param.9, s32[]{:T(128)S(6)} %xor.19, s32[]{:T(128)S(6)} %xor.20, s32[]{:T(128)S(6)} %mul.10, s32[]{:T(128)S(6)} %xor.21, s32[]{:T(128)S(6)} %axis_index.22), kind=kLoop, calls=%fused_computation.12 | loop fusion | flops 5760 | bytes 2580 | tf_op jit(solution)/shard_map/mul | solution.py:320
  4.4 0.7 %add.10 = s32[320]{0:T(512)S(1)} add(s32[320]{0:T(512)S(1)} %fusion.1, s32[320]{0:T(512)} %param.10) | non-fusion elementwise | flops 320 | bytes 3840 | tf_op jit(solution)/shard_map/add | solution.py:320
  5.1 0.0 collective-permute-start
  5.1 0.0 collective-permute-start.3
  5.1 2.0 %collective-permute-start.5 = (bf16[320,256]{1,0:T(8,128)(2,1)}, bf16[320,256]{1,0:T(8,128)(2,1)S(1)}, u32[]{:S(2)}, u32[]{:S(2)}) collective-permute-start(bf16[320,256]{1,0:T(8,128)(2,1)} %refs_0_.4), channel_id=1, source_target_pairs={{0,16},{8,24},{16,0},{24,8},{1,17},{9,25},{17,1},{25,9},{2,18},{10... | collective-permute-start | bytes 491528 | tf_op jit(solution)/shard_map/ppermute | solution.py:303
  7.1 0.8 %shard_map.102 = (bf16[640,320]{1,0:T(8,128)(2,1)S(1)}, bf16[8,8,256]{2,1,0:T(8,128)(2,1)S(1)}) custom-call(s32[1,320]{1,0:T(1,128)S(1)} %add.11.code_ref), custom_call_target="tpu_custom_call" | custom-call | bytes 1024 | tf_op jit(solution)/shard_map/pallas_call | solution.py:286
  7.9 0.0 collective-permute-done.code_ref
  7.9 0.1 collective-permute-start.1
  8.0 0.8 %shard_map.103 = (bf16[640,320]{1,0:T(8,128)(2,1)S(1)}, bf16[8,8,256]{2,1,0:T(8,128)(2,1)S(1)}) custom-call(s32[1,320]{1,0:T(1,128)S(1)} %collective-permute-done.code_ref), custom_call_target="tpu_custom_call" | custom-call | flops 1073741824 | bytes 1024 | tf_op jit(solution)/shard_map/pallas_call | solution.py:286
  8.9 0.0 collective-permute-done.3
  8.9 0.0 collective-permute-done.2.refs_2_.refs_4_
  8.9 0.6 %collective-permute-start.6 = (bf16[320,256]{1,0:T(8,128)(2,1)S(1)}, bf16[320,256]{1,0:T(8,128)(2,1)S(1)}, u32[]{:S(2)}, u32[]{:S(2)}) collective-permute-start(bf16[320,256]{1,0:T(8,128)(2,1)S(1)} %collective-permute-done.2.refs_2_.refs_4_), channel_id=1, source_target_pairs={{0,8},{8,0},{16,24},{24,16},{1,9},{9,1},{17,25},{25,17},{2,10},{10... | collective-permute-start | bytes 491528 | tf_op jit(solution)/shard_map/ppermute | solution.py:303
  9.4 0.0 copy-done.4
  9.4 0.1 pad_add_fusion
  9.5 0.0 collective-permute-start.4
  9.5 0.1 collective-permute-done.1.refs_1_.refs_3_
  9.6 0.0 copy-done.2
  9.6 0.0 copy-done.3
  9.6 0.5 %shard_map.104 = (f32[3,320,320]{2,1,0:T(8,128)S(1)}, f32[8,320]{1,0:T(8,128)S(1)}) custom-call(bf16[320,256]{1,0:T(8,128)(2,1)S(1)} %copy-done.2, bf16[320,256]{1,0:T(8,128)(2,1)S(1)} %copy-done.3, bf16[320,256]{1,0:T(8,128)(2,1)S(1)} %collective-permute-done.1.refs_1_.refs_3_, bf16[320,256]{1,0:T(8,128)(2,1)S(1)} %collective-permute-done.2.refs_2_.refs_4_), custom_call_target="tpu_custom_call" | custom-call | flops 536870912 | bytes 1024 | tf_op jit(solution)/shard_map/pallas_call | solution.py:286
  10.2 0.5 %collective-permute-done.4 = s32[640]{0:T(1024)S(1)} collective-permute-done((s32[640]{0:T(1024)S(1)}, s32[640]{0:T(1024)S(1)}, u32[]{:S(2)}, u32[]{:S(2)}) %collective-permute-start.4) | collective-permute-done | bytes 2592 | tf_op jit(solution)/shard_map/ppermute | solution.py:303
  10.7 0.4 %shard_map.105 = (f32[4,320,128]{2,1,0:T(8,128)S(1)}, f32[3,320,320]{2,1,0:T(8,128)S(1)}, f32[8,320]{1,0:T(8,128)S(1)}) custom-call(f32[3,320,320]{2,1,0:T(8,128)S(1)} %get-tuple-element.40.e_ref, s32[1,640]{1,0:T(1,128)S(1)} %reshape.59.near_ref, s32[1,640]{1,0:T(1,128)S(1)} %reshape.60.mate_ref), custom_call_target="tpu_custom_call" | custom-call | bytes 1024 | tf_op jit(solution)/shard_map/pallas_call | solution.py:286
  11.1 0.9 %collective-permute-done.5.refs_1_ = bf16[320,256]{1,0:T(8,128)(2,1)S(1)} collective-permute-done((bf16[320,256]{1,0:T(8,128)(2,1)}, bf16[320,256]{1,0:T(8,128)(2,1)S(1)}, u32[]{:S(2)}, u32[]{:S(2)}) %collective-permute-start.5) | collective-permute-done | bytes 163872 | tf_op jit(solution)/shard_map/ppermute | solution.py:303
  11.9 0.0 collective-permute-done.6.refs_5_.refs_3_
  11.9 1.5 %shard_map.106 = (f32[320,256]{1,0:T(8,128)S(1)}, f32[320,256]{1,0:T(8,128)S(1)}, f32[1,320,320]{2,1,0:T(8,128)S(1)}, f32[8,320]{1,0:T(8,128)S(1)}) custom-call(bf16[320,256]{1,0:T(8,128)(2,1)S(1)} %copy-done.2, bf16[320,256]{1,0:T(8,128)(2,1)S(1)} %collective-permute-done.5.refs_1_, bf16[320,256]{1,0:T(8,128)(2,1)S(1)} %copy-done.3, ...), custom_call_target="tpu_custom_call" | custom-call | bytes 1024 | tf_op jit(solution)/shard_map/pallas_call | solution.py:286
  13.5 0.4 %shard_map.108 = bf16[640,256]{1,0:T(8,128)(2,1)S(1)} custom-call(bf16[640,320]{1,0:T(8,128)(2,1)S(1)} %get-tuple-element.49.pick_ref, bf16[640,320]{1,0:T(8,128)(2,1)S(1)} %get-tuple-element.50.mate_pick_ref, f32[320,256]{1,0:T(8,128)S(1)} %get-tuple-element.51.mine_ref, f32[320,256]{1,0:T(8,128)S(1)} %get-tuple-element.52.mate_ref), custom_call_target="tpu_custom_call" | custom-call | bytes 1024 | tf_op jit(solution)/shard_map/pallas_call | solution.py:286
  13.8 0.1 collective-permute-start.7
  13.9 0.5 %shard_map.109.keep_ref = f32[640,256]{1,0:T(8,128)S(1)} custom-call(bf16[640,320]{1,0:T(8,128)(2,1)S(1)} %get-tuple-element.49.pick_ref, bf16[640,320]{1,0:T(8,128)(2,1)S(1)} %get-tuple-element.50.mate_pick_ref, f32[320,256]{1,0:T(8,128)S(1)} %get-tuple-element.51.mine_ref, f32[320,256]{1,0:T(8,128)S(1)} %get-tuple-element.52.mate_ref), custom_call_target="tpu_custom_call" | custom-call | flops 536870912 | bytes 1024 | tf_op jit(solution)/shard_map/pallas_call | solution.py:286
  14.4 1.3 %shard_map.107 = (f32[320,256]{1,0:T(8,128)}, f32[320]{0:T(512)}) custom-call(f32[3,320,320]{2,1,0:T(8,128)S(1)} %get-tuple-element.42.refs_7_.e_ref, f32[1,320,320]{2,1,0:T(8,128)S(1)} %get-tuple-element.46.late_ref, f32[8,320]{1,0:T(8,128)S(1)} %get-tuple-element.47.factor_ref, bf16[320,256]{1,0:T(8,128)(2,1)S(1)} %copy-done.3, ...), custom_call_target="tpu_custom_call" | custom-call | flops 1073741824 | bytes 1024 | tf_op jit(solution)/shard_map/pallas_call | solution.py:286
  15.7 0.0 collective-permute-done.7.given_ref
  15.7 0.3 %shard_map.110 = (bf16[2,88,256]{2,1,0:T(8,128)(2,1)S(1)}, bf16[2,88,256]{2,1,0:T(8,128)(2,1)S(1)}, bf16[88,256]{1,0:T(8,128)(2,1)S(1)}, bf16[88,256]{1,0:T(8,12...) custom-call(f32[640,256]{1,0:T(8,128)S(1)} %shard_map.109.keep_ref, ...), custom_call_target="tpu_custom_call" | custom-call | bytes 1024 | tf_op jit(solution)/shard_map/pallas_call | solution.py:286
  16.0 2.9 %collective-permute-start.8 = (bf16[2,88,256]{2,1,0:T(8,128)(2,1)S(1)}, bf16[2,88,256]{2,1,0:T(8,128)(2,1)S(1)}, u32[]{:S(2)}, u32[]{:S(2)}) collective-permute-start(bf16[2,88,256]{2,1,0:T(8,128)(2,1)S(1)} %get-tuple-element.59), channel_id=1, source_target_pairs={{0,4},{1,5},{2,6},{3,7},{4,0},{5,1},{6,2},{7,3},{8,13},{9,12},{10,... | collective-permute-start | bytes 270344 | tf_op jit(solution)/shard_map/ppermute | solution.py:427
  18.9 1.3 %collective-permute-start.9 = (bf16[2,88,256]{2,1,0:T(8,128)(2,1)S(1)}, bf16[2,88,256]{2,1,0:T(8,128)(2,1)S(1)}, u32[]{:S(2)}, u32[]{:S(2)}) collective-permute-start(bf16[2,88,256]{2,1,0:T(8,128)(2,1)S(1)} %get-tuple-element.60), channel_id=1, source_target_pairs={{0,6},{1,7},{2,4},{3,5},{4,2},{5,3},{6,0},{7,1},{8,15},{9,14},{10,... | collective-permute-start | bytes 270344 | tf_op jit(solution)/shard_map/ppermute | solution.py:427
  20.2 1.2 %collective-permute-start.10 = (bf16[88,256]{1,0:T(8,128)(2,1)S(1)}, bf16[88,256]{1,0:T(8,128)(2,1)S(1)}, u32[]{:S(2)}, u32[]{:S(2)}) collective-permute-start(bf16[88,256]{1,0:T(8,128)(2,1)S(1)} %get-tuple-element.61), channel_id=1, source_target_pairs={{0,3},{1,2},{2,1},{3,0},{4,7},{5,6},{6,5},{7,4},{8,11},{9,10},{10,... | collective-permute-start | bytes 135176 | tf_op jit(solution)/shard_map/ppermute | solution.py:303
  21.4 0.5 %collective-permute-start.11 = (bf16[88,256]{1,0:T(8,128)(2,1)S(1)}, bf16[88,256]{1,0:T(8,128)(2,1)S(1)}, u32[]{:S(2)}, u32[]{:S(2)}) collective-permute-start(bf16[88,256]{1,0:T(8,128)(2,1)S(1)} %get-tuple-element.62), channel_id=1, source_target_pairs={{0,1},{1,0},{2,3},{3,2},{4,5},{5,4},{6,7},{7,6},{8,9},{9,8},{10,11... | collective-permute-start | bytes 135176 | tf_op jit(solution)/shard_map/ppermute | solution.py:303
  21.9 1.8 %collective-permute-start.12 = (bf16[88,256]{1,0:T(8,128)(2,1)S(1)}, bf16[88,256]{1,0:T(8,128)(2,1)S(1)}, u32[]{:S(2)}, u32[]{:S(2)}) collective-permute-start(bf16[88,256]{1,0:T(8,128)(2,1)S(1)} %get-tuple-element.63), channel_id=1, source_target_pairs={{0,2},{1,3},{2,0},{3,1},{4,6},{5,7},{6,4},{7,5},{8,10},{9,11},{10,... | collective-permute-start | bytes 135176 | tf_op jit(solution)/shard_map/ppermute | solution.py:303
  23.7 0.1 collective-permute-done.8.refs_1_
  23.9 0.8 %collective-permute-start.13 = (bf16[88,256]{1,0:T(8,128)(2,1)S(1)}, bf16[88,256]{1,0:T(8,128)(2,1)S(1)}, u32[]{:S(2)}, u32[]{:S(2)}) collective-permute-start(bf16[88,256]{1,0:T(8,128)(2,1)S(1)} %slice_bitcast_fusion.1), channel_id=1, source_target_pairs={{0,8},{8,0},{16,24},{24,16},{1,9},{9,1},{17,25},{25,17},{2,10},{10... | collective-permute-start | bytes 135176 | tf_op jit(solution)/shard_map/ppermute | solution.py:303
  24.7 1.5 %collective-permute-done.9.refs_2_ = bf16[2,88,256]{2,1,0:T(8,128)(2,1)S(1)} collective-permute-done((bf16[2,88,256]{2,1,0:T(8,128)(2,1)S(1)}, bf16[2,88,256]{2,1,0:T(8,128)(2,1)S(1)}, u32[]{:S(2)}, u32[]{:S(2)}) %collective-permute-start.9) | collective-permute-done | bytes 90144 | tf_op jit(solution)/shard_map/ppermute | solution.py:427
  26.3 0.9 %collective-permute-start.14 = (bf16[88,256]{1,0:T(8,128)(2,1)S(1)}, bf16[88,256]{1,0:T(8,128)(2,1)S(1)}, u32[]{:S(2)}, u32[]{:S(2)}) collective-permute-start(bf16[88,256]{1,0:T(8,128)(2,1)S(1)} %slice_bitcast_fusion), channel_id=1, source_target_pairs={{0,8},{8,0},{16,24},{24,16},{1,9},{9,1},{17,25},{25,17},{2,10},{10... | collective-permute-start | bytes 135176 | tf_op jit(solution)/shard_map/ppermute | solution.py:303
  27.1 0.5 %shard_map.111.refs_0_ = f32[640,256]{1,0:T(8,128)S(1)} custom-call(bf16[88,256]{1,0:T(8,128)(2,1)S(1)} %get-tuple-element.58.refs_0_, bf16[2,88,256]{2,1,0:T(8,128)(2,1)S(1)} %collective-permute-done.8.refs_1_, bf16[2,88,256]{2,1,0:T(8,128)(2,1)S(1)} %collective-permute-done.9.refs_2_), custom_call_target="tpu_custom_call" | custom-call | flops 268435456 | bytes 1024 | tf_op jit(solution)/shard_map/pallas_call | solution.py:286
  27.7 0.3 %collective-permute-done.10.refs_1_ = bf16[88,256]{1,0:T(8,128)(2,1)S(1)} collective-permute-done((bf16[88,256]{1,0:T(8,128)(2,1)S(1)}, bf16[88,256]{1,0:T(8,128)(2,1)S(1)}, u32[]{:S(2)}, u32[]{:S(2)}) %collective-permute-start.10) | collective-permute-done | bytes 45088 | tf_op jit(solution)/shard_map/ppermute | solution.py:303
  28.0 0.0 collective-permute-done.11.refs_2_
  28.0 0.6 %collective-permute-done.12.refs_3_ = bf16[88,256]{1,0:T(8,128)(2,1)S(1)} collective-permute-done((bf16[88,256]{1,0:T(8,128)(2,1)S(1)}, bf16[88,256]{1,0:T(8,128)(2,1)S(1)}, u32[]{:S(2)}, u32[]{:S(2)}) %collective-permute-start.12) | collective-permute-done | bytes 45088 | tf_op jit(solution)/shard_map/ppermute | solution.py:303
  28.6 0.0 collective-permute-done.13.refs_4_
  28.6 0.0 collective-permute-done.14.refs_5_
  28.6 0.0 copy-done.1
  28.6 1.9 %shard_map.112 = (f32[640,256]{1,0:T(8,128)}, f32[640,256]{1,0:T(8,128)}) custom-call(f32[640,256]{1,0:T(8,128)S(1)} %shard_map.111.refs_0_, bf16[88,256]{1,0:T(8,128)(2,1)S(1)} %collective-permute-done.10.refs_1_, bf16[88,256]{1,0:T(8,128)(2,1)S(1)} %collective-permute-done.11.refs_2_, bf16[88,256]{1,0:T(8,128)(2,1)S(1)} %collective-permute-done.12.refs_3_, ...), custom_call_target="tpu_custom_call" | custom-call | tf_op jit(solution)/shard_map/pallas_call | solution.py:471
  (11 shorter events, 0.0 us)
Async XLA Ops:
  0.6 8.2 %collective-permute-start.2 = (bf16[320,256]{1,0:T(8,128)(2,1)}, bf16[320,256]{1,0:T(8,128)(2,1)S(1)}, u32[]{:S(2)}, u32[]{:S(2)}) collective-permute-start(bf16[320,256]{1,0:T(8,128)(2,1)} %refs_0_.5), channel_id=1, source_target_pairs={{0,16},{8,24},{16,0},{24,8},{1,17},{9,25},{17,1},{25,9},{2,18},{10... | collective-permute-start | bytes 491528 | tf_op jit(solution)/shard_map/ppermute | solution.py:303
  5.1 2.9 %collective-permute-start = (s32[1,320]{1,0:T(1,128)S(1)}, s32[1,320]{1,0:T(1,128)S(1)}, u32[]{:S(2)}, u32[]{:S(2)}) collective-permute-start(s32[1,320]{1,0:T(1,128)S(1)} %add.11.code_ref), channel_id=1, source_target_pairs={{0,8},{8,0},{16,24},{24,16},{1,9},{9,1},{17,25},{25,17},{2,10},{10... | collective-permute-start | bytes 3848 | tf_op jit(solution)/shard_map/ppermute | solution.py:303
  5.1 3.8 %collective-permute-start.3 = (s32[320]{0:T(512)}, s32[320]{0:T(512)S(1)}, u32[]{:S(2)}, u32[]{:S(2)}) collective-permute-start(s32[320]{0:T(512)} %param.11), channel_id=1, source_target_pairs={{0,16},{8,24},{16,0},{24,8},{1,17},{9,25},{17,1},{25,9},{2,18},{10... | collective-permute-start | bytes 3848 | tf_op jit(solution)/shard_map/ppermute | solution.py:303
  5.1 6.8 %collective-permute-start.5 = (bf16[320,256]{1,0:T(8,128)(2,1)}, bf16[320,256]{1,0:T(8,128)(2,1)S(1)}, u32[]{:S(2)}, u32[]{:S(2)}) collective-permute-start(bf16[320,256]{1,0:T(8,128)(2,1)} %refs_0_.4), channel_id=1, source_target_pairs={{0,16},{8,24},{16,0},{24,8},{1,17},{9,25},{17,1},{25,9},{2,18},{10... | collective-permute-start | bytes 491528 | tf_op jit(solution)/shard_map/ppermute | solution.py:303
  7.9 1.5 %copy-start.4 = (s32[320]{0:T(512)S(1)}, s32[320]{0:T(512)}, u32[]{:S(2)}) copy-start(s32[320]{0:T(512)} %param.11) | copy-start | bytes 3844
  7.9 1.7 %copy-start.2 = (bf16[320,256]{1,0:T(8,128)(2,1)S(1)}, bf16[320,256]{1,0:T(8,128)(2,1)}, u32[]{:S(2)}) copy-start(bf16[320,256]{1,0:T(8,128)(2,1)} %refs_0_.4) | copy-start | bytes 491524
  7.9 1.7 %copy-start.3 = (bf16[320,256]{1,0:T(8,128)(2,1)S(1)}, bf16[320,256]{1,0:T(8,128)(2,1)}, u32[]{:S(2)}) copy-start(bf16[320,256]{1,0:T(8,128)(2,1)} %refs_0_.5) | copy-start | bytes 491524
  7.9 1.7 %collective-permute-start.1 = (bf16[320,256]{1,0:T(8,128)(2,1)}, bf16[320,256]{1,0:T(8,128)(2,1)S(1)}, u32[]{:S(2)}, u32[]{:S(2)}) collective-permute-start(bf16[320,256]{1,0:T(8,128)(2,1)} %refs_0_.5), channel_id=1, source_target_pairs={{0,8},{8,0},{16,24},{24,16},{1,9},{9,1},{17,25},{25,17},{2,10},{10... | collective-permute-start | bytes 491528 | tf_op jit(solution)/shard_map/ppermute | solution.py:303
  8.9 3.1 %collective-permute-start.6 = (bf16[320,256]{1,0:T(8,128)(2,1)S(1)}, bf16[320,256]{1,0:T(8,128)(2,1)S(1)}, u32[]{:S(2)}, u32[]{:S(2)}) collective-permute-start(bf16[320,256]{1,0:T(8,128)(2,1)S(1)} %collective-permute-done.2.refs_2_.refs_4_), channel_id=1, source_target_pairs={{0,8},{8,0},{16,24},{24,16},{1,9},{9,1},{17,25},{25,17},{2,10},{10... | collective-permute-start | bytes 491528 | tf_op jit(solution)/shard_map/ppermute | solution.py:303
  9.5 1.2 %collective-permute-start.4 = (s32[640]{0:T(1024)S(1)}, s32[640]{0:T(1024)S(1)}, u32[]{:S(2)}, u32[]{:S(2)}) collective-permute-start(s32[640]{0:T(1024)S(1)} %pad_add_fusion), channel_id=1, source_target_pairs={{0,8},{8,0},{16,24},{24,16},{1,9},{9,1},{17,25},{25,17},{2,10},{10... | collective-permute-start | bytes 7688 | tf_op jit(solution)/shard_map/ppermute | solution.py:303
  13.8 1.9 %collective-permute-start.7 = (bf16[640,256]{1,0:T(8,128)(2,1)S(1)}, bf16[640,256]{1,0:T(8,128)(2,1)S(1)}, u32[]{:S(2)}, u32[]{:S(2)}) collective-permute-start(bf16[640,256]{1,0:T(8,128)(2,1)S(1)} %shard_map.108), channel_id=1, source_target_pairs={{0,8},{8,0},{16,24},{24,16},{1,9},{9,1},{17,25},{25,17},{2,10},{10... | collective-permute-start | bytes 983048 | tf_op jit(solution)/shard_map/ppermute | solution.py:303
  15.7 12.8 %copy-start = (f32[640,256]{1,0:T(8,128)S(1)}, f32[640,256]{1,0:T(8,128)}, u32[]{:S(2)}) copy-start(f32[640,256]{1,0:T(8,128)} %refs_6_.1) | copy-start | bytes 1966084
  15.7 12.8 %copy-start.1 = (f32[640,256]{1,0:T(8,128)S(1)}, f32[640,256]{1,0:T(8,128)}, u32[]{:S(2)}) copy-start(f32[640,256]{1,0:T(8,128)} %refs_7_.1) | copy-start | bytes 1966084
  16.0 7.8 %collective-permute-start.8 = (bf16[2,88,256]{2,1,0:T(8,128)(2,1)S(1)}, bf16[2,88,256]{2,1,0:T(8,128)(2,1)S(1)}, u32[]{:S(2)}, u32[]{:S(2)}) collective-permute-start(bf16[2,88,256]{2,1,0:T(8,128)(2,1)S(1)} %get-tuple-element.59), channel_id=1, source_target_pairs={{0,4},{1,5},{2,6},{3,7},{4,0},{5,1},{6,2},{7,3},{8,13},{9,12},{10,... | collective-permute-start | bytes 270344 | tf_op jit(solution)/shard_map/ppermute | solution.py:427
  18.9 7.4 %collective-permute-start.9 = (bf16[2,88,256]{2,1,0:T(8,128)(2,1)S(1)}, bf16[2,88,256]{2,1,0:T(8,128)(2,1)S(1)}, u32[]{:S(2)}, u32[]{:S(2)}) collective-permute-start(bf16[2,88,256]{2,1,0:T(8,128)(2,1)S(1)} %get-tuple-element.60), channel_id=1, source_target_pairs={{0,6},{1,7},{2,4},{3,5},{4,2},{5,3},{6,0},{7,1},{8,15},{9,14},{10,... | collective-permute-start | bytes 270344 | tf_op jit(solution)/shard_map/ppermute | solution.py:427
  20.2 7.7 %collective-permute-start.10 = (bf16[88,256]{1,0:T(8,128)(2,1)S(1)}, bf16[88,256]{1,0:T(8,128)(2,1)S(1)}, u32[]{:S(2)}, u32[]{:S(2)}) collective-permute-start(bf16[88,256]{1,0:T(8,128)(2,1)S(1)} %get-tuple-element.61), channel_id=1, source_target_pairs={{0,3},{1,2},{2,1},{3,0},{4,7},{5,6},{6,5},{7,4},{8,11},{9,10},{10,... | collective-permute-start | bytes 135176 | tf_op jit(solution)/shard_map/ppermute | solution.py:303
  21.4 6.6 %collective-permute-start.11 = (bf16[88,256]{1,0:T(8,128)(2,1)S(1)}, bf16[88,256]{1,0:T(8,128)(2,1)S(1)}, u32[]{:S(2)}, u32[]{:S(2)}) collective-permute-start(bf16[88,256]{1,0:T(8,128)(2,1)S(1)} %get-tuple-element.62), channel_id=1, source_target_pairs={{0,1},{1,0},{2,3},{3,2},{4,5},{5,4},{6,7},{7,6},{8,9},{9,8},{10,11... | collective-permute-start | bytes 135176 | tf_op jit(solution)/shard_map/ppermute | solution.py:303
  21.9 6.6 %collective-permute-start.12 = (bf16[88,256]{1,0:T(8,128)(2,1)S(1)}, bf16[88,256]{1,0:T(8,128)(2,1)S(1)}, u32[]{:S(2)}, u32[]{:S(2)}) collective-permute-start(bf16[88,256]{1,0:T(8,128)(2,1)S(1)} %get-tuple-element.63), channel_id=1, source_target_pairs={{0,2},{1,3},{2,0},{3,1},{4,6},{5,7},{6,4},{7,5},{8,10},{9,11},{10,... | collective-permute-start | bytes 135176 | tf_op jit(solution)/shard_map/ppermute | solution.py:303
  23.9 4.7 %collective-permute-start.13 = (bf16[88,256]{1,0:T(8,128)(2,1)S(1)}, bf16[88,256]{1,0:T(8,128)(2,1)S(1)}, u32[]{:S(2)}, u32[]{:S(2)}) collective-permute-start(bf16[88,256]{1,0:T(8,128)(2,1)S(1)} %slice_bitcast_fusion.1), channel_id=1, source_target_pairs={{0,8},{8,0},{16,24},{24,16},{1,9},{9,1},{17,25},{25,17},{2,10},{10... | collective-permute-start | bytes 135176 | tf_op jit(solution)/shard_map/ppermute | solution.py:303
  26.3 2.3 %collective-permute-start.14 = (bf16[88,256]{1,0:T(8,128)(2,1)S(1)}, bf16[88,256]{1,0:T(8,128)(2,1)S(1)}, u32[]{:S(2)}, u32[]{:S(2)}) collective-permute-start(bf16[88,256]{1,0:T(8,128)(2,1)S(1)} %slice_bitcast_fusion), channel_id=1, source_target_pairs={{0,8},{8,0},{16,24},{24,16},{1,9},{9,1},{17,25},{25,17},{2,10},{10... | collective-permute-start | bytes 135176 | tf_op jit(solution)/shard_map/ppermute | solution.py:303

commit v16 on v15

--- a/solution.py
+++ b/solution.py
@@ -253,10 +253,11 @@
     return dot(jnp.concatenate([put, put], axis=1), values_ref[...])
 
 
-def first_kernel(slots, *refs):
-    got_refs, (out_ref, values_ref, ids_ref) = refs[:-3], refs[-3:]
-    unpack(slots, True, got_refs, values_ref, ids_ref)
-    out_ref[...] = scatter(values_ref, ids_ref, 0, out_ref.shape[0])
+def first_kernel(slots, partial, *refs):
+    inputs, (out_ref, values_ref, ids_ref) = refs[:-3], refs[-3:]
+    unpack(slots, True, inputs[partial:], values_ref, ids_ref)
+    sums = scatter(values_ref, ids_ref, 0, out_ref.shape[0])
+    out_ref[...] = sums + inputs[0][...] if partial else sums
 
 
 def update_kernel(slots, partial, *refs):
@@ -457,17 +458,18 @@
             pltpu.VMEM((TAIL, packets * slots), F32),
         ]
 
-    count = 3
     before = []
     if paired:
-        before = call(
-            functools.partial(first_kernel, slots),
-            [((rows, D), F32)],
-            *got[:count],
-            scratch=scratch(count),
-            flops=1 << 28,
-        )
-        got = got[count:]
+        for part_of in (got[:3], got[3:5]):
+            before = call(
+                functools.partial(first_kernel, slots, len(before)),
+                [((rows, D), F32)],
+                *before,
+                *part_of,
+                scratch=scratch(len(part_of)),
+                flops=1 << 28,
+            )
+        got = got[5:]
     table_new, accum_new = pl.pallas_call(
         functools.partial(update_kernel, slots, paired),
         out_shape=[jax.ShapeDtypeStruct(table.shape, F32)] * 2,

time: 30.8 us -> 30.7 us (level)
  waiting for transfers between devices: 4.07 us -> 3.58 us
    ppermute x13, waiting for transfers between devices: 2.41 us -> 1.92 us  [swap(): lax.ppermute(x, axis, [(i, i ^ k) for i in range(lax.axis_size(axis))])]
    pallas_call x10 -> x11, Pallas kernels: 7.05 us -> 7.53 us  [call(): pl.pallas_call(kernel, out_shape=[jax.ShapeDtypeStruct(s, t) for s, t in...]
  transfers between devices with their start and end apart: 15 -> 15, of which waited for: 7 -> 7; matrix products, arithmetic and copies ran while one was open for 5% -> 5% of each run, Pallas kernels for 16% -> 18%
where the time goes in v16:
time: 30.7 us; the launch traced here: 30.3 us
  starting transfers between devices  15.2 us (50%)
  Pallas kernels  9.19 us (30%)
  waiting for transfers between devices  3.58 us (12%)
  other arithmetic  1.47 us (5%)
  between operations  0.76 us (2%)
    ppermute x13, starting transfers between devices, swap(): lax.ppermute(x, axis, [(i, i ^ k) for i in range(lax.axis_size(axis))])  11 us
    pallas_call x11, Pallas kernels, call(): pl.pallas_call(kernel, out_shape=[jax.ShapeDtypeStruct(s, t) for s, t in...  7.53 us
    ppermute x2, starting transfers between devices, shards(): far.append(lax.ppermute(packed[p], ('wide', 'group'), pairs))  4.2 us
    ppermute x13, waiting for transfers between devices, swap(): lax.ppermute(x, axis, [(i, i ^ k) for i in range(lax.axis_size(axis))])  1.92 us
    pallas_call x1, Pallas kernels, shards(): pl.pallas_call(functools.partial(update_kernel, slots, paired), out_shape...  1.66 us
    ppermute x2, waiting for transfers between devices, shards(): far.append(lax.ppermute(packed[p], ('wide', 'group'), pairs))  1.66 us
    mul x1, other arithmetic, shards(): codes = owner * ROW_CODES + item_offset.reshape(1, block)  0.71 us
    add x1, other arithmetic, shards(): codes = owner * ROW_CODES + item_offset.reshape(1, block)  0.68 us
  transfers between devices with their start and end apart: 15, of which 7 were waited for; matrix products, arithmetic and copies ran while one was open for 5% of the time, Pallas kernels for 18%

profile of v16, /device:TPU:0, one launch (start us, length us, event | category | flops | bytes accessed | tf_op | source)
XLA Modules:
  0.0 30.3 jit_solution(17868166125124448310)
XLA Ops:
  0.6 3.0 %collective-permute-start.2 = (bf16[320,256]{1,0:T(8,128)(2,1)}, bf16[320,256]{1,0:T(8,128)(2,1)S(1)}, u32[]{:S(2)}, u32[]{:S(2)}) collective-permute-start(bf16[320,256]{1,0:T(8,128)(2,1)} %refs_0_.5), channel_id=1, source_target_pairs={{0,16},{8,24},{16,0},{24,8},{1,17},{9,25},{17,1},{25,9},{2,18},{10... | collective-permute-start | bytes 491528 | tf_op jit(solution)/shard_map/ppermute | solution.py:304
  3.7 0.7 %fusion.1 = s32[320]{0:T(512)S(1)} fusion(s32[320,1]{0,1:T(1,128)} %param.9, s32[]{:T(128)S(6)} %xor.19, s32[]{:T(128)S(6)} %xor.20, s32[]{:T(128)S(6)} %mul.10, s32[]{:T(128)S(6)} %xor.21, s32[]{:T(128)S(6)} %axis_index.22), kind=kLoop, calls=%fused_computation.12 | loop fusion | flops 5760 | bytes 2580 | tf_op jit(solution)/shard_map/mul | solution.py:321
  4.4 0.7 %add.10 = s32[320]{0:T(512)S(1)} add(s32[320]{0:T(512)S(1)} %fusion.1, s32[320]{0:T(512)} %param.10) | non-fusion elementwise | flops 320 | bytes 3840 | tf_op jit(solution)/shard_map/add | solution.py:321
  5.1 0.0 collective-permute-start
  5.1 0.0 collective-permute-start.3
  5.1 2.0 %collective-permute-start.5 = (bf16[320,256]{1,0:T(8,128)(2,1)}, bf16[320,256]{1,0:T(8,128)(2,1)S(1)}, u32[]{:S(2)}, u32[]{:S(2)}) collective-permute-start(bf16[320,256]{1,0:T(8,128)(2,1)} %refs_0_.4), channel_id=1, source_target_pairs={{0,16},{8,24},{16,0},{24,8},{1,17},{9,25},{17,1},{25,9},{2,18},{10... | collective-permute-start | bytes 491528 | tf_op jit(solution)/shard_map/ppermute | solution.py:304
  7.1 0.8 %shard_map.102 = (bf16[640,320]{1,0:T(8,128)(2,1)S(1)}, bf16[8,8,256]{2,1,0:T(8,128)(2,1)S(1)}) custom-call(s32[1,320]{1,0:T(1,128)S(1)} %add.11.code_ref), custom_call_target="tpu_custom_call" | custom-call | bytes 1024 | tf_op jit(solution)/shard_map/pallas_call | solution.py:287
  7.9 0.0 collective-permute-done.code_ref
  7.9 0.1 collective-permute-start.1
  8.0 0.8 %shard_map.103 = (bf16[640,320]{1,0:T(8,128)(2,1)S(1)}, bf16[8,8,256]{2,1,0:T(8,128)(2,1)S(1)}) custom-call(s32[1,320]{1,0:T(1,128)S(1)} %collective-permute-done.code_ref), custom_call_target="tpu_custom_call" | custom-call | flops 1073741824 | bytes 1024 | tf_op jit(solution)/shard_map/pallas_call | solution.py:287
  8.9 0.0 collective-permute-done.3
  8.9 0.0 collective-permute-done.2.refs_2_.refs_4_
  8.9 0.6 %collective-permute-start.6 = (bf16[320,256]{1,0:T(8,128)(2,1)S(1)}, bf16[320,256]{1,0:T(8,128)(2,1)S(1)}, u32[]{:S(2)}, u32[]{:S(2)}) collective-permute-start(bf16[320,256]{1,0:T(8,128)(2,1)S(1)} %collective-permute-done.2.refs_2_.refs_4_), channel_id=1, source_target_pairs={{0,8},{8,0},{16,24},{24,16},{1,9},{9,1},{17,25},{25,17},{2,10},{10... | collective-permute-start | bytes 491528 | tf_op jit(solution)/shard_map/ppermute | solution.py:304
  9.4 0.0 copy-done.4
  9.4 0.1 pad_add_fusion
  9.5 0.0 collective-permute-start.4
  9.5 0.1 collective-permute-done.1.refs_1_.refs_3_
  9.6 0.5 %shard_map.104 = (f32[3,320,320]{2,1,0:T(8,128)S(1)}, f32[8,320]{1,0:T(8,128)S(1)}) custom-call(bf16[320,256]{1,0:T(8,128)(2,1)S(1)} %copy-done.2, bf16[320,256]{1,0:T(8,128)(2,1)S(1)} %copy-done.3, bf16[320,256]{1,0:T(8,128)(2,1)S(1)} %collective-permute-done.1.refs_1_.refs_3_, bf16[320,256]{1,0:T(8,128)(2,1)S(1)} %collective-permute-done.2.refs_2_.refs_4_), custom_call_target="tpu_custom_call" | custom-call | flops 536870912 | bytes 1024 | tf_op jit(solution)/shard_map/pallas_call | solution.py:287
  10.2 0.5 %collective-permute-done.4 = s32[640]{0:T(1024)S(1)} collective-permute-done((s32[640]{0:T(1024)S(1)}, s32[640]{0:T(1024)S(1)}, u32[]{:S(2)}, u32[]{:S(2)}) %collective-permute-start.4) | collective-permute-done | bytes 2592 | tf_op jit(solution)/shard_map/ppermute | solution.py:304
  10.7 0.4 %shard_map.105 = (f32[4,320,128]{2,1,0:T(8,128)S(1)}, f32[3,320,320]{2,1,0:T(8,128)S(1)}, f32[8,320]{1,0:T(8,128)S(1)}) custom-call(f32[3,320,320]{2,1,0:T(8,128)S(1)} %get-tuple-element.40.e_ref, s32[1,640]{1,0:T(1,128)S(1)} %reshape.59.near_ref, s32[1,640]{1,0:T(1,128)S(1)} %reshape.60.mate_ref), custom_call_target="tpu_custom_call" | custom-call | bytes 1024 | tf_op jit(solution)/shard_map/pallas_call | solution.py:287
  11.1 0.9 %collective-permute-done.5.refs_1_ = bf16[320,256]{1,0:T(8,128)(2,1)S(1)} collective-permute-done((bf16[320,256]{1,0:T(8,128)(2,1)}, bf16[320,256]{1,0:T(8,128)(2,1)S(1)}, u32[]{:S(2)}, u32[]{:S(2)}) %collective-permute-start.5) | collective-permute-done | bytes 163872 | tf_op jit(solution)/shard_map/ppermute | solution.py:304
  11.9 0.0 collective-permute-done.6.refs_5_.refs_3_
  11.9 1.5 %shard_map.106 = (f32[320,256]{1,0:T(8,128)S(1)}, f32[320,256]{1,0:T(8,128)S(1)}, f32[1,320,320]{2,1,0:T(8,128)S(1)}, f32[8,320]{1,0:T(8,128)S(1)}) custom-call(bf16[320,256]{1,0:T(8,128)(2,1)S(1)} %copy-done.2, bf16[320,256]{1,0:T(8,128)(2,1)S(1)} %collective-permute-done.5.refs_1_, bf16[320,256]{1,0:T(8,128)(2,1)S(1)} %copy-done.3, ...), custom_call_target="tpu_custom_call" | custom-call | bytes 1024 | tf_op jit(solution)/shard_map/pallas_call | solution.py:287
  13.5 0.4 %shard_map.108 = bf16[640,256]{1,0:T(8,128)(2,1)S(1)} custom-call(bf16[640,320]{1,0:T(8,128)(2,1)S(1)} %get-tuple-element.49.pick_ref, bf16[640,320]{1,0:T(8,128)(2,1)S(1)} %get-tuple-element.50.mate_pick_ref, f32[320,256]{1,0:T(8,128)S(1)} %get-tuple-element.51.mine_ref, f32[320,256]{1,0:T(8,128)S(1)} %get-tuple-element.52.mate_ref), custom_call_target="tpu_custom_call" | custom-call | bytes 1024 | tf_op jit(solution)/shard_map/pallas_call | solution.py:287
  13.8 0.1 collective-permute-start.7
  13.9 0.5 %shard_map.109.keep_ref = f32[640,256]{1,0:T(8,128)S(1)} custom-call(bf16[640,320]{1,0:T(8,128)(2,1)S(1)} %get-tuple-element.49.pick_ref, bf16[640,320]{1,0:T(8,128)(2,1)S(1)} %get-tuple-element.50.mate_pick_ref, f32[320,256]{1,0:T(8,128)S(1)} %get-tuple-element.51.mine_ref, f32[320,256]{1,0:T(8,128)S(1)} %get-tuple-element.52.mate_ref), custom_call_target="tpu_custom_call" | custom-call | flops 536870912 | bytes 1024 | tf_op jit(solution)/shard_map/pallas_call | solution.py:287
  14.4 1.3 %shard_map.107 = (f32[320,256]{1,0:T(8,128)}, f32[320]{0:T(512)}) custom-call(f32[3,320,320]{2,1,0:T(8,128)S(1)} %get-tuple-element.42.refs_7_.e_ref, f32[1,320,320]{2,1,0:T(8,128)S(1)} %get-tuple-element.46.late_ref, f32[8,320]{1,0:T(8,128)S(1)} %get-tuple-element.47.factor_ref, bf16[320,256]{1,0:T(8,128)(2,1)S(1)} %copy-done.3, ...), custom_call_target="tpu_custom_call" | custom-call | flops 1073741824 | bytes 1024 | tf_op jit(solution)/shard_map/pallas_call | solution.py:287
  15.7 0.0 collective-permute-done.7.given_ref
  15.7 0.3 %shard_map.110 = (bf16[2,88,256]{2,1,0:T(8,128)(2,1)S(1)}, bf16[2,88,256]{2,1,0:T(8,128)(2,1)S(1)}, bf16[88,256]{1,0:T(8,128)(2,1)S(1)}, bf16[88,256]{1,0:T(8,12...) custom-call(f32[640,256]{1,0:T(8,128)S(1)} %shard_map.109.keep_ref, ...), custom_call_target="tpu_custom_call" | custom-call | bytes 1024 | tf_op jit(solution)/shard_map/pallas_call | solution.py:287
  16.0 0.0 copy-start
  16.0 0.0 copy-start.1
  16.1 2.9 %collective-permute-start.8 = (bf16[2,88,256]{2,1,0:T(8,128)(2,1)S(1)}, bf16[2,88,256]{2,1,0:T(8,128)(2,1)S(1)}, u32[]{:S(2)}, u32[]{:S(2)}) collective-permute-start(bf16[2,88,256]{2,1,0:T(8,128)(2,1)S(1)} %get-tuple-element.59), channel_id=1, source_target_pairs={{0,4},{1,5},{2,6},{3,7},{4,0},{5,1},{6,2},{7,3},{8,13},{9,12},{10,... | collective-permute-start | bytes 270344 | tf_op jit(solution)/shard_map/ppermute | solution.py:428
  18.9 1.3 %collective-permute-start.9 = (bf16[2,88,256]{2,1,0:T(8,128)(2,1)S(1)}, bf16[2,88,256]{2,1,0:T(8,128)(2,1)S(1)}, u32[]{:S(2)}, u32[]{:S(2)}) collective-permute-start(bf16[2,88,256]{2,1,0:T(8,128)(2,1)S(1)} %get-tuple-element.60), channel_id=1, source_target_pairs={{0,6},{1,7},{2,4},{3,5},{4,2},{5,3},{6,0},{7,1},{8,15},{9,14},{10,... | collective-permute-start | bytes 270344 | tf_op jit(solution)/shard_map/ppermute | solution.py:428
  20.3 1.2 %collective-permute-start.10 = (bf16[88,256]{1,0:T(8,128)(2,1)S(1)}, bf16[88,256]{1,0:T(8,128)(2,1)S(1)}, u32[]{:S(2)}, u32[]{:S(2)}) collective-permute-start(bf16[88,256]{1,0:T(8,128)(2,1)S(1)} %get-tuple-element.61), channel_id=1, source_target_pairs={{0,3},{1,2},{2,1},{3,0},{4,7},{5,6},{6,5},{7,4},{8,11},{9,10},{10,... | collective-permute-start | bytes 135176 | tf_op jit(solution)/shard_map/ppermute | solution.py:304
  21.4 0.5 %collective-permute-start.11 = (bf16[88,256]{1,0:T(8,128)(2,1)S(1)}, bf16[88,256]{1,0:T(8,128)(2,1)S(1)}, u32[]{:S(2)}, u32[]{:S(2)}) collective-permute-start(bf16[88,256]{1,0:T(8,128)(2,1)S(1)} %get-tuple-element.62), channel_id=1, source_target_pairs={{0,1},{1,0},{2,3},{3,2},{4,5},{5,4},{6,7},{7,6},{8,9},{9,8},{10,11... | collective-permute-start | bytes 135176 | tf_op jit(solution)/shard_map/ppermute | solution.py:304
  22.0 1.8 %collective-permute-start.12 = (bf16[88,256]{1,0:T(8,128)(2,1)S(1)}, bf16[88,256]{1,0:T(8,128)(2,1)S(1)}, u32[]{:S(2)}, u32[]{:S(2)}) collective-permute-start(bf16[88,256]{1,0:T(8,128)(2,1)S(1)} %get-tuple-element.63), channel_id=1, source_target_pairs={{0,2},{1,3},{2,0},{3,1},{4,6},{5,7},{6,4},{7,5},{8,10},{9,11},{10,... | collective-permute-start | bytes 135176 | tf_op jit(solution)/shard_map/ppermute | solution.py:304
  23.7 0.1 collective-permute-done.8.refs_1_
  23.9 0.8 %collective-permute-start.13 = (bf16[88,256]{1,0:T(8,128)(2,1)S(1)}, bf16[88,256]{1,0:T(8,128)(2,1)S(1)}, u32[]{:S(2)}, u32[]{:S(2)}) collective-permute-start(bf16[88,256]{1,0:T(8,128)(2,1)S(1)} %slice_bitcast_fusion.1), channel_id=1, source_target_pairs={{0,8},{8,0},{16,24},{24,16},{1,9},{9,1},{17,25},{25,17},{2,10},{10... | collective-permute-start | bytes 135176 | tf_op jit(solution)/shard_map/ppermute | solution.py:304
  24.7 1.5 %collective-permute-done.9.refs_2_ = bf16[2,88,256]{2,1,0:T(8,128)(2,1)S(1)} collective-permute-done((bf16[2,88,256]{2,1,0:T(8,128)(2,1)S(1)}, bf16[2,88,256]{2,1,0:T(8,128)(2,1)S(1)}, u32[]{:S(2)}, u32[]{:S(2)}) %collective-permute-start.9) | collective-permute-done | bytes 90144 | tf_op jit(solution)/shard_map/ppermute | solution.py:428
  26.3 0.9 %collective-permute-start.14 = (bf16[88,256]{1,0:T(8,128)(2,1)S(1)}, bf16[88,256]{1,0:T(8,128)(2,1)S(1)}, u32[]{:S(2)}, u32[]{:S(2)}) collective-permute-start(bf16[88,256]{1,0:T(8,128)(2,1)S(1)} %slice_bitcast_fusion), channel_id=1, source_target_pairs={{0,8},{8,0},{16,24},{24,16},{1,9},{9,1},{17,25},{25,17},{2,10},{10... | collective-permute-start | bytes 135176 | tf_op jit(solution)/shard_map/ppermute | solution.py:304
  27.1 0.5 %shard_map.111.refs_0_ = f32[640,256]{1,0:T(8,128)S(1)} custom-call(bf16[88,256]{1,0:T(8,128)(2,1)S(1)} %get-tuple-element.58.refs_0_, bf16[2,88,256]{2,1,0:T(8,128)(2,1)S(1)} %collective-permute-done.8.refs_1_, bf16[2,88,256]{2,1,0:T(8,128)(2,1)S(1)} %collective-permute-done.9.refs_2_), custom_call_target="tpu_custom_call" | custom-call | flops 268435456 | bytes 1024 | tf_op jit(solution)/shard_map/pallas_call | solution.py:287
  27.7 0.3 %collective-permute-done.10.refs_1_ = bf16[88,256]{1,0:T(8,128)(2,1)S(1)} collective-permute-done((bf16[88,256]{1,0:T(8,128)(2,1)S(1)}, bf16[88,256]{1,0:T(8,128)(2,1)S(1)}, u32[]{:S(2)}, u32[]{:S(2)}) %collective-permute-start.10) | collective-permute-done | bytes 45088 | tf_op jit(solution)/shard_map/ppermute | solution.py:304
  28.0 0.0 collective-permute-done.11.refs_2_
  28.0 0.5 %shard_map.112.refs_0_ = f32[640,256]{1,0:T(8,128)S(1)} custom-call(f32[640,256]{1,0:T(8,128)S(1)} %shard_map.111.refs_0_, bf16[88,256]{1,0:T(8,128)(2,1)S(1)} %collective-permute-done.10.refs_1_, bf16[88,256]{1,0:T(8,128)(2,1)S(1)} %collective-permute-done.11.refs_2_), custom_call_target="tpu_custom_call" | custom-call | flops 268435456 | bytes 1024 | tf_op jit(solution)/shard_map/pallas_call | solution.py:287
  28.5 0.1 collective-permute-done.12.refs_1_
  28.6 0.0 collective-permute-done.13.refs_2_
  28.6 0.0 collective-permute-done.14.refs_3_
  28.6 1.7 %shard_map.113 = (f32[640,256]{1,0:T(8,128)}, f32[640,256]{1,0:T(8,128)}) custom-call(f32[640,256]{1,0:T(8,128)S(1)} %shard_map.112.refs_0_, bf16[88,256]{1,0:T(8,128)(2,1)S(1)} %collective-permute-done.12.refs_1_, bf16[88,256]{1,0:T(8,128)(2,1)S(1)} %collective-permute-done.13.refs_2_, bf16[88,256]{1,0:T(8,128)(2,1)S(1)} %collective-permute-done.14.refs_3_, ...), custom_call_target="tpu_custom_call" | custom-call | tf_op jit(solution)/shard_map/pallas_call | solution.py:473
  (12 shorter events, 0.0 us)
Async XLA Ops:
  0.6 8.2 %collective-permute-start.2 = (bf16[320,256]{1,0:T(8,128)(2,1)}, bf16[320,256]{1,0:T(8,128)(2,1)S(1)}, u32[]{:S(2)}, u32[]{:S(2)}) collective-permute-start(bf16[320,256]{1,0:T(8,128)(2,1)} %refs_0_.5), channel_id=1, source_target_pairs={{0,16},{8,24},{16,0},{24,8},{1,17},{9,25},{17,1},{25,9},{2,18},{10... | collective-permute-start | bytes 491528 | tf_op jit(solution)/shard_map/ppermute | solution.py:304
  5.1 2.9 %collective-permute-start = (s32[1,320]{1,0:T(1,128)S(1)}, s32[1,320]{1,0:T(1,128)S(1)}, u32[]{:S(2)}, u32[]{:S(2)}) collective-permute-start(s32[1,320]{1,0:T(1,128)S(1)} %add.11.code_ref), channel_id=1, source_target_pairs={{0,8},{8,0},{16,24},{24,16},{1,9},{9,1},{17,25},{25,17},{2,10},{10... | collective-permute-start | bytes 3848 | tf_op jit(solution)/shard_map/ppermute | solution.py:304
  5.1 3.8 %collective-permute-start.3 = (s32[320]{0:T(512)}, s32[320]{0:T(512)S(1)}, u32[]{:S(2)}, u32[]{:S(2)}) collective-permute-start(s32[320]{0:T(512)} %param.11), channel_id=1, source_target_pairs={{0,16},{8,24},{16,0},{24,8},{1,17},{9,25},{17,1},{25,9},{2,18},{10... | collective-permute-start | bytes 3848 | tf_op jit(solution)/shard_map/ppermute | solution.py:304
  5.1 6.8 %collective-permute-start.5 = (bf16[320,256]{1,0:T(8,128)(2,1)}, bf16[320,256]{1,0:T(8,128)(2,1)S(1)}, u32[]{:S(2)}, u32[]{:S(2)}) collective-permute-start(bf16[320,256]{1,0:T(8,128)(2,1)} %refs_0_.4), channel_id=1, source_target_pairs={{0,16},{8,24},{16,0},{24,8},{1,17},{9,25},{17,1},{25,9},{2,18},{10... | collective-permute-start | bytes 491528 | tf_op jit(solution)/shard_map/ppermute | solution.py:304
  7.9 1.5 %copy-start.4 = (s32[320]{0:T(512)S(1)}, s32[320]{0:T(512)}, u32[]{:S(2)}) copy-start(s32[320]{0:T(512)} %param.11) | copy-start | bytes 3844
  7.9 1.7 %copy-start.2 = (bf16[320,256]{1,0:T(8,128)(2,1)S(1)}, bf16[320,256]{1,0:T(8,128)(2,1)}, u32[]{:S(2)}) copy-start(bf16[320,256]{1,0:T(8,128)(2,1)} %refs_0_.4) | copy-start | bytes 491524
  7.9 1.7 %copy-start.3 = (bf16[320,256]{1,0:T(8,128)(2,1)S(1)}, bf16[320,256]{1,0:T(8,128)(2,1)}, u32[]{:S(2)}) copy-start(bf16[320,256]{1,0:T(8,128)(2,1)} %refs_0_.5) | copy-start | bytes 491524
  7.9 1.7 %collective-permute-start.1 = (bf16[320,256]{1,0:T(8,128)(2,1)}, bf16[320,256]{1,0:T(8,128)(2,1)S(1)}, u32[]{:S(2)}, u32[]{:S(2)}) collective-permute-start(bf16[320,256]{1,0:T(8,128)(2,1)} %refs_0_.5), channel_id=1, source_target_pairs={{0,8},{8,0},{16,24},{24,16},{1,9},{9,1},{17,25},{25,17},{2,10},{10... | collective-permute-start | bytes 491528 | tf_op jit(solution)/shard_map/ppermute | solution.py:304
  8.9 3.1 %collective-permute-start.6 = (bf16[320,256]{1,0:T(8,128)(2,1)S(1)}, bf16[320,256]{1,0:T(8,128)(2,1)S(1)}, u32[]{:S(2)}, u32[]{:S(2)}) collective-permute-start(bf16[320,256]{1,0:T(8,128)(2,1)S(1)} %collective-permute-done.2.refs_2_.refs_4_), channel_id=1, source_target_pairs={{0,8},{8,0},{16,24},{24,16},{1,9},{9,1},{17,25},{25,17},{2,10},{10... | collective-permute-start | bytes 491528 | tf_op jit(solution)/shard_map/ppermute | solution.py:304
  9.5 1.2 %collective-permute-start.4 = (s32[640]{0:T(1024)S(1)}, s32[640]{0:T(1024)S(1)}, u32[]{:S(2)}, u32[]{:S(2)}) collective-permute-start(s32[640]{0:T(1024)S(1)} %pad_add_fusion), channel_id=1, source_target_pairs={{0,8},{8,0},{16,24},{24,16},{1,9},{9,1},{17,25},{25,17},{2,10},{10... | collective-permute-start | bytes 7688 | tf_op jit(solution)/shard_map/ppermute | solution.py:304
  13.8 1.9 %collective-permute-start.7 = (bf16[640,256]{1,0:T(8,128)(2,1)S(1)}, bf16[640,256]{1,0:T(8,128)(2,1)S(1)}, u32[]{:S(2)}, u32[]{:S(2)}) collective-permute-start(bf16[640,256]{1,0:T(8,128)(2,1)S(1)} %shard_map.108), channel_id=1, source_target_pairs={{0,8},{8,0},{16,24},{24,16},{1,9},{9,1},{17,25},{25,17},{2,10},{10... | collective-permute-start | bytes 983048 | tf_op jit(solution)/shard_map/ppermute | solution.py:304
  16.0 12.5 %copy-start = (f32[640,256]{1,0:T(8,128)S(1)}, f32[640,256]{1,0:T(8,128)}, u32[]{:S(2)}) copy-start(f32[640,256]{1,0:T(8,128)} %refs_4_.1) | copy-start | bytes 1966084
  16.0 12.5 %copy-start.1 = (f32[640,256]{1,0:T(8,128)S(1)}, f32[640,256]{1,0:T(8,128)}, u32[]{:S(2)}) copy-start(f32[640,256]{1,0:T(8,128)} %refs_5_.1) | copy-start | bytes 1966084
  16.1 7.8 %collective-permute-start.8 = (bf16[2,88,256]{2,1,0:T(8,128)(2,1)S(1)}, bf16[2,88,256]{2,1,0:T(8,128)(2,1)S(1)}, u32[]{:S(2)}, u32[]{:S(2)}) collective-permute-start(bf16[2,88,256]{2,1,0:T(8,128)(2,1)S(1)} %get-tuple-element.59), channel_id=1, source_target_pairs={{0,4},{1,5},{2,6},{3,7},{4,0},{5,1},{6,2},{7,3},{8,13},{9,12},{10,... | collective-permute-start | bytes 270344 | tf_op jit(solution)/shard_map/ppermute | solution.py:428
  18.9 7.4 %collective-permute-start.9 = (bf16[2,88,256]{2,1,0:T(8,128)(2,1)S(1)}, bf16[2,88,256]{2,1,0:T(8,128)(2,1)S(1)}, u32[]{:S(2)}, u32[]{:S(2)}) collective-permute-start(bf16[2,88,256]{2,1,0:T(8,128)(2,1)S(1)} %get-tuple-element.60), channel_id=1, source_target_pairs={{0,6},{1,7},{2,4},{3,5},{4,2},{5,3},{6,0},{7,1},{8,15},{9,14},{10,... | collective-permute-start | bytes 270344 | tf_op jit(solution)/shard_map/ppermute | solution.py:428
  20.3 7.7 %collective-permute-start.10 = (bf16[88,256]{1,0:T(8,128)(2,1)S(1)}, bf16[88,256]{1,0:T(8,128)(2,1)S(1)}, u32[]{:S(2)}, u32[]{:S(2)}) collective-permute-start(bf16[88,256]{1,0:T(8,128)(2,1)S(1)} %get-tuple-element.61), channel_id=1, source_target_pairs={{0,3},{1,2},{2,1},{3,0},{4,7},{5,6},{6,5},{7,4},{8,11},{9,10},{10,... | collective-permute-start | bytes 135176 | tf_op jit(solution)/shard_map/ppermute | solution.py:304
  21.4 6.6 %collective-permute-start.11 = (bf16[88,256]{1,0:T(8,128)(2,1)S(1)}, bf16[88,256]{1,0:T(8,128)(2,1)S(1)}, u32[]{:S(2)}, u32[]{:S(2)}) collective-permute-start(bf16[88,256]{1,0:T(8,128)(2,1)S(1)} %get-tuple-element.62), channel_id=1, source_target_pairs={{0,1},{1,0},{2,3},{3,2},{4,5},{5,4},{6,7},{7,6},{8,9},{9,8},{10,11... | collective-permute-start | bytes 135176 | tf_op jit(solution)/shard_map/ppermute | solution.py:304
  22.0 6.6 %collective-permute-start.12 = (bf16[88,256]{1,0:T(8,128)(2,1)S(1)}, bf16[88,256]{1,0:T(8,128)(2,1)S(1)}, u32[]{:S(2)}, u32[]{:S(2)}) collective-permute-start(bf16[88,256]{1,0:T(8,128)(2,1)S(1)} %get-tuple-element.63), channel_id=1, source_target_pairs={{0,2},{1,3},{2,0},{3,1},{4,6},{5,7},{6,4},{7,5},{8,10},{9,11},{10,... | collective-permute-start | bytes 135176 | tf_op jit(solution)/shard_map/ppermute | solution.py:304
  23.9 4.7 %collective-permute-start.13 = (bf16[88,256]{1,0:T(8,128)(2,1)S(1)}, bf16[88,256]{1,0:T(8,128)(2,1)S(1)}, u32[]{:S(2)}, u32[]{:S(2)}) collective-permute-start(bf16[88,256]{1,0:T(8,128)(2,1)S(1)} %slice_bitcast_fusion.1), channel_id=1, source_target_pairs={{0,8},{8,0},{16,24},{24,16},{1,9},{9,1},{17,25},{25,17},{2,10},{10... | collective-permute-start | bytes 135176 | tf_op jit(solution)/shard_map/ppermute | solution.py:304
  26.3 2.3 %collective-permute-start.14 = (bf16[88,256]{1,0:T(8,128)(2,1)S(1)}, bf16[88,256]{1,0:T(8,128)(2,1)S(1)}, u32[]{:S(2)}, u32[]{:S(2)}) collective-permute-start(bf16[88,256]{1,0:T(8,128)(2,1)S(1)} %slice_bitcast_fusion), channel_id=1, source_target_pairs={{0,8},{8,0},{16,24},{24,16},{1,9},{9,1},{17,25},{25,17},{2,10},{10... | collective-permute-start | bytes 135176 | tf_op jit(solution)/shard_map/ppermute | solution.py:304

commit v17 on v16

--- a/solution.py
+++ b/solution.py
@@ -276,7 +276,7 @@
         new_ref[1, here] = accum_new
         copies.append(pltpu.make_async_copy(new_ref.at[1, here], accum_out.at[here], sems.at[1, c]))
         copies[-1].start()
-        new_ref[0, here] = table_ref[here] - 0.1 * grad / (jnp.sqrt(accum_new) + 1e-08)
+        new_ref[0, here] = table_ref[here] - 0.1 * grad / (accum_new * lax.rsqrt(accum_new) + 1e-08)
         copies.append(pltpu.make_async_copy(new_ref.at[0, here], table_out.at[here], sems.at[0, c]))
         copies[-1].start()
     for copy in copies:
@@ -307,7 +307,7 @@
     far_items = [swap(items, k) for k in range(2, n, 2)]
     far_queries = [swap(queries, k) for k in range(2, n, 2)]
 
-    owner = item_owner.reshape(1, block)
+    owner = item_owner
     if paired:
         partner = owner ^ lax.axis_index("group")
         flip = lax.axis_index("wide") % 2 * 2
@@ -318,7 +318,7 @@
                 owner = jnp.where(partner == FAR[k][core], place, owner)
         for k in range(4):
             owner = jnp.where(partner == NEAR[k], 4 + k, owner)
-    codes = owner * ROW_CODES + item_offset.reshape(1, block)
+    codes = (owner * ROW_CODES + item_offset.reshape(block, 1)).reshape(1, block)
 
     def route(codes, flip, flops):
         return call(

time: 30.7 us -> 30.4 us (level)
  other arithmetic: 1.47 us -> 0.78 us
    reshape x0 -> x1, other arithmetic: none -> 0.71 us  [shards(): (owner * ROW_CODES + item_offset.reshape(block, 1)).reshape(1, block)]
    mul x1 -> x0, other arithmetic: 0.71 us -> none  [shards(): codes = owner * ROW_CODES + item_offset.reshape(1, block)]
    add x1 -> x0, other arithmetic: 0.68 us -> none  [shards(): codes = owner * ROW_CODES + item_offset.reshape(1, block)]
  transfers between devices with their start and end apart: 15 -> 15, of which waited for: 7 -> 5; matrix products, arithmetic and copies ran while one was open for 5% -> 3% of each run, Pallas kernels for 18% -> 18%
where the time goes in v17:
time: 30.4 us; the launch traced here: 29.9 us
  starting transfers between devices  15.4 us (51%)
  Pallas kernels  9.16 us (30%)
  waiting for transfers between devices  3.71 us (12%)
  other arithmetic  0.78 us (3%)
  between operations  0.77 us (3%)
    ppermute x13, starting transfers between devices, swap(): lax.ppermute(x, axis, [(i, i ^ k) for i in range(lax.axis_size(axis))])  11.2 us
    pallas_call x11, Pallas kernels, call(): pl.pallas_call(kernel, out_shape=[jax.ShapeDtypeStruct(s, t) for s, t in...  7.53 us
    ppermute x2, starting transfers between devices, shards(): far.append(lax.ppermute(packed[p], ('wide', 'group'), pairs))  4.22 us
    ppermute x13, waiting for transfers between devices, swap(): lax.ppermute(x, axis, [(i, i ^ k) for i in range(lax.axis_size(axis))])  2.15 us
    pallas_call x1, Pallas kernels, shards(): pl.pallas_call(functools.partial(update_kernel, slots, paired), out_shape...  1.63 us
    ppermute x2, waiting for transfers between devices, shards(): far.append(lax.ppermute(packed[p], ('wide', 'group'), pairs))  1.56 us
    reshape x1, other arithmetic, shards(): (owner * ROW_CODES + item_offset.reshape(block, 1)).reshape(1, block)  0.71 us
  transfers between devices with their start and end apart: 15, of which 5 were waited for; matrix products, arithmetic and copies ran while one was open for 3% of the time, Pallas kernels for 18%

profile of v17, /device:TPU:0, one launch (start us, length us, event | category | flops | bytes accessed | tf_op | source)
XLA Modules:
  0.0 29.9 jit_solution(1385688673655634801)
XLA Ops:
  0.6 3.0 %collective-permute-start.2 = (bf16[320,256]{1,0:T(8,128)(2,1)}, bf16[320,256]{1,0:T(8,128)(2,1)S(1)}, u32[]{:S(2)}, u32[]{:S(2)}) collective-permute-start(bf16[320,256]{1,0:T(8,128)(2,1)} %refs_0_.5), channel_id=1, source_target_pairs={{0,16},{8,24},{16,0},{24,8},{1,17},{9,25},{17,1},{25,9},{2,18},{10... | collective-permute-start | bytes 491528 | tf_op jit(solution)/shard_map/ppermute | solution.py:304
  3.7 0.7 %fusion.2.code_ref = s32[1,320]{1,0:T(1,128)S(1)} fusion(s32[320]{0:T(512)} %param.10, s32[320,1]{0,1:T(1,128)} %param.9, s32[]{:T(128)S(6)} %mul.9, s32[]{:T(128)S(6)} %xor.19, s32[]{:T(128)S(6)} %xor.18, s32[]{:T(128)S(6)} %xor.17, s32[]{:T(128)S(6)} %axis_index.22), kind=kLoop, calls=%fused_computation.13 | loop fusion | flops 6080 | bytes 3860 | tf_op jit(solution)/shard_map/reshape | solution.py:321
  4.4 0.1 collective-permute-start
  4.5 0.1 collective-permute-start.3
  4.6 2.0 %collective-permute-start.5 = (bf16[320,256]{1,0:T(8,128)(2,1)}, bf16[320,256]{1,0:T(8,128)(2,1)S(1)}, u32[]{:S(2)}, u32[]{:S(2)}) collective-permute-start(bf16[320,256]{1,0:T(8,128)(2,1)} %refs_0_.4), channel_id=1, source_target_pairs={{0,16},{8,24},{16,0},{24,8},{1,17},{9,25},{17,1},{25,9},{2,18},{10... | collective-permute-start | bytes 491528 | tf_op jit(solution)/shard_map/ppermute | solution.py:304
  6.5 0.8 %shard_map.102 = (bf16[640,320]{1,0:T(8,128)(2,1)S(1)}, bf16[8,8,256]{2,1,0:T(8,128)(2,1)S(1)}) custom-call(s32[1,320]{1,0:T(1,128)S(1)} %fusion.2.code_ref), custom_call_target="tpu_custom_call" | custom-call | bytes 1024 | tf_op jit(solution)/shard_map/pallas_call | solution.py:287
  7.4 0.0 collective-permute-done.code_ref
  7.4 0.1 collective-permute-start.1
  7.5 0.8 %shard_map.103 = (bf16[640,320]{1,0:T(8,128)(2,1)S(1)}, bf16[8,8,256]{2,1,0:T(8,128)(2,1)S(1)}) custom-call(s32[1,320]{1,0:T(1,128)S(1)} %collective-permute-done.code_ref), custom_call_target="tpu_custom_call" | custom-call | flops 1073741824 | bytes 1024 | tf_op jit(solution)/shard_map/pallas_call | solution.py:287
  8.3 0.0 collective-permute-done.3
  8.4 0.0 collective-permute-done.2.refs_2_.refs_4_
  8.4 0.5 %collective-permute-start.6 = (bf16[320,256]{1,0:T(8,128)(2,1)S(1)}, bf16[320,256]{1,0:T(8,128)(2,1)S(1)}, u32[]{:S(2)}, u32[]{:S(2)}) collective-permute-start(bf16[320,256]{1,0:T(8,128)(2,1)S(1)} %collective-permute-done.2.refs_2_.refs_4_), channel_id=1, source_target_pairs={{0,8},{8,0},{16,24},{24,16},{1,9},{9,1},{17,25},{25,17},{2,10},{10... | collective-permute-start | bytes 491528 | tf_op jit(solution)/shard_map/ppermute | solution.py:304
  8.9 0.1 pad_add_fusion
  9.0 0.0 collective-permute-start.4
  9.0 0.1 collective-permute-done.1.refs_1_.refs_3_
  9.1 0.0 copy-done.2
  9.1 0.5 %shard_map.104 = (f32[3,320,320]{2,1,0:T(8,128)S(1)}, f32[8,320]{1,0:T(8,128)S(1)}) custom-call(bf16[320,256]{1,0:T(8,128)(2,1)S(1)} %copy-done.2, bf16[320,256]{1,0:T(8,128)(2,1)S(1)} %copy-done.3, bf16[320,256]{1,0:T(8,128)(2,1)S(1)} %collective-permute-done.1.refs_1_.refs_3_, bf16[320,256]{1,0:T(8,128)(2,1)S(1)} %collective-permute-done.2.refs_2_.refs_4_), custom_call_target="tpu_custom_call" | custom-call | flops 536870912 | bytes 1024 | tf_op jit(solution)/shard_map/pallas_call | solution.py:287
  9.6 0.5 %collective-permute-done.4 = s32[640]{0:T(1024)S(1)} collective-permute-done((s32[640]{0:T(1024)S(1)}, s32[640]{0:T(1024)S(1)}, u32[]{:S(2)}, u32[]{:S(2)}) %collective-permute-start.4) | collective-permute-done | bytes 2592 | tf_op jit(solution)/shard_map/ppermute | solution.py:304
  10.1 0.4 %shard_map.105 = (f32[4,320,128]{2,1,0:T(8,128)S(1)}, f32[3,320,320]{2,1,0:T(8,128)S(1)}, f32[8,320]{1,0:T(8,128)S(1)}) custom-call(f32[3,320,320]{2,1,0:T(8,128)S(1)} %get-tuple-element.40.e_ref, s32[1,640]{1,0:T(1,128)S(1)} %reshape.22.near_ref, s32[1,640]{1,0:T(1,128)S(1)} %reshape.23.mate_ref), custom_call_target="tpu_custom_call" | custom-call | bytes 1024 | tf_op jit(solution)/shard_map/pallas_call | solution.py:287
  10.5 1.1 %collective-permute-done.5.refs_1_ = bf16[320,256]{1,0:T(8,128)(2,1)S(1)} collective-permute-done((bf16[320,256]{1,0:T(8,128)(2,1)}, bf16[320,256]{1,0:T(8,128)(2,1)S(1)}, u32[]{:S(2)}, u32[]{:S(2)}) %collective-permute-start.5) | collective-permute-done | bytes 163872 | tf_op jit(solution)/shard_map/ppermute | solution.py:304
  11.6 0.0 collective-permute-done.6.refs_5_.refs_3_
  11.6 1.5 %shard_map.106 = (f32[320,256]{1,0:T(8,128)S(1)}, f32[320,256]{1,0:T(8,128)S(1)}, f32[1,320,320]{2,1,0:T(8,128)S(1)}, f32[8,320]{1,0:T(8,128)S(1)}) custom-call(bf16[320,256]{1,0:T(8,128)(2,1)S(1)} %copy-done.2, bf16[320,256]{1,0:T(8,128)(2,1)S(1)} %collective-permute-done.5.refs_1_, bf16[320,256]{1,0:T(8,128)(2,1)S(1)} %copy-done.3, ...), custom_call_target="tpu_custom_call" | custom-call | bytes 1024 | tf_op jit(solution)/shard_map/pallas_call | solution.py:287
  13.2 0.4 %shard_map.108 = bf16[640,256]{1,0:T(8,128)(2,1)S(1)} custom-call(bf16[640,320]{1,0:T(8,128)(2,1)S(1)} %get-tuple-element.49.pick_ref, bf16[640,320]{1,0:T(8,128)(2,1)S(1)} %get-tuple-element.50.mate_pick_ref, f32[320,256]{1,0:T(8,128)S(1)} %get-tuple-element.51.mine_ref, f32[320,256]{1,0:T(8,128)S(1)} %get-tuple-element.52.mate_ref), custom_call_target="tpu_custom_call" | custom-call | bytes 1024 | tf_op jit(solution)/shard_map/pallas_call | solution.py:287
  13.5 0.1 collective-permute-start.7
  13.6 0.5 %shard_map.109.keep_ref = f32[640,256]{1,0:T(8,128)S(1)} custom-call(bf16[640,320]{1,0:T(8,128)(2,1)S(1)} %get-tuple-element.49.pick_ref, bf16[640,320]{1,0:T(8,128)(2,1)S(1)} %get-tuple-element.50.mate_pick_ref, f32[320,256]{1,0:T(8,128)S(1)} %get-tuple-element.51.mine_ref, f32[320,256]{1,0:T(8,128)S(1)} %get-tuple-element.52.mate_ref), custom_call_target="tpu_custom_call" | custom-call | flops 536870912 | bytes 1024 | tf_op jit(solution)/shard_map/pallas_call | solution.py:287
  14.1 1.3 %shard_map.107 = (f32[320,256]{1,0:T(8,128)}, f32[320]{0:T(512)}) custom-call(f32[3,320,320]{2,1,0:T(8,128)S(1)} %get-tuple-element.42.refs_7_.e_ref, f32[1,320,320]{2,1,0:T(8,128)S(1)} %get-tuple-element.46.late_ref, f32[8,320]{1,0:T(8,128)S(1)} %get-tuple-element.47.factor_ref, bf16[320,256]{1,0:T(8,128)(2,1)S(1)} %copy-done.3, ...), custom_call_target="tpu_custom_call" | custom-call | flops 1073741824 | bytes 1024 | tf_op jit(solution)/shard_map/pallas_call | solution.py:287
  15.4 0.0 collective-permute-done.7.given_ref
  15.4 0.3 %shard_map.110 = (bf16[2,88,256]{2,1,0:T(8,128)(2,1)S(1)}, bf16[2,88,256]{2,1,0:T(8,128)(2,1)S(1)}, bf16[88,256]{1,0:T(8,128)(2,1)S(1)}, bf16[88,256]{1,0:T(8,12...) custom-call(f32[640,256]{1,0:T(8,128)S(1)} %shard_map.109.keep_ref, ...), custom_call_target="tpu_custom_call" | custom-call | bytes 1024 | tf_op jit(solution)/shard_map/pallas_call | solution.py:287
  15.7 0.0 copy-start
  15.7 0.0 copy-start.1
  15.7 2.9 %collective-permute-start.8 = (bf16[2,88,256]{2,1,0:T(8,128)(2,1)S(1)}, bf16[2,88,256]{2,1,0:T(8,128)(2,1)S(1)}, u32[]{:S(2)}, u32[]{:S(2)}) collective-permute-start(bf16[2,88,256]{2,1,0:T(8,128)(2,1)S(1)} %get-tuple-element.59), channel_id=1, source_target_pairs={{0,4},{1,5},{2,6},{3,7},{4,0},{5,1},{6,2},{7,3},{8,13},{9,12},{10,... | collective-permute-start | bytes 270344 | tf_op jit(solution)/shard_map/ppermute | solution.py:428
  18.6 1.3 %collective-permute-start.9 = (bf16[2,88,256]{2,1,0:T(8,128)(2,1)S(1)}, bf16[2,88,256]{2,1,0:T(8,128)(2,1)S(1)}, u32[]{:S(2)}, u32[]{:S(2)}) collective-permute-start(bf16[2,88,256]{2,1,0:T(8,128)(2,1)S(1)} %get-tuple-element.60), channel_id=1, source_target_pairs={{0,6},{1,7},{2,4},{3,5},{4,2},{5,3},{6,0},{7,1},{8,15},{9,14},{10,... | collective-permute-start | bytes 270344 | tf_op jit(solution)/shard_map/ppermute | solution.py:428
  20.0 1.2 %collective-permute-start.10 = (bf16[88,256]{1,0:T(8,128)(2,1)S(1)}, bf16[88,256]{1,0:T(8,128)(2,1)S(1)}, u32[]{:S(2)}, u32[]{:S(2)}) collective-permute-start(bf16[88,256]{1,0:T(8,128)(2,1)S(1)} %get-tuple-element.61), channel_id=1, source_target_pairs={{0,3},{1,2},{2,1},{3,0},{4,7},{5,6},{6,5},{7,4},{8,11},{9,10},{10,... | collective-permute-start | bytes 135176 | tf_op jit(solution)/shard_map/ppermute | solution.py:304
  21.1 0.5 %collective-permute-start.11 = (bf16[88,256]{1,0:T(8,128)(2,1)S(1)}, bf16[88,256]{1,0:T(8,128)(2,1)S(1)}, u32[]{:S(2)}, u32[]{:S(2)}) collective-permute-start(bf16[88,256]{1,0:T(8,128)(2,1)S(1)} %get-tuple-element.62), channel_id=1, source_target_pairs={{0,1},{1,0},{2,3},{3,2},{4,5},{5,4},{6,7},{7,6},{8,9},{9,8},{10,11... | collective-permute-start | bytes 135176 | tf_op jit(solution)/shard_map/ppermute | solution.py:304
  21.7 1.8 %collective-permute-start.12 = (bf16[88,256]{1,0:T(8,128)(2,1)S(1)}, bf16[88,256]{1,0:T(8,128)(2,1)S(1)}, u32[]{:S(2)}, u32[]{:S(2)}) collective-permute-start(bf16[88,256]{1,0:T(8,128)(2,1)S(1)} %get-tuple-element.63), channel_id=1, source_target_pairs={{0,2},{1,3},{2,0},{3,1},{4,6},{5,7},{6,4},{7,5},{8,10},{9,11},{10,... | collective-permute-start | bytes 135176 | tf_op jit(solution)/shard_map/ppermute | solution.py:304
  23.5 0.0 collective-permute-done.8.refs_1_
  23.5 0.9 %collective-permute-start.13 = (bf16[88,256]{1,0:T(8,128)(2,1)S(1)}, bf16[88,256]{1,0:T(8,128)(2,1)S(1)}, u32[]{:S(2)}, u32[]{:S(2)}) collective-permute-start(bf16[88,256]{1,0:T(8,128)(2,1)S(1)} %slice_bitcast_fusion.1), channel_id=1, source_target_pairs={{0,8},{8,0},{16,24},{24,16},{1,9},{9,1},{17,25},{25,17},{2,10},{10... | collective-permute-start | bytes 135176 | tf_op jit(solution)/shard_map/ppermute | solution.py:304
  24.4 1.6 %collective-permute-done.9.refs_2_ = bf16[2,88,256]{2,1,0:T(8,128)(2,1)S(1)} collective-permute-done((bf16[2,88,256]{2,1,0:T(8,128)(2,1)S(1)}, bf16[2,88,256]{2,1,0:T(8,128)(2,1)S(1)}, u32[]{:S(2)}, u32[]{:S(2)}) %collective-permute-start.9) | collective-permute-done | bytes 90144 | tf_op jit(solution)/shard_map/ppermute | solution.py:428
  26.0 0.9 %collective-permute-start.14 = (bf16[88,256]{1,0:T(8,128)(2,1)S(1)}, bf16[88,256]{1,0:T(8,128)(2,1)S(1)}, u32[]{:S(2)}, u32[]{:S(2)}) collective-permute-start(bf16[88,256]{1,0:T(8,128)(2,1)S(1)} %slice_bitcast_fusion), channel_id=1, source_target_pairs={{0,8},{8,0},{16,24},{24,16},{1,9},{9,1},{17,25},{25,17},{2,10},{10... | collective-permute-start | bytes 135176 | tf_op jit(solution)/shard_map/ppermute | solution.py:304
  26.9 0.5 %shard_map.111.refs_0_ = f32[640,256]{1,0:T(8,128)S(1)} custom-call(bf16[88,256]{1,0:T(8,128)(2,1)S(1)} %get-tuple-element.58.refs_0_, bf16[2,88,256]{2,1,0:T(8,128)(2,1)S(1)} %collective-permute-done.8.refs_1_, bf16[2,88,256]{2,1,0:T(8,128)(2,1)S(1)} %collective-permute-done.9.refs_2_), custom_call_target="tpu_custom_call" | custom-call | flops 268435456 | bytes 1024 | tf_op jit(solution)/shard_map/pallas_call | solution.py:287
  27.4 0.3 %collective-permute-done.10.refs_1_ = bf16[88,256]{1,0:T(8,128)(2,1)S(1)} collective-permute-done((bf16[88,256]{1,0:T(8,128)(2,1)S(1)}, bf16[88,256]{1,0:T(8,128)(2,1)S(1)}, u32[]{:S(2)}, u32[]{:S(2)}) %collective-permute-start.10) | collective-permute-done | bytes 45088 | tf_op jit(solution)/shard_map/ppermute | solution.py:304
  27.7 0.0 collective-permute-done.11.refs_2_
  27.7 0.5 %shard_map.112.refs_0_ = f32[640,256]{1,0:T(8,128)S(1)} custom-call(f32[640,256]{1,0:T(8,128)S(1)} %shard_map.111.refs_0_, bf16[88,256]{1,0:T(8,128)(2,1)S(1)} %collective-permute-done.10.refs_1_, bf16[88,256]{1,0:T(8,128)(2,1)S(1)} %collective-permute-done.11.refs_2_), custom_call_target="tpu_custom_call" | custom-call | flops 268435456 | bytes 1024 | tf_op jit(solution)/shard_map/pallas_call | solution.py:287
  28.2 0.0 collective-permute-done.12.refs_1_
  28.2 0.0 collective-permute-done.13.refs_2_
  28.2 0.0 collective-permute-done.14.refs_3_
  28.3 0.0 copy-done.1
  28.3 1.6 %shard_map.113 = (f32[640,256]{1,0:T(8,128)}, f32[640,256]{1,0:T(8,128)}) custom-call(f32[640,256]{1,0:T(8,128)S(1)} %shard_map.112.refs_0_, bf16[88,256]{1,0:T(8,128)(2,1)S(1)} %collective-permute-done.12.refs_1_, bf16[88,256]{1,0:T(8,128)(2,1)S(1)} %collective-permute-done.13.refs_2_, bf16[88,256]{1,0:T(8,128)(2,1)S(1)} %collective-permute-done.14.refs_3_, ...), custom_call_target="tpu_custom_call" | custom-call | tf_op jit(solution)/shard_map/pallas_call | solution.py:473
  (10 shorter events, 0.0 us)
Async XLA Ops:
  0.6 7.7 %collective-permute-start.2 = (bf16[320,256]{1,0:T(8,128)(2,1)}, bf16[320,256]{1,0:T(8,128)(2,1)S(1)}, u32[]{:S(2)}, u32[]{:S(2)}) collective-permute-start(bf16[320,256]{1,0:T(8,128)(2,1)} %refs_0_.5), channel_id=1, source_target_pairs={{0,16},{8,24},{16,0},{24,8},{1,17},{9,25},{17,1},{25,9},{2,18},{10... | collective-permute-start | bytes 491528 | tf_op jit(solution)/shard_map/ppermute | solution.py:304
  4.4 3.0 %collective-permute-start = (s32[1,320]{1,0:T(1,128)S(1)}, s32[1,320]{1,0:T(1,128)S(1)}, u32[]{:S(2)}, u32[]{:S(2)}) collective-permute-start(s32[1,320]{1,0:T(1,128)S(1)} %fusion.2.code_ref), channel_id=1, source_target_pairs={{0,8},{8,0},{16,24},{24,16},{1,9},{9,1},{17,25},{25,17},{2,10},{10... | collective-permute-start | bytes 3848 | tf_op jit(solution)/shard_map/ppermute | solution.py:304
  4.5 3.9 %collective-permute-start.3 = (s32[320]{0:T(512)}, s32[320]{0:T(512)S(1)}, u32[]{:S(2)}, u32[]{:S(2)}) collective-permute-start(s32[320]{0:T(512)} %param.11), channel_id=1, source_target_pairs={{0,16},{8,24},{16,0},{24,8},{1,17},{9,25},{17,1},{25,9},{2,18},{10... | collective-permute-start | bytes 3848 | tf_op jit(solution)/shard_map/ppermute | solution.py:304
  4.6 7.1 %collective-permute-start.5 = (bf16[320,256]{1,0:T(8,128)(2,1)}, bf16[320,256]{1,0:T(8,128)(2,1)S(1)}, u32[]{:S(2)}, u32[]{:S(2)}) collective-permute-start(bf16[320,256]{1,0:T(8,128)(2,1)} %refs_0_.4), channel_id=1, source_target_pairs={{0,16},{8,24},{16,0},{24,8},{1,17},{9,25},{17,1},{25,9},{2,18},{10... | collective-permute-start | bytes 491528 | tf_op jit(solution)/shard_map/ppermute | solution.py:304
  7.4 1.5 %copy-start.4 = (s32[320]{0:T(512)S(1)}, s32[320]{0:T(512)}, u32[]{:S(2)}) copy-start(s32[320]{0:T(512)} %param.11) | copy-start | bytes 3844
  7.4 1.7 %copy-start.2 = (bf16[320,256]{1,0:T(8,128)(2,1)S(1)}, bf16[320,256]{1,0:T(8,128)(2,1)}, u32[]{:S(2)}) copy-start(bf16[320,256]{1,0:T(8,128)(2,1)} %refs_0_.4) | copy-start | bytes 491524
  7.4 1.7 %copy-start.3 = (bf16[320,256]{1,0:T(8,128)(2,1)S(1)}, bf16[320,256]{1,0:T(8,128)(2,1)}, u32[]{:S(2)}) copy-start(bf16[320,256]{1,0:T(8,128)(2,1)} %refs_0_.5) | copy-start | bytes 491524
  7.4 1.7 %collective-permute-start.1 = (bf16[320,256]{1,0:T(8,128)(2,1)}, bf16[320,256]{1,0:T(8,128)(2,1)S(1)}, u32[]{:S(2)}, u32[]{:S(2)}) collective-permute-start(bf16[320,256]{1,0:T(8,128)(2,1)} %refs_0_.5), channel_id=1, source_target_pairs={{0,8},{8,0},{16,24},{24,16},{1,9},{9,1},{17,25},{25,17},{2,10},{10... | collective-permute-start | bytes 491528 | tf_op jit(solution)/shard_map/ppermute | solution.py:304
  8.4 3.3 %collective-permute-start.6 = (bf16[320,256]{1,0:T(8,128)(2,1)S(1)}, bf16[320,256]{1,0:T(8,128)(2,1)S(1)}, u32[]{:S(2)}, u32[]{:S(2)}) collective-permute-start(bf16[320,256]{1,0:T(8,128)(2,1)S(1)} %collective-permute-done.2.refs_2_.refs_4_), channel_id=1, source_target_pairs={{0,8},{8,0},{16,24},{24,16},{1,9},{9,1},{17,25},{25,17},{2,10},{10... | collective-permute-start | bytes 491528 | tf_op jit(solution)/shard_map/ppermute | solution.py:304
  9.0 1.2 %collective-permute-start.4 = (s32[640]{0:T(1024)S(1)}, s32[640]{0:T(1024)S(1)}, u32[]{:S(2)}, u32[]{:S(2)}) collective-permute-start(s32[640]{0:T(1024)S(1)} %pad_add_fusion), channel_id=1, source_target_pairs={{0,8},{8,0},{16,24},{24,16},{1,9},{9,1},{17,25},{25,17},{2,10},{10... | collective-permute-start | bytes 7688 | tf_op jit(solution)/shard_map/ppermute | solution.py:304
  13.5 1.9 %collective-permute-start.7 = (bf16[640,256]{1,0:T(8,128)(2,1)S(1)}, bf16[640,256]{1,0:T(8,128)(2,1)S(1)}, u32[]{:S(2)}, u32[]{:S(2)}) collective-permute-start(bf16[640,256]{1,0:T(8,128)(2,1)S(1)} %shard_map.108), channel_id=1, source_target_pairs={{0,8},{8,0},{16,24},{24,16},{1,9},{9,1},{17,25},{25,17},{2,10},{10... | collective-permute-start | bytes 983048 | tf_op jit(solution)/shard_map/ppermute | solution.py:304
  15.7 12.5 %copy-start = (f32[640,256]{1,0:T(8,128)S(1)}, f32[640,256]{1,0:T(8,128)}, u32[]{:S(2)}) copy-start(f32[640,256]{1,0:T(8,128)} %refs_4_.1) | copy-start | bytes 1966084
  15.7 12.5 %copy-start.1 = (f32[640,256]{1,0:T(8,128)S(1)}, f32[640,256]{1,0:T(8,128)}, u32[]{:S(2)}) copy-start(f32[640,256]{1,0:T(8,128)} %refs_5_.1) | copy-start | bytes 1966084
  15.7 7.7 %collective-permute-start.8 = (bf16[2,88,256]{2,1,0:T(8,128)(2,1)S(1)}, bf16[2,88,256]{2,1,0:T(8,128)(2,1)S(1)}, u32[]{:S(2)}, u32[]{:S(2)}) collective-permute-start(bf16[2,88,256]{2,1,0:T(8,128)(2,1)S(1)} %get-tuple-element.59), channel_id=1, source_target_pairs={{0,4},{1,5},{2,6},{3,7},{4,0},{5,1},{6,2},{7,3},{8,13},{9,12},{10,... | collective-permute-start | bytes 270344 | tf_op jit(solution)/shard_map/ppermute | solution.py:428
  18.6 7.4 %collective-permute-start.9 = (bf16[2,88,256]{2,1,0:T(8,128)(2,1)S(1)}, bf16[2,88,256]{2,1,0:T(8,128)(2,1)S(1)}, u32[]{:S(2)}, u32[]{:S(2)}) collective-permute-start(bf16[2,88,256]{2,1,0:T(8,128)(2,1)S(1)} %get-tuple-element.60), channel_id=1, source_target_pairs={{0,6},{1,7},{2,4},{3,5},{4,2},{5,3},{6,0},{7,1},{8,15},{9,14},{10,... | collective-permute-start | bytes 270344 | tf_op jit(solution)/shard_map/ppermute | solution.py:428
  20.0 7.7 %collective-permute-start.10 = (bf16[88,256]{1,0:T(8,128)(2,1)S(1)}, bf16[88,256]{1,0:T(8,128)(2,1)S(1)}, u32[]{:S(2)}, u32[]{:S(2)}) collective-permute-start(bf16[88,256]{1,0:T(8,128)(2,1)S(1)} %get-tuple-element.61), channel_id=1, source_target_pairs={{0,3},{1,2},{2,1},{3,0},{4,7},{5,6},{6,5},{7,4},{8,11},{9,10},{10,... | collective-permute-start | bytes 135176 | tf_op jit(solution)/shard_map/ppermute | solution.py:304
  21.1 6.6 %collective-permute-start.11 = (bf16[88,256]{1,0:T(8,128)(2,1)S(1)}, bf16[88,256]{1,0:T(8,128)(2,1)S(1)}, u32[]{:S(2)}, u32[]{:S(2)}) collective-permute-start(bf16[88,256]{1,0:T(8,128)(2,1)S(1)} %get-tuple-element.62), channel_id=1, source_target_pairs={{0,1},{1,0},{2,3},{3,2},{4,5},{5,4},{6,7},{7,6},{8,9},{9,8},{10,11... | collective-permute-start | bytes 135176 | tf_op jit(solution)/shard_map/ppermute | solution.py:304
  21.7 6.6 %collective-permute-start.12 = (bf16[88,256]{1,0:T(8,128)(2,1)S(1)}, bf16[88,256]{1,0:T(8,128)(2,1)S(1)}, u32[]{:S(2)}, u32[]{:S(2)}) collective-permute-start(bf16[88,256]{1,0:T(8,128)(2,1)S(1)} %get-tuple-element.63), channel_id=1, source_target_pairs={{0,2},{1,3},{2,0},{3,1},{4,6},{5,7},{6,4},{7,5},{8,10},{9,11},{10,... | collective-permute-start | bytes 135176 | tf_op jit(solution)/shard_map/ppermute | solution.py:304
  23.5 4.8 %collective-permute-start.13 = (bf16[88,256]{1,0:T(8,128)(2,1)S(1)}, bf16[88,256]{1,0:T(8,128)(2,1)S(1)}, u32[]{:S(2)}, u32[]{:S(2)}) collective-permute-start(bf16[88,256]{1,0:T(8,128)(2,1)S(1)} %slice_bitcast_fusion.1), channel_id=1, source_target_pairs={{0,8},{8,0},{16,24},{24,16},{1,9},{9,1},{17,25},{25,17},{2,10},{10... | collective-permute-start | bytes 135176 | tf_op jit(solution)/shard_map/ppermute | solution.py:304
  26.0 2.3 %collective-permute-start.14 = (bf16[88,256]{1,0:T(8,128)(2,1)S(1)}, bf16[88,256]{1,0:T(8,128)(2,1)S(1)}, u32[]{:S(2)}, u32[]{:S(2)}) collective-permute-start(bf16[88,256]{1,0:T(8,128)(2,1)S(1)} %slice_bitcast_fusion), channel_id=1, source_target_pairs={{0,8},{8,0},{16,24},{24,16},{1,9},{9,1},{17,25},{25,17},{2,10},{10... | collective-permute-start | bytes 135176 | tf_op jit(solution)/shard_map/ppermute | solution.py:304
